TPU v7x, 32 devices: a whole 2x2x4 slice. The times are simulated.
32 devices in a mesh: gx: 4 (over z), gy: 8 (over y, x, core).
Axes of the slice: x: 2, y: 2, z: 4, core: 2. Of those that a mesh axis runs over, the one named last changes fastest.
Arguments:
- tokens: bfloat16 [1024, 2048], P('gx', 'gy'), may hold values from -6 to 6
- attention_gain: float32 [2048], replicated, may hold values from 0.1 to 1.9
- projection_weight: bfloat16 [2048, 3, 2048], P('gx', None, 'gy'), may hold values from -0.21875 to 0.21875
- output_weight: bfloat16 [2048, 2048], P('gx', 'gy'), may hold values from -0.125 to 0.125
- prompt_cache: bfloat16 [8, 2, 8192, 2048], P('gx', None, None, 'gy'), may hold values from -500 to 500
- cache_length: int32 [8], P('gx'), may hold values from 512 to 8192, as said below
- prompt_group: int32 [16], P('gx'), may hold values from 0 to 7, as said below
- parents: int32 [16, 64], P('gx'), may hold values from -1 to 62, as said below
- accepted_path: int32 [16, 8], P('gx'), may hold values from 0 to 63, as said below
- expert_gain: float32 [2048], replicated, may hold values from 0.1 to 1.9
- gate_up_weight: bfloat16 [32, 2048, 2, 1024], P('gy', None, None, 'gx'), may hold values from -0.125 to 0.125
- down_weight: bfloat16 [32, 1024, 2048], P('gy', 'gx'), may hold values from -0.1875 to 0.1875
- route_experts: int32 [1024, 8], replicated, may hold values from 0 to 31, all different within a row; in each aligned block of 256 rows (0 to 255, 256 to 511, ...) at most 80 rows name the same one
- route_gates: bfloat16 [1024, 8], replicated, may hold values from 0.049804688 to 0.5
Outputs:
- mixed: bfloat16 [1024, 2048], P('gx', 'gy')
- compacted: bfloat16 [128, 2, 2048], P('gx', None, 'gy')
Inputs may be any that keep to these rules, and one draw needn't show every extreme that they name: `cache_length`: one group in every draw has exactly 8192 valid slots. `prompt_group`: request r belongs to one of the 2 groups (r // 4) * 2 to (r // 4) * 2 + 1. `parents`: node 0 of each tree is its root with parent -1; every other node's parent is a node of lower number. `accepted_path`: each row starts at node 0, rises strictly, and each entry after the first is a child of the entry before it. `route_experts`: each row names 8 different experts; in each aligned block of 256 rows no expert is named by more than 80 rows.
All inputs are finite; a program needn't handle non-finite values.
Results may differ from a plain program's by a relative error of at most 0.012.
The roundings to bfloat16 on the way count: a program that leaves them out, or rounds other values in their place, can miss the bound.
Values may be sent and summed in bfloat16 or wider, within the bound.
No kernel may reach another device: no remote copies, remote signals or barrier semaphores. Data moves between devices by JAX's collectives and lax.ppermute only.
A program may use at most 128 MiB of HBM per device.

v0:
```python
import math

import jax
import jax.numpy as jnp
from jax import lax
from jax.sharding import PartitionSpec as P

HD = 128
ROUTE_MOST = 80


def rms_scale(values, gain):
    values = values.astype(jnp.float32)
    mean_square = jnp.mean(values * values, axis=-1, keepdims=True)
    return values * lax.rsqrt(mean_square + 1e-05) * gain


def ancestor_table(parents):
    nodes = parents.shape[-1]
    column = jnp.arange(nodes, dtype=jnp.int32)
    reach = (parents[:, :, None] == column[None, None, :]).astype(jnp.float32)
    reach = reach + jnp.eye(nodes, dtype=jnp.float32)[None]
    for square in range((nodes - 1).bit_length()):
        reach = jnp.minimum(
            jnp.einsum("rij,rjk->rik", reach, reach, precision=lax.Precision.HIGHEST), 1.0
        )
    return reach


def attend_request(query, key_new, value_new, cache_keys, cache_values, length, reach):
    scale = 1.0 / math.sqrt(query.shape[-1])
    cached = (
        jnp.einsum("qhd,khd->hqk", query, cache_keys, preferred_element_type=jnp.float32) * scale
    )
    drafted = jnp.einsum("qhd,khd->hqk", query, key_new, preferred_element_type=jnp.float32) * scale
    visible = jnp.arange(cache_keys.shape[0], dtype=jnp.int32) < length
    cached = jnp.where(visible[None, None, :], cached, -jnp.inf)
    drafted = jnp.where(reach[None] > 0, drafted, -jnp.inf)
    scores = jnp.concatenate([cached, drafted], axis=-1)
    highest = jnp.max(scores, axis=-1, keepdims=True)
    powered = jnp.exp(scores - highest)
    weights = (powered / jnp.sum(powered, axis=-1, keepdims=True)).astype(jnp.bfloat16)
    width = cache_keys.shape[0]
    mixed = jnp.einsum(
        "hqk,khd->qhd", weights[..., :width], cache_values, preferred_element_type=jnp.float32
    )
    mixed = mixed + jnp.einsum(
        "hqk,khd->qhd", weights[..., width:], value_new, preferred_element_type=jnp.float32
    )
    return mixed.astype(jnp.bfloat16)


def full_features(local_part):
    return lax.all_gather(local_part, "gy", axis=1, tiled=True)


def per_device(
    tokens,
    attention_gain,
    projection_weight,
    output_weight,
    prompt_cache,
    cache_length,
    prompt_group,
    parents,
    accepted_path,
    expert_gain,
    gate_up_weight,
    down_weight,
    route_experts,
    route_gates,
):
    full_tokens = full_features(tokens)
    normed = rms_scale(full_tokens, attention_gain).astype(jnp.bfloat16)
    projection_full, output_full = (
        lax.all_gather(projection_weight, "gx", axis=0, tiled=True),
        lax.all_gather(output_weight, "gx", axis=0, tiled=True),
    )
    projected = jnp.einsum(
        "td,dcn->tcn", normed, projection_full, preferred_element_type=jnp.float32
    ).astype(jnp.bfloat16)
    request_count = parents.shape[0]
    draft_count = parents.shape[1]
    heads_width = projected.shape[2]
    local_heads = heads_width // HD
    per_request = projected.reshape(request_count, draft_count, 3, heads_width)
    picked = jnp.take_along_axis(per_request[:, :, 1:], accepted_path[:, :, None, None], axis=1)
    compacted = picked.reshape(-1, 2, heads_width)
    reach = ancestor_table(parents)
    groups_local = prompt_cache.shape[0]
    cache_slots = prompt_cache.shape[2]
    local_group = prompt_group % groups_local
    split = per_request.reshape(request_count, draft_count, 3, local_heads, HD)
    cache_split = prompt_cache.reshape(groups_local, 2, cache_slots, local_heads, HD)

    def one_request(inputs):
        query, key_new, value_new, group, reach_one = inputs
        pair = lax.dynamic_index_in_dim(cache_split, group, 0, keepdims=False)
        length = lax.dynamic_index_in_dim(cache_length, group, 0, keepdims=False)
        return attend_request(query, key_new, value_new, pair[0], pair[1], length, reach_one)

    attended = lax.map(
        one_request, (split[:, :, 0], split[:, :, 1], split[:, :, 2], local_group, reach)
    )
    attended = attended.reshape(request_count * draft_count, heads_width)
    head_terms = lax.dot_general(
        attended, output_full, (((1,), (1,)), ((), ())), preferred_element_type=jnp.float32
    )
    attention_out = lax.psum_scatter(head_terms, "gy", scatter_dimension=1, tiled=True)
    stream = (tokens.astype(jnp.float32) + attention_out).astype(jnp.bfloat16)
    full_stream = full_features(stream)
    expert_input = rms_scale(full_stream, expert_gain).astype(jnp.bfloat16)
    all_rows = lax.all_gather(expert_input, "gx", axis=0, tiled=True)
    total_tokens = route_experts.shape[0]
    width = all_rows.shape[1]
    gx_count = lax.axis_size("gx")
    gy_count = lax.axis_size("gy")
    block_tokens = total_tokens // gx_count
    expert_count = gate_up_weight.shape[0]
    expert_ids = lax.axis_index("gy") * expert_count + jnp.arange(expert_count, dtype=jnp.int32)
    hit = route_experts[:, :, None] == expert_ids[None, None, :]
    match = jnp.sum(hit.astype(jnp.int32), axis=1).reshape(gx_count, block_tokens, expert_count)
    weight = jnp.sum(jnp.where(hit, route_gates.astype(jnp.float32)[:, :, None], 0.0), axis=1)
    weight = weight.reshape(gx_count, block_tokens, expert_count)
    position = jnp.cumsum(match, axis=1) - match
    slot_ids = jnp.arange(ROUTE_MOST, dtype=jnp.int32)
    selected = (position[:, :, :, None] == slot_ids) & (match[:, :, :, None] > 0)
    local_token = jnp.arange(block_tokens, dtype=jnp.int32)[None, :, None, None]
    block_start = (jnp.arange(gx_count, dtype=jnp.int32) * block_tokens)[:, None, None]
    slot_index = jnp.sum(jnp.where(selected, local_token, 0), axis=1) + block_start
    slot_gate = jnp.sum(jnp.where(selected, weight[:, :, :, None], 0.0), axis=1)
    slot_index = jnp.transpose(slot_index, (1, 0, 2))
    slot_gate = jnp.transpose(slot_gate, (1, 0, 2))
    packed = jnp.take(all_rows, slot_index.reshape(-1), axis=0).reshape(
        expert_count, gx_count * ROUTE_MOST, width
    )
    both = jnp.einsum("esd,edgf->esgf", packed, gate_up_weight, preferred_element_type=jnp.float32)
    hidden = (jax.nn.silu(both[:, :, 0]) * both[:, :, 1]).astype(jnp.bfloat16)
    partial_value = jnp.einsum(
        "esf,efd->esd", hidden, down_weight, preferred_element_type=jnp.float32
    )
    partial_value = (
        partial_value * slot_gate.reshape(expert_count, gx_count * ROUTE_MOST)[:, :, None]
    )
    summed = jax.ops.segment_sum(
        partial_value.reshape(-1, width), slot_index.reshape(-1), num_segments=total_tokens
    )
    feature_width = width // gy_count
    arranged = summed.reshape(gx_count, block_tokens, gy_count, feature_width)
    arranged = jnp.transpose(arranged, (0, 2, 1, 3)).reshape(
        gx_count * gy_count * block_tokens, feature_width
    )
    expert_out = lax.psum_scatter(arranged, ("gx", "gy"), scatter_dimension=0, tiled=True)
    mixed = (stream.astype(jnp.float32) + expert_out).astype(jnp.bfloat16)
    return (mixed, compacted)


def solution(mesh):
    placed = (
        P("gx", "gy"),
        P(),
        P("gx", None, "gy"),
        P("gx", "gy"),
        P("gx", None, None, "gy"),
        P("gx"),
        P("gx"),
        P("gx", None),
        P("gx", None),
        P(),
        P("gy", None, None, "gx"),
        P("gy", "gx", None),
        P(),
        P(),
    )
    return jax.shard_map(
        per_device,
        mesh=mesh,
        in_specs=placed,
        out_specs=(P("gx", "gy"), P("gx", None, "gy")),
        check_vma=False,
    )
```

profile of v0, /device:TPU:0, one launch (start us, length us, event | category | flops | bytes accessed | tf_op | source)
XLA Modules:
  0.0 532.8 jit_solution(3741729409115928963)
XLA Ops:
  7.2 0.7 all-gather.6.cloned.1.call-update
  7.9 0.7 all-gather.8.cloned.1.call-update
  8.7 0.7 all-gather.10.cloned.1.call-update
  9.5 21.2 %copy.56 = bf16[2,2,8192,256]{2,3,1,0:T(8,128)(2,1)} copy(bf16[2,2,8192,256]{3,2,1,0:T(8,128)(2,1)} %param.20) | data formatting | bytes 33554432 | tf_op args[4]
  32.4 3.8 all-gather.6.cloned.1.call-done
  36.2 1.5 fusion.30
  37.7 63.5 %all-gather.8.cloned.1.call-done = bf16[2048,3,256]{2,0,1:T(8,128)(2,1)} async-done(((bf16[512,3,256]{2,0,1:T(8,128)(2,1)}), bf16[2048,3,256]{2,0,1:T(8,128)(2,1)}) %all-gather.8.cloned.1.call-update) | async-done | bytes 3145744 | tf_op jit(solution)/shard_map/all_gather | solution.py:76
  101.2 3.3 convolution_convert_fusion
  105.0 51.6 %while.10 = (s32[]{:T(128)}, bf16[4,64,2,128]{3,2,1,0:T(2,128)(2,1)S(1)}, s32[4]{0:T(128)S(1)}, bf16[2,2,8192,2,128]{2,4,3,1,0:T(8,128)(2,1)}, s32[2]{0:T(128)S(...) while((s32[]{:T(128)}, ...), condition=%wide.region_5.6_spmd, body=%wide.region_1.5_spmd.sunk | while | flops 551677696 | bytes 25725152 | solution.py:102
  108.2 0.7 iota_compare_fusion.6
  108.8 3.5 fusion.91
  112.6 0.8 fusion.92
  113.3 0.7 divide_convert_fusion.2
  114.1 3.8 fusion.93
  121.1 0.7 iota_compare_fusion.6
  121.8 3.4 fusion.91
  125.5 0.8 fusion.92
  126.3 0.7 divide_convert_fusion.2
  127.0 3.7 fusion.93
  134.0 0.7 iota_compare_fusion.6
  134.7 3.4 fusion.91
  138.4 0.8 fusion.92
  139.1 0.7 divide_convert_fusion.2
  139.9 3.7 fusion.93
  146.9 0.7 iota_compare_fusion.6
  147.6 3.4 fusion.91
  151.3 0.8 fusion.92
  152.0 0.7 divide_convert_fusion.2
  152.7 3.7 fusion.93
  156.7 3.1 fusion.47
  159.9 40.1 %reduce-scatter.3.cloned.1.call-done = f32[256,256]{1,0:T(8,128)} async-done(((f32[256,2048]{1,0:T(8,128)}), f32[256,256]{1,0:T(8,128)}) %reduce-scatter.3.cloned.1.call-update) | async-done | bytes 262160 | tf_op jit(solution)/shard_map/reduce_scatter | solution.py:109
  200.0 1.6 add_convert_fusion.1
  201.7 24.3 %all-gather.12.cloned.1.call-done = bf16[256,2048]{1,0:T(8,128)(2,1)} async-done(((bf16[256,256]{1,0:T(8,128)(2,1)}), bf16[256,2048]{1,0:T(8,128)(2,1)}) %all-gather.12.cloned.1.call-update) | async-done | bytes 1048592 | tf_op jit(solution)/shard_map/all_gather | solution.py:54
  226.0 1.5 fusion.33
  227.5 2.5 fusion.35
  230.5 4.8 reduce-window.6
  237.2 73.8 %all-gather.14.cloned.1.call-done = bf16[1024,2048]{1,0:T(8,128)(2,1)} async-done(((bf16[256,2048]{1,0:T(8,128)(2,1)}), bf16[1024,2048]{1,0:T(8,128)(2,1)}) %all-gather.14.cloned.1.call-update) | async-done | bytes 4194320 | tf_op jit(solution)/shard_map/all_gather | solution.py:113
  311.0 13.6 %gather_fusion = bf16[1280,2048]{1,0:T(8,128)(2,1)} fusion(bf16[1024,2048]{1,0:T(8,128)(2,1)} %all-gather.14.cloned.1.call-done, s32[2048]{0:T(1024)S(1)} %pad_clamp_fusion), kind=kCustom, calls=%fused_computation | custom fusion | bytes 10490880 | tf_op jit(solution)/shard_map/jit(_take)/gather | solution.py:134
  324.6 8.0 %fusion.22 = f32[4,320,2,256]{3,1,2,0:T(8,128)S(1)} fusion(bf16[4,2048,2,256]{3,2,1,0:T(2,128)(2,1)} %param.26, bf16[4,320,2048]{2,1,0:T(8,128)(2,1)} %bitcast.137, pred[4,320]{1,0:T(4,128)(4,1)S(1)} %compare_and_fusion), kind=kOutput, calls=%fused_computation.36 | convolution fusion | flops 2686976000 | bytes 16254208 | tf_op jit(solution)/shard_map/esd,edgf->esgf/dot_general | solution.py:137
  332.6 5.7 %broadcast_multiply_fusion = f32[4,320,2048]{2,1,0:T(8,128)} fusion(f32[4,320]{1,0:T(4,128)S(1)} %mul.85, bf16[4,256,2048]{2,1,0:T(8,128)(2,1)S(1)} %copy-done, f32[4,320,2,256]{3,1,2,0:T(8,128)S(1)} %fusion.22), kind=kOutput, calls=%fused_computation.39 | convolution fusion | flops 1346764800 | bytes 17306624 | tf_op jit(solution)/shard_map/esf,efd->esd/dot_general | solution.py:139
  338.2 25.0 %scatter_custom_fusion = f32[1024,2048]{1,0:T(8,128)} fusion(s32[1280]{0:T(1024)S(1)} %reshape.190, f32[1280,2048]{1,0:T(8,128)} %bitcast.136, f32[]{:T(128)} %constant.88.clone.1), kind=kCustom, calls=%fused_computation.42 | custom fusion | flops 2621440 | bytes 8389120 | tf_op jit(solution)/shard_map/scatter-add | solution.py:145
  363.2 7.5 %copy.85 = f32[128,8,8,256]{3,2,1,0:T(8,128)S(1)} copy(f32[128,8,8,256]{3,1,2,0:T(8,128)} %bitcast.134) | data formatting | bytes 16777216
  371.2 5.8 %copy.71 = f32[4,8,256,256]{3,2,1,0:T(8,128)} copy(f32[4,8,256,256]{3,1,2,0:T(8,128)S(1)} %bitcast_bitcast_fusion) | data formatting | bytes 16777216 | tf_op jit(solution)/shard_map/transpose | solution.py:150
  377.1 0.7 copy-done.6
  378.2 0.7 gather_fusion.1
  378.9 0.7 broadcast_select_fusion
  379.6 144.7 %reduce-scatter.5.cloned.1.call-done = f32[256,256]{1,0:T(8,128)} async-done(((f32[8192,256]{1,0:T(8,128)}), f32[256,256]{1,0:T(8,128)}) %reduce-scatter.5.cloned.1.call-update) | async-done | bytes 262160 | tf_op jit(solution)/shard_map/reduce_scatter | solution.py:153
  524.3 1.6 add_convert_fusion
  (110 shorter events, 12.1 us)
Async XLA Ops:
  7.2 29.0 %all-gather.6.cloned.1.call-start = ((), (), s32[]{:S(2)}) async-start(), calls=%async_computation.2 | async-start | bytes 1179648 | tf_op jit(solution)/shard_map/all_gather | solution.py:54
  7.9 93.3 %all-gather.8.cloned.1.call-start = ((), (), s32[]{:S(2)}) async-start(), calls=%async_computation.3 | async-start | bytes 3932160 | tf_op jit(solution)/shard_map/all_gather | solution.py:76
  8.6 148.1 %all-gather.10.cloned.1.call-start = ((), (), s32[]{:S(2)}) async-start(), calls=%async_computation.4 | async-start | bytes 1310720 | tf_op jit(solution)/shard_map/all_gather | solution.py:77
  9.4 190.6 %reduce-scatter.3.cloned.1.call-start = ((), (), s32[]{:S(2)}) async-start(), calls=%async_computation.5 | async-start | bytes 2359296 | tf_op jit(solution)/shard_map/reduce_scatter | solution.py:109
  9.5 21.2 %copy-start.7 = (s32[4,64]{1,0:T(4,128)S(1)}, s32[4,64]{1,0:T(4,128)}, u32[]{:S(2)}) copy-start(s32[4,64]{1,0:T(4,128)} %param.23) | copy-start | bytes 3076
  9.5 22.9 %copy-start.9 = (s32[4]{0:T(128)S(1)}, s32[4]{0:T(128)}, u32[]{:S(2)}) copy-start(s32[4]{0:T(128)} %param.22) | copy-start | bytes 52
  9.5 91.8 %copy-start.8 = (f32[2048]{0:T(1024)S(1)}, f32[2048]{0:T(1024)}, u32[]{:S(2)}) copy-start(f32[2048]{0:T(1024)} %param.17) | copy-start | bytes 24580
  37.7 67.3 %copy-start.10 = (s32[2]{0:T(128)S(1)}, s32[2]{0:T(128)}, u32[]{:S(2)}) copy-start(s32[2]{0:T(128)} %param.21) | copy-start | bytes 28
  156.7 43.3 %copy-start.2 = (bf16[256,256]{1,0:T(8,128)(2,1)S(1)}, bf16[256,256]{1,0:T(8,128)(2,1)}, u32[]{:S(2)}) copy-start(bf16[256,256]{1,0:T(8,128)(2,1)} %param.16) | copy-start | bytes 393220
  156.7 70.9 %copy-start.5 = (f32[2048]{0:T(1024)S(1)}, f32[2048]{0:T(1024)}, u32[]{:S(2)}) copy-start(f32[2048]{0:T(1024)} %param.25) | copy-start | bytes 24580
  159.8 70.5 %copy-start.3 = (s32[1024,8]{0,1:T(8,128)S(1)}, s32[1024,8]{0,1:T(8,128)}, u32[]{:S(2)}) copy-start(s32[1024,8]{0,1:T(8,128)} %param.28) | copy-start | bytes 98308
  159.8 76.8 %copy-start.4 = (bf16[1024,8]{0,1:T(8,128)(2,1)S(1)}, bf16[1024,8]{0,1:T(8,128)(2,1)}, u32[]{:S(2)}) copy-start(bf16[1024,8]{0,1:T(8,128)(2,1)} %param.29) | copy-start | bytes 49156
  159.8 66.2 %all-gather.12.cloned.1.call-start = ((), (), s32[]{:S(2)}) async-start(), calls=%async_computation.6 | async-start | bytes 1179648 | tf_op jit(solution)/shard_map/all_gather | solution.py:54
  201.6 109.4 %all-gather.14.cloned.1.call-start = ((), (), s32[]{:S(2)}) async-start(), calls=%async_computation.7 | async-start | bytes 5242880 | tf_op jit(solution)/shard_map/all_gather | solution.py:113
  230.1 294.2 %reduce-scatter.5.cloned.1.call-start = ((), (), s32[]{:S(2)}) async-start(), calls=%async_computation.8 | async-start | bytes 8650752 | tf_op jit(solution)/shard_map/reduce_scatter | solution.py:153
  324.6 8.0 %copy-start = (bf16[4,256,2048]{2,1,0:T(8,128)(2,1)S(1)}, bf16[4,256,2048]{2,1,0:T(8,128)(2,1)}, u32[]{:S(2)}) copy-start(bf16[4,256,2048]{2,1,0:T(8,128)(2,1)} %param.27) | copy-start | bytes 12582916
  377.0 0.7 copy-start.6
  377.0 147.3 %copy-start.1 = (bf16[256,256]{1,0:T(8,128)(2,1)S(1)}, bf16[256,256]{1,0:T(8,128)(2,1)}, u32[]{:S(2)}) copy-start(bf16[256,256]{1,0:T(8,128)(2,1)} %add_convert_fusion.1) | copy-start | bytes 393220
Sparse Core Ops, SparseCore 0:
  9.9 26.2 all-gather.5
  37.7 63.4 all-gather.7
  102.8 26.6 all-gather.9
  160.0 39.9 reduce-scatter.2
  202.4 23.5 all-gather.11
  230.2 80.7 all-gather.13
  377.2 147.0 reduce-scatter.4
where the time goes:
time: 534 us; the launch traced here: 533 us
  waiting for transfers between devices  352 us (66%)
  local copies, waits for them, and re-layouts  56.5 us (11%)
  matrix products  51.8 us (10%)
  other arithmetic  49.1 us (9%)
  between operations  14.5 us (3%)
  loops' own time  8.02 us (2%)
    reduce_scatter x1, waiting for transfers between devices, per_device(): lax.psum_scatter(arranged, ('gx', 'gy'), scatter_dimension=0, tiled=True)  145 us
    all_gather x1, waiting for transfers between devices, per_device(): all_rows = lax.all_gather(expert_input, 'gx', axis=0, tiled=True)  73.8 us
    all_gather x1, waiting for transfers between devices, per_device(): lax.all_gather(projection_weight, 'gx', axis=0, tiled=True)  63.5 us
    reduce_scatter x1, waiting for transfers between devices, per_device(): lax.psum_scatter(head_terms, 'gy', scatter_dimension=1, tiled=True)  40.1 us
    unnamed x26, local copies, waits for them, and re-layouts  29.7 us
    all_gather x2, waiting for transfers between devices, full_features(): return lax.all_gather(local_part, 'gy', axis=1, tiled=True)  28.1 us
    scatter-add x1, other arithmetic, per_device(): jax.ops.segment_sum(partial_value.reshape(-1, width), slot_index.reshape(...  25 us
    dot_general x4, matrix products, attend_request(): jnp.einsum('hqk,khd->qhd', weights[..., :width], cache_values, preferred_...  15 us
  transfers between devices with their start and end apart: 7, of which 6 were waited for; matrix products, arithmetic and copies ran while one was open for 15% of the time, Pallas kernels for 0%

commit v1 on v0

v1 whole, which is shorter than its diff:
```python
import math

import jax
import jax.numpy as jnp
from jax import lax
from jax.experimental import pallas as pl
from jax.experimental.pallas import tpu as pltpu
from jax.sharding import PartitionSpec as P

HD = 128
CACHE_BLOCK = 2048
VMEM_LIMIT = 56 * 1024 * 1024
BF16 = jnp.bfloat16
F32 = jnp.float32


def vmem():
    return pl.BlockSpec(memory_space=pltpu.VMEM)


def smem():
    return pl.BlockSpec(memory_space=pltpu.SMEM)


def params():
    return pltpu.CompilerParams(vmem_limit_bytes=VMEM_LIMIT)


def swap(value, axis, mask):
    count = lax.axis_size(axis)
    return lax.ppermute(value, axis, [(one, one ^ mask) for one in range(count)])


def ancestor_table(parents):
    nodes = parents.shape[-1]
    column = jnp.arange(nodes, dtype=jnp.int32)
    reach = (parents[:, :, None] == column[None, None, :]).astype(F32)
    reach = reach + jnp.eye(nodes, dtype=F32)[None]
    for _ in range((nodes - 1).bit_length()):
        reach = jnp.minimum(jnp.einsum("rij,rjk->rik", reach, reach), 1.0)
    return reach


def query_kernel(count, ids, gain, weight, *refs):
    pieces, normed, query = refs[:count], refs[count], refs[count + 1]
    me = ids[1]
    width = pieces[0].shape[1]
    total = jnp.zeros((pieces[0].shape[0], 1), F32)
    for piece in pieces:
        value = piece[...].astype(F32)
        total = total + jnp.sum(value * value, axis=1, keepdims=True)
    scale = lax.rsqrt(total / (width * count) + 1e-05)
    for mask, piece in enumerate(pieces):
        columns = pl.ds(pl.multiple_of((me ^ mask) * width, width), width)
        value = piece[...].astype(F32) * scale * gain[:, columns]
        normed[:, columns] = value.astype(BF16)
    query[...] = jnp.dot(normed[...], weight[...], preferred_element_type=F32).astype(BF16)


def blocked_query(query, request, draft, heads):
    rows = query[request * draft : (request + 1) * draft, :]
    if heads == 1:
        return rows
    column = lax.broadcasted_iota(jnp.int32, rows.shape, 1) // HD
    return jnp.concatenate(
        [jnp.where(column == head, rows, jnp.zeros_like(rows)) for head in range(heads)], axis=0
    )


def cache_kernel(requests, draft, heads, lengths, owner, query, cache, top, mass, mixed, wide):
    group, block = pl.program_id(0), pl.program_id(1)
    slots = cache.shape[2]

    @pl.when((group == 0) & (block == 0))
    def _():
        top[...] = jnp.full(top.shape, -jnp.inf, F32)
        mass[...] = jnp.zeros(mass.shape, F32)
        mixed[...] = jnp.zeros(mixed.shape, F32)
        for request in range(requests):
            wide[request] = blocked_query(query[...], request, draft, heads)

    left = lengths[group] - block * slots
    scale = 1.0 / math.sqrt(HD)
    for request in range(requests):

        @pl.when((owner[request] == group) & (left > 0))
        def _():
            scores = (
                lax.dot_general(
                    wide[request],
                    cache[0, 0],
                    (((1,), (1,)), ((), ())),
                    preferred_element_type=F32,
                )
                * scale
            )
            column = lax.broadcasted_iota(jnp.int32, scores.shape, 1)
            scores = jnp.where(column < left, scores, -jnp.inf)
            before = top[request]
            now = jnp.maximum(before, jnp.max(scores, axis=1, keepdims=True))
            powered = jnp.exp(scores - now[:, :1])
            fade = jnp.exp(before - now)
            top[request] = now
            mass[request] = mass[request] * fade + jnp.sum(powered, axis=1, keepdims=True)
            mixed[request] = mixed[request] * fade[:, :1] + jnp.dot(
                powered.astype(BF16), cache[0, 1], preferred_element_type=F32
            )


def draft_kernel(
    requests, draft, heads, count, ids, normed, query, weight, output, reach, rows, top, mass,
    mixed, terms, picked, key, value, attended
):
    me = ids[1]
    parts, depth = weight.shape[0], weight.shape[2]
    for which, kept in ((0, key), (1, value)):
        total = jnp.zeros(kept.shape, F32)
        for part in range(parts):
            total = total + jnp.dot(
                normed[:, part * depth : (part + 1) * depth],
                weight[part, which],
                preferred_element_type=F32,
            )
        kept[...] = total.astype(BF16)
    tokens = key.shape[0]
    chosen = (
        lax.broadcasted_iota(jnp.int32, (rows.shape[0], tokens), 1) == rows[...]
    ).astype(BF16)
    picked[0] = jnp.dot(chosen, key[...], preferred_element_type=F32).astype(BF16)
    picked[1] = jnp.dot(chosen, value[...], preferred_element_type=F32).astype(BF16)
    scale = 1.0 / math.sqrt(HD)
    for request in range(requests):
        own = slice(request * draft, (request + 1) * draft)
        wide = blocked_query(query[...], request, draft, heads)
        scores = (
            lax.dot_general(
                wide, key[own, :], (((1,), (1,)), ((), ())), preferred_element_type=F32
            )
            * scale
        )
        seen = jnp.concatenate([reach[request]] * heads, axis=0)
        scores = jnp.where(seen > 0, scores, -jnp.inf)
        before = top[request][:, :1]
        now = jnp.maximum(before, jnp.max(scores, axis=1, keepdims=True))
        powered = jnp.exp(scores - now)
        fade = jnp.exp(before - now)
        sums = mass[request][:, :1] * fade + jnp.sum(powered, axis=1, keepdims=True)
        total = mixed[request] * fade + jnp.dot(
            powered.astype(BF16), value[own, :], preferred_element_type=F32
        )
        total = (total / sums).astype(BF16)
        for head in range(heads):
            attended[own, head * HD : (head + 1) * HD] = total[
                head * draft : (head + 1) * draft, head * HD : (head + 1) * HD
            ]
    width = terms.shape[2]
    for mask in range(count):
        place = pl.ds(pl.multiple_of((me ^ mask) * width, width), width)
        terms[mask] = lax.dot_general(
            attended[...],
            output[place, :],
            (((1,), (1,)), ((), ())),
            preferred_element_type=F32,
        ).astype(BF16)


def hidden_kernel(count, ids, gain, gates, weight, *refs):
    pieces, hidden, normed = refs[:count], refs[count], refs[count + 1]
    me_x, me_y = ids[0], ids[1]
    blocks, rows, width = pieces[0].shape

    @pl.when(pl.program_id(0) == 0)
    def _():
        for block in range(blocks):
            total = jnp.zeros((rows, 1), F32)
            for piece in pieces:
                value = piece[block].astype(F32)
                total = total + jnp.sum(value * value, axis=1, keepdims=True)
            scale = lax.rsqrt(total / (width * count) + 1e-05)
            for mask, piece in enumerate(pieces):
                columns = pl.ds(pl.multiple_of((me_y ^ mask) * width, width), width)
                value = piece[block].astype(F32) * scale * gain[:, columns]
                normed[block * rows : (block + 1) * rows, columns] = value.astype(BF16)

    units = weight.shape[2] // 2
    for block in range(blocks):
        place = slice(block * rows, (block + 1) * rows)
        both = jnp.dot(normed[place, :], weight[0], preferred_element_type=F32)
        gate, up = both[:, :units], both[:, units:]
        source = pl.ds(pl.multiple_of((me_x ^ block) * rows, rows), rows)
        value = gate / (1.0 + jnp.exp(-gate)) * up * gates[0, source, :]
        hidden[place, :] = value.astype(BF16)


def down_kernel(first, ids, hidden, weight, terms):
    me = ids[1]
    width = terms.shape[2]
    for place in range(terms.shape[0]):
        mask = 2 * place + first
        columns = pl.ds(pl.multiple_of((me ^ mask) * width, width), width)
        terms[place] = jnp.dot(
            hidden[...], weight[:, columns], preferred_element_type=F32
        ).astype(BF16)


def per_device(
    tokens,
    attention_gain,
    projection_weight,
    output_weight,
    prompt_cache,
    cache_length,
    prompt_group,
    parents,
    accepted_path,
    expert_gain,
    gate_up_weight,
    down_weight,
    route_experts,
    route_gates,
):
    gx_count, gy_count = lax.axis_size("gx"), lax.axis_size("gy")
    ids = jnp.stack([lax.axis_index("gx"), lax.axis_index("gy")]).astype(jnp.int32)
    rows, width = tokens.shape
    depth = attention_gain.shape[0]
    requests, draft = parents.shape
    groups = prompt_cache.shape[0]
    heads = width // HD

    by_part = jnp.transpose(projection_weight, (1, 0, 2))
    query_weight = lax.all_gather(by_part[0], "gx", axis=0, tiled=True)
    pair_weight = lax.all_gather(by_part[1:], "gx", axis=0, tiled=False)
    output_full = lax.all_gather(output_weight, "gx", axis=0, tiled=True)

    pieces = gather_gy(tokens)
    normed, query = pl.pallas_call(
        lambda *refs: query_kernel(gy_count, *refs),
        out_shape=(
            jax.ShapeDtypeStruct((rows, depth), BF16),
            jax.ShapeDtypeStruct((rows, width), BF16),
        ),
        in_specs=[smem()] + [vmem()] * (2 + gy_count),
        out_specs=(vmem(), vmem()),
        compiler_params=params(),
        name="query",
    )(ids, attention_gain.reshape(1, depth), query_weight, *pieces)

    slots = prompt_cache.shape[2]
    step = min(CACHE_BLOCK, slots)
    wide_rows = heads * draft
    constant = lambda *_: (0, 0, 0)
    top, mass, mixed = pl.pallas_call(
        lambda *refs: cache_kernel(requests, draft, heads, *refs),
        grid_spec=pltpu.PrefetchScalarGridSpec(
            num_scalar_prefetch=2,
            grid=(groups, slots // step),
            in_specs=[
                pl.BlockSpec((rows, width), lambda *_: (0, 0)),
                pl.BlockSpec(
                    (1, 2, step, width),
                    lambda group, block, lengths, owner: (
                        group,
                        0,
                        jnp.minimum(block, (lengths[group] - 1) // step),
                        0,
                    ),
                ),
            ],
            out_specs=[
                pl.BlockSpec((requests, wide_rows, HD), constant),
                pl.BlockSpec((requests, wide_rows, HD), constant),
                pl.BlockSpec((requests, wide_rows, width), constant),
            ],
            scratch_shapes=[pltpu.VMEM((requests, wide_rows, width), BF16)],
        ),
        out_shape=(
            jax.ShapeDtypeStruct((requests, wide_rows, HD), F32),
            jax.ShapeDtypeStruct((requests, wide_rows, HD), F32),
            jax.ShapeDtypeStruct((requests, wide_rows, width), F32),
        ),
        compiler_params=params(),
        name="cache",
    )(cache_length, prompt_group % groups, query, prompt_cache)

    accepted = accepted_path.shape[1]
    chosen = (jnp.arange(requests, dtype=jnp.int32)[:, None] * draft + accepted_path).reshape(-1, 1)
    terms, picked = pl.pallas_call(
        lambda *refs: draft_kernel(requests, draft, heads, gy_count, *refs),
        out_shape=(
            jax.ShapeDtypeStruct((gy_count, rows, width), BF16),
            jax.ShapeDtypeStruct((2, requests * accepted, width), BF16),
        ),
        in_specs=[smem()] + [vmem()] * 9,
        out_specs=(vmem(), vmem()),
        scratch_shapes=[
            pltpu.VMEM((rows, width), BF16),
            pltpu.VMEM((rows, width), BF16),
            pltpu.VMEM((rows, width), BF16),
        ],
        compiler_params=params(),
        name="draft",
    )(
        ids, normed, query, pair_weight, output_full, ancestor_table(parents), chosen, top, mass,
        mixed
    )
    compacted = jnp.transpose(picked, (1, 0, 2))

    near = swap(terms[1::2], "gy", 1)
    summed = terms[0::2].astype(F32) + near.astype(F32)
    stream = tokens.astype(F32) + summed[0]
    for place in range(1, gy_count // 2):
        stream = stream + swap(summed[place].astype(BF16), "gy", 2 * place).astype(F32)
    stream = stream.astype(BF16)

    blocks = jnp.stack([stream] + [swap(stream, "gx", mask) for mask in range(1, gx_count)])
    everything = gather_gy(blocks)

    experts = gate_up_weight.shape[0]
    units = gate_up_weight.shape[3]
    total_tokens = gx_count * rows
    expert_ids = lax.axis_index("gy") * experts + jnp.arange(experts, dtype=jnp.int32)
    hit = route_experts[None] == expert_ids[:, None, None]
    gates = jnp.sum(jnp.where(hit, route_gates.astype(F32)[None], 0.0), axis=2)[:, :, None]
    gate_up = gate_up_weight.reshape(experts, depth, 2 * units)
    hidden = pl.pallas_call(
        lambda *refs: hidden_kernel(gy_count, *refs),
        grid=(experts,),
        in_specs=[
            smem(),
            pl.BlockSpec((1, depth), lambda expert: (0, 0)),
            pl.BlockSpec((1, total_tokens, 1), lambda expert: (expert, 0, 0)),
            pl.BlockSpec((1, depth, 2 * units), lambda expert: (expert, 0, 0)),
        ]
        + [vmem()] * gy_count,
        out_specs=pl.BlockSpec((total_tokens, units), lambda expert: (0, expert)),
        out_shape=jax.ShapeDtypeStruct((total_tokens, experts * units), BF16),
        scratch_shapes=[pltpu.VMEM((total_tokens, depth), BF16)],
        compiler_params=params(),
        name="hidden",
    )(ids, expert_gain.reshape(1, depth), gates, gate_up, *everything)

    down = down_weight.reshape(experts * units, depth)

    def partial_sums(first):
        return pl.pallas_call(
            lambda *refs: down_kernel(first, *refs),
            out_shape=jax.ShapeDtypeStruct((gy_count // 2, total_tokens, width), BF16),
            in_specs=[smem(), vmem(), vmem()],
            out_specs=vmem(),
            compiler_params=params(),
            name="down",
        )(ids, hidden, down)

    far_terms = partial_sums(1)
    near = swap(far_terms, "gy", 1)
    own_terms = partial_sums(0)
    summed = own_terms.astype(F32) + near.astype(F32)
    total = summed[0]
    for place in range(1, gy_count // 2):
        total = total + swap(summed[place].astype(BF16), "gy", 2 * place).astype(F32)
    total = total.reshape(gx_count, rows, width)
    result = stream.astype(F32) + total[0]
    for mask in range(1, gx_count):
        result = result + swap(total[mask].astype(BF16), "gx", mask).astype(F32)
    return (result.astype(BF16), compacted)


def gather_gy(value):
    count = lax.axis_size("gy")
    even = [value] + [swap(value, "gy", mask) for mask in range(2, count, 2)]
    pieces = []
    for one in even:
        pieces += [one, swap(one, "gy", 1)]
    return pieces


def solution(mesh):
    placed = (
        P("gx", "gy"),
        P(),
        P("gx", None, "gy"),
        P("gx", "gy"),
        P("gx", None, None, "gy"),
        P("gx"),
        P("gx"),
        P("gx", None),
        P("gx", None),
        P(),
        P("gy", None, None, "gx"),
        P("gy", "gx", None),
        P(),
        P(),
    )
    return jax.shard_map(
        per_device,
        mesh=mesh,
        in_specs=placed,
        out_specs=(P("gx", "gy"), P("gx", None, "gy")),
        check_vma=False,
    )
```

time: 534 us -> 274 us (0.51)
  waiting for transfers between devices: 352 us -> 151 us
  Pallas kernels: 0 us -> 52.9 us
  matrix products: 51.8 us -> 1.7 us
  other arithmetic: 49.1 us -> 6 us
  local copies, waits for them, and re-layouts: 56.5 us -> 23.4 us
  starting transfers between devices: 0.46 us -> 24.3 us
  loops' own time: 8.02 us -> 0 us
    reduce_scatter x2 -> x0, waiting for transfers between devices: 185 us -> none  [the longest x1 145 us: per_device(): lax.psum_scatter(arranged, ('gx', 'gy'), scatter_dimension=0, tiled=True)]
    all_gather x5 -> x3, waiting for transfers between devices: 165 us -> 73.6 us  [the longest x1 47 us: per_device(): pair_weight = lax.all_gather(by_part[1:], 'gx', axis=0, tiled=False)]
    ppermute x0 -> x28, waiting for transfers between devices: none -> 77 us  [swap(): lax.ppermute(value, axis, [(one, one ^ mask) for one in range(count)])]
    pallas_call x0 -> x6, Pallas kernels: none -> 52.9 us  [the longest x1 16 us: per_device(): pl.pallas_call(lambda *refs: hidden_kernel(gy_count, *refs), grid=(expert...]
    dot_general x26 -> x3, matrix products: 51.8 us -> 1.7 us  [ancestor_table(): reach = jnp.minimum(jnp.einsum('rij,rjk->rik', reach, reach), 1.0)]
    unnamed x26 -> x43, local copies, waits for them, and re-layouts: 29.7 us -> 1.68 us
    scatter-add x1 -> x0, other arithmetic: 25 us -> none  [per_device(): jax.ops.segment_sum(partial_value.reshape(-1, width), slot_index.reshape(...]
    ppermute x0 -> x28, starting transfers between devices: none -> 24.2 us  [swap(): lax.ppermute(value, axis, [(one, one ^ mask) for one in range(count)])]
  transfers between devices with their start and end apart: 7 -> 31, of which waited for: 6 -> 20; matrix products, arithmetic and copies ran while one was open for 15% -> 8% of each run, Pallas kernels for 0% -> 9%
where the time goes in v1:
time: 274 us
  waiting for transfers between devices  151 us (55%)
  Pallas kernels  52.9 us (19%)
  starting transfers between devices  24.3 us (9%)
  local copies, waits for them, and re-layouts  23.4 us (9%)
  between operations  14.1 us (5%)
  other arithmetic  6 us (2%)
    ppermute x28, waiting for transfers between devices, swap(): lax.ppermute(value, axis, [(one, one ^ mask) for one in range(count)])  77 us
    all_gather x1, waiting for transfers between devices, per_device(): pair_weight = lax.all_gather(by_part[1:], 'gx', axis=0, tiled=False)  47 us
    ppermute x28, starting transfers between devices, swap(): lax.ppermute(value, axis, [(one, one ^ mask) for one in range(count)])  24.2 us
    pallas_call x1, Pallas kernels, per_device(): pl.pallas_call(lambda *refs: hidden_kernel(gy_count, *refs), grid=(expert...  16 us
    all_gather x1, waiting for transfers between devices, per_device(): query_weight = lax.all_gather(by_part[0], 'gx', axis=0, tiled=True)  15.3 us
    pallas_call x1, Pallas kernels, per_device(): pl.pallas_call(lambda *refs: cache_kernel(requests, draft, heads, *refs),...  14.5 us
    reshape x1, local copies, waits for them, and re-layouts, per_device(): gate_up = gate_up_weight.reshape(experts, depth, 2 * units)  14.1 us
    pallas_call x2, Pallas kernels, partial_sums(): pl.pallas_call(lambda *refs: down_kernel(first, *refs), out_shape=jax.Sha...  13.1 us
  transfers between devices with their start and end apart: 31, of which 20 were waited for; matrix products, arithmetic and copies ran while one was open for 8% of the time, Pallas kernels for 9%

profile of v1, /device:TPU:0, one launch (start us, length us, event | category | flops | bytes accessed | tf_op | source)
XLA Modules:
  0.0 273.6 jit_solution(6789879297475948719)
XLA Ops:
  7.3 1.7 slice.77
  9.8 1.9 slice.78
  11.7 3.0 %collective-permute-start.3 = (bf16[256,256]{1,0:T(8,128)(2,1)S(1)}, bf16[256,256]{1,0:T(8,128)(2,1)S(1)}, u32[]{:S(2)}, u32[]{:S(2)}) collective-permute-start(bf16[256,256]{1,0:T(8,128)(2,1)S(1)} %copy-done.6), channel_id=1, source_target_pairs={{0,4},{1,5},{2,6},{3,7},{4,0},{5,1},{6,2},{7,3},{8,12},{9,13},{10,... | collective-permute-start | bytes 393224 | tf_op jit(solution)/shard_map/ppermute | solution.py:31
  14.7 1.5 collective-permute-start.1
  17.0 0.9 convolution_minimum_fusion.refs_5_
  18.5 1.6 collective-permute-done.1.refs_5_
  20.1 2.9 %collective-permute-done.5.refs_9_ = bf16[256,256]{1,0:T(8,128)(2,1)S(1)} collective-permute-done((bf16[256,256]{1,0:T(8,128)(2,1)S(1)}, bf16[256,256]{1,0:T(8,128)(2,1)S(1)}, u32[]{:S(2)}, u32[]{:S(2)}) %collective-permute-start.5) | collective-permute-done | bytes 131104 | tf_op jit(solution)/shard_map/ppermute | solution.py:31
  25.0 15.3 %all-gather.8.cloned.1.call-done = bf16[1,2048,256]{2,1,0:T(8,128)(2,1)} async-done(((bf16[1,512,256]{2,1,0:T(8,128)(2,1)}), bf16[1,2048,256]{2,1,0:T(8,128)(2,1)}) %all-gather.8.cloned.1.call-update) | async-done | bytes 1048592 | tf_op jit(solution)/shard_map/all_gather | solution.py:231
  40.3 3.3 %query.1 = (bf16[256,2048]{1,0:T(8,128)(2,1)}, bf16[256,256]{1,0:T(8,128)(2,1)}) custom-call(s32[2]{0:T(128)} %pad_add_fusion.refs_0_, f32[1,2048]{1,0:T(1,128)} %bitcast.63, bf16[2048,256]{1,0:T(8,128)(2,1)} %bitcast.55, bf16[256,256]{1,0:T(8,128)(2,1)} %refs_3_.2, bf16[256,256]{1,0:T(8,128)(2,1)} %copy-done.10, bf16[256,256]{1,0:T(8,128)(2,1)} %copy-done.9, ...), custom_call_target="tpu_custom_call" | custom-call | tf_op jit(solution)/shard_map/query/pallas_call | solution.py:236
  43.6 14.5 %cache.1 = (f32[4,128,128]{2,1,0:T(8,128)}, f32[4,128,128]{2,1,0:T(8,128)}, f32[4,128,256]{2,1,0:T(8,128)}) custom-call(s32[2]{0:T(128)} %refs_0_.1, s32[4]{0:T(128)} %and_select_fusion.refs_1_, bf16[256,256]{1,0:T(8,128)(2,1)} %get-tuple-element.10.refs_2_, bf16[2,2,8192,256]{3,2,1,0:T(8,128)(2,1)} %refs_3_.3), custom_call_target="tpu_custom_call" | custom-call | tf_op jit(solution)/shard_map/cache/pallas_call | solution.py:252
  58.1 11.3 %all-gather.6.cloned.1.call-done.refs_4_ = bf16[2048,256]{1,0:T(8,128)(2,1)} async-done(((bf16[512,256]{1,0:T(8,128)(2,1)}), bf16[2048,256]{1,0:T(8,128)(2,1)}) %all-gather.6.cloned.1.call-update) | async-done | bytes 1048592 | tf_op jit(solution)/shard_map/all_gather | solution.py:233
  69.3 47.0 %all-gather.10.cloned.1.call-done = bf16[8,512,256]{2,1,0:T(8,128)(2,1)} async-done(((bf16[2,512,256]{2,1,0:T(8,128)(2,1)}), bf16[8,512,256]{2,1,0:T(8,128)(2,1)}) %all-gather.10.cloned.1.call-update) | async-done | bytes 2097168 | tf_op jit(solution)/shard_map/all_gather | solution.py:232
  116.4 6.0 %draft.1 = (bf16[8,256,256]{2,1,0:T(8,128)(2,1)}, bf16[2,32,256]{2,1,0:T(8,128)(2,1)}) custom-call(s32[2]{0:T(128)} %pad_add_fusion.refs_0_, bf16[256,2048]{1,0:T(8,128)(2,1)} %get-tuple-element.9.refs_1_, bf16[256,256]{1,0:T(8,128)(2,1)} %get-tuple-element.10.refs_2_, bf16[4,2,512,256]{3,2,1,0:T(8,128)(2,1)} %bitcast.53, ...), custom_call_target="tpu_custom_call" | custom-call | tf_op jit(solution)/shard_map/draft/pallas_call | solution.py:287
  122.4 1.1 slice.64
  123.6 1.9 collective-permute-done.7
  125.5 1.2 fusion.28
  126.7 1.5 collective-permute-start.8
  128.2 1.5 collective-permute-start.10
  130.2 2.7 collective-permute-done.8
  132.9 3.2 %collective-permute-done.10 = bf16[256,256]{1,0:T(8,128)(2,1)S(1)} collective-permute-done((bf16[256,256]{1,0:T(8,128)(2,1)S(1)}, bf16[256,256]{1,0:T(8,128)(2,1)S(1)}, u32[]{:S(2)}, u32[]{:S(2)}) %collective-permute-start.10) | collective-permute-done | bytes 131104 | tf_op jit(solution)/shard_map/ppermute | solution.py:31
  136.1 1.4 collective-permute-done.9
  137.6 1.2 collective-permute-start.13
  139.0 3.0 %collective-permute-start.11 = (bf16[256,256]{1,0:T(8,128)(2,1)S(1)}, bf16[256,256]{1,0:T(8,128)(2,1)S(1)}, u32[]{:S(2)}, u32[]{:S(2)}) collective-permute-start(bf16[256,256]{1,0:T(8,128)(2,1)S(1)} %fusion.11), channel_id=1, source_target_pairs={{0,8},{8,0},{16,24},{24,16},{1,9},{9,1},{17,25},{25,17},{2,10},{10... | collective-permute-start | bytes 393224 | tf_op jit(solution)/shard_map/ppermute | solution.py:31
  142.0 3.8 %collective-permute-done.13 = bf16[256,256]{1,0:T(8,128)(2,1)S(1)} collective-permute-done((bf16[256,256]{1,0:T(8,128)(2,1)S(1)}, bf16[256,256]{1,0:T(8,128)(2,1)S(1)}, u32[]{:S(2)}, u32[]{:S(2)}) %collective-permute-start.13) | collective-permute-done | bytes 131104 | tf_op jit(solution)/shard_map/ppermute | solution.py:31
  145.9 4.5 %collective-permute-done.12 = bf16[256,256]{1,0:T(8,128)(2,1)S(1)} collective-permute-done((bf16[256,256]{1,0:T(8,128)(2,1)S(1)}, bf16[256,256]{1,0:T(8,128)(2,1)S(1)}, u32[]{:S(2)}, u32[]{:S(2)}) %collective-permute-start.12) | collective-permute-done | bytes 131104 | tf_op jit(solution)/shard_map/ppermute | solution.py:31
  150.5 1.5 collective-permute-start.19
  152.0 1.5 collective-permute-start.17
  154.0 12.3 %collective-permute-done.19.refs_10_ = bf16[4,256,256]{2,1,0:T(8,128)(2,1)S(1)} collective-permute-done((bf16[4,256,256]{2,1,0:T(8,128)(2,1)S(1)}, bf16[4,256,256]{2,1,0:T(8,128)(2,1)S(1)}, u32[]{:S(2)}, u32[]{:S(2)}) %collective-permute-start.19) | collective-permute-done | bytes 524320 | tf_op jit(solution)/shard_map/ppermute | solution.py:31
  166.3 9.3 %collective-permute-done.17.refs_8_ = bf16[4,256,256]{2,1,0:T(8,128)(2,1)S(1)} collective-permute-done((bf16[4,256,256]{2,1,0:T(8,128)(2,1)S(1)}, bf16[4,256,256]{2,1,0:T(8,128)(2,1)S(1)}, u32[]{:S(2)}, u32[]{:S(2)}) %collective-permute-start.17) | collective-permute-done | bytes 524320 | tf_op jit(solution)/shard_map/ppermute | solution.py:31
  176.3 2.1 copy.31.refs_2_
  178.4 14.1 %reshape.57.refs_3_ = bf16[4,2048,512]{2,1,0:T(8,128)(2,1)} reshape(bf16[4,2048,2,256]{3,2,1,0:T(2,128)(2,1)} %param.24) | data formatting | bytes 16777216 | tf_op jit(solution)/shard_map/reshape | solution.py:324
  192.6 0.7 copy-done.4
  193.6 16.0 %hidden.1.refs_1_ = bf16[1024,1024]{1,0:T(8,128)(2,1)} custom-call(s32[2]{0:T(128)} %pad_add_fusion.refs_0_, f32[1,2048]{1,0:T(1,128)} %bitcast.64, f32[4,1024,1]{2,1,0:T(8,128)} %copy.31.refs_2_, bf16[4,2048,512]{2,1,0:T(8,128)(2,1)} %reshape.57.refs_3_, bf16[4,256,256]{2,1,0:T(8,128)(2,1)} %copy-done, bf16[4,256,256]{2,1,0:T(8,128)(2,1)} %copy-done.4, ...), custom_call_target="tpu_custom_call" | custom-call | tf_op jit(solution)/shard_map/hidden/pallas_call | solution.py:325
  209.6 6.5 %down.3 = bf16[4,1024,256]{2,1,0:T(8,128)(2,1)} custom-call(s32[2]{0:T(128)} %pad_add_fusion.refs_0_, bf16[1024,1024]{1,0:T(8,128)(2,1)} %hidden.1.refs_1_, bf16[1024,2048]{1,0:T(8,128)(2,1)} %bitcast.51), custom_call_target="tpu_custom_call" | custom-call | tf_op jit(solution)/shard_map/down/pallas_call | solution.py:345
  216.2 6.6 %down.2 = bf16[4,1024,256]{2,1,0:T(8,128)(2,1)} custom-call(s32[2]{0:T(128)} %pad_add_fusion.refs_0_, bf16[1024,1024]{1,0:T(8,128)(2,1)} %hidden.1.refs_1_, bf16[1024,2048]{1,0:T(8,128)(2,1)} %bitcast.52), custom_call_target="tpu_custom_call" | custom-call | tf_op jit(solution)/shard_map/down/pallas_call | solution.py:345
  222.8 2.3 convert_add_fusion
  225.1 0.8 collective-permute-start.22
  226.0 1.2 collective-permute-start.24
  227.2 1.5 collective-permute-start.23
  228.7 11.2 %collective-permute-done.22 = bf16[1024,256]{1,0:T(8,128)(2,1)S(1)} collective-permute-done((bf16[1024,256]{1,0:T(8,128)(2,1)S(1)}, bf16[1024,256]{1,0:T(8,128)(2,1)S(1)}, u32[]{:S(2)}, u32[]{:S(2)}) %collective-permute-start.22) | collective-permute-done | bytes 524320 | tf_op jit(solution)/shard_map/ppermute | solution.py:31
  239.9 10.8 %collective-permute-done.24 = bf16[1024,256]{1,0:T(8,128)(2,1)S(1)} collective-permute-done((bf16[1024,256]{1,0:T(8,128)(2,1)S(1)}, bf16[1024,256]{1,0:T(8,128)(2,1)S(1)}, u32[]{:S(2)}, u32[]{:S(2)}) %collective-permute-start.24) | collective-permute-done | bytes 524320 | tf_op jit(solution)/shard_map/ppermute | solution.py:31
  250.7 1.4 collective-permute-done.23
  252.4 2.0 collective-permute-start.27
  254.4 1.5 collective-permute-start.26
  256.6 3.0 %collective-permute-done.25 = bf16[256,256]{1,0:T(8,128)(2,1)S(1)} collective-permute-done((bf16[256,256]{1,0:T(8,128)(2,1)S(1)}, bf16[256,256]{1,0:T(8,128)(2,1)S(1)}, u32[]{:S(2)}, u32[]{:S(2)}) %collective-permute-start.25) | collective-permute-done | bytes 131104 | tf_op jit(solution)/shard_map/ppermute | solution.py:31
  259.6 1.8 collective-permute-done.27
  261.4 4.9 %collective-permute-done.26 = bf16[256,256]{1,0:T(8,128)(2,1)S(1)} collective-permute-done((bf16[256,256]{1,0:T(8,128)(2,1)S(1)}, bf16[256,256]{1,0:T(8,128)(2,1)S(1)}, u32[]{:S(2)}, u32[]{:S(2)}) %collective-permute-start.26) | collective-permute-done | bytes 131104 | tf_op jit(solution)/shard_map/ppermute | solution.py:31
  266.4 0.8 fusion.6
  (92 shorter events, 7.8 us)
Async XLA Ops:
  7.2 9.1 %copy-start.19 = (s32[4,64]{1,0:T(4,128)S(1)}, s32[4,64]{1,0:T(4,128)}, u32[]{:S(2)}) copy-start(s32[4,64]{1,0:T(4,128)} %param.21) | copy-start | bytes 3076
  7.2 10.8 %copy-start.18 = (s32[4,8]{1,0:T(4,128)S(1)}, s32[4,8]{1,0:T(4,128)}, u32[]{:S(2)}) copy-start(s32[4,8]{1,0:T(4,128)} %param.22) | copy-start | bytes 388
  7.2 15.8 %copy-start.20 = (s32[4]{0:T(128)S(1)}, s32[4]{0:T(128)}, u32[]{:S(2)}) copy-start(s32[4]{0:T(128)} %param.20) | copy-start | bytes 52
  7.2 33.1 %all-gather.8.cloned.1.call-start = ((), (), s32[]{:S(2)}) async-start(), calls=%async_computation.1 | async-start | bytes 1310720 | tf_op jit(solution)/shard_map/all_gather | solution.py:231
  9.0 60.4 %all-gather.6.cloned.1.call-start = ((), (), s32[]{:S(2)}) async-start(), calls=%async_computation | async-start | bytes 1310720 | tf_op jit(solution)/shard_map/all_gather | solution.py:233
  9.7 106.6 %all-gather.10.cloned.1.call-start = ((), (), s32[]{:S(2)}) async-start(), calls=%async_computation.2 | async-start | bytes 2621440 | tf_op jit(solution)/shard_map/all_gather | solution.py:232
  11.7 6.5 %collective-permute-start.3 = (bf16[256,256]{1,0:T(8,128)(2,1)S(1)}, bf16[256,256]{1,0:T(8,128)(2,1)S(1)}, u32[]{:S(2)}, u32[]{:S(2)}) collective-permute-start(bf16[256,256]{1,0:T(8,128)(2,1)S(1)} %copy-done.6), channel_id=1, source_target_pairs={{0,4},{1,5},{2,6},{3,7},{4,0},{5,1},{6,2},{7,3},{8,12},{9,13},{10,... | collective-permute-start | bytes 393224 | tf_op jit(solution)/shard_map/ppermute | solution.py:31
  14.7 5.4 %collective-permute-start.1 = (bf16[256,256]{1,0:T(8,128)(2,1)S(1)}, bf16[256,256]{1,0:T(8,128)(2,1)S(1)}, u32[]{:S(2)}, u32[]{:S(2)}) collective-permute-start(bf16[256,256]{1,0:T(8,128)(2,1)S(1)} %copy-done.6), channel_id=1, source_target_pairs={{0,2},{1,3},{2,0},{3,1},{4,6},{5,7},{6,4},{7,5},{8,10},{9,11},{10,... | collective-permute-start | bytes 393224 | tf_op jit(solution)/shard_map/ppermute | solution.py:31
  16.2 8.7 %collective-permute-start = (bf16[256,256]{1,0:T(8,128)(2,1)S(1)}, bf16[256,256]{1,0:T(8,128)(2,1)S(1)}, u32[]{:S(2)}, u32[]{:S(2)}) collective-permute-start(bf16[256,256]{1,0:T(8,128)(2,1)S(1)} %copy-done.6), channel_id=1, source_target_pairs={{0,1},{1,0},{2,3},{3,2},{4,5},{5,4},{6,7},{7,6},{8,9},{9,8},{10,11... | collective-permute-start | bytes 393224 | tf_op jit(solution)/shard_map/ppermute | solution.py:31
  16.2 6.8 %collective-permute-start.5 = (bf16[256,256]{1,0:T(8,128)(2,1)S(1)}, bf16[256,256]{1,0:T(8,128)(2,1)S(1)}, u32[]{:S(2)}, u32[]{:S(2)}) collective-permute-start(bf16[256,256]{1,0:T(8,128)(2,1)S(1)} %copy-done.6), channel_id=1, source_target_pairs={{0,6},{1,7},{2,4},{3,5},{4,2},{5,3},{6,0},{7,1},{8,14},{9,15},{10,... | collective-permute-start | bytes 393224 | tf_op jit(solution)/shard_map/ppermute | solution.py:31
  18.2 22.1 %copy-start.8 = (bf16[256,256]{1,0:T(8,128)(2,1)}, bf16[256,256]{1,0:T(8,128)(2,1)S(1)}, u32[]{:S(2)}) copy-start(bf16[256,256]{1,0:T(8,128)(2,1)S(1)} %collective-permute-done.3.refs_7_) | copy-start | bytes 393220
  18.2 6.7 %collective-permute-start.4 = (bf16[256,256]{1,0:T(8,128)(2,1)S(1)}, bf16[256,256]{1,0:T(8,128)(2,1)S(1)}, u32[]{:S(2)}, u32[]{:S(2)}) collective-permute-start(bf16[256,256]{1,0:T(8,128)(2,1)S(1)} %collective-permute-done.3.refs_7_), channel_id=1, source_target_pairs={{0,1},{1,0},{2,3},{3,2},{4,5},{5,4},{6,7},{7,6},{8,9},{9,8},{10,11... | collective-permute-start | bytes 393224 | tf_op jit(solution)/shard_map/ppermute | solution.py:31
  20.1 20.2 %copy-start.9 = (bf16[256,256]{1,0:T(8,128)(2,1)}, bf16[256,256]{1,0:T(8,128)(2,1)S(1)}, u32[]{:S(2)}) copy-start(bf16[256,256]{1,0:T(8,128)(2,1)S(1)} %collective-permute-done.1.refs_5_) | copy-start | bytes 393220
  20.1 4.9 %collective-permute-start.2 = (bf16[256,256]{1,0:T(8,128)(2,1)S(1)}, bf16[256,256]{1,0:T(8,128)(2,1)S(1)}, u32[]{:S(2)}, u32[]{:S(2)}) collective-permute-start(bf16[256,256]{1,0:T(8,128)(2,1)S(1)} %collective-permute-done.1.refs_5_), channel_id=1, source_target_pairs={{0,1},{1,0},{2,3},{3,2},{4,5},{5,4},{6,7},{7,6},{8,9},{9,8},{10,11... | collective-permute-start | bytes 393224 | tf_op jit(solution)/shard_map/ppermute | solution.py:31
  23.0 17.3 %copy-start.11 = (bf16[256,256]{1,0:T(8,128)(2,1)}, bf16[256,256]{1,0:T(8,128)(2,1)S(1)}, u32[]{:S(2)}) copy-start(bf16[256,256]{1,0:T(8,128)(2,1)S(1)} %collective-permute-done.5.refs_9_) | copy-start | bytes 393220
  23.0 2.0 collective-permute-start.6
  24.9 15.3 %copy-start.10 = (bf16[256,256]{1,0:T(8,128)(2,1)}, bf16[256,256]{1,0:T(8,128)(2,1)S(1)}, u32[]{:S(2)}) copy-start(bf16[256,256]{1,0:T(8,128)(2,1)S(1)} %collective-permute-done.refs_4_) | copy-start | bytes 393220
  24.9 15.3 %copy-start.12 = (bf16[256,256]{1,0:T(8,128)(2,1)}, bf16[256,256]{1,0:T(8,128)(2,1)S(1)}, u32[]{:S(2)}) copy-start(bf16[256,256]{1,0:T(8,128)(2,1)S(1)} %collective-permute-done.4.refs_8_) | copy-start | bytes 393220
  25.0 15.3 %copy-start.13 = (bf16[256,256]{1,0:T(8,128)(2,1)}, bf16[256,256]{1,0:T(8,128)(2,1)S(1)}, u32[]{:S(2)}) copy-start(bf16[256,256]{1,0:T(8,128)(2,1)S(1)} %collective-permute-done.2.refs_6_) | copy-start | bytes 393220
  25.0 15.3 %copy-start.14 = (bf16[256,256]{1,0:T(8,128)(2,1)}, bf16[256,256]{1,0:T(8,128)(2,1)S(1)}, u32[]{:S(2)}) copy-start(bf16[256,256]{1,0:T(8,128)(2,1)S(1)} %collective-permute-done.6.refs_10_) | copy-start | bytes 393220
  122.4 15.1 %copy-start.7 = (bf16[256,256]{1,0:T(8,128)(2,1)S(1)}, bf16[256,256]{1,0:T(8,128)(2,1)}, u32[]{:S(2)}) copy-start(bf16[256,256]{1,0:T(8,128)(2,1)} %refs_3_.2) | copy-start | bytes 393220
  123.5 52.7 %copy-start.17 = (bf16[1024,8]{0,1:T(8,128)(2,1)S(1)}, bf16[1024,8]{0,1:T(8,128)(2,1)}, u32[]{:S(2)}) copy-start(bf16[1024,8]{0,1:T(8,128)(2,1)} %param.27) | copy-start | bytes 49156
  123.5 52.7 %copy-start.15 = (s32[1024,8]{0,1:T(8,128)S(1)}, s32[1024,8]{0,1:T(8,128)}, u32[]{:S(2)}) copy-start(s32[1024,8]{0,1:T(8,128)} %param.26) | copy-start | bytes 98308
  123.5 2.0 collective-permute-start.7
  126.7 6.3 %collective-permute-start.8 = (bf16[256,256]{1,0:T(8,128)(2,1)S(1)}, bf16[256,256]{1,0:T(8,128)(2,1)S(1)}, u32[]{:S(2)}, u32[]{:S(2)}) collective-permute-start(bf16[256,256]{1,0:T(8,128)(2,1)S(1)} %get-tuple-element.36), channel_id=1, source_target_pairs={{0,2},{1,3},{2,0},{3,1},{4,6},{5,7},{6,4},{7,5},{8,10},{9,11},{10,... | collective-permute-start | bytes 393224 | tf_op jit(solution)/shard_map/ppermute | solution.py:31
  128.2 7.9 %collective-permute-start.10 = (bf16[256,256]{1,0:T(8,128)(2,1)S(1)}, bf16[256,256]{1,0:T(8,128)(2,1)S(1)}, u32[]{:S(2)}, u32[]{:S(2)}) collective-permute-start(bf16[256,256]{1,0:T(8,128)(2,1)S(1)} %get-tuple-element.37), channel_id=1, source_target_pairs={{0,6},{1,7},{2,4},{3,5},{4,2},{5,3},{6,0},{7,1},{8,14},{9,15},{10,... | collective-permute-start | bytes 393224 | tf_op jit(solution)/shard_map/ppermute | solution.py:31
  129.7 7.8 %collective-permute-start.9 = (bf16[256,256]{1,0:T(8,128)(2,1)S(1)}, bf16[256,256]{1,0:T(8,128)(2,1)S(1)}, u32[]{:S(2)}, u32[]{:S(2)}) collective-permute-start(bf16[256,256]{1,0:T(8,128)(2,1)S(1)} %get-tuple-element.38), channel_id=1, source_target_pairs={{0,4},{1,5},{2,6},{3,7},{4,0},{5,1},{6,2},{7,3},{8,12},{9,13},{10,... | collective-permute-start | bytes 393224 | tf_op jit(solution)/shard_map/ppermute | solution.py:31
  137.6 8.3 %collective-permute-start.13 = (bf16[256,256]{1,0:T(8,128)(2,1)S(1)}, bf16[256,256]{1,0:T(8,128)(2,1)S(1)}, u32[]{:S(2)}, u32[]{:S(2)}) collective-permute-start(bf16[256,256]{1,0:T(8,128)(2,1)S(1)} %fusion.11), channel_id=1, source_target_pairs={{0,24},{8,16},{16,8},{24,0},{1,25},{9,17},{17,9},{25,1},{2,26},{10... | collective-permute-start | bytes 393224 | tf_op jit(solution)/shard_map/ppermute | solution.py:31
  138.8 11.6 %collective-permute-start.12 = (bf16[256,256]{1,0:T(8,128)(2,1)S(1)}, bf16[256,256]{1,0:T(8,128)(2,1)S(1)}, u32[]{:S(2)}, u32[]{:S(2)}) collective-permute-start(bf16[256,256]{1,0:T(8,128)(2,1)S(1)} %fusion.11), channel_id=1, source_target_pairs={{0,16},{8,24},{16,0},{24,8},{1,17},{9,25},{17,1},{25,9},{2,18},{10... | collective-permute-start | bytes 393224 | tf_op jit(solution)/shard_map/ppermute | solution.py:31
  139.0 11.4 %collective-permute-start.11 = (bf16[256,256]{1,0:T(8,128)(2,1)S(1)}, bf16[256,256]{1,0:T(8,128)(2,1)S(1)}, u32[]{:S(2)}, u32[]{:S(2)}) collective-permute-start(bf16[256,256]{1,0:T(8,128)(2,1)S(1)} %fusion.11), channel_id=1, source_target_pairs={{0,8},{8,0},{16,24},{24,16},{1,9},{9,1},{17,25},{25,17},{2,10},{10... | collective-permute-start | bytes 393224 | tf_op jit(solution)/shard_map/ppermute | solution.py:31
  150.4 42.1 %copy-start = (bf16[4,256,256]{2,1,0:T(8,128)(2,1)}, bf16[4,256,256]{2,1,0:T(8,128)(2,1)S(1)}, u32[]{:S(2)}) copy-start(bf16[4,256,256]{2,1,0:T(8,128)(2,1)S(1)} %pad_maximum_fusion.refs_4_) | copy-start | bytes 1572868
  150.5 15.9 %collective-permute-start.19 = (bf16[4,256,256]{2,1,0:T(8,128)(2,1)S(1)}, bf16[4,256,256]{2,1,0:T(8,128)(2,1)S(1)}, u32[]{:S(2)}, u32[]{:S(2)}) collective-permute-start(bf16[4,256,256]{2,1,0:T(8,128)(2,1)S(1)} %pad_maximum_fusion.refs_4_), channel_id=1, source_target_pairs={{0,6},{1,7},{2,4},{3,5},{4,2},{5,3},{6,0},{7,1},{8,14},{9,15},{10,... | collective-permute-start | bytes 1572872 | tf_op jit(solution)/shard_map/ppermute | solution.py:31
  152.0 23.7 %collective-permute-start.17 = (bf16[4,256,256]{2,1,0:T(8,128)(2,1)S(1)}, bf16[4,256,256]{2,1,0:T(8,128)(2,1)S(1)}, u32[]{:S(2)}, u32[]{:S(2)}) collective-permute-start(bf16[4,256,256]{2,1,0:T(8,128)(2,1)S(1)} %pad_maximum_fusion.refs_4_), channel_id=1, source_target_pairs={{0,4},{1,5},{2,6},{3,7},{4,0},{5,1},{6,2},{7,3},{8,12},{9,13},{10,... | collective-permute-start | bytes 1572872 | tf_op jit(solution)/shard_map/ppermute | solution.py:31
  153.4 22.2 %collective-permute-start.15 = (bf16[4,256,256]{2,1,0:T(8,128)(2,1)S(1)}, bf16[4,256,256]{2,1,0:T(8,128)(2,1)S(1)}, u32[]{:S(2)}, u32[]{:S(2)}) collective-permute-start(bf16[4,256,256]{2,1,0:T(8,128)(2,1)S(1)} %pad_maximum_fusion.refs_4_), channel_id=1, source_target_pairs={{0,2},{1,3},{2,0},{3,1},{4,6},{5,7},{6,4},{7,5},{8,10},{9,11},{10,... | collective-permute-start | bytes 1572872 | tf_op jit(solution)/shard_map/ppermute | solution.py:31
  154.0 38.5 %collective-permute-start.14 = (bf16[4,256,256]{2,1,0:T(8,128)(2,1)S(1)}, bf16[4,256,256]{2,1,0:T(8,128)(2,1)S(1)}, u32[]{:S(2)}, u32[]{:S(2)}) collective-permute-start(bf16[4,256,256]{2,1,0:T(8,128)(2,1)S(1)} %pad_maximum_fusion.refs_4_), channel_id=1, source_target_pairs={{0,1},{1,0},{2,3},{3,2},{4,5},{5,4},{6,7},{7,6},{8,9},{9,8},{10,11... | collective-permute-start | bytes 1572872 | tf_op jit(solution)/shard_map/ppermute | solution.py:31
  166.3 26.2 %copy-start.1 = (bf16[4,256,256]{2,1,0:T(8,128)(2,1)}, bf16[4,256,256]{2,1,0:T(8,128)(2,1)S(1)}, u32[]{:S(2)}) copy-start(bf16[4,256,256]{2,1,0:T(8,128)(2,1)S(1)} %collective-permute-done.19.refs_10_) | copy-start | bytes 1572868
  166.3 26.3 %collective-permute-start.20 = (bf16[4,256,256]{2,1,0:T(8,128)(2,1)S(1)}, bf16[4,256,256]{2,1,0:T(8,128)(2,1)S(1)}, u32[]{:S(2)}, u32[]{:S(2)}) collective-permute-start(bf16[4,256,256]{2,1,0:T(8,128)(2,1)S(1)} %collective-permute-done.19.refs_10_), channel_id=1, source_target_pairs={{0,1},{1,0},{2,3},{3,2},{4,5},{5,4},{6,7},{7,6},{8,9},{9,8},{10,11... | collective-permute-start | bytes 1572872 | tf_op jit(solution)/shard_map/ppermute | solution.py:31
  175.7 16.9 %copy-start.2 = (bf16[4,256,256]{2,1,0:T(8,128)(2,1)}, bf16[4,256,256]{2,1,0:T(8,128)(2,1)S(1)}, u32[]{:S(2)}) copy-start(bf16[4,256,256]{2,1,0:T(8,128)(2,1)S(1)} %collective-permute-done.17.refs_8_) | copy-start | bytes 1572868
  175.7 16.9 %collective-permute-start.18 = (bf16[4,256,256]{2,1,0:T(8,128)(2,1)S(1)}, bf16[4,256,256]{2,1,0:T(8,128)(2,1)}, u32[]{:S(2)}, u32[]{:S(2)}) collective-permute-start(bf16[4,256,256]{2,1,0:T(8,128)(2,1)S(1)} %collective-permute-done.17.refs_8_), channel_id=1, source_target_pairs={{0,1},{1,0},{2,3},{3,2},{4,5},{5,4},{6,7},{7,6},{8,9},{9,8},{10,11... | collective-permute-start | bytes 1572872 | tf_op jit(solution)/shard_map/ppermute | solution.py:31
  175.7 16.9 %copy-start.3 = (bf16[4,256,256]{2,1,0:T(8,128)(2,1)}, bf16[4,256,256]{2,1,0:T(8,128)(2,1)S(1)}, u32[]{:S(2)}) copy-start(bf16[4,256,256]{2,1,0:T(8,128)(2,1)S(1)} %collective-permute-done.15.refs_6_) | copy-start | bytes 1572868
  175.7 16.9 %collective-permute-start.16 = (bf16[4,256,256]{2,1,0:T(8,128)(2,1)S(1)}, bf16[4,256,256]{2,1,0:T(8,128)(2,1)}, u32[]{:S(2)}, u32[]{:S(2)}) collective-permute-start(bf16[4,256,256]{2,1,0:T(8,128)(2,1)S(1)} %collective-permute-done.15.refs_6_), channel_id=1, source_target_pairs={{0,1},{1,0},{2,3},{3,2},{4,5},{5,4},{6,7},{7,6},{8,9},{9,8},{10,11... | collective-permute-start | bytes 1572872 | tf_op jit(solution)/shard_map/ppermute | solution.py:31
  216.1 6.6 %collective-permute-start.21 = (bf16[4,1024,256]{2,1,0:T(8,128)(2,1)}, bf16[4,1024,256]{2,1,0:T(8,128)(2,1)S(1)}, u32[]{:S(2)}, u32[]{:S(2)}) collective-permute-start(bf16[4,1024,256]{2,1,0:T(8,128)(2,1)} %down.3), channel_id=1, source_target_pairs={{0,1},{1,0},{2,3},{3,2},{4,5},{5,4},{6,7},{7,6},{8,9},{9,8},{10,11... | collective-permute-start | bytes 6291464 | tf_op jit(solution)/shard_map/ppermute | solution.py:31
  225.1 14.8 %collective-permute-start.22 = (bf16[1024,256]{1,0:T(8,128)(2,1)S(1)}, bf16[1024,256]{1,0:T(8,128)(2,1)S(1)}, u32[]{:S(2)}, u32[]{:S(2)}) collective-permute-start(bf16[1024,256]{1,0:T(8,128)(2,1)S(1)} %get-tuple-element.28), channel_id=1, source_target_pairs={{0,2},{1,3},{2,0},{3,1},{4,6},{5,7},{6,4},{7,5},{8,10},{9,11},{10,... | collective-permute-start | bytes 1572872 | tf_op jit(solution)/shard_map/ppermute | solution.py:31
  226.0 24.8 %collective-permute-start.24 = (bf16[1024,256]{1,0:T(8,128)(2,1)S(1)}, bf16[1024,256]{1,0:T(8,128)(2,1)S(1)}, u32[]{:S(2)}, u32[]{:S(2)}) collective-permute-start(bf16[1024,256]{1,0:T(8,128)(2,1)S(1)} %get-tuple-element.29), channel_id=1, source_target_pairs={{0,6},{1,7},{2,4},{3,5},{4,2},{5,3},{6,0},{7,1},{8,14},{9,15},{10,... | collective-permute-start | bytes 1572872 | tf_op jit(solution)/shard_map/ppermute | solution.py:31
  227.2 24.9 %collective-permute-start.23 = (bf16[1024,256]{1,0:T(8,128)(2,1)S(1)}, bf16[1024,256]{1,0:T(8,128)(2,1)S(1)}, u32[]{:S(2)}, u32[]{:S(2)}) collective-permute-start(bf16[1024,256]{1,0:T(8,128)(2,1)S(1)} %get-tuple-element.30), channel_id=1, source_target_pairs={{0,4},{1,5},{2,6},{3,7},{4,0},{5,1},{6,2},{7,3},{8,12},{9,13},{10,... | collective-permute-start | bytes 1572872 | tf_op jit(solution)/shard_map/ppermute | solution.py:31
  252.4 7.2 %collective-permute-start.25 = (bf16[256,256]{1,0:T(8,128)(2,1)S(1)}, bf16[256,256]{1,0:T(8,128)(2,1)S(1)}, u32[]{:S(2)}, u32[]{:S(2)}) collective-permute-start(bf16[256,256]{1,0:T(8,128)(2,1)S(1)} %get-tuple-element.33), channel_id=1, source_target_pairs={{0,8},{8,0},{16,24},{24,16},{1,9},{9,1},{17,25},{25,17},{2,10},{10... | collective-permute-start | bytes 393224 | tf_op jit(solution)/shard_map/ppermute | solution.py:31
  252.4 9.0 %collective-permute-start.27 = (bf16[256,256]{1,0:T(8,128)(2,1)S(1)}, bf16[256,256]{1,0:T(8,128)(2,1)S(1)}, u32[]{:S(2)}, u32[]{:S(2)}) collective-permute-start(bf16[256,256]{1,0:T(8,128)(2,1)S(1)} %get-tuple-element.34), channel_id=1, source_target_pairs={{0,24},{8,16},{16,8},{24,0},{1,25},{9,17},{17,9},{25,1},{2,26},{10... | collective-permute-start | bytes 393224 | tf_op jit(solution)/shard_map/ppermute | solution.py:31
  254.4 11.9 %collective-permute-start.26 = (bf16[256,256]{1,0:T(8,128)(2,1)S(1)}, bf16[256,256]{1,0:T(8,128)(2,1)S(1)}, u32[]{:S(2)}, u32[]{:S(2)}) collective-permute-start(bf16[256,256]{1,0:T(8,128)(2,1)S(1)} %get-tuple-element.35), channel_id=1, source_target_pairs={{0,16},{8,24},{16,0},{24,8},{1,17},{9,25},{17,1},{25,9},{2,18},{10... | collective-permute-start | bytes 393224 | tf_op jit(solution)/shard_map/ppermute | solution.py:31
  (4 other events, 10.1 us)
Sparse Core Ops, SparseCore 0:
  9.6 30.6 all-gather.7
  41.8 27.4 all-gather.5
  70.9 45.4 all-gather.9

commit v2 on v1

v2 whole, which is shorter than its diff:
```python
import math

import jax
import jax.numpy as jnp
from jax import lax
from jax.experimental import pallas as pl
from jax.experimental.pallas import tpu as pltpu
from jax.sharding import PartitionSpec as P

HD = 128
CACHE_BLOCK = 2048
VMEM_LIMIT = 56 * 1024 * 1024
BF16 = jnp.bfloat16
F32 = jnp.float32


def vmem():
    return pl.BlockSpec(memory_space=pltpu.VMEM)


def smem():
    return pl.BlockSpec(memory_space=pltpu.SMEM)


def params():
    return pltpu.CompilerParams(vmem_limit_bytes=VMEM_LIMIT)


def swap(value, axis, mask):
    count = lax.axis_size(axis)
    return lax.ppermute(value, axis, [(one, one ^ mask) for one in range(count)])


def cost(flops, size):
    return pl.CostEstimate(flops=flops, bytes_accessed=size, transcendentals=0)


def ancestor_table(parents):
    nodes = parents.shape[-1]
    column = jnp.arange(nodes, dtype=jnp.int32)
    reach = (parents[:, :, None] == column[None, None, :]).astype(F32)
    reach = reach + jnp.eye(nodes, dtype=F32)[None]
    for _ in range((nodes - 1).bit_length()):
        reach = jnp.minimum(jnp.einsum("rij,rjk->rik", reach, reach), 1.0)
    return reach


def project_kernel(count, ids, gain, weight, *refs):
    pieces, outs, scaled = refs[:count], refs[count:-1], refs[-1]
    me_x, me_y = ids[0], ids[1]
    rows, width = pieces[0].shape
    share = scaled.shape[1] // width
    for mask, piece in enumerate(pieces):
        source = me_y ^ mask
        block, part = source // share, source % share
        columns = pl.ds(pl.multiple_of((me_x * share + part) * width, width), width)
        value = (piece[...].astype(F32) * gain[:, columns]).astype(BF16)
        scaled[
            pl.ds(pl.multiple_of(block * rows, rows), rows),
            pl.ds(pl.multiple_of(part * width, width), width),
        ] = value
    blocks = len(outs) // 2
    for mask in range(blocks):
        place = pl.ds(pl.multiple_of((me_x ^ mask) * rows, rows), rows)
        for which in range(3):
            value = jnp.dot(scaled[place, :], weight[which], preferred_element_type=F32)
            if which == 0:
                outs[mask][...] = value.astype(outs[mask].dtype)
            else:
                out = outs[blocks + mask]
                out[which - 1] = value.astype(out.dtype)


def blocked_query(query, request, draft, heads):
    rows = query[request * draft : (request + 1) * draft, :]
    if heads == 1:
        return rows
    column = lax.broadcasted_iota(jnp.int32, rows.shape, 1) // HD
    return jnp.concatenate(
        [jnp.where(column == head, rows, jnp.zeros_like(rows)) for head in range(heads)], axis=0
    )


def cache_kernel(
    requests, draft, heads, parts, lengths, owner, scale_of, *refs
):
    terms, (cache, top, mass, mixed, query, wide) = refs[:parts], refs[parts:]
    group, block = pl.program_id(0), pl.program_id(1)
    slots = cache.shape[2]

    @pl.when((group == 0) & (block == 0))
    def _():
        top[...] = jnp.full(top.shape, -jnp.inf, F32)
        mass[...] = jnp.zeros(mass.shape, F32)
        mixed[...] = jnp.zeros(mixed.shape, F32)
        total = terms[0][...]
        for term in terms[1:]:
            total = total + term[...].astype(F32)
        query[...] = (total * scale_of[...]).astype(BF16)
        for request in range(requests):
            wide[request] = blocked_query(query[...], request, draft, heads)

    left = lengths[group] - block * slots
    scale = 1.0 / math.sqrt(HD)
    for request in range(requests):

        @pl.when((owner[request] == group) & (left > 0))
        def _():
            scores = (
                lax.dot_general(
                    wide[request],
                    cache[0, 0],
                    (((1,), (1,)), ((), ())),
                    preferred_element_type=F32,
                )
                * scale
            )
            column = lax.broadcasted_iota(jnp.int32, scores.shape, 1)
            scores = jnp.where(column < left, scores, -jnp.inf)
            before = top[request]
            now = jnp.maximum(before, jnp.max(scores, axis=1, keepdims=True))
            powered = jnp.exp(scores - now[:, :1])
            fade = jnp.exp(before - now)
            top[request] = now
            mass[request] = mass[request] * fade + jnp.sum(powered, axis=1, keepdims=True)
            mixed[request] = mixed[request] * fade[:, :1] + jnp.dot(
                powered.astype(BF16), cache[0, 1], preferred_element_type=F32
            )


def draft_kernel(requests, draft, heads, parts, scale_of, *refs):
    pairs = refs[:parts]
    query, reach, rows, top, mass, mixed, attended, picked, key, value = refs[parts:]
    for which, kept in ((0, key), (1, value)):
        total = pairs[0][which]
        for pair in pairs[1:]:
            total = total + pair[which].astype(F32)
        kept[...] = (total * scale_of[...]).astype(BF16)
    tokens = key.shape[0]
    chosen = (
        lax.broadcasted_iota(jnp.int32, (rows.shape[0], tokens), 1) == rows[...]
    ).astype(BF16)
    picked[0] = jnp.dot(chosen, key[...], preferred_element_type=F32).astype(BF16)
    picked[1] = jnp.dot(chosen, value[...], preferred_element_type=F32).astype(BF16)
    scale = 1.0 / math.sqrt(HD)
    for request in range(requests):
        own = slice(request * draft, (request + 1) * draft)
        wide = blocked_query(query[...], request, draft, heads)
        scores = (
            lax.dot_general(
                wide, key[own, :], (((1,), (1,)), ((), ())), preferred_element_type=F32
            )
            * scale
        )
        seen = jnp.concatenate([reach[request]] * heads, axis=0)
        scores = jnp.where(seen > 0, scores, -jnp.inf)
        before = top[request][:, :1]
        now = jnp.maximum(before, jnp.max(scores, axis=1, keepdims=True))
        powered = jnp.exp(scores - now)
        fade = jnp.exp(before - now)
        sums = mass[request][:, :1] * fade + jnp.sum(powered, axis=1, keepdims=True)
        total = mixed[request] * fade + jnp.dot(
            powered.astype(BF16), value[own, :], preferred_element_type=F32
        )
        total = (total / sums).astype(BF16)
        for head in range(heads):
            attended[own, head * HD : (head + 1) * HD] = total[
                head * draft : (head + 1) * draft, head * HD : (head + 1) * HD
            ]


def output_kernel(count, ids, attended, output, *outs):
    me = ids[1]
    rows, width = outs[0].shape[-2:]
    for mask in range(count):
        place = pl.ds(pl.multiple_of((me ^ mask) * width, width), width)
        value = lax.dot_general(
            attended[...],
            output[place, :],
            (((1,), (1,)), ((), ())),
            preferred_element_type=F32,
        ).astype(BF16)
        outs[mask % 2][mask // 2] = value


def expert_kernel(count, unit, ids, gain, gates, weight, down, *refs):
    pieces, (odd, even, normed, total) = refs[:count], refs[count:]
    me_x, me_y = ids[0], ids[1]
    rows, width = pieces[0].shape
    step = pl.program_id(0)

    @pl.when(step == 0)
    def _():
        squares = jnp.zeros((rows, 1), F32)
        for piece in pieces:
            value = piece[...].astype(F32)
            squares = squares + jnp.sum(value * value, axis=1, keepdims=True)
        scale = lax.rsqrt(squares / (width * count) + 1e-05)
        for mask, piece in enumerate(pieces):
            columns = pl.ds(pl.multiple_of((me_y ^ mask) * width, width), width)
            value = piece[...].astype(F32) * scale * gain[:, columns]
            normed[:, columns] = value.astype(BF16)

    units = weight.shape[2] // 2
    both = jnp.dot(normed[...], weight[0], preferred_element_type=F32)
    gate, up = both[:, :units], both[:, units:]
    hidden = (gate / (1.0 + jnp.exp(-gate)) * up).astype(BF16)
    source = pl.ds(pl.multiple_of((me_x ^ unit) * rows, rows), rows)
    value = jnp.dot(hidden, down[0], preferred_element_type=F32) * gates[0, source, :]

    @pl.when(step == 0)
    def _():
        total[...] = value

    @pl.when(step > 0)
    def _():
        total[...] += value

    @pl.when(step == pl.num_programs(0) - 1)
    def _():
        for mask in range(count):
            columns = pl.ds(pl.multiple_of((me_y ^ mask) * width, width), width)
            (odd if mask % 2 else even)[mask // 2] = total[:, columns].astype(BF16)


def per_device(
    tokens,
    attention_gain,
    projection_weight,
    output_weight,
    prompt_cache,
    cache_length,
    prompt_group,
    parents,
    accepted_path,
    expert_gain,
    gate_up_weight,
    down_weight,
    route_experts,
    route_gates,
):
    gx_count, gy_count = lax.axis_size("gx"), lax.axis_size("gy")
    ids = jnp.stack([lax.axis_index("gx"), lax.axis_index("gy")]).astype(jnp.int32)
    rows, width = tokens.shape
    depth = attention_gain.shape[0]
    requests, draft = parents.shape
    groups = prompt_cache.shape[0]
    heads = width // HD

    output_full = lax.all_gather(output_weight, "gx", axis=0, tiled=True)

    wide_tokens = tokens.astype(F32)
    squares = jnp.sum(wide_tokens * wide_tokens, axis=1, keepdims=True)
    for bit in range(gy_count.bit_length() - 1):
        squares = squares + swap(squares, "gy", 1 << bit)
    row_scale = lax.rsqrt(squares / depth + 1e-05)

    share = gy_count // gx_count
    route = [
        (a * gy_count + b, (b // share) * gy_count + a * share + b % share)
        for a in range(gx_count)
        for b in range(gy_count)
    ]
    pieces = gather_gy(lax.ppermute(tokens, ("gx", "gy"), route))
    types = [F32] + [BF16] * (gx_count - 1)
    projected = pl.pallas_call(
        lambda *refs: project_kernel(gy_count, *refs),
        out_shape=[jax.ShapeDtypeStruct((rows, width), kind) for kind in types]
        + [jax.ShapeDtypeStruct((2, rows, width), kind) for kind in types],
        in_specs=[smem()] + [vmem()] * (2 + gy_count),
        out_specs=[vmem()] * (2 * gx_count),
        scratch_shapes=[pltpu.VMEM((gx_count * rows, share * width), BF16)],
        compiler_params=params(),
        name="project",
    )(
        ids, attention_gain.reshape(1, depth), jnp.transpose(projection_weight, (1, 0, 2)), *pieces
    )
    query_terms, pair_terms = projected[:gx_count], projected[gx_count:]
    query_terms = [query_terms[0]] + [
        swap(query_terms[mask], "gx", mask) for mask in range(1, gx_count)
    ]
    pair_terms = [pair_terms[0]] + [
        swap(pair_terms[mask], "gx", mask) for mask in range(1, gx_count)
    ]

    experts = gate_up_weight.shape[0]
    units = gate_up_weight.shape[3]
    gate_up = gate_up_weight.reshape(experts, depth, 2 * units)
    gate_up, query_terms[0] = lax.optimization_barrier((gate_up, query_terms[0]))

    slots = prompt_cache.shape[2]
    step = min(CACHE_BLOCK, slots)
    wide_rows = heads * draft
    constant = lambda *_: (0, 0, 0)
    flat = lambda *_: (0, 0)
    top, mass, mixed, query = pl.pallas_call(
        lambda *refs: cache_kernel(requests, draft, heads, gx_count, *refs),
        grid_spec=pltpu.PrefetchScalarGridSpec(
            num_scalar_prefetch=2,
            grid=(groups, slots // step),
            in_specs=[pl.BlockSpec((rows, 1), flat)]
            + [pl.BlockSpec((rows, width), flat)] * gx_count
            + [
                pl.BlockSpec(
                    (1, 2, step, width),
                    lambda group, block, lengths, owner: (
                        group,
                        0,
                        jnp.minimum(block, (lengths[group] - 1) // step),
                        0,
                    ),
                ),
            ],
            out_specs=[
                pl.BlockSpec((requests, wide_rows, HD), constant),
                pl.BlockSpec((requests, wide_rows, HD), constant),
                pl.BlockSpec((requests, wide_rows, width), constant),
                pl.BlockSpec((rows, width), flat),
            ],
            scratch_shapes=[pltpu.VMEM((requests, wide_rows, width), BF16)],
        ),
        out_shape=(
            jax.ShapeDtypeStruct((requests, wide_rows, HD), F32),
            jax.ShapeDtypeStruct((requests, wide_rows, HD), F32),
            jax.ShapeDtypeStruct((requests, wide_rows, width), F32),
            jax.ShapeDtypeStruct((rows, width), BF16),
        ),
        compiler_params=params(),
        cost_estimate=cost(20 * rows * slots * width, 4 * groups * slots * width),
        name="cache",
    )(cache_length, prompt_group % groups, row_scale, *query_terms, prompt_cache)

    accepted = accepted_path.shape[1]
    chosen = (jnp.arange(requests, dtype=jnp.int32)[:, None] * draft + accepted_path).reshape(-1, 1)
    attended, picked = pl.pallas_call(
        lambda *refs: draft_kernel(requests, draft, heads, gx_count, *refs),
        out_shape=(
            jax.ShapeDtypeStruct((rows, width), BF16),
            jax.ShapeDtypeStruct((2, requests * accepted, width), BF16),
        ),
        in_specs=[vmem()] * (gx_count + 7),
        out_specs=(vmem(), vmem()),
        scratch_shapes=[
            pltpu.VMEM((rows, width), BF16),
            pltpu.VMEM((rows, width), BF16),
        ],
        compiler_params=params(),
        name="draft",
    )(row_scale, *pair_terms, query, ancestor_table(parents), chosen, top, mass, mixed)
    compacted = jnp.transpose(picked, (1, 0, 2))

    half = jax.ShapeDtypeStruct((gy_count // 2, rows, width), BF16)
    even, odd = pl.pallas_call(
        lambda *refs: output_kernel(gy_count, *refs),
        out_shape=(half, half),
        in_specs=[smem(), vmem(), vmem()],
        out_specs=(vmem(), vmem()),
        compiler_params=params(),
        name="output",
    )(ids, attended, output_full)

    summed = even.astype(F32) + swap(odd, "gy", 1).astype(F32)
    stream = tokens.astype(F32) + summed[0]
    for place in range(1, gy_count // 2):
        stream = stream + swap(summed[place].astype(BF16), "gy", 2 * place).astype(F32)
    stream = stream.astype(BF16)

    expert_ids = lax.axis_index("gy") * experts + jnp.arange(experts, dtype=jnp.int32)
    hit = route_experts[None] == expert_ids[:, None, None]
    gates = jnp.sum(jnp.where(hit, route_gates.astype(F32)[None], 0.0), axis=2)[:, :, None]
    result = stream.astype(F32)
    for unit in range(gx_count):
        one = stream if unit == 0 else swap(stream, "gx", unit)
        everything = double_gy(one, unit % 2)
        odd, even = pl.pallas_call(
            lambda *refs: expert_kernel(gy_count, unit, *refs),
            grid=(experts,),
            in_specs=[
                smem(),
                pl.BlockSpec((1, depth), lambda expert: (0, 0)),
                pl.BlockSpec((1, gx_count * rows, 1), lambda expert: (expert, 0, 0)),
                pl.BlockSpec((1, depth, 2 * units), lambda expert: (expert, 0, 0)),
                pl.BlockSpec((1, units, depth), lambda expert: (expert, 0, 0)),
            ]
            + [vmem()] * gy_count,
            out_specs=[vmem(), vmem()],
            out_shape=(half, half),
            scratch_shapes=[pltpu.VMEM((rows, depth), BF16), pltpu.VMEM((rows, depth), F32)],
            compiler_params=params(),
            cost_estimate=cost(
                6 * rows * depth * experts * units, 6 * depth * experts * units
            ),
            name="experts",
        )(ids, expert_gain.reshape(1, depth), gates, gate_up, down_weight, *everything)
        summed = even.astype(F32) + swap(odd, "gy", 1).astype(F32)
        total = halve_gy(summed, unit % 2)
        if unit:
            total = swap(total.astype(BF16), "gx", unit).astype(F32)
        result = result + total
    return (result.astype(BF16), compacted)


def gather_gy(value):
    count = lax.axis_size("gy")
    even = [value] + [swap(value, "gy", mask) for mask in range(2, count, 2)]
    pieces = []
    for one in even:
        pieces += [one, swap(one, "gy", 1)]
    return pieces


def far_bits(turn):
    bits = list(range(1, lax.axis_size("gy").bit_length() - 1))
    return bits[::-1] if turn else bits


def double_gy(value, turn):
    held = {0: value}
    for bit in far_bits(turn):
        held.update({mask | 1 << bit: swap(one, "gy", 1 << bit) for mask, one in held.items()})
    held.update({mask | 1: swap(one, "gy", 1) for mask, one in held.items()})
    return [held[mask] for mask in range(len(held))]


def halve_gy(value, turn):
    held = [(2 * place, value[place]) for place in range(value.shape[0])]
    for bit in far_bits(turn):
        mine = [(mask, one) for mask, one in held if not mask >> bit & 1]
        sent = jnp.stack([one for mask, one in held if mask >> bit & 1]).astype(BF16)
        got = swap(sent, "gy", 1 << bit).astype(F32)
        held = [(mask, one + got[place]) for place, (mask, one) in enumerate(mine)]
    return held[0][1]


def solution(mesh):
    placed = (
        P("gx", "gy"),
        P(),
        P("gx", None, "gy"),
        P("gx", "gy"),
        P("gx", None, None, "gy"),
        P("gx"),
        P("gx"),
        P("gx", None),
        P("gx", None),
        P(),
        P("gy", None, None, "gx"),
        P("gy", "gx", None),
        P(),
        P(),
    )
    return jax.shard_map(
        per_device,
        mesh=mesh,
        in_specs=placed,
        out_specs=(P("gx", "gy"), P("gx", None, "gy")),
        check_vma=False,
    )
```

time: 274 us -> 230 us (0.84)
  waiting for transfers between devices: 151 us -> 40.9 us
  starting transfers between devices: 24.3 us -> 67 us
  Pallas kernels: 52.9 us -> 72.2 us
    all_gather x2 -> x0, waiting for transfers between devices: 62.3 us -> none  [the longest x1 47 us: per_device(): pair_weight = lax.all_gather(by_part[1:], 'gx', axis=0, tiled=False)]
    ppermute x28 -> x66, starting transfers between devices: 24.2 us -> 65.4 us  [swap(): lax.ppermute(value, axis, [(one, one ^ mask) for one in range(count)])]
    ppermute x28 -> x66, waiting for transfers between devices: 77 us -> 40.9 us  [swap(): lax.ppermute(value, axis, [(one, one ^ mask) for one in range(count)])]
    pallas_call x6 -> x8, Pallas kernels: 52.9 us -> 72.2 us  [the longest x4 43.2 us: per_device(): pl.pallas_call(lambda *refs: expert_kernel(gy_count, unit, *refs), grid=(...]
    all_gather x1, waiting for transfers between devices: 11.3 us -> 0.01 us  [per_device(): output_full = lax.all_gather(output_weight, 'gx', axis=0, tiled=True)]
    slice x4 -> x2, local copies, waits for them, and re-layouts: 4.7 us -> 0.04 us  [halve_gy(): held = [(2 * place, value[place]) for place in range(value.shape[0])]]
    unnamed x43 -> x115, local copies, waits for them, and re-layouts: 1.68 us -> 6.15 us
  transfers between devices with their start and end apart: 31 -> 68, of which waited for: 20 -> 17; matrix products, arithmetic and copies ran while one was open for 8% -> 11% of each run, Pallas kernels for 9% -> 30%
where the time goes in v2:
time: 230 us; the launch traced here: 228 us
  Pallas kernels  72.2 us (31%)
  starting transfers between devices  67 us (29%)
  waiting for transfers between devices  40.9 us (18%)
  local copies, waits for them, and re-layouts  23.1 us (10%)
  between operations  14.8 us (6%)
  other arithmetic  7.51 us (3%)
  matrix products  2.53 us (1%)
    ppermute x66, starting transfers between devices, swap(): lax.ppermute(value, axis, [(one, one ^ mask) for one in range(count)])  65.4 us
    pallas_call x4, Pallas kernels, per_device(): pl.pallas_call(lambda *refs: expert_kernel(gy_count, unit, *refs), grid=(...  43.2 us
    ppermute x66, waiting for transfers between devices, swap(): lax.ppermute(value, axis, [(one, one ^ mask) for one in range(count)])  40.9 us
    pallas_call x1, Pallas kernels, per_device(): pl.pallas_call(lambda *refs: cache_kernel(requests, draft, heads, gx_coun...  18.8 us
    reshape x1, local copies, waits for them, and re-layouts, per_device(): gate_up = gate_up_weight.reshape(experts, depth, 2 * units)  14 us
    unnamed x115, local copies, waits for them, and re-layouts  6.15 us
  transfers between devices with their start and end apart: 68, of which 17 were waited for; matrix products, arithmetic and copies ran while one was open for 11% of the time, Pallas kernels for 30%

profile of v2, /device:TPU:0, one launch (start us, length us, event | category | flops | bytes accessed | tf_op | source)
XLA Modules:
  0.0 228.1 jit_solution(8119593344866005147)
XLA Ops:
  7.2 1.6 collective-permute-start.3
  10.5 1.3 convolution_minimum_fusion.4
  13.0 11.0 %collective-permute-start.5 = (bf16[256,256]{1,0:T(8,128)(2,1)S(1)}, bf16[256,256]{1,0:T(8,128)(2,1)S(1)}, u32[]{:S(2)}, u32[]{:S(2)}) collective-permute-start(bf16[256,256]{1,0:T(8,128)(2,1)S(1)} %collective-permute-done.3.refs_3_), channel_id=1, source_target_pairs={{0,2},{1,3},{2,0},{3,1},{4,6},{5,7},{6,4},{7,5},{8,10},{9,11},{10,... | collective-permute-start | bytes 393224 | tf_op jit(solution)/shard_map/ppermute | solution.py:31
  24.0 1.5 collective-permute-start.9
  26.2 2.1 collective-permute-start.1
  28.9 2.2 collective-permute-done.7.refs_7_
  31.5 1.2 and_select_fusion.refs_1_
  32.8 1.2 collective-permute-start.2
  34.7 14.0 %reshape.58.refs_3_ = bf16[4,2048,512]{2,1,0:T(8,128)(2,1)} reshape(bf16[4,2048,2,256]{3,2,1,0:T(2,128)(2,1)} %param.24) | data formatting | bytes 16777216 | tf_op jit(solution)/shard_map/reshape | solution.py:288
  50.2 3.6 %project.1 = (f32[256,256]{1,0:T(8,128)}, bf16[256,256]{1,0:T(8,128)(2,1)}, bf16[256,256]{1,0:T(8,128)(2,1)}, bf16[256,256]{1,0:T(8,128)(2,1)}, f32[2,256,256]{2...) custom-call(s32[2]{0:T(128)} %pad_add_fusion.refs_0_, ...), custom_call_target="tpu_custom_call" | custom-call | tf_op jit(solution)/shard_map/project/pallas_call | solution.py:266
  53.8 4.4 %collective-permute-start.15 = (bf16[256,256]{1,0:T(8,128)(2,1)}, bf16[256,256]{1,0:T(8,128)(2,1)S(1)}, u32[]{:S(2)}, u32[]{:S(2)}) collective-permute-start(bf16[256,256]{1,0:T(8,128)(2,1)} %get-tuple-element.35), channel_id=1, source_target_pairs={{0,16},{8,24},{16,0},{24,8},{1,17},{9,25},{17,1},{25,9},{2,18},{10... | collective-permute-start | bytes 393224 | tf_op jit(solution)/shard_map/ppermute | solution.py:31
  59.5 3.8 %collective-permute-start.12 = (bf16[2,256,256]{2,1,0:T(8,128)(2,1)}, bf16[2,256,256]{2,1,0:T(8,128)(2,1)S(1)}, u32[]{:S(2)}, u32[]{:S(2)}) collective-permute-start(bf16[2,256,256]{2,1,0:T(8,128)(2,1)} %get-tuple-element.30), channel_id=1, source_target_pairs={{0,16},{8,24},{16,0},{24,8},{1,17},{9,25},{17,1},{25,9},{2,18},{10... | collective-permute-start | bytes 786440 | tf_op jit(solution)/shard_map/ppermute | solution.py:31
  63.3 1.5 collective-permute-start.13
  64.9 3.6 %collective-permute-done.15.refs_5_ = bf16[256,256]{1,0:T(8,128)(2,1)S(1)} collective-permute-done((bf16[256,256]{1,0:T(8,128)(2,1)}, bf16[256,256]{1,0:T(8,128)(2,1)S(1)}, u32[]{:S(2)}, u32[]{:S(2)}) %collective-permute-start.15) | collective-permute-done | bytes 131104 | tf_op jit(solution)/shard_map/ppermute | solution.py:31
  69.8 18.8 %cache.1 = (f32[4,128,128]{2,1,0:T(8,128)}, f32[4,128,128]{2,1,0:T(8,128)}, f32[4,128,256]{2,1,0:T(8,128)}, bf16[256,256]{1,0:T(8,128)(2,1)}) custom-call(s32[2]{0:T(128)} %refs_0_.1, s32[4]{0:T(128)} %and_select_fusion.refs_1_, f32[256,1]{1,0:T(8,128)} %add_rsqrt_fusion.refs_2_.refs_0_, f32[256,256]{1,0:T(8,128)} %get-tuple-element.33.refs_3_, ...), custom_call_target="tpu_custom_call" | custom-call | flops 10737418240 | bytes 16777216 | tf_op jit(solution)/shard_map/cache/pallas_call | solution.py:296
  89.5 3.8 %draft.1 = (bf16[256,256]{1,0:T(8,128)(2,1)}, bf16[2,32,256]{2,1,0:T(8,128)(2,1)}) custom-call(f32[256,1]{1,0:T(8,128)} %add_rsqrt_fusion.refs_2_.refs_0_, f32[2,256,256]{2,1,0:T(8,128)} %get-tuple-element.28.refs_1_, bf16[2,256,256]{2,1,0:T(8,128)(2,1)} %copy-done.7, bf16[2,256,256]{2,1,0:T(8,128)(2,1)} %copy-done.8, bf16[2,256,256]{2,1,0:T(8,128)(2,1)} %copy-done.9, ...), custom_call_target="tpu_custom_call" | custom-call | tf_op jit(solution)/shard_map/draft/pallas_call | solution.py:335
  93.3 2.8 %output.1 = (bf16[4,256,256]{2,1,0:T(8,128)(2,1)}, bf16[4,256,256]{2,1,0:T(8,128)(2,1)}) custom-call(s32[2]{0:T(128)} %pad_add_fusion.refs_0_, bf16[256,256]{1,0:T(8,128)(2,1)} %get-tuple-element.41.refs_1_, bf16[2048,256]{1,0:T(8,128)(2,1)} %all-gather.2.cloned.1.call-done.refs_2_), custom_call_target="tpu_custom_call" | custom-call | tf_op jit(solution)/shard_map/output/pallas_call | solution.py:353
  96.1 2.1 collective-permute-done.17
  98.3 1.2 fusion.41
  99.5 1.3 collective-permute-start.20
  101.7 1.3 collective-permute-start.18
  103.0 3.8 %collective-permute-done.20 = bf16[256,256]{1,0:T(8,128)(2,1)S(1)} collective-permute-done((bf16[256,256]{1,0:T(8,128)(2,1)S(1)}, bf16[256,256]{1,0:T(8,128)(2,1)S(1)}, u32[]{:S(2)}, u32[]{:S(2)}) %collective-permute-start.20) | collective-permute-done | bytes 131104 | tf_op jit(solution)/shard_map/ppermute | solution.py:31
  106.8 2.0 collective-permute-done.19
  109.7 1.1 collective-permute-start.24
  110.8 1.8 collective-permute-start.55
  112.7 4.4 %collective-permute-start.43 = (bf16[256,256]{1,0:T(8,128)(2,1)S(1)}, bf16[256,256]{1,0:T(8,128)(2,1)S(1)}, u32[]{:S(2)}, u32[]{:S(2)}) collective-permute-start(bf16[256,256]{1,0:T(8,128)(2,1)S(1)} %fusion.4.refs_5_), channel_id=1, source_target_pairs={{0,16},{8,24},{16,0},{24,8},{1,17},{9,25},{17,1},{25,9},{2,18},{10... | collective-permute-start | bytes 393224 | tf_op jit(solution)/shard_map/ppermute | solution.py:31
  118.9 7.4 %collective-permute-done.43.refs_5_ = bf16[256,256]{1,0:T(8,128)(2,1)S(1)} collective-permute-done((bf16[256,256]{1,0:T(8,128)(2,1)S(1)}, bf16[256,256]{1,0:T(8,128)(2,1)S(1)}, u32[]{:S(2)}, u32[]{:S(2)}) %collective-permute-start.43) | collective-permute-done | bytes 131104 | tf_op jit(solution)/shard_map/ppermute | solution.py:31
  126.4 1.3 collective-permute-start.57
  129.5 1.1 collective-permute-start.47
  130.6 2.1 collective-permute-done.57.refs_7_
  132.7 1.3 collective-permute-done.59.refs_9_
  134.6 2.0 copy.33.refs_2_
  138.0 1.2 collective-permute-start.49
  139.2 10.8 %experts.4 = (bf16[4,256,256]{2,1,0:T(8,128)(2,1)}, bf16[4,256,256]{2,1,0:T(8,128)(2,1)}) custom-call(s32[2]{0:T(128)} %pad_add_fusion.refs_0_, f32[1,2048]{1,0:T(1,128)} %bitcast.41, f32[4,1024,1]{2,1,0:T(8,128)} %copy.33.refs_2_, bf16[4,2048,512]{2,1,0:T(8,128)(2,1)} %reshape.58.refs_3_, bf16[4,256,2048]{2,1,0:T(8,128)(2,1)} %refs_4_.7, ...), custom_call_target="tpu_custom_call" | custom-call | flops 3221225472 | bytes 12582912 | tf_op jit(solution)/shard_map/experts/pallas_call | solution.py:375
  150.1 1.7 collective-permute-start.33
  153.4 10.8 %experts.7 = (bf16[4,256,256]{2,1,0:T(8,128)(2,1)}, bf16[4,256,256]{2,1,0:T(8,128)(2,1)}) custom-call(s32[2]{0:T(128)} %pad_add_fusion.refs_0_, f32[1,2048]{1,0:T(1,128)} %bitcast.42, f32[4,1024,1]{2,1,0:T(8,128)} %copy.33.refs_2_, bf16[4,2048,512]{2,1,0:T(8,128)(2,1)} %reshape.58.refs_3_, bf16[4,256,2048]{2,1,0:T(8,128)(2,1)} %refs_4_.7, ...), custom_call_target="tpu_custom_call" | custom-call | flops 3221225472 | bytes 12582912 | tf_op jit(solution)/shard_map/experts/pallas_call | solution.py:375
  166.1 10.8 %experts.6 = (bf16[4,256,256]{2,1,0:T(8,128)(2,1)}, bf16[4,256,256]{2,1,0:T(8,128)(2,1)}) custom-call(s32[2]{0:T(128)} %pad_add_fusion.refs_0_, f32[1,2048]{1,0:T(1,128)} %bitcast.43, f32[4,1024,1]{2,1,0:T(8,128)} %copy.33.refs_2_, bf16[4,2048,512]{2,1,0:T(8,128)(2,1)} %reshape.58.refs_3_, bf16[4,256,2048]{2,1,0:T(8,128)(2,1)} %refs_4_.7, ...), custom_call_target="tpu_custom_call" | custom-call | flops 3221225472 | bytes 12582912 | tf_op jit(solution)/shard_map/experts/pallas_call | solution.py:375
  178.8 10.8 %experts.5 = (bf16[4,256,256]{2,1,0:T(8,128)(2,1)}, bf16[4,256,256]{2,1,0:T(8,128)(2,1)}) custom-call(s32[2]{0:T(128)} %pad_add_fusion.refs_0_, f32[1,2048]{1,0:T(1,128)} %bitcast.44, f32[4,1024,1]{2,1,0:T(8,128)} %copy.33.refs_2_, bf16[4,2048,512]{2,1,0:T(8,128)(2,1)} %reshape.58.refs_3_, bf16[4,256,2048]{2,1,0:T(8,128)(2,1)} %refs_4_.7, ...), custom_call_target="tpu_custom_call" | custom-call | flops 3221225472 | bytes 12582912 | tf_op jit(solution)/shard_map/experts/pallas_call | solution.py:375
  190.0 1.7 collective-permute-start.29
  191.8 1.1 collective-permute-start.64
  193.6 1.2 collective-permute-start.40
  194.8 4.3 %collective-permute-done.29 = bf16[2,256,256]{2,1,0:T(8,128)(2,1)S(1)} collective-permute-done((bf16[2,256,256]{2,1,0:T(8,128)(2,1)S(1)}, bf16[2,256,256]{2,1,0:T(8,128)(2,1)S(1)}, u32[]{:S(2)}, u32[]{:S(2)}) %collective-permute-start.29) | collective-permute-done | bytes 262176 | tf_op jit(solution)/shard_map/ppermute | solution.py:31
  202.1 2.6 %collective-permute-done.52 = bf16[2,256,256]{2,1,0:T(8,128)(2,1)S(1)} collective-permute-done((bf16[2,256,256]{2,1,0:T(8,128)(2,1)S(1)}, bf16[2,256,256]{2,1,0:T(8,128)(2,1)S(1)}, u32[]{:S(2)}, u32[]{:S(2)}) %collective-permute-start.52) | collective-permute-done | bytes 262176 | tf_op jit(solution)/shard_map/ppermute | solution.py:31
  207.8 2.0 collective-permute-start.66
  209.8 1.7 collective-permute-done.53
  212.0 2.1 collective-permute-start.42
  214.7 1.1 collective-permute-done.66
  215.8 4.6 %collective-permute-done.54 = bf16[256,256]{1,0:T(8,128)(2,1)S(1)} collective-permute-done((bf16[256,256]{1,0:T(8,128)(2,1)S(1)}, bf16[256,256]{1,0:T(8,128)(2,1)S(1)}, u32[]{:S(2)}, u32[]{:S(2)}) %collective-permute-start.54) | collective-permute-done | bytes 131104 | tf_op jit(solution)/shard_map/ppermute | solution.py:31
  (256 shorter events, 32.3 us)
Async XLA Ops:
  7.2 86.2 %all-gather.2.cloned.1.call-start = ((), (), s32[]{:S(2)}) async-start(), calls=%async_computation | async-start | bytes 1310720 | tf_op jit(solution)/shard_map/all_gather | solution.py:250
  9.9 16.3 %collective-permute-start = (f32[256,1]{1,0:T(8,128)S(1)}, f32[256,1]{1,0:T(8,128)S(1)}, u32[]{:S(2)}, u32[]{:S(2)}) collective-permute-start(f32[256,1]{1,0:T(8,128)S(1)} %copy.31), channel_id=1, source_target_pairs={{0,1},{1,0},{2,3},{3,2},{4,5},{5,4},{6,7},{7,6},{8,9},{9,8},{10,11... | collective-permute-start | bytes 3080 | tf_op jit(solution)/shard_map/ppermute | solution.py:31
  13.0 15.3 %collective-permute-start.5 = (bf16[256,256]{1,0:T(8,128)(2,1)S(1)}, bf16[256,256]{1,0:T(8,128)(2,1)S(1)}, u32[]{:S(2)}, u32[]{:S(2)}) collective-permute-start(bf16[256,256]{1,0:T(8,128)(2,1)S(1)} %collective-permute-done.3.refs_3_), channel_id=1, source_target_pairs={{0,2},{1,3},{2,0},{3,1},{4,6},{5,7},{6,4},{7,5},{8,10},{9,11},{10,... | collective-permute-start | bytes 393224 | tf_op jit(solution)/shard_map/ppermute | solution.py:31
  28.3 21.1 %collective-permute-start.4 = (bf16[256,256]{1,0:T(8,128)(2,1)S(1)}, bf16[256,256]{1,0:T(8,128)(2,1)S(1)}, u32[]{:S(2)}, u32[]{:S(2)}) collective-permute-start(bf16[256,256]{1,0:T(8,128)(2,1)S(1)} %collective-permute-done.3.refs_3_), channel_id=1, source_target_pairs={{0,1},{1,0},{2,3},{3,2},{4,5},{5,4},{6,7},{7,6},{8,9},{9,8},{10,11... | collective-permute-start | bytes 393224 | tf_op jit(solution)/shard_map/ppermute | solution.py:31
  28.3 21.0 %collective-permute-start.6 = (bf16[256,256]{1,0:T(8,128)(2,1)S(1)}, bf16[256,256]{1,0:T(8,128)(2,1)S(1)}, u32[]{:S(2)}, u32[]{:S(2)}) collective-permute-start(bf16[256,256]{1,0:T(8,128)(2,1)S(1)} %collective-permute-done.5.refs_5_), channel_id=1, source_target_pairs={{0,1},{1,0},{2,3},{3,2},{4,5},{5,4},{6,7},{7,6},{8,9},{9,8},{10,11... | collective-permute-start | bytes 393224 | tf_op jit(solution)/shard_map/ppermute | solution.py:31
  31.0 18.4 %collective-permute-start.8 = (bf16[256,256]{1,0:T(8,128)(2,1)S(1)}, bf16[256,256]{1,0:T(8,128)(2,1)S(1)}, u32[]{:S(2)}, u32[]{:S(2)}) collective-permute-start(bf16[256,256]{1,0:T(8,128)(2,1)S(1)} %collective-permute-done.7.refs_7_), channel_id=1, source_target_pairs={{0,1},{1,0},{2,3},{3,2},{4,5},{5,4},{6,7},{7,6},{8,9},{9,8},{10,11... | collective-permute-start | bytes 393224 | tf_op jit(solution)/shard_map/ppermute | solution.py:31
  31.0 18.4 %collective-permute-start.10 = (bf16[256,256]{1,0:T(8,128)(2,1)S(1)}, bf16[256,256]{1,0:T(8,128)(2,1)S(1)}, u32[]{:S(2)}, u32[]{:S(2)}) collective-permute-start(bf16[256,256]{1,0:T(8,128)(2,1)S(1)} %collective-permute-done.9.refs_9_), channel_id=1, source_target_pairs={{0,1},{1,0},{2,3},{3,2},{4,5},{5,4},{6,7},{7,6},{8,9},{9,8},{10,11... | collective-permute-start | bytes 393224 | tf_op jit(solution)/shard_map/ppermute | solution.py:31
  32.8 25.5 %collective-permute-start.2 = (f32[256,1]{1,0:T(8,128)S(1)}, f32[256,1]{1,0:T(8,128)S(1)}, u32[]{:S(2)}, u32[]{:S(2)}) collective-permute-start(f32[256,1]{1,0:T(8,128)S(1)} %add.137), channel_id=1, source_target_pairs={{0,4},{1,5},{2,6},{3,7},{4,0},{5,1},{6,2},{7,3},{8,12},{9,13},{10,... | collective-permute-start | bytes 3080 | tf_op jit(solution)/shard_map/ppermute | solution.py:31
  53.8 9.5 %collective-permute-start.14 = (bf16[256,256]{1,0:T(8,128)(2,1)}, bf16[256,256]{1,0:T(8,128)(2,1)S(1)}, u32[]{:S(2)}, u32[]{:S(2)}) collective-permute-start(bf16[256,256]{1,0:T(8,128)(2,1)} %get-tuple-element.34), channel_id=1, source_target_pairs={{0,8},{8,0},{16,24},{24,16},{1,9},{9,1},{17,25},{25,17},{2,10},{10... | collective-permute-start | bytes 393224 | tf_op jit(solution)/shard_map/ppermute | solution.py:31
  53.8 14.7 %collective-permute-start.15 = (bf16[256,256]{1,0:T(8,128)(2,1)}, bf16[256,256]{1,0:T(8,128)(2,1)S(1)}, u32[]{:S(2)}, u32[]{:S(2)}) collective-permute-start(bf16[256,256]{1,0:T(8,128)(2,1)} %get-tuple-element.35), channel_id=1, source_target_pairs={{0,16},{8,24},{16,0},{24,8},{1,17},{9,25},{17,1},{25,9},{2,18},{10... | collective-permute-start | bytes 393224 | tf_op jit(solution)/shard_map/ppermute | solution.py:31
  58.2 10.2 %collective-permute-start.16 = (bf16[256,256]{1,0:T(8,128)(2,1)}, bf16[256,256]{1,0:T(8,128)(2,1)S(1)}, u32[]{:S(2)}, u32[]{:S(2)}) collective-permute-start(bf16[256,256]{1,0:T(8,128)(2,1)} %get-tuple-element.36), channel_id=1, source_target_pairs={{0,24},{8,16},{16,8},{24,0},{1,25},{9,17},{17,9},{25,1},{2,26},{10... | collective-permute-start | bytes 393224 | tf_op jit(solution)/shard_map/ppermute | solution.py:31
  58.9 29.7 %collective-permute-start.11 = (bf16[2,256,256]{2,1,0:T(8,128)(2,1)}, bf16[2,256,256]{2,1,0:T(8,128)(2,1)S(1)}, u32[]{:S(2)}, u32[]{:S(2)}) collective-permute-start(bf16[2,256,256]{2,1,0:T(8,128)(2,1)} %get-tuple-element.29), channel_id=1, source_target_pairs={{0,8},{8,0},{16,24},{24,16},{1,9},{9,1},{17,25},{25,17},{2,10},{10... | collective-permute-start | bytes 786440 | tf_op jit(solution)/shard_map/ppermute | solution.py:31
  59.5 29.1 %collective-permute-start.12 = (bf16[2,256,256]{2,1,0:T(8,128)(2,1)}, bf16[2,256,256]{2,1,0:T(8,128)(2,1)S(1)}, u32[]{:S(2)}, u32[]{:S(2)}) collective-permute-start(bf16[2,256,256]{2,1,0:T(8,128)(2,1)} %get-tuple-element.30), channel_id=1, source_target_pairs={{0,16},{8,24},{16,0},{24,8},{1,17},{9,25},{17,1},{25,9},{2,18},{10... | collective-permute-start | bytes 786440 | tf_op jit(solution)/shard_map/ppermute | solution.py:31
  63.3 25.3 %collective-permute-start.13 = (bf16[2,256,256]{2,1,0:T(8,128)(2,1)}, bf16[2,256,256]{2,1,0:T(8,128)(2,1)S(1)}, u32[]{:S(2)}, u32[]{:S(2)}) collective-permute-start(bf16[2,256,256]{2,1,0:T(8,128)(2,1)} %get-tuple-element.31), channel_id=1, source_target_pairs={{0,24},{8,16},{16,8},{24,0},{1,25},{9,17},{17,9},{25,1},{2,26},{10... | collective-permute-start | bytes 786440 | tf_op jit(solution)/shard_map/ppermute | solution.py:31
  100.8 8.0 %collective-permute-start.19 = (bf16[256,256]{1,0:T(8,128)(2,1)S(1)}, bf16[256,256]{1,0:T(8,128)(2,1)S(1)}, u32[]{:S(2)}, u32[]{:S(2)}) collective-permute-start(bf16[256,256]{1,0:T(8,128)(2,1)S(1)} %get-tuple-element.72), channel_id=1, source_target_pairs={{0,4},{1,5},{2,6},{3,7},{4,0},{5,1},{6,2},{7,3},{8,12},{9,13},{10,... | collective-permute-start | bytes 393224 | tf_op jit(solution)/shard_map/ppermute | solution.py:31
  108.9 8.2 %collective-permute-start.21 = (bf16[256,256]{1,0:T(8,128)(2,1)S(1)}, bf16[256,256]{1,0:T(8,128)(2,1)S(1)}, u32[]{:S(2)}, u32[]{:S(2)}) collective-permute-start(bf16[256,256]{1,0:T(8,128)(2,1)S(1)} %fusion.4.refs_5_), channel_id=1, source_target_pairs={{0,1},{1,0},{2,3},{3,2},{4,5},{5,4},{6,7},{7,6},{8,9},{9,8},{10,11... | collective-permute-start | bytes 393224 | tf_op jit(solution)/shard_map/ppermute | solution.py:31
  109.0 8.2 %collective-permute-start.22 = (bf16[256,256]{1,0:T(8,128)(2,1)S(1)}, bf16[256,256]{1,0:T(8,128)(2,1)S(1)}, u32[]{:S(2)}, u32[]{:S(2)}) collective-permute-start(bf16[256,256]{1,0:T(8,128)(2,1)S(1)} %fusion.4.refs_5_), channel_id=1, source_target_pairs={{0,2},{1,3},{2,0},{3,1},{4,6},{5,7},{6,4},{7,5},{8,10},{9,11},{10,... | collective-permute-start | bytes 393224 | tf_op jit(solution)/shard_map/ppermute | solution.py:31
  112.7 13.7 %collective-permute-start.43 = (bf16[256,256]{1,0:T(8,128)(2,1)S(1)}, bf16[256,256]{1,0:T(8,128)(2,1)S(1)}, u32[]{:S(2)}, u32[]{:S(2)}) collective-permute-start(bf16[256,256]{1,0:T(8,128)(2,1)S(1)} %fusion.4.refs_5_), channel_id=1, source_target_pairs={{0,16},{8,24},{16,0},{24,8},{1,17},{9,25},{17,1},{25,9},{2,18},{10... | collective-permute-start | bytes 393224 | tf_op jit(solution)/shard_map/ppermute | solution.py:31
  117.1 9.3 %collective-permute-start.31 = (bf16[256,256]{1,0:T(8,128)(2,1)S(1)}, bf16[256,256]{1,0:T(8,128)(2,1)S(1)}, u32[]{:S(2)}, u32[]{:S(2)}) collective-permute-start(bf16[256,256]{1,0:T(8,128)(2,1)S(1)} %fusion.4.refs_5_), channel_id=1, source_target_pairs={{0,8},{8,0},{16,24},{24,16},{1,9},{9,1},{17,25},{25,17},{2,10},{10... | collective-permute-start | bytes 393224 | tf_op jit(solution)/shard_map/ppermute | solution.py:31
  117.2 10.5 %collective-permute-start.23 = (bf16[256,256]{1,0:T(8,128)(2,1)S(1)}, bf16[256,256]{1,0:T(8,128)(2,1)S(1)}, u32[]{:S(2)}, u32[]{:S(2)}) collective-permute-start(bf16[256,256]{1,0:T(8,128)(2,1)S(1)} %collective-permute-done.22.refs_7_), channel_id=1, source_target_pairs={{0,1},{1,0},{2,3},{3,2},{4,5},{5,4},{6,7},{7,6},{8,9},{9,8},{10,11... | collective-permute-start | bytes 393224 | tf_op jit(solution)/shard_map/ppermute | solution.py:31
  117.2 11.5 %collective-permute-start.25 = (bf16[256,256]{1,0:T(8,128)(2,1)S(1)}, bf16[256,256]{1,0:T(8,128)(2,1)S(1)}, u32[]{:S(2)}, u32[]{:S(2)}) collective-permute-start(bf16[256,256]{1,0:T(8,128)(2,1)S(1)} %collective-permute-done.24.refs_9_), channel_id=1, source_target_pairs={{0,1},{1,0},{2,3},{3,2},{4,5},{5,4},{6,7},{7,6},{8,9},{9,8},{10,11... | collective-permute-start | bytes 393224 | tf_op jit(solution)/shard_map/ppermute | solution.py:31
  118.0 10.7 %collective-permute-start.26 = (bf16[256,256]{1,0:T(8,128)(2,1)S(1)}, bf16[256,256]{1,0:T(8,128)(2,1)S(1)}, u32[]{:S(2)}, u32[]{:S(2)}) collective-permute-start(bf16[256,256]{1,0:T(8,128)(2,1)S(1)} %collective-permute-done.22.refs_7_), channel_id=1, source_target_pairs={{0,4},{1,5},{2,6},{3,7},{4,0},{5,1},{6,2},{7,3},{8,12},{9,13},{10,... | collective-permute-start | bytes 393224 | tf_op jit(solution)/shard_map/ppermute | solution.py:31
  128.7 8.7 %collective-permute-start.45 = (bf16[256,256]{1,0:T(8,128)(2,1)S(1)}, bf16[256,256]{1,0:T(8,128)(2,1)S(1)}, u32[]{:S(2)}, u32[]{:S(2)}) collective-permute-start(bf16[256,256]{1,0:T(8,128)(2,1)S(1)} %collective-permute-done.43.refs_5_), channel_id=1, source_target_pairs={{0,2},{1,3},{2,0},{3,1},{4,6},{5,7},{6,4},{7,5},{8,10},{9,11},{10,... | collective-permute-start | bytes 393224 | tf_op jit(solution)/shard_map/ppermute | solution.py:31
  136.6 13.5 %collective-permute-start.35 = (bf16[256,256]{1,0:T(8,128)(2,1)S(1)}, bf16[256,256]{1,0:T(8,128)(2,1)S(1)}, u32[]{:S(2)}, u32[]{:S(2)}) collective-permute-start(bf16[256,256]{1,0:T(8,128)(2,1)S(1)} %collective-permute-done.31.refs_5_), channel_id=1, source_target_pairs={{0,4},{1,5},{2,6},{3,7},{4,0},{5,1},{6,2},{7,3},{8,12},{9,13},{10,... | collective-permute-start | bytes 393224 | tf_op jit(solution)/shard_map/ppermute | solution.py:31
  137.4 14.5 %collective-permute-start.60 = (bf16[256,256]{1,0:T(8,128)(2,1)S(1)}, bf16[256,256]{1,0:T(8,128)(2,1)S(1)}, u32[]{:S(2)}, u32[]{:S(2)}) collective-permute-start(bf16[256,256]{1,0:T(8,128)(2,1)S(1)} %collective-permute-done.59.refs_9_), channel_id=1, source_target_pairs={{0,1},{1,0},{2,3},{3,2},{4,5},{5,4},{6,7},{7,6},{8,9},{9,8},{10,11... | collective-permute-start | bytes 393224 | tf_op jit(solution)/shard_map/ppermute | solution.py:31
  137.5 14.3 %collective-permute-start.58 = (bf16[256,256]{1,0:T(8,128)(2,1)S(1)}, bf16[256,256]{1,0:T(8,128)(2,1)S(1)}, u32[]{:S(2)}, u32[]{:S(2)}) collective-permute-start(bf16[256,256]{1,0:T(8,128)(2,1)S(1)} %collective-permute-done.57.refs_7_), channel_id=1, source_target_pairs={{0,1},{1,0},{2,3},{3,2},{4,5},{5,4},{6,7},{7,6},{8,9},{9,8},{10,11... | collective-permute-start | bytes 393224 | tf_op jit(solution)/shard_map/ppermute | solution.py:31
  138.0 14.3 %collective-permute-start.49 = (bf16[256,256]{1,0:T(8,128)(2,1)S(1)}, bf16[256,256]{1,0:T(8,128)(2,1)S(1)}, u32[]{:S(2)}, u32[]{:S(2)}) collective-permute-start(bf16[256,256]{1,0:T(8,128)(2,1)S(1)} %collective-permute-done.45.refs_7_), channel_id=1, source_target_pairs={{0,4},{1,5},{2,6},{3,7},{4,0},{5,1},{6,2},{7,3},{8,12},{9,13},{10,... | collective-permute-start | bytes 393224 | tf_op jit(solution)/shard_map/ppermute | solution.py:31
  139.1 13.6 %collective-permute-start.62 = (bf16[256,256]{1,0:T(8,128)(2,1)S(1)}, bf16[256,256]{1,0:T(8,128)(2,1)S(1)}, u32[]{:S(2)}, u32[]{:S(2)}) collective-permute-start(bf16[256,256]{1,0:T(8,128)(2,1)S(1)} %collective-permute-done.61.refs_11_), channel_id=1, source_target_pairs={{0,1},{1,0},{2,3},{3,2},{4,5},{5,4},{6,7},{7,6},{8,9},{9,8},{10,11... | collective-permute-start | bytes 393224 | tf_op jit(solution)/shard_map/ppermute | solution.py:31
  150.1 14.1 %collective-permute-start.33 = (bf16[256,256]{1,0:T(8,128)(2,1)S(1)}, bf16[256,256]{1,0:T(8,128)(2,1)S(1)}, u32[]{:S(2)}, u32[]{:S(2)}) collective-permute-start(bf16[256,256]{1,0:T(8,128)(2,1)S(1)} %collective-permute-done.31.refs_5_), channel_id=1, source_target_pairs={{0,2},{1,3},{2,0},{3,1},{4,6},{5,7},{6,4},{7,5},{8,10},{9,11},{10,... | collective-permute-start | bytes 393224 | tf_op jit(solution)/shard_map/ppermute | solution.py:31
  151.8 12.5 %collective-permute-start.46 = (bf16[256,256]{1,0:T(8,128)(2,1)S(1)}, bf16[256,256]{1,0:T(8,128)(2,1)S(1)}, u32[]{:S(2)}, u32[]{:S(2)}) collective-permute-start(bf16[256,256]{1,0:T(8,128)(2,1)S(1)} %collective-permute-done.45.refs_7_), channel_id=1, source_target_pairs={{0,1},{1,0},{2,3},{3,2},{4,5},{5,4},{6,7},{7,6},{8,9},{9,8},{10,11... | collective-permute-start | bytes 393224 | tf_op jit(solution)/shard_map/ppermute | solution.py:31
  152.0 12.9 %collective-permute-start.48 = (bf16[256,256]{1,0:T(8,128)(2,1)S(1)}, bf16[256,256]{1,0:T(8,128)(2,1)S(1)}, u32[]{:S(2)}, u32[]{:S(2)}) collective-permute-start(bf16[256,256]{1,0:T(8,128)(2,1)S(1)} %collective-permute-done.47.refs_9_), channel_id=1, source_target_pairs={{0,1},{1,0},{2,3},{3,2},{4,5},{5,4},{6,7},{7,6},{8,9},{9,8},{10,11... | collective-permute-start | bytes 393224 | tf_op jit(solution)/shard_map/ppermute | solution.py:31
  152.3 12.6 %collective-permute-start.37 = (bf16[256,256]{1,0:T(8,128)(2,1)S(1)}, bf16[256,256]{1,0:T(8,128)(2,1)S(1)}, u32[]{:S(2)}, u32[]{:S(2)}) collective-permute-start(bf16[256,256]{1,0:T(8,128)(2,1)S(1)} %collective-permute-done.35.refs_9_), channel_id=1, source_target_pairs={{0,2},{1,3},{2,0},{3,1},{4,6},{5,7},{6,4},{7,5},{8,10},{9,11},{10,... | collective-permute-start | bytes 393224 | tf_op jit(solution)/shard_map/ppermute | solution.py:31
  152.7 12.7 %collective-permute-start.50 = (bf16[256,256]{1,0:T(8,128)(2,1)S(1)}, bf16[256,256]{1,0:T(8,128)(2,1)S(1)}, u32[]{:S(2)}, u32[]{:S(2)}) collective-permute-start(bf16[256,256]{1,0:T(8,128)(2,1)S(1)} %collective-permute-done.49.refs_11_), channel_id=1, source_target_pairs={{0,1},{1,0},{2,3},{3,2},{4,5},{5,4},{6,7},{7,6},{8,9},{9,8},{10,11... | collective-permute-start | bytes 393224 | tf_op jit(solution)/shard_map/ppermute | solution.py:31
  164.2 12.6 %collective-permute-start.32 = (bf16[256,256]{1,0:T(8,128)(2,1)S(1)}, bf16[256,256]{1,0:T(8,128)(2,1)S(1)}, u32[]{:S(2)}, u32[]{:S(2)}) collective-permute-start(bf16[256,256]{1,0:T(8,128)(2,1)S(1)} %collective-permute-done.31.refs_5_), channel_id=1, source_target_pairs={{0,1},{1,0},{2,3},{3,2},{4,5},{5,4},{6,7},{7,6},{8,9},{9,8},{10,11... | collective-permute-start | bytes 393224 | tf_op jit(solution)/shard_map/ppermute | solution.py:31
  164.3 13.2 %collective-permute-start.36 = (bf16[256,256]{1,0:T(8,128)(2,1)S(1)}, bf16[256,256]{1,0:T(8,128)(2,1)S(1)}, u32[]{:S(2)}, u32[]{:S(2)}) collective-permute-start(bf16[256,256]{1,0:T(8,128)(2,1)S(1)} %collective-permute-done.35.refs_9_), channel_id=1, source_target_pairs={{0,1},{1,0},{2,3},{3,2},{4,5},{5,4},{6,7},{7,6},{8,9},{9,8},{10,11... | collective-permute-start | bytes 393224 | tf_op jit(solution)/shard_map/ppermute | solution.py:31
  164.8 12.2 %collective-permute-start.34 = (bf16[256,256]{1,0:T(8,128)(2,1)S(1)}, bf16[256,256]{1,0:T(8,128)(2,1)S(1)}, u32[]{:S(2)}, u32[]{:S(2)}) collective-permute-start(bf16[256,256]{1,0:T(8,128)(2,1)S(1)} %collective-permute-done.33.refs_7_), channel_id=1, source_target_pairs={{0,1},{1,0},{2,3},{3,2},{4,5},{5,4},{6,7},{7,6},{8,9},{9,8},{10,11... | collective-permute-start | bytes 393224 | tf_op jit(solution)/shard_map/ppermute | solution.py:31
  164.9 24.8 %collective-permute-start.28 = (bf16[4,256,256]{2,1,0:T(8,128)(2,1)S(1)}, bf16[4,256,256]{2,1,0:T(8,128)(2,1)S(1)}, u32[]{:S(2)}, u32[]{:S(2)}) collective-permute-start(bf16[4,256,256]{2,1,0:T(8,128)(2,1)S(1)} %copy-done.52), channel_id=1, source_target_pairs={{0,1},{1,0},{2,3},{3,2},{4,5},{5,4},{6,7},{7,6},{8,9},{9,8},{10,11... | collective-permute-start | bytes 1572872 | tf_op jit(solution)/shard_map/ppermute | solution.py:31
  165.4 12.1 %collective-permute-start.38 = (bf16[256,256]{1,0:T(8,128)(2,1)S(1)}, bf16[256,256]{1,0:T(8,128)(2,1)S(1)}, u32[]{:S(2)}, u32[]{:S(2)}) collective-permute-start(bf16[256,256]{1,0:T(8,128)(2,1)S(1)} %collective-permute-done.37.refs_11_), channel_id=1, source_target_pairs={{0,1},{1,0},{2,3},{3,2},{4,5},{5,4},{6,7},{7,6},{8,9},{9,8},{10,11... | collective-permute-start | bytes 393224 | tf_op jit(solution)/shard_map/ppermute | solution.py:31
  176.9 14.8 %collective-permute-start.63 = (bf16[4,256,256]{2,1,0:T(8,128)(2,1)S(1)}, bf16[4,256,256]{2,1,0:T(8,128)(2,1)S(1)}, u32[]{:S(2)}, u32[]{:S(2)}) collective-permute-start(bf16[4,256,256]{2,1,0:T(8,128)(2,1)S(1)} %copy-done.53), channel_id=1, source_target_pairs={{0,1},{1,0},{2,3},{3,2},{4,5},{5,4},{6,7},{7,6},{8,9},{9,8},{10,11... | collective-permute-start | bytes 1572872 | tf_op jit(solution)/shard_map/ppermute | solution.py:31
  177.0 15.9 %collective-permute-start.51 = (bf16[4,256,256]{2,1,0:T(8,128)(2,1)}, bf16[4,256,256]{2,1,0:T(8,128)(2,1)S(1)}, u32[]{:S(2)}, u32[]{:S(2)}) collective-permute-start(bf16[4,256,256]{2,1,0:T(8,128)(2,1)} %get-tuple-element.50), channel_id=1, source_target_pairs={{0,1},{1,0},{2,3},{3,2},{4,5},{5,4},{6,7},{7,6},{8,9},{9,8},{10,11... | collective-permute-start | bytes 1572872 | tf_op jit(solution)/shard_map/ppermute | solution.py:31
  190.0 9.2 %collective-permute-start.29 = (bf16[2,256,256]{2,1,0:T(8,128)(2,1)S(1)}, bf16[2,256,256]{2,1,0:T(8,128)(2,1)S(1)}, u32[]{:S(2)}, u32[]{:S(2)}) collective-permute-start(bf16[2,256,256]{2,1,0:T(8,128)(2,1)S(1)} %pad_maximum_fusion), channel_id=1, source_target_pairs={{0,2},{1,3},{2,0},{3,1},{4,6},{5,7},{6,4},{7,5},{8,10},{9,11},{10,... | collective-permute-start | bytes 786440 | tf_op jit(solution)/shard_map/ppermute | solution.py:31
  191.8 9.2 %collective-permute-start.64 = (bf16[2,256,256]{2,1,0:T(8,128)(2,1)S(1)}, bf16[2,256,256]{2,1,0:T(8,128)(2,1)S(1)}, u32[]{:S(2)}, u32[]{:S(2)}) collective-permute-start(bf16[2,256,256]{2,1,0:T(8,128)(2,1)S(1)} %stack.38), channel_id=1, source_target_pairs={{0,4},{1,5},{2,6},{3,7},{4,0},{5,1},{6,2},{7,3},{8,12},{9,13},{10,... | collective-permute-start | bytes 786440 | tf_op jit(solution)/shard_map/ppermute | solution.py:31
  193.2 11.6 %collective-permute-start.52 = (bf16[2,256,256]{2,1,0:T(8,128)(2,1)S(1)}, bf16[2,256,256]{2,1,0:T(8,128)(2,1)S(1)}, u32[]{:S(2)}, u32[]{:S(2)}) collective-permute-start(bf16[2,256,256]{2,1,0:T(8,128)(2,1)S(1)} %pad_maximum_fusion.1), channel_id=1, source_target_pairs={{0,2},{1,3},{2,0},{3,1},{4,6},{5,7},{6,4},{7,5},{8,10},{9,11},{10,... | collective-permute-start | bytes 786440 | tf_op jit(solution)/shard_map/ppermute | solution.py:31
  193.6 13.0 %collective-permute-start.40 = (bf16[2,256,256]{2,1,0:T(8,128)(2,1)S(1)}, bf16[2,256,256]{2,1,0:T(8,128)(2,1)S(1)}, u32[]{:S(2)}, u32[]{:S(2)}) collective-permute-start(bf16[2,256,256]{2,1,0:T(8,128)(2,1)S(1)} %stack.39), channel_id=1, source_target_pairs={{0,4},{1,5},{2,6},{3,7},{4,0},{5,1},{6,2},{7,3},{8,12},{9,13},{10,... | collective-permute-start | bytes 786440 | tf_op jit(solution)/shard_map/ppermute | solution.py:31
  199.2 15.5 %collective-permute-start.30 = (bf16[1,256,256]{2,1,0:T(8,128)(2,1)S(1)}, bf16[1,256,256]{2,1,0:T(8,128)(2,1)S(1)}, u32[]{:S(2)}, u32[]{:S(2)}) collective-permute-start(bf16[1,256,256]{2,1,0:T(8,128)(2,1)S(1)} %fusion.14), channel_id=1, source_target_pairs={{0,4},{1,5},{2,6},{3,7},{4,0},{5,1},{6,2},{7,3},{8,12},{9,13},{10,... | collective-permute-start | bytes 393224 | tf_op jit(solution)/shard_map/ppermute | solution.py:31
  207.8 8.0 %collective-permute-start.66 = (bf16[256,256]{1,0:T(8,128)(2,1)S(1)}, bf16[256,256]{1,0:T(8,128)(2,1)S(1)}, u32[]{:S(2)}, u32[]{:S(2)}) collective-permute-start(bf16[256,256]{1,0:T(8,128)(2,1)S(1)} %fusion.24), channel_id=1, source_target_pairs={{0,24},{8,16},{16,8},{24,0},{1,25},{9,17},{17,9},{25,1},{2,26},{10... | collective-permute-start | bytes 393224 | tf_op jit(solution)/shard_map/ppermute | solution.py:31
  211.5 8.8 %collective-permute-start.54 = (bf16[256,256]{1,0:T(8,128)(2,1)S(1)}, bf16[256,256]{1,0:T(8,128)(2,1)S(1)}, u32[]{:S(2)}, u32[]{:S(2)}) collective-permute-start(bf16[256,256]{1,0:T(8,128)(2,1)S(1)} %fusion.23), channel_id=1, source_target_pairs={{0,16},{8,24},{16,0},{24,8},{1,17},{9,25},{17,1},{25,9},{2,18},{10... | collective-permute-start | bytes 393224 | tf_op jit(solution)/shard_map/ppermute | solution.py:31
  212.0 8.5 %collective-permute-start.42 = (bf16[256,256]{1,0:T(8,128)(2,1)S(1)}, bf16[256,256]{1,0:T(8,128)(2,1)S(1)}, u32[]{:S(2)}, u32[]{:S(2)}) collective-permute-start(bf16[256,256]{1,0:T(8,128)(2,1)S(1)} %fusion.22), channel_id=1, source_target_pairs={{0,8},{8,0},{16,24},{24,16},{1,9},{9,1},{17,25},{25,17},{2,10},{10... | collective-permute-start | bytes 393224 | tf_op jit(solution)/shard_map/ppermute | solution.py:31
  (77 other events, 984.3 us)
Sparse Core Ops, SparseCore 0:
  10.6 31.2 all-gather.1

commit v3 on v2

--- a/solution.py
+++ b/solution.py
@@ -8,10 +8,11 @@
 from jax.sharding import PartitionSpec as P
 
 HD = 128
-CACHE_BLOCK = 2048
+CACHE_BLOCK = 1024
 VMEM_LIMIT = 56 * 1024 * 1024
 BF16 = jnp.bfloat16
 F32 = jnp.float32
+EXPONENT = math.log2(math.e) / math.sqrt(HD)
 
 
 def vmem():
@@ -82,11 +83,12 @@
 
 
 def cache_kernel(
-    requests, draft, heads, parts, lengths, owner, scale_of, *refs
+    requests, draft, heads, parts, lengths, first, held, place, scale_of, *refs
 ):
     terms, (cache, top, mass, mixed, query, wide) = refs[:parts], refs[parts:]
     group, block = pl.program_id(0), pl.program_id(1)
     slots = cache.shape[2]
+    size = heads * draft
 
     @pl.when((group == 0) & (block == 0))
     def _():
@@ -98,37 +100,35 @@
             total = total + term[...].astype(F32)
         query[...] = (total * scale_of[...]).astype(BF16)
         for request in range(requests):
-            wide[request] = blocked_query(query[...], request, draft, heads)
+            rows = pl.ds(pl.multiple_of(place[request] * size, size), size)
+            wide[rows, :] = blocked_query(query[...], request, draft, heads)
 
     left = lengths[group] - block * slots
-    scale = 1.0 / math.sqrt(HD)
-    for request in range(requests):
-
-        @pl.when((owner[request] == group) & (left > 0))
+    for count in range(1, requests + 1):
+
+        @pl.when((held[group] == count) & (left > 0))
         def _():
-            scores = (
-                lax.dot_general(
-                    wide[request],
-                    cache[0, 0],
-                    (((1,), (1,)), ((), ())),
-                    preferred_element_type=F32,
-                )
-                * scale
+            rows = pl.ds(pl.multiple_of(first[group] * size, size), count * size)
+            scores = lax.dot_general(
+                wide[rows, :],
+                cache[0, 0],
+                (((1,), (1,)), ((), ())),
+                preferred_element_type=F32,
             )
-            column = lax.broadcasted_iota(jnp.int32, scores.shape, 1)
-            scores = jnp.where(column < left, scores, -jnp.inf)
-            before = top[request]
+            column = lax.broadcasted_iota(jnp.int32, (1, slots), 1)
+            scores = scores + jnp.where(column < left, 0.0, -jnp.inf)
+            before = top[rows, :]
             now = jnp.maximum(before, jnp.max(scores, axis=1, keepdims=True))
-            powered = jnp.exp(scores - now[:, :1])
-            fade = jnp.exp(before - now)
-            top[request] = now
-            mass[request] = mass[request] * fade + jnp.sum(powered, axis=1, keepdims=True)
-            mixed[request] = mixed[request] * fade[:, :1] + jnp.dot(
+            powered = jnp.exp2((scores - now[:, :1]) * EXPONENT)
+            fade = jnp.exp2((before - now) * EXPONENT)
+            top[rows, :] = now
+            mass[rows, :] = mass[rows, :] * fade + jnp.sum(powered, axis=1, keepdims=True)
+            mixed[rows, :] = mixed[rows, :] * fade[:, :1] + jnp.dot(
                 powered.astype(BF16), cache[0, 1], preferred_element_type=F32
             )
 
 
-def draft_kernel(requests, draft, heads, parts, scale_of, *refs):
+def draft_kernel(requests, draft, heads, parts, place, scale_of, *refs):
     pairs = refs[:parts]
     query, reach, rows, top, mass, mixed, attended, picked, key, value = refs[parts:]
     for which, kept in ((0, key), (1, value)):
@@ -142,24 +142,22 @@
     ).astype(BF16)
     picked[0] = jnp.dot(chosen, key[...], preferred_element_type=F32).astype(BF16)
     picked[1] = jnp.dot(chosen, value[...], preferred_element_type=F32).astype(BF16)
-    scale = 1.0 / math.sqrt(HD)
+    size = heads * draft
     for request in range(requests):
         own = slice(request * draft, (request + 1) * draft)
+        kept = pl.ds(pl.multiple_of(place[request] * size, size), size)
         wide = blocked_query(query[...], request, draft, heads)
-        scores = (
-            lax.dot_general(
-                wide, key[own, :], (((1,), (1,)), ((), ())), preferred_element_type=F32
-            )
-            * scale
+        scores = lax.dot_general(
+            wide, key[own, :], (((1,), (1,)), ((), ())), preferred_element_type=F32
         )
         seen = jnp.concatenate([reach[request]] * heads, axis=0)
         scores = jnp.where(seen > 0, scores, -jnp.inf)
-        before = top[request][:, :1]
+        before = top[kept, :][:, :1]
         now = jnp.maximum(before, jnp.max(scores, axis=1, keepdims=True))
-        powered = jnp.exp(scores - now)
-        fade = jnp.exp(before - now)
-        sums = mass[request][:, :1] * fade + jnp.sum(powered, axis=1, keepdims=True)
-        total = mixed[request] * fade + jnp.dot(
+        powered = jnp.exp2((scores - now) * EXPONENT)
+        fade = jnp.exp2((before - now) * EXPONENT)
+        sums = mass[kept, :][:, :1] * fade + jnp.sum(powered, axis=1, keepdims=True)
+        total = mixed[kept, :] * fade + jnp.dot(
             powered.astype(BF16), value[own, :], preferred_element_type=F32
         )
         total = (total / sums).astype(BF16)
@@ -183,44 +181,53 @@
         outs[mask % 2][mask // 2] = value
 
 
-def expert_kernel(count, unit, ids, gain, gates, weight, down, *refs):
-    pieces, (odd, even, normed, total) = refs[:count], refs[count:]
+def expert_kernel(count, masks, ids, gain, gates, weight, down, *refs):
+    blocks = len(masks)
+    pieces, outs, (normed, total) = refs[: blocks * count], refs[blocks * count : -2], refs[-2:]
     me_x, me_y = ids[0], ids[1]
     rows, width = pieces[0].shape
     step = pl.program_id(0)
 
     @pl.when(step == 0)
     def _():
-        squares = jnp.zeros((rows, 1), F32)
-        for piece in pieces:
-            value = piece[...].astype(F32)
-            squares = squares + jnp.sum(value * value, axis=1, keepdims=True)
-        scale = lax.rsqrt(squares / (width * count) + 1e-05)
-        for mask, piece in enumerate(pieces):
-            columns = pl.ds(pl.multiple_of((me_y ^ mask) * width, width), width)
-            value = piece[...].astype(F32) * scale * gain[:, columns]
-            normed[:, columns] = value.astype(BF16)
+        for block in range(blocks):
+            own = pieces[block * count : (block + 1) * count]
+            place = slice(block * rows, (block + 1) * rows)
+            squares = jnp.zeros((rows, 1), F32)
+            for piece in own:
+                value = piece[...].astype(F32)
+                squares = squares + jnp.sum(value * value, axis=1, keepdims=True)
+            scale = lax.rsqrt(squares / (width * count) + 1e-05)
+            for mask, piece in enumerate(own):
+                columns = pl.ds(pl.multiple_of((me_y ^ mask) * width, width), width)
+                value = piece[...].astype(F32) * scale * gain[:, columns]
+                normed[place, columns] = value.astype(BF16)
 
     units = weight.shape[2] // 2
     both = jnp.dot(normed[...], weight[0], preferred_element_type=F32)
     gate, up = both[:, :units], both[:, units:]
     hidden = (gate / (1.0 + jnp.exp(-gate)) * up).astype(BF16)
-    source = pl.ds(pl.multiple_of((me_x ^ unit) * rows, rows), rows)
-    value = jnp.dot(hidden, down[0], preferred_element_type=F32) * gates[0, source, :]
-
-    @pl.when(step == 0)
-    def _():
-        total[...] = value
-
-    @pl.when(step > 0)
-    def _():
-        total[...] += value
+    value = jnp.dot(hidden, down[0], preferred_element_type=F32)
+    for block, mask in enumerate(masks):
+        place = slice(block * rows, (block + 1) * rows)
+        source = pl.ds(pl.multiple_of((me_x ^ mask) * rows, rows), rows)
+        part = value[place, :] * gates[0, source, :]
+
+        @pl.when(step == 0)
+        def _():
+            total[place, :] = part
+
+        @pl.when(step > 0)
+        def _():
+            total[place, :] += part
 
     @pl.when(step == pl.num_programs(0) - 1)
     def _():
-        for mask in range(count):
-            columns = pl.ds(pl.multiple_of((me_y ^ mask) * width, width), width)
-            (odd if mask % 2 else even)[mask // 2] = total[:, columns].astype(BF16)
+        for block in range(blocks):
+            place = slice(block * rows, (block + 1) * rows)
+            for mask in range(count):
+                columns = pl.ds(pl.multiple_of((me_y ^ mask) * width, width), width)
+                outs[2 * block + mask % 2][mask // 2] = total[place, columns].astype(BF16)
 
 
 def per_device(
@@ -261,7 +268,12 @@
         for a in range(gx_count)
         for b in range(gy_count)
     ]
-    pieces = gather_gy(lax.ppermute(tokens, ("gx", "gy"), route))
+    moved = lax.ppermute(tokens, ("gx", "gy"), route)
+    experts = gate_up_weight.shape[0]
+    units = gate_up_weight.shape[3]
+    gate_up = gate_up_weight.reshape(experts, depth, 2 * units)
+    gate_up, moved = lax.optimization_barrier((gate_up, moved))
+    pieces = gather_gy(moved)
     types = [F32] + [BF16] * (gx_count - 1)
     projected = pl.pallas_call(
         lambda *refs: project_kernel(gy_count, *refs),
@@ -283,52 +295,58 @@
         swap(pair_terms[mask], "gx", mask) for mask in range(1, gx_count)
     ]
 
-    experts = gate_up_weight.shape[0]
-    units = gate_up_weight.shape[3]
-    gate_up = gate_up_weight.reshape(experts, depth, 2 * units)
-    gate_up, query_terms[0] = lax.optimization_barrier((gate_up, query_terms[0]))
+    owner = prompt_group % groups
+    order = jnp.arange(requests, dtype=jnp.int32)
+    ahead = (owner[None, :] < owner[:, None]) | (
+        (owner[None, :] == owner[:, None]) & (order[None, :] < order[:, None])
+    )
+    place = jnp.sum(ahead.astype(jnp.int32), axis=1)
+    group_ids = jnp.arange(groups, dtype=jnp.int32)
+    held = jnp.sum((owner[None, :] == group_ids[:, None]).astype(jnp.int32), axis=1)
+    first = jnp.sum((owner[None, :] < group_ids[:, None]).astype(jnp.int32), axis=1)
 
     slots = prompt_cache.shape[2]
     step = min(CACHE_BLOCK, slots)
     wide_rows = heads * draft
-    constant = lambda *_: (0, 0, 0)
     flat = lambda *_: (0, 0)
     top, mass, mixed, query = pl.pallas_call(
         lambda *refs: cache_kernel(requests, draft, heads, gx_count, *refs),
         grid_spec=pltpu.PrefetchScalarGridSpec(
-            num_scalar_prefetch=2,
+            num_scalar_prefetch=4,
             grid=(groups, slots // step),
             in_specs=[pl.BlockSpec((rows, 1), flat)]
             + [pl.BlockSpec((rows, width), flat)] * gx_count
             + [
                 pl.BlockSpec(
                     (1, 2, step, width),
-                    lambda group, block, lengths, owner: (
+                    lambda group, block, lengths, first, held, place: (
                         group,
                         0,
-                        jnp.minimum(block, (lengths[group] - 1) // step),
+                        jnp.where(
+                            held[group] > 0, jnp.minimum(block, (lengths[group] - 1) // step), 0
+                        ),
                         0,
                     ),
                 ),
             ],
             out_specs=[
-                pl.BlockSpec((requests, wide_rows, HD), constant),
-                pl.BlockSpec((requests, wide_rows, HD), constant),
-                pl.BlockSpec((requests, wide_rows, width), constant),
+                pl.BlockSpec((requests * wide_rows, HD), flat),
+                pl.BlockSpec((requests * wide_rows, HD), flat),
+                pl.BlockSpec((requests * wide_rows, width), flat),
                 pl.BlockSpec((rows, width), flat),
             ],
-            scratch_shapes=[pltpu.VMEM((requests, wide_rows, width), BF16)],
+            scratch_shapes=[pltpu.VMEM((requests * wide_rows, width), BF16)],
         ),
         out_shape=(
-            jax.ShapeDtypeStruct((requests, wide_rows, HD), F32),
-            jax.ShapeDtypeStruct((requests, wide_rows, HD), F32),
-            jax.ShapeDtypeStruct((requests, wide_rows, width), F32),
+            jax.ShapeDtypeStruct((requests * wide_rows, HD), F32),
+            jax.ShapeDtypeStruct((requests * wide_rows, HD), F32),
+            jax.ShapeDtypeStruct((requests * wide_rows, width), F32),
             jax.ShapeDtypeStruct((rows, width), BF16),
         ),
         compiler_params=params(),
         cost_estimate=cost(20 * rows * slots * width, 4 * groups * slots * width),
         name="cache",
-    )(cache_length, prompt_group % groups, row_scale, *query_terms, prompt_cache)
+    )(cache_length, first, held, place, row_scale, *query_terms, prompt_cache)
 
     accepted = accepted_path.shape[1]
     chosen = (jnp.arange(requests, dtype=jnp.int32)[:, None] * draft + accepted_path).reshape(-1, 1)
@@ -338,7 +356,7 @@
             jax.ShapeDtypeStruct((rows, width), BF16),
             jax.ShapeDtypeStruct((2, requests * accepted, width), BF16),
         ),
-        in_specs=[vmem()] * (gx_count + 7),
+        in_specs=[smem()] + [vmem()] * (gx_count + 7),
         out_specs=(vmem(), vmem()),
         scratch_shapes=[
             pltpu.VMEM((rows, width), BF16),
@@ -346,7 +364,7 @@
         ],
         compiler_params=params(),
         name="draft",
-    )(row_scale, *pair_terms, query, ancestor_table(parents), chosen, top, mass, mixed)
+    )(place, row_scale, *pair_terms, query, ancestor_table(parents), chosen, top, mass, mixed)
     compacted = jnp.transpose(picked, (1, 0, 2))
 
     half = jax.ShapeDtypeStruct((gy_count // 2, rows, width), BF16)
@@ -368,12 +386,20 @@
     expert_ids = lax.axis_index("gy") * experts + jnp.arange(experts, dtype=jnp.int32)
     hit = route_experts[None] == expert_ids[:, None, None]
     gates = jnp.sum(jnp.where(hit, route_gates.astype(F32)[None], 0.0), axis=2)[:, :, None]
+    blocks = [stream] + [swap(stream, "gx", mask) for mask in range(1, gx_count)]
+    together = 2
+    everything = [double_gy(one, mask % 2) for mask, one in enumerate(blocks[:together])]
     result = stream.astype(F32)
-    for unit in range(gx_count):
-        one = stream if unit == 0 else swap(stream, "gx", unit)
-        everything = double_gy(one, unit % 2)
-        odd, even = pl.pallas_call(
-            lambda *refs: expert_kernel(gy_count, unit, *refs),
+    pending, waiting = [], []
+    for start in range(0, gx_count, together):
+        masks = range(start, start + together)
+        inputs = [one for pieces in everything for one in pieces]
+        after = blocks[start + together : start + 2 * together]
+        inputs, waiting, after = lax.optimization_barrier((inputs, waiting, after))
+        far = [gather_far(one) for one in after]
+        arrived = [send_far(one) for one in waiting]
+        terms = pl.pallas_call(
+            lambda *refs: expert_kernel(gy_count, masks, *refs),
             grid=(experts,),
             in_specs=[
                 smem(),
@@ -382,31 +408,54 @@
                 pl.BlockSpec((1, depth, 2 * units), lambda expert: (expert, 0, 0)),
                 pl.BlockSpec((1, units, depth), lambda expert: (expert, 0, 0)),
             ]
-            + [vmem()] * gy_count,
-            out_specs=[vmem(), vmem()],
-            out_shape=(half, half),
-            scratch_shapes=[pltpu.VMEM((rows, depth), BF16), pltpu.VMEM((rows, depth), F32)],
+            + [vmem()] * (together * gy_count),
+            out_specs=[vmem()] * (2 * together),
+            out_shape=[half] * (2 * together),
+            scratch_shapes=[
+                pltpu.VMEM((together * rows, depth), BF16),
+                pltpu.VMEM((together * rows, depth), F32),
+            ],
             compiler_params=params(),
             cost_estimate=cost(
-                6 * rows * depth * experts * units, 6 * depth * experts * units
+                6 * together * rows * depth * experts * units, 6 * depth * experts * units
             ),
             name="experts",
-        )(ids, expert_gain.reshape(1, depth), gates, gate_up, down_weight, *everything)
-        summed = even.astype(F32) + swap(odd, "gy", 1).astype(F32)
-        total = halve_gy(summed, unit % 2)
-        if unit:
-            total = swap(total.astype(BF16), "gx", unit).astype(F32)
+        )(ids, expert_gain.reshape(1, depth), gates, gate_up, down_weight, *inputs)
+        terms, far, arrived = lax.optimization_barrier((terms, far, arrived))
+        pending += [
+            (start - together + place, sum([one.astype(F32) for one in got], held[0]))
+            for place, (held, got) in enumerate(zip(waiting, arrived))
+        ]
+        near = [swap(odd, "gy", 1) for odd in terms[1::2]]
+        everything = [gather_near(one) for one in far]
+        waiting = []
+        for mask, even, odd in zip(masks, terms[0::2], near):
+            summed = even.astype(F32) + odd.astype(F32)
+            if start + together < gx_count:
+                waiting.append([summed[0]] + [one.astype(BF16) for one in summed[1:]])
+            else:
+                pending.append((mask, halve_gy(summed, mask % 2)))
+    for mask, total in pending:
+        if mask:
+            total = swap(total.astype(BF16), "gx", mask).astype(F32)
         result = result + total
     return (result.astype(BF16), compacted)
 
 
+def send_far(held):
+    return [swap(one, "gy", 2 * place) for place, one in enumerate(held) if place]
+
+
+def gather_far(value):
+    return [value] + [swap(value, "gy", mask) for mask in range(2, lax.axis_size("gy"), 2)]
+
+
+def gather_near(even):
+    return [one for held in even for one in (held, swap(held, "gy", 1))]
+
+
 def gather_gy(value):
-    count = lax.axis_size("gy")
-    even = [value] + [swap(value, "gy", mask) for mask in range(2, count, 2)]
-    pieces = []
-    for one in even:
-        pieces += [one, swap(one, "gy", 1)]
-    return pieces
+    return gather_near(gather_far(value))
 
 
 def far_bits(turn):

time: 230 us -> 226 us (0.983)
  Pallas kernels: 72.2 us -> 63.3 us
  other arithmetic: 7.51 us -> 11 us
  local copies, waits for them, and re-layouts: 23.1 us -> 20.1 us
  starting transfers between devices: 67 us -> 69.6 us
  waiting for transfers between devices: 40.9 us -> 43.3 us
    pallas_call x4 -> x2, Pallas kernels: 43.2 us -> 32 us  [per_device(): pl.pallas_call(lambda *refs: expert_kernel(gy_count, masks, *refs), grid=...]
    unnamed x115 -> x109, local copies, waits for them, and re-layouts: 6.15 us -> 3.08 us
    ppermute x66 -> x68, starting transfers between devices: 65.4 us -> 68 us  [swap(): lax.ppermute(value, axis, [(one, one ^ mask) for one in range(count)])]
    ppermute x66 -> x68, waiting for transfers between devices: 40.9 us -> 43.3 us  [swap(): lax.ppermute(value, axis, [(one, one ^ mask) for one in range(count)])]
    another operation x1 -> x3, other arithmetic: 1.17 us -> 3.49 us
  transfers between devices with their start and end apart: 68 -> 70, of which waited for: 17 -> 23; matrix products, arithmetic and copies ran while one was open for 11% -> 13% of each run, Pallas kernels for 30% -> 27%
where the time goes in v3:
time: 226 us; the launch traced here: 224 us
  starting transfers between devices  69.6 us (31%)
  Pallas kernels  63.3 us (28%)
  waiting for transfers between devices  43.3 us (19%)
  local copies, waits for them, and re-layouts  20.1 us (9%)
  between operations  14.9 us (7%)
  other arithmetic  11 us (5%)
    ppermute x68, starting transfers between devices, swap(): lax.ppermute(value, axis, [(one, one ^ mask) for one in range(count)])  68 us
    ppermute x68, waiting for transfers between devices, swap(): lax.ppermute(value, axis, [(one, one ^ mask) for one in range(count)])  43.3 us
    pallas_call x2, Pallas kernels, per_device(): pl.pallas_call(lambda *refs: expert_kernel(gy_count, masks, *refs), grid=...  32 us
    pallas_call x1, Pallas kernels, per_device(): pl.pallas_call(lambda *refs: cache_kernel(requests, draft, heads, gx_coun...  21.1 us
    reshape x1, local copies, waits for them, and re-layouts, per_device(): gate_up = gate_up_weight.reshape(experts, depth, 2 * units)  14.1 us
  transfers between devices with their start and end apart: 70, of which 23 were waited for; matrix products, arithmetic and copies ran while one was open for 13% of the time, Pallas kernels for 27%

profile of v3, /device:TPU:0, one launch (start us, length us, event | category | flops | bytes accessed | tf_op | source)
XLA Modules:
  0.0 223.9 jit_solution(9479032711646445179)
XLA Ops:
  7.2 1.6 collective-permute-start.3
  10.5 14.1 %reshape.57.refs_3_ = bf16[4,2048,512]{2,1,0:T(8,128)(2,1)} reshape(bf16[4,2048,2,256]{3,2,1,0:T(2,128)(2,1)} %param.24) | data formatting | bytes 16777216 | tf_op jit(solution)/shard_map/reshape | solution.py:274
  26.4 7.4 %collective-permute-start.9 = (bf16[256,256]{1,0:T(8,128)(2,1)S(1)}, bf16[256,256]{1,0:T(8,128)(2,1)S(1)}, u32[]{:S(2)}, u32[]{:S(2)}) collective-permute-start(bf16[256,256]{1,0:T(8,128)(2,1)S(1)} %collective-permute-done.3.refs_3_), channel_id=1, source_target_pairs={{0,6},{1,7},{2,4},{3,5},{4,2},{5,3},{6,0},{7,1},{8,14},{9,15},{10,... | collective-permute-start | bytes 393224 | tf_op jit(solution)/shard_map/ppermute | solution.py:32
  35.2 1.5 collective-permute-start.1
  36.7 1.4 collective-permute-done.9.refs_9_
  38.1 2.3 %collective-permute-done.5.refs_5_ = bf16[256,256]{1,0:T(8,128)(2,1)S(1)} collective-permute-done((bf16[256,256]{1,0:T(8,128)(2,1)S(1)}, bf16[256,256]{1,0:T(8,128)(2,1)S(1)}, u32[]{:S(2)}, u32[]{:S(2)}) %collective-permute-start.5) | collective-permute-done | bytes 131104 | tf_op jit(solution)/shard_map/ppermute | solution.py:32
  42.9 1.3 collective-permute-start.2
  46.3 3.6 %project.1 = (f32[256,256]{1,0:T(8,128)}, bf16[256,256]{1,0:T(8,128)(2,1)}, bf16[256,256]{1,0:T(8,128)(2,1)}, bf16[256,256]{1,0:T(8,128)(2,1)}, f32[2,256,256]{2...) custom-call(s32[2]{0:T(128)} %pad_add_fusion.refs_0_, ...), custom_call_target="tpu_custom_call" | custom-call | tf_op jit(solution)/shard_map/project/pallas_call | solution.py:278
  50.5 2.3 %collective-permute-start.15 = (bf16[256,256]{1,0:T(8,128)(2,1)}, bf16[256,256]{1,0:T(8,128)(2,1)S(1)}, u32[]{:S(2)}, u32[]{:S(2)}) collective-permute-start(bf16[256,256]{1,0:T(8,128)(2,1)} %get-tuple-element.99), channel_id=1, source_target_pairs={{0,16},{8,24},{16,0},{24,8},{1,17},{9,25},{17,1},{25,9},{2,18},{10... | collective-permute-start | bytes 393224 | tf_op jit(solution)/shard_map/ppermute | solution.py:32
  52.8 1.4 collective-permute-start.16
  55.0 3.0 %collective-permute-start.12 = (bf16[2,256,256]{2,1,0:T(8,128)(2,1)}, bf16[2,256,256]{2,1,0:T(8,128)(2,1)S(1)}, u32[]{:S(2)}, u32[]{:S(2)}) collective-permute-start(bf16[2,256,256]{2,1,0:T(8,128)(2,1)} %get-tuple-element.95), channel_id=1, source_target_pairs={{0,16},{8,24},{16,0},{24,8},{1,17},{9,25},{17,1},{25,9},{2,18},{10... | collective-permute-start | bytes 786440 | tf_op jit(solution)/shard_map/ppermute | solution.py:32
  57.9 1.6 collective-permute-start.13
  59.5 3.8 %collective-permute-done.15.refs_7_ = bf16[256,256]{1,0:T(8,128)(2,1)S(1)} collective-permute-done((bf16[256,256]{1,0:T(8,128)(2,1)}, bf16[256,256]{1,0:T(8,128)(2,1)S(1)}, u32[]{:S(2)}, u32[]{:S(2)}) %collective-permute-start.15) | collective-permute-done | bytes 131104 | tf_op jit(solution)/shard_map/ppermute | solution.py:32
  64.0 21.1 %cache.1 = (f32[512,128]{1,0:T(8,128)}, f32[512,128]{1,0:T(8,128)}, f32[512,256]{1,0:T(8,128)}, bf16[256,256]{1,0:T(8,128)(2,1)}) custom-call(s32[2]{0:T(128)} %refs_0_.1, s32[2]{0:T(128)} %get-tuple-element.189.refs_1_, s32[2]{0:T(128)} %get-tuple-element.188.refs_2_, s32[4]{0:T(128)} %convert_reduce_fusion.refs_3_.refs_0_, ...), custom_call_target="tpu_custom_call" | custom-call | flops 10737418240 | bytes 16777216 | tf_op jit(solution)/shard_map/cache/pallas_call | solution.py:312
  86.0 3.8 %draft.1 = (bf16[256,256]{1,0:T(8,128)(2,1)}, bf16[2,32,256]{2,1,0:T(8,128)(2,1)}) custom-call(s32[4]{0:T(128)} %convert_reduce_fusion.refs_3_.refs_0_, f32[256,1]{1,0:T(8,128)} %add_rsqrt_fusion.refs_4_.refs_1_, f32[2,256,256]{2,1,0:T(8,128)} %get-tuple-element.93.refs_2_, bf16[2,256,256]{2,1,0:T(8,128)(2,1)} %copy-done.3, bf16[2,256,256]{2,1,0:T(8,128)(2,1)} %copy-done.4, ...), custom_call_target="tpu_custom_call" | custom-call | tf_op jit(solution)/shard_map/draft/pallas_call | solution.py:353
  89.8 2.8 %output.1 = (bf16[4,256,256]{2,1,0:T(8,128)(2,1)}, bf16[4,256,256]{2,1,0:T(8,128)(2,1)}) custom-call(s32[2]{0:T(128)} %pad_add_fusion.refs_0_, bf16[256,256]{1,0:T(8,128)(2,1)} %get-tuple-element.105.refs_1_, bf16[2048,256]{1,0:T(8,128)(2,1)} %all-gather.2.cloned.1.call-done.refs_2_), custom_call_target="tpu_custom_call" | custom-call | tf_op jit(solution)/shard_map/output/pallas_call | solution.py:371
  92.6 2.1 collective-permute-done.17
  97.2 1.9 collective-permute-start.19
  99.5 2.5 %collective-permute-done.18 = bf16[256,256]{1,0:T(8,128)(2,1)S(1)} collective-permute-done((bf16[256,256]{1,0:T(8,128)(2,1)S(1)}, bf16[256,256]{1,0:T(8,128)(2,1)S(1)}, u32[]{:S(2)}, u32[]{:S(2)}) %collective-permute-start.18) | collective-permute-done | bytes 131104 | tf_op jit(solution)/shard_map/ppermute | solution.py:32
  102.0 3.4 %collective-permute-done.19 = bf16[256,256]{1,0:T(8,128)(2,1)S(1)} collective-permute-done((bf16[256,256]{1,0:T(8,128)(2,1)S(1)}, bf16[256,256]{1,0:T(8,128)(2,1)S(1)}, u32[]{:S(2)}, u32[]{:S(2)}) %collective-permute-start.19) | collective-permute-done | bytes 131104 | tf_op jit(solution)/shard_map/ppermute | solution.py:32
  105.5 2.6 %collective-permute-start.28 = (bf16[256,256]{1,0:T(8,128)(2,1)S(1)}, bf16[256,256]{1,0:T(8,128)(2,1)S(1)}, u32[]{:S(2)}, u32[]{:S(2)}) collective-permute-start(bf16[256,256]{1,0:T(8,128)(2,1)S(1)} %fusion.4.refs_5_), channel_id=1, source_target_pairs={{0,8},{8,0},{16,24},{24,16},{1,9},{9,1},{17,25},{25,17},{2,10},{10... | collective-permute-start | bytes 393224 | tf_op jit(solution)/shard_map/ppermute | solution.py:32
  108.1 1.4 collective-permute-start.22
  111.1 1.6 collective-permute-start.37
  113.1 1.7 collective-permute-start.32
  115.2 1.6 collective-permute-start.30
  116.9 5.4 %collective-permute-done.36.refs_5_ = bf16[256,256]{1,0:T(8,128)(2,1)S(1)} collective-permute-done((bf16[256,256]{1,0:T(8,128)(2,1)S(1)}, bf16[256,256]{1,0:T(8,128)(2,1)S(1)}, u32[]{:S(2)}, u32[]{:S(2)}) %collective-permute-start.36) | collective-permute-done | bytes 131104 | tf_op jit(solution)/shard_map/ppermute | solution.py:32
  122.8 1.6 collective-permute-start.34
  125.4 2.8 %collective-permute-done.34.refs_19_ = bf16[256,256]{1,0:T(8,128)(2,1)S(1)} collective-permute-done((bf16[256,256]{1,0:T(8,128)(2,1)S(1)}, bf16[256,256]{1,0:T(8,128)(2,1)S(1)}, u32[]{:S(2)}, u32[]{:S(2)}) %collective-permute-start.34) | collective-permute-done | bytes 131104 | tf_op jit(solution)/shard_map/ppermute | solution.py:32
  129.6 1.6 collective-permute-start.38
  131.4 1.9 copy.31.refs_2_
  133.6 1.6 collective-permute-start.40
  135.2 1.6 collective-permute-start.41
  137.1 1.6 collective-permute-start.43
  138.8 16.1 %experts.2 = (bf16[4,256,256]{2,1,0:T(8,128)(2,1)}, bf16[4,256,256]{2,1,0:T(8,128)(2,1)}, bf16[4,256,256]{2,1,0:T(8,128)(2,1)}, bf16[4,256,256]{2,1,0:T(8,128)(2,1)}) custom-call(s32[2]{0:T(128)} %pad_add_fusion.refs_0_, f32[1,2048]{1,0:T(1,128)} %bitcast.47, f32[4,1024,1]{2,1,0:T(8,128)} %copy.31.refs_2_, bf16[4,2048,512]{2,1,0:T(8,128)(2,1)} %reshape.57.refs_3_, ...), custom_call_target="tpu_custom_call" | custom-call | flops 6442450944 | bytes 12582912 | tf_op jit(solution)/shard_map/experts/pallas_call | solution.py:401
  162.2 1.6 collective-permute-start.54
  164.1 1.6 collective-permute-start.56
  165.7 1.6 collective-permute-start.57
  168.0 1.6 collective-permute-start.59
  169.6 15.9 %experts.3 = (bf16[4,256,256]{2,1,0:T(8,128)(2,1)}, bf16[4,256,256]{2,1,0:T(8,128)(2,1)}, bf16[4,256,256]{2,1,0:T(8,128)(2,1)}, bf16[4,256,256]{2,1,0:T(8,128)(2,1)}) custom-call(s32[2]{0:T(128)} %pad_add_fusion.refs_0_, f32[1,2048]{1,0:T(1,128)} %bitcast.48, f32[4,1024,1]{2,1,0:T(8,128)} %copy.31.refs_2_, bf16[4,2048,512]{2,1,0:T(8,128)(2,1)} %reshape.57.refs_3_, ...), custom_call_target="tpu_custom_call" | custom-call | flops 6442450944 | bytes 12582912 | tf_op jit(solution)/shard_map/experts/pallas_call | solution.py:401
  186.2 1.6 collective-permute-done.61
  189.0 1.9 collective-permute-start.62
  192.5 3.3 %collective-permute-start.60 = (bf16[256,256]{1,0:T(8,128)(2,1)S(1)}, bf16[256,256]{1,0:T(8,128)(2,1)S(1)}, u32[]{:S(2)}, u32[]{:S(2)}) collective-permute-start(bf16[256,256]{1,0:T(8,128)(2,1)S(1)} %add_convert_fusion.1), channel_id=1, source_target_pairs={{0,8},{8,0},{16,24},{24,16},{1,9},{9,1},{17,25},{25,17},{2,10},{10... | collective-permute-start | bytes 393224 | tf_op jit(solution)/shard_map/ppermute | solution.py:32
  195.8 1.7 collective-permute-done.62
  197.6 2.1 collective-permute-start.63
  200.9 2.1 collective-permute-done.63
  203.1 3.5 %collective-permute-start.64 = (bf16[256,256]{1,0:T(8,128)(2,1)S(1)}, bf16[256,256]{1,0:T(8,128)(2,1)S(1)}, u32[]{:S(2)}, u32[]{:S(2)}) collective-permute-start(bf16[256,256]{1,0:T(8,128)(2,1)S(1)} %fusion.11), channel_id=1, source_target_pairs={{0,16},{8,24},{16,0},{24,8},{1,17},{9,25},{17,1},{25,9},{2,18},{10... | collective-permute-start | bytes 393224 | tf_op jit(solution)/shard_map/ppermute | solution.py:32
  206.6 2.2 collective-permute-start.68
  209.5 6.7 %collective-permute-done.64 = bf16[256,256]{1,0:T(8,128)(2,1)S(1)} collective-permute-done((bf16[256,256]{1,0:T(8,128)(2,1)S(1)}, bf16[256,256]{1,0:T(8,128)(2,1)S(1)}, u32[]{:S(2)}, u32[]{:S(2)}) %collective-permute-start.64) | collective-permute-done | bytes 131104 | tf_op jit(solution)/shard_map/ppermute | solution.py:32
  (250 shorter events, 35.6 us)
Async XLA Ops:
  7.2 82.7 %all-gather.2.cloned.1.call-start = ((), (), s32[]{:S(2)}) async-start(), calls=%async_computation | async-start | bytes 1310720 | tf_op jit(solution)/shard_map/all_gather | solution.py:257
  7.2 19.2 %collective-permute-start.3 = (bf16[256,256]{1,0:T(8,128)(2,1)}, bf16[256,256]{1,0:T(8,128)(2,1)S(1)}, u32[]{:S(2)}, u32[]{:S(2)}) collective-permute-start(bf16[256,256]{1,0:T(8,128)(2,1)} %param.14), channel_id=1, source_target_pairs={{0,0},{1,1},{2,8},{3,9},{4,16},{5,17},{6,24},{7,25},{8,2},{9,3},{1... | collective-permute-start | bytes 393224 | tf_op jit(solution)/shard_map/ppermute | solution.py:271
  9.9 25.3 %collective-permute-start = (f32[256,1]{1,0:T(8,128)S(1)}, f32[256,1]{1,0:T(8,128)S(1)}, u32[]{:S(2)}, u32[]{:S(2)}) collective-permute-start(f32[256,1]{1,0:T(8,128)S(1)} %copy.29), channel_id=1, source_target_pairs={{0,1},{1,0},{2,3},{3,2},{4,5},{5,4},{6,7},{7,6},{8,9},{9,8},{10,11... | collective-permute-start | bytes 3080 | tf_op jit(solution)/shard_map/ppermute | solution.py:32
  26.4 11.7 %collective-permute-start.9 = (bf16[256,256]{1,0:T(8,128)(2,1)S(1)}, bf16[256,256]{1,0:T(8,128)(2,1)S(1)}, u32[]{:S(2)}, u32[]{:S(2)}) collective-permute-start(bf16[256,256]{1,0:T(8,128)(2,1)S(1)} %collective-permute-done.3.refs_3_), channel_id=1, source_target_pairs={{0,6},{1,7},{2,4},{3,5},{4,2},{5,3},{6,0},{7,1},{8,14},{9,15},{10,... | collective-permute-start | bytes 393224 | tf_op jit(solution)/shard_map/ppermute | solution.py:32
  33.8 6.7 %collective-permute-start.5 = (bf16[256,256]{1,0:T(8,128)(2,1)S(1)}, bf16[256,256]{1,0:T(8,128)(2,1)S(1)}, u32[]{:S(2)}, u32[]{:S(2)}) collective-permute-start(bf16[256,256]{1,0:T(8,128)(2,1)S(1)} %collective-permute-done.3.refs_3_), channel_id=1, source_target_pairs={{0,2},{1,3},{2,0},{3,1},{4,6},{5,7},{6,4},{7,5},{8,10},{9,11},{10,... | collective-permute-start | bytes 393224 | tf_op jit(solution)/shard_map/ppermute | solution.py:32
  33.8 7.0 %collective-permute-start.7 = (bf16[256,256]{1,0:T(8,128)(2,1)S(1)}, bf16[256,256]{1,0:T(8,128)(2,1)S(1)}, u32[]{:S(2)}, u32[]{:S(2)}) collective-permute-start(bf16[256,256]{1,0:T(8,128)(2,1)S(1)} %collective-permute-done.3.refs_3_), channel_id=1, source_target_pairs={{0,4},{1,5},{2,6},{3,7},{4,0},{5,1},{6,2},{7,3},{8,12},{9,13},{10,... | collective-permute-start | bytes 393224 | tf_op jit(solution)/shard_map/ppermute | solution.py:32
  35.2 7.6 %collective-permute-start.1 = (f32[256,1]{1,0:T(8,128)S(1)}, f32[256,1]{1,0:T(8,128)S(1)}, u32[]{:S(2)}, u32[]{:S(2)}) collective-permute-start(f32[256,1]{1,0:T(8,128)S(1)} %add.129), channel_id=1, source_target_pairs={{0,2},{1,3},{2,0},{3,1},{4,6},{5,7},{6,4},{7,5},{8,10},{9,11},{10,... | collective-permute-start | bytes 3080 | tf_op jit(solution)/shard_map/ppermute | solution.py:32
  36.7 8.8 %collective-permute-start.4 = (bf16[256,256]{1,0:T(8,128)(2,1)S(1)}, bf16[256,256]{1,0:T(8,128)(2,1)S(1)}, u32[]{:S(2)}, u32[]{:S(2)}) collective-permute-start(bf16[256,256]{1,0:T(8,128)(2,1)S(1)} %collective-permute-done.3.refs_3_), channel_id=1, source_target_pairs={{0,1},{1,0},{2,3},{3,2},{4,5},{5,4},{6,7},{7,6},{8,9},{9,8},{10,11... | collective-permute-start | bytes 393224 | tf_op jit(solution)/shard_map/ppermute | solution.py:32
  38.1 7.4 %collective-permute-start.10 = (bf16[256,256]{1,0:T(8,128)(2,1)S(1)}, bf16[256,256]{1,0:T(8,128)(2,1)S(1)}, u32[]{:S(2)}, u32[]{:S(2)}) collective-permute-start(bf16[256,256]{1,0:T(8,128)(2,1)S(1)} %collective-permute-done.9.refs_9_), channel_id=1, source_target_pairs={{0,1},{1,0},{2,3},{3,2},{4,5},{5,4},{6,7},{7,6},{8,9},{9,8},{10,11... | collective-permute-start | bytes 393224 | tf_op jit(solution)/shard_map/ppermute | solution.py:32
  40.4 5.1 %collective-permute-start.6 = (bf16[256,256]{1,0:T(8,128)(2,1)S(1)}, bf16[256,256]{1,0:T(8,128)(2,1)S(1)}, u32[]{:S(2)}, u32[]{:S(2)}) collective-permute-start(bf16[256,256]{1,0:T(8,128)(2,1)S(1)} %collective-permute-done.5.refs_5_), channel_id=1, source_target_pairs={{0,1},{1,0},{2,3},{3,2},{4,5},{5,4},{6,7},{7,6},{8,9},{9,8},{10,11... | collective-permute-start | bytes 393224 | tf_op jit(solution)/shard_map/ppermute | solution.py:32
  42.9 11.4 %collective-permute-start.2 = (f32[256,1]{1,0:T(8,128)S(1)}, f32[256,1]{1,0:T(8,128)S(1)}, u32[]{:S(2)}, u32[]{:S(2)}) collective-permute-start(f32[256,1]{1,0:T(8,128)S(1)} %add.130), channel_id=1, source_target_pairs={{0,4},{1,5},{2,6},{3,7},{4,0},{5,1},{6,2},{7,3},{8,12},{9,13},{10,... | collective-permute-start | bytes 3080 | tf_op jit(solution)/shard_map/ppermute | solution.py:32
  49.9 8.0 %collective-permute-start.14 = (bf16[256,256]{1,0:T(8,128)(2,1)}, bf16[256,256]{1,0:T(8,128)(2,1)S(1)}, u32[]{:S(2)}, u32[]{:S(2)}) collective-permute-start(bf16[256,256]{1,0:T(8,128)(2,1)} %get-tuple-element.98), channel_id=1, source_target_pairs={{0,8},{8,0},{16,24},{24,16},{1,9},{9,1},{17,25},{25,17},{2,10},{10... | collective-permute-start | bytes 393224 | tf_op jit(solution)/shard_map/ppermute | solution.py:32
  50.5 12.8 %collective-permute-start.15 = (bf16[256,256]{1,0:T(8,128)(2,1)}, bf16[256,256]{1,0:T(8,128)(2,1)S(1)}, u32[]{:S(2)}, u32[]{:S(2)}) collective-permute-start(bf16[256,256]{1,0:T(8,128)(2,1)} %get-tuple-element.99), channel_id=1, source_target_pairs={{0,16},{8,24},{16,0},{24,8},{1,17},{9,25},{17,1},{25,9},{2,18},{10... | collective-permute-start | bytes 393224 | tf_op jit(solution)/shard_map/ppermute | solution.py:32
  52.8 10.5 %collective-permute-start.16 = (bf16[256,256]{1,0:T(8,128)(2,1)}, bf16[256,256]{1,0:T(8,128)(2,1)S(1)}, u32[]{:S(2)}, u32[]{:S(2)}) collective-permute-start(bf16[256,256]{1,0:T(8,128)(2,1)} %get-tuple-element.100), channel_id=1, source_target_pairs={{0,24},{8,16},{16,8},{24,0},{1,25},{9,17},{17,9},{25,1},{2,26},{10... | collective-permute-start | bytes 393224 | tf_op jit(solution)/shard_map/ppermute | solution.py:32
  55.0 30.1 %collective-permute-start.11 = (bf16[2,256,256]{2,1,0:T(8,128)(2,1)}, bf16[2,256,256]{2,1,0:T(8,128)(2,1)S(1)}, u32[]{:S(2)}, u32[]{:S(2)}) collective-permute-start(bf16[2,256,256]{2,1,0:T(8,128)(2,1)} %get-tuple-element.94), channel_id=1, source_target_pairs={{0,8},{8,0},{16,24},{24,16},{1,9},{9,1},{17,25},{25,17},{2,10},{10... | collective-permute-start | bytes 786440 | tf_op jit(solution)/shard_map/ppermute | solution.py:32
  55.0 30.1 %collective-permute-start.12 = (bf16[2,256,256]{2,1,0:T(8,128)(2,1)}, bf16[2,256,256]{2,1,0:T(8,128)(2,1)S(1)}, u32[]{:S(2)}, u32[]{:S(2)}) collective-permute-start(bf16[2,256,256]{2,1,0:T(8,128)(2,1)} %get-tuple-element.95), channel_id=1, source_target_pairs={{0,16},{8,24},{16,0},{24,8},{1,17},{9,25},{17,1},{25,9},{2,18},{10... | collective-permute-start | bytes 786440 | tf_op jit(solution)/shard_map/ppermute | solution.py:32
  57.9 27.2 %collective-permute-start.13 = (bf16[2,256,256]{2,1,0:T(8,128)(2,1)}, bf16[2,256,256]{2,1,0:T(8,128)(2,1)S(1)}, u32[]{:S(2)}, u32[]{:S(2)}) collective-permute-start(bf16[2,256,256]{2,1,0:T(8,128)(2,1)} %get-tuple-element.96), channel_id=1, source_target_pairs={{0,24},{8,16},{16,8},{24,0},{1,25},{9,17},{17,9},{25,1},{2,26},{10... | collective-permute-start | bytes 786440 | tf_op jit(solution)/shard_map/ppermute | solution.py:32
  95.9 6.1 %collective-permute-start.18 = (bf16[256,256]{1,0:T(8,128)(2,1)S(1)}, bf16[256,256]{1,0:T(8,128)(2,1)S(1)}, u32[]{:S(2)}, u32[]{:S(2)}) collective-permute-start(bf16[256,256]{1,0:T(8,128)(2,1)S(1)} %get-tuple-element.206), channel_id=1, source_target_pairs={{0,2},{1,3},{2,0},{3,1},{4,6},{5,7},{6,4},{7,5},{8,10},{9,11},{10,... | collective-permute-start | bytes 393224 | tf_op jit(solution)/shard_map/ppermute | solution.py:32
  97.2 8.2 %collective-permute-start.19 = (bf16[256,256]{1,0:T(8,128)(2,1)S(1)}, bf16[256,256]{1,0:T(8,128)(2,1)S(1)}, u32[]{:S(2)}, u32[]{:S(2)}) collective-permute-start(bf16[256,256]{1,0:T(8,128)(2,1)S(1)} %get-tuple-element.208), channel_id=1, source_target_pairs={{0,4},{1,5},{2,6},{3,7},{4,0},{5,1},{6,2},{7,3},{8,12},{9,13},{10,... | collective-permute-start | bytes 393224 | tf_op jit(solution)/shard_map/ppermute | solution.py:32
  99.1 6.3 %collective-permute-start.20 = (bf16[256,256]{1,0:T(8,128)(2,1)S(1)}, bf16[256,256]{1,0:T(8,128)(2,1)S(1)}, u32[]{:S(2)}, u32[]{:S(2)}) collective-permute-start(bf16[256,256]{1,0:T(8,128)(2,1)S(1)} %get-tuple-element.207), channel_id=1, source_target_pairs={{0,6},{1,7},{2,4},{3,5},{4,2},{5,3},{6,0},{7,1},{8,14},{9,15},{10,... | collective-permute-start | bytes 393224 | tf_op jit(solution)/shard_map/ppermute | solution.py:32
  105.5 5.6 %collective-permute-start.28 = (bf16[256,256]{1,0:T(8,128)(2,1)S(1)}, bf16[256,256]{1,0:T(8,128)(2,1)S(1)}, u32[]{:S(2)}, u32[]{:S(2)}) collective-permute-start(bf16[256,256]{1,0:T(8,128)(2,1)S(1)} %fusion.4.refs_5_), channel_id=1, source_target_pairs={{0,8},{8,0},{16,24},{24,16},{1,9},{9,1},{17,25},{25,17},{2,10},{10... | collective-permute-start | bytes 393224 | tf_op jit(solution)/shard_map/ppermute | solution.py:32
  109.6 5.3 %collective-permute-start.24 = (bf16[256,256]{1,0:T(8,128)(2,1)S(1)}, bf16[256,256]{1,0:T(8,128)(2,1)S(1)}, u32[]{:S(2)}, u32[]{:S(2)}) collective-permute-start(bf16[256,256]{1,0:T(8,128)(2,1)S(1)} %fusion.4.refs_5_), channel_id=1, source_target_pairs={{0,4},{1,5},{2,6},{3,7},{4,0},{5,1},{6,2},{7,3},{8,12},{9,13},{10,... | collective-permute-start | bytes 393224 | tf_op jit(solution)/shard_map/ppermute | solution.py:32
  110.3 12.0 %collective-permute-start.36 = (bf16[256,256]{1,0:T(8,128)(2,1)S(1)}, bf16[256,256]{1,0:T(8,128)(2,1)S(1)}, u32[]{:S(2)}, u32[]{:S(2)}) collective-permute-start(bf16[256,256]{1,0:T(8,128)(2,1)S(1)} %fusion.4.refs_5_), channel_id=1, source_target_pairs={{0,16},{8,24},{16,0},{24,8},{1,17},{9,25},{17,1},{25,9},{2,18},{10... | collective-permute-start | bytes 393224 | tf_op jit(solution)/shard_map/ppermute | solution.py:32
  111.1 11.2 %collective-permute-start.37 = (bf16[256,256]{1,0:T(8,128)(2,1)S(1)}, bf16[256,256]{1,0:T(8,128)(2,1)S(1)}, u32[]{:S(2)}, u32[]{:S(2)}) collective-permute-start(bf16[256,256]{1,0:T(8,128)(2,1)S(1)} %fusion.4.refs_5_), channel_id=1, source_target_pairs={{0,24},{8,16},{16,8},{24,0},{1,25},{9,17},{17,9},{25,1},{2,26},{10... | collective-permute-start | bytes 393224 | tf_op jit(solution)/shard_map/ppermute | solution.py:32
  113.1 9.7 %collective-permute-start.32 = (bf16[256,256]{1,0:T(8,128)(2,1)S(1)}, bf16[256,256]{1,0:T(8,128)(2,1)S(1)}, u32[]{:S(2)}, u32[]{:S(2)}) collective-permute-start(bf16[256,256]{1,0:T(8,128)(2,1)S(1)} %collective-permute-done.28.refs_13_), channel_id=1, source_target_pairs={{0,4},{1,5},{2,6},{3,7},{4,0},{5,1},{6,2},{7,3},{8,12},{9,13},{10,... | collective-permute-start | bytes 393224 | tf_op jit(solution)/shard_map/ppermute | solution.py:32
  114.8 9.6 %collective-permute-start.26 = (bf16[256,256]{1,0:T(8,128)(2,1)S(1)}, bf16[256,256]{1,0:T(8,128)(2,1)S(1)}, u32[]{:S(2)}, u32[]{:S(2)}) collective-permute-start(bf16[256,256]{1,0:T(8,128)(2,1)S(1)} %collective-permute-done.22.refs_7_), channel_id=1, source_target_pairs={{0,4},{1,5},{2,6},{3,7},{4,0},{5,1},{6,2},{7,3},{8,12},{9,13},{10,... | collective-permute-start | bytes 393224 | tf_op jit(solution)/shard_map/ppermute | solution.py:32
  115.2 9.2 %collective-permute-start.30 = (bf16[256,256]{1,0:T(8,128)(2,1)S(1)}, bf16[256,256]{1,0:T(8,128)(2,1)S(1)}, u32[]{:S(2)}, u32[]{:S(2)}) collective-permute-start(bf16[256,256]{1,0:T(8,128)(2,1)S(1)} %collective-permute-done.28.refs_13_), channel_id=1, source_target_pairs={{0,2},{1,3},{2,0},{3,1},{4,6},{5,7},{6,4},{7,5},{8,10},{9,11},{10,... | collective-permute-start | bytes 393224 | tf_op jit(solution)/shard_map/ppermute | solution.py:32
  122.8 5.5 %collective-permute-start.34 = (bf16[256,256]{1,0:T(8,128)(2,1)S(1)}, bf16[256,256]{1,0:T(8,128)(2,1)S(1)}, u32[]{:S(2)}, u32[]{:S(2)}) collective-permute-start(bf16[256,256]{1,0:T(8,128)(2,1)S(1)} %collective-permute-done.32.refs_17_), channel_id=1, source_target_pairs={{0,2},{1,3},{2,0},{3,1},{4,6},{5,7},{6,4},{7,5},{8,10},{9,11},{10,... | collective-permute-start | bytes 393224 | tf_op jit(solution)/shard_map/ppermute | solution.py:32
  129.6 7.5 %collective-permute-start.38 = (bf16[256,256]{1,0:T(8,128)(2,1)S(1)}, bf16[256,256]{1,0:T(8,128)(2,1)S(1)}, u32[]{:S(2)}, u32[]{:S(2)}) collective-permute-start(bf16[256,256]{1,0:T(8,128)(2,1)S(1)} %collective-permute-done.36.refs_5_), channel_id=1, source_target_pairs={{0,2},{1,3},{2,0},{3,1},{4,6},{5,7},{6,4},{7,5},{8,10},{9,11},{10,... | collective-permute-start | bytes 393224 | tf_op jit(solution)/shard_map/ppermute | solution.py:32
  133.3 21.6 %collective-permute-start.39 = (bf16[256,256]{1,0:T(8,128)(2,1)S(1)}, bf16[256,256]{1,0:T(8,128)(2,1)S(1)}, u32[]{:S(2)}, u32[]{:S(2)}) collective-permute-start(bf16[256,256]{1,0:T(8,128)(2,1)S(1)} %collective-permute-done.36.refs_5_), channel_id=1, source_target_pairs={{0,4},{1,5},{2,6},{3,7},{4,0},{5,1},{6,2},{7,3},{8,12},{9,13},{10,... | collective-permute-start | bytes 393224 | tf_op jit(solution)/shard_map/ppermute | solution.py:32
  133.6 21.3 %collective-permute-start.40 = (bf16[256,256]{1,0:T(8,128)(2,1)S(1)}, bf16[256,256]{1,0:T(8,128)(2,1)S(1)}, u32[]{:S(2)}, u32[]{:S(2)}) collective-permute-start(bf16[256,256]{1,0:T(8,128)(2,1)S(1)} %collective-permute-done.36.refs_5_), channel_id=1, source_target_pairs={{0,6},{1,7},{2,4},{3,5},{4,2},{5,3},{6,0},{7,1},{8,14},{9,15},{10,... | collective-permute-start | bytes 393224 | tf_op jit(solution)/shard_map/ppermute | solution.py:32
  135.2 19.8 %collective-permute-start.41 = (bf16[256,256]{1,0:T(8,128)(2,1)S(1)}, bf16[256,256]{1,0:T(8,128)(2,1)S(1)}, u32[]{:S(2)}, u32[]{:S(2)}) collective-permute-start(bf16[256,256]{1,0:T(8,128)(2,1)S(1)} %collective-permute-done.37.refs_13_), channel_id=1, source_target_pairs={{0,2},{1,3},{2,0},{3,1},{4,6},{5,7},{6,4},{7,5},{8,10},{9,11},{10,... | collective-permute-start | bytes 393224 | tf_op jit(solution)/shard_map/ppermute | solution.py:32
  136.8 18.1 %collective-permute-start.42 = (bf16[256,256]{1,0:T(8,128)(2,1)S(1)}, bf16[256,256]{1,0:T(8,128)(2,1)S(1)}, u32[]{:S(2)}, u32[]{:S(2)}) collective-permute-start(bf16[256,256]{1,0:T(8,128)(2,1)S(1)} %collective-permute-done.37.refs_13_), channel_id=1, source_target_pairs={{0,4},{1,5},{2,6},{3,7},{4,0},{5,1},{6,2},{7,3},{8,12},{9,13},{10,... | collective-permute-start | bytes 393224 | tf_op jit(solution)/shard_map/ppermute | solution.py:32
  137.1 17.9 %collective-permute-start.43 = (bf16[256,256]{1,0:T(8,128)(2,1)S(1)}, bf16[256,256]{1,0:T(8,128)(2,1)S(1)}, u32[]{:S(2)}, u32[]{:S(2)}) collective-permute-start(bf16[256,256]{1,0:T(8,128)(2,1)S(1)} %collective-permute-done.37.refs_13_), channel_id=1, source_target_pairs={{0,6},{1,7},{2,4},{3,5},{4,2},{5,3},{6,0},{7,1},{8,14},{9,15},{10,... | collective-permute-start | bytes 393224 | tf_op jit(solution)/shard_map/ppermute | solution.py:32
  162.2 5.8 %collective-permute-start.54 = (bf16[256,256]{1,0:T(8,128)(2,1)S(1)}, bf16[256,256]{1,0:T(8,128)(2,1)S(1)}, u32[]{:S(2)}, u32[]{:S(2)}) collective-permute-start(bf16[256,256]{1,0:T(8,128)(2,1)S(1)} %get-tuple-element.164), channel_id=1, source_target_pairs={{0,2},{1,3},{2,0},{3,1},{4,6},{5,7},{6,4},{7,5},{8,10},{9,11},{10,... | collective-permute-start | bytes 393224 | tf_op jit(solution)/shard_map/ppermute | solution.py:32
  163.8 21.8 %collective-permute-start.55 = (bf16[256,256]{1,0:T(8,128)(2,1)S(1)}, bf16[256,256]{1,0:T(8,128)(2,1)S(1)}, u32[]{:S(2)}, u32[]{:S(2)}) collective-permute-start(bf16[256,256]{1,0:T(8,128)(2,1)S(1)} %get-tuple-element.165), channel_id=1, source_target_pairs={{0,4},{1,5},{2,6},{3,7},{4,0},{5,1},{6,2},{7,3},{8,12},{9,13},{10,... | collective-permute-start | bytes 393224 | tf_op jit(solution)/shard_map/ppermute | solution.py:32
  164.1 21.5 %collective-permute-start.56 = (bf16[256,256]{1,0:T(8,128)(2,1)S(1)}, bf16[256,256]{1,0:T(8,128)(2,1)S(1)}, u32[]{:S(2)}, u32[]{:S(2)}) collective-permute-start(bf16[256,256]{1,0:T(8,128)(2,1)S(1)} %get-tuple-element.166), channel_id=1, source_target_pairs={{0,6},{1,7},{2,4},{3,5},{4,2},{5,3},{6,0},{7,1},{8,14},{9,15},{10,... | collective-permute-start | bytes 393224 | tf_op jit(solution)/shard_map/ppermute | solution.py:32
  165.7 19.9 %collective-permute-start.57 = (bf16[256,256]{1,0:T(8,128)(2,1)S(1)}, bf16[256,256]{1,0:T(8,128)(2,1)S(1)}, u32[]{:S(2)}, u32[]{:S(2)}) collective-permute-start(bf16[256,256]{1,0:T(8,128)(2,1)S(1)} %get-tuple-element.167), channel_id=1, source_target_pairs={{0,2},{1,3},{2,0},{3,1},{4,6},{5,7},{6,4},{7,5},{8,10},{9,11},{10,... | collective-permute-start | bytes 393224 | tf_op jit(solution)/shard_map/ppermute | solution.py:32
  167.3 18.3 %collective-permute-start.58 = (bf16[256,256]{1,0:T(8,128)(2,1)S(1)}, bf16[256,256]{1,0:T(8,128)(2,1)S(1)}, u32[]{:S(2)}, u32[]{:S(2)}) collective-permute-start(bf16[256,256]{1,0:T(8,128)(2,1)S(1)} %get-tuple-element.168), channel_id=1, source_target_pairs={{0,4},{1,5},{2,6},{3,7},{4,0},{5,1},{6,2},{7,3},{8,12},{9,13},{10,... | collective-permute-start | bytes 393224 | tf_op jit(solution)/shard_map/ppermute | solution.py:32
  168.0 17.6 %collective-permute-start.59 = (bf16[256,256]{1,0:T(8,128)(2,1)S(1)}, bf16[256,256]{1,0:T(8,128)(2,1)S(1)}, u32[]{:S(2)}, u32[]{:S(2)}) collective-permute-start(bf16[256,256]{1,0:T(8,128)(2,1)S(1)} %get-tuple-element.169), channel_id=1, source_target_pairs={{0,6},{1,7},{2,4},{3,5},{4,2},{5,3},{6,0},{7,1},{8,14},{9,15},{10,... | collective-permute-start | bytes 393224 | tf_op jit(solution)/shard_map/ppermute | solution.py:32
  185.7 5.2 %collective-permute-start.65 = (bf16[4,256,256]{2,1,0:T(8,128)(2,1)}, bf16[4,256,256]{2,1,0:T(8,128)(2,1)S(1)}, u32[]{:S(2)}, u32[]{:S(2)}) collective-permute-start(bf16[4,256,256]{2,1,0:T(8,128)(2,1)} %get-tuple-element.180), channel_id=1, source_target_pairs={{0,1},{1,0},{2,3},{3,2},{4,5},{5,4},{6,7},{7,6},{8,9},{9,8},{10,11... | collective-permute-start | bytes 1572872 | tf_op jit(solution)/shard_map/ppermute | solution.py:32
  189.0 8.5 %collective-permute-start.62 = (bf16[2,256,256]{2,1,0:T(8,128)(2,1)S(1)}, bf16[2,256,256]{2,1,0:T(8,128)(2,1)S(1)}, u32[]{:S(2)}, u32[]{:S(2)}) collective-permute-start(bf16[2,256,256]{2,1,0:T(8,128)(2,1)S(1)} %pad_maximum_fusion), channel_id=1, source_target_pairs={{0,2},{1,3},{2,0},{3,1},{4,6},{5,7},{6,4},{7,5},{8,10},{9,11},{10,... | collective-permute-start | bytes 786440 | tf_op jit(solution)/shard_map/ppermute | solution.py:32
  192.1 8.4 %collective-permute-start.66 = (bf16[2,256,256]{2,1,0:T(8,128)(2,1)S(1)}, bf16[2,256,256]{2,1,0:T(8,128)(2,1)S(1)}, u32[]{:S(2)}, u32[]{:S(2)}) collective-permute-start(bf16[2,256,256]{2,1,0:T(8,128)(2,1)S(1)} %stack.25), channel_id=1, source_target_pairs={{0,4},{1,5},{2,6},{3,7},{4,0},{5,1},{6,2},{7,3},{8,12},{9,13},{10,... | collective-permute-start | bytes 786440 | tf_op jit(solution)/shard_map/ppermute | solution.py:32
  192.5 17.0 %collective-permute-start.60 = (bf16[256,256]{1,0:T(8,128)(2,1)S(1)}, bf16[256,256]{1,0:T(8,128)(2,1)S(1)}, u32[]{:S(2)}, u32[]{:S(2)}) collective-permute-start(bf16[256,256]{1,0:T(8,128)(2,1)S(1)} %add_convert_fusion.1), channel_id=1, source_target_pairs={{0,8},{8,0},{16,24},{24,16},{1,9},{9,1},{17,25},{25,17},{2,10},{10... | collective-permute-start | bytes 393224 | tf_op jit(solution)/shard_map/ppermute | solution.py:32
  197.6 5.4 %collective-permute-start.63 = (bf16[1,256,256]{2,1,0:T(8,128)(2,1)S(1)}, bf16[1,256,256]{2,1,0:T(8,128)(2,1)S(1)}, u32[]{:S(2)}, u32[]{:S(2)}) collective-permute-start(bf16[1,256,256]{2,1,0:T(8,128)(2,1)S(1)} %fusion.8), channel_id=1, source_target_pairs={{0,4},{1,5},{2,6},{3,7},{4,0},{5,1},{6,2},{7,3},{8,12},{9,13},{10,... | collective-permute-start | bytes 393224 | tf_op jit(solution)/shard_map/ppermute | solution.py:32
  200.6 6.0 %collective-permute-start.67 = (bf16[1,256,256]{2,1,0:T(8,128)(2,1)S(1)}, bf16[1,256,256]{2,1,0:T(8,128)(2,1)S(1)}, u32[]{:S(2)}, u32[]{:S(2)}) collective-permute-start(bf16[1,256,256]{2,1,0:T(8,128)(2,1)S(1)} %fusion.5), channel_id=1, source_target_pairs={{0,2},{1,3},{2,0},{3,1},{4,6},{5,7},{6,4},{7,5},{8,10},{9,11},{10,... | collective-permute-start | bytes 393224 | tf_op jit(solution)/shard_map/ppermute | solution.py:32
  203.1 13.2 %collective-permute-start.64 = (bf16[256,256]{1,0:T(8,128)(2,1)S(1)}, bf16[256,256]{1,0:T(8,128)(2,1)S(1)}, u32[]{:S(2)}, u32[]{:S(2)}) collective-permute-start(bf16[256,256]{1,0:T(8,128)(2,1)S(1)} %fusion.11), channel_id=1, source_target_pairs={{0,16},{8,24},{16,0},{24,8},{1,17},{9,25},{17,1},{25,9},{2,18},{10... | collective-permute-start | bytes 393224 | tf_op jit(solution)/shard_map/ppermute | solution.py:32
  206.6 9.6 %collective-permute-start.68 = (bf16[256,256]{1,0:T(8,128)(2,1)S(1)}, bf16[256,256]{1,0:T(8,128)(2,1)S(1)}, u32[]{:S(2)}, u32[]{:S(2)}) collective-permute-start(bf16[256,256]{1,0:T(8,128)(2,1)S(1)} %fusion.12), channel_id=1, source_target_pairs={{0,24},{8,16},{16,8},{24,0},{1,25},{9,17},{17,9},{25,1},{2,26},{10... | collective-permute-start | bytes 393224 | tf_op jit(solution)/shard_map/ppermute | solution.py:32
  (76 other events, 898.6 us)
Sparse Core Ops, SparseCore 0:
  10.6 31.2 all-gather.1

commit v4 on v3

--- a/solution.py
+++ b/solution.py
@@ -181,17 +181,22 @@
         outs[mask % 2][mask // 2] = value
 
 
-def expert_kernel(count, masks, ids, gain, gates, weight, down, *refs):
+def expert_kernel(count, masks, stacked, ids, gain, gates, gate_weight, up_weight, down, *refs):
     blocks = len(masks)
-    pieces, outs, (normed, total) = refs[: blocks * count], refs[blocks * count : -2], refs[-2:]
+    pieces, (odd, even, normed, hidden, held, arrival) = refs[:-6], refs[-6:]
     me_x, me_y = ids[0], ids[1]
-    rows, width = pieces[0].shape
+    rows, width = pieces[0].shape[-2:]
     step = pl.program_id(0)
+    fetch = pltpu.make_async_copy(down, held, arrival)
 
     @pl.when(step == 0)
     def _():
+        fetch.start()
         for block in range(blocks):
-            own = pieces[block * count : (block + 1) * count]
+            if stacked:
+                own = [piece.at[block] for piece in pieces]
+            else:
+                own = pieces[block * count : (block + 1) * count]
             place = slice(block * rows, (block + 1) * rows)
             squares = jnp.zeros((rows, 1), F32)
             for piece in own:
@@ -203,31 +208,25 @@
                 value = piece[...].astype(F32) * scale * gain[:, columns]
                 normed[place, columns] = value.astype(BF16)
 
-    units = weight.shape[2] // 2
-    both = jnp.dot(normed[...], weight[0], preferred_element_type=F32)
-    gate, up = both[:, :units], both[:, units:]
-    hidden = (gate / (1.0 + jnp.exp(-gate)) * up).astype(BF16)
-    value = jnp.dot(hidden, down[0], preferred_element_type=F32)
+    gate = jnp.dot(normed[...], gate_weight[0], preferred_element_type=F32)
+    up = jnp.dot(normed[...], up_weight[0], preferred_element_type=F32)
+    value = gate / (1.0 + jnp.exp(-gate)) * up
     for block, mask in enumerate(masks):
         place = slice(block * rows, (block + 1) * rows)
         source = pl.ds(pl.multiple_of((me_x ^ mask) * rows, rows), rows)
-        part = value[place, :] * gates[0, source, :]
-
-        @pl.when(step == 0)
-        def _():
-            total[place, :] = part
-
-        @pl.when(step > 0)
-        def _():
-            total[place, :] += part
+        hidden[step, place, :] = (value[place, :] * gates[0, source, :]).astype(BF16)
 
     @pl.when(step == pl.num_programs(0) - 1)
     def _():
-        for block in range(blocks):
-            place = slice(block * rows, (block + 1) * rows)
-            for mask in range(count):
-                columns = pl.ds(pl.multiple_of((me_y ^ mask) * width, width), width)
-                outs[2 * block + mask % 2][mask // 2] = total[place, columns].astype(BF16)
+        fetch.wait()
+        every = jnp.concatenate([hidden[one] for one in range(hidden.shape[0])], axis=1)
+        for mask in range(count):
+            columns = pl.ds(pl.multiple_of((me_y ^ mask) * width, width), width)
+            terms = jnp.dot(every, held[:, columns], preferred_element_type=F32).astype(BF16)
+            for block in range(blocks):
+                (odd if mask % 2 else even)[mask // 2, block] = terms[
+                    block * rows : (block + 1) * rows, :
+                ]
 
 
 def per_device(
@@ -271,9 +270,14 @@
     moved = lax.ppermute(tokens, ("gx", "gy"), route)
     experts = gate_up_weight.shape[0]
     units = gate_up_weight.shape[3]
-    gate_up = gate_up_weight.reshape(experts, depth, 2 * units)
-    gate_up, moved = lax.optimization_barrier((gate_up, moved))
-    pieces = gather_gy(moved)
+    expert_ids = lax.axis_index("gy") * experts + jnp.arange(experts, dtype=jnp.int32)
+    hit = route_experts[None] == expert_ids[:, None, None]
+    gates = jnp.sum(jnp.where(hit, route_gates.astype(F32)[None], 0.0), axis=2)[:, :, None]
+    gate_weight, moved = lax.optimization_barrier((gate_up_weight[:, :, 0], moved))
+    far = gather_far(moved)
+    source, moved = lax.optimization_barrier((gate_up_weight, moved))
+    up_weight, gates, far = lax.optimization_barrier((source[:, :, 1], gates, far))
+    pieces = gather_near(far)
     types = [F32] + [BF16] * (gx_count - 1)
     projected = pl.pallas_call(
         lambda *refs: project_kernel(gy_count, *refs),
@@ -383,67 +387,68 @@
         stream = stream + swap(summed[place].astype(BF16), "gy", 2 * place).astype(F32)
     stream = stream.astype(BF16)
 
-    expert_ids = lax.axis_index("gy") * experts + jnp.arange(experts, dtype=jnp.int32)
-    hit = route_experts[None] == expert_ids[:, None, None]
-    gates = jnp.sum(jnp.where(hit, route_gates.astype(F32)[None], 0.0), axis=2)[:, :, None]
+    units_of = [(one, one + 2) for one in range(gx_count) if not one & 2]
     blocks = [stream] + [swap(stream, "gx", mask) for mask in range(1, gx_count)]
-    together = 2
-    everything = [double_gy(one, mask % 2) for mask, one in enumerate(blocks[:together])]
+    inputs = [one for turn, mask in enumerate(units_of[0]) for one in double_gy(blocks[mask], turn)]
     result = stream.astype(F32)
-    pending, waiting = [], []
-    for start in range(0, gx_count, together):
-        masks = range(start, start + together)
-        inputs = [one for pieces in everything for one in pieces]
-        after = blocks[start + together : start + 2 * together]
+    pending, waiting, last = [], [], None
+    half = jax.ShapeDtypeStruct((gy_count // 2, 2, rows, width), BF16)
+    for number, masks in enumerate(units_of):
+        after = []
+        if number + 1 < len(units_of):
+            after = [jnp.stack([blocks[mask] for mask in units_of[number + 1]])]
         inputs, waiting, after = lax.optimization_barrier((inputs, waiting, after))
         far = [gather_far(one) for one in after]
-        arrived = [send_far(one) for one in waiting]
-        terms = pl.pallas_call(
-            lambda *refs: expert_kernel(gy_count, masks, *refs),
+        arrived = [swap(one, "gy", 2 * place) for place, one in enumerate(waiting) if place]
+        odd, even = pl.pallas_call(
+            lambda *refs: expert_kernel(gy_count, masks, number > 0, *refs),
             grid=(experts,),
             in_specs=[
                 smem(),
                 pl.BlockSpec((1, depth), lambda expert: (0, 0)),
                 pl.BlockSpec((1, gx_count * rows, 1), lambda expert: (expert, 0, 0)),
-                pl.BlockSpec((1, depth, 2 * units), lambda expert: (expert, 0, 0)),
-                pl.BlockSpec((1, units, depth), lambda expert: (expert, 0, 0)),
+                pl.BlockSpec((1, depth, units), lambda expert: (expert, 0, 0)),
+                pl.BlockSpec((1, depth, units), lambda expert: (expert, 0, 0)),
+                pl.BlockSpec(memory_space=pl.ANY),
             ]
-            + [vmem()] * (together * gy_count),
-            out_specs=[vmem()] * (2 * together),
-            out_shape=[half] * (2 * together),
+            + [vmem()] * len(inputs),
+            out_specs=[vmem(), vmem()],
+            out_shape=(half, half),
             scratch_shapes=[
-                pltpu.VMEM((together * rows, depth), BF16),
-                pltpu.VMEM((together * rows, depth), F32),
+                pltpu.VMEM((2 * rows, depth), BF16),
+                pltpu.VMEM((experts, 2 * rows, units), BF16),
+                pltpu.VMEM((experts * units, depth), BF16),
+                pltpu.SemaphoreType.DMA,
             ],
             compiler_params=params(),
-            cost_estimate=cost(
-                6 * together * rows * depth * experts * units, 6 * depth * experts * units
-            ),
+            cost_estimate=cost(12 * rows * depth * experts * units, 6 * depth * experts * units),
             name="experts",
-        )(ids, expert_gain.reshape(1, depth), gates, gate_up, down_weight, *inputs)
-        terms, far, arrived = lax.optimization_barrier((terms, far, arrived))
-        pending += [
-            (start - together + place, sum([one.astype(F32) for one in got], held[0]))
-            for place, (held, got) in enumerate(zip(waiting, arrived))
-        ]
-        near = [swap(odd, "gy", 1) for odd in terms[1::2]]
-        everything = [gather_near(one) for one in far]
-        waiting = []
-        for mask, even, odd in zip(masks, terms[0::2], near):
-            summed = even.astype(F32) + odd.astype(F32)
-            if start + together < gx_count:
-                waiting.append([summed[0]] + [one.astype(BF16) for one in summed[1:]])
-            else:
-                pending.append((mask, halve_gy(summed, mask % 2)))
+        )(
+            ids,
+            expert_gain.reshape(1, depth),
+            gates,
+            gate_weight,
+            up_weight,
+            down_weight.reshape(experts * units, depth),
+            *inputs,
+        )
+        odd, even, far, arrived = lax.optimization_barrier((odd, even, far, arrived))
+        if waiting:
+            total = sum([one.astype(F32) for one in arrived], waiting[0])
+            pending += list(zip(last, total))
+        last = masks
+        near = swap(odd, "gy", 1)
+        inputs = [one for pieces in far for one in gather_near(pieces)]
+        summed = even.astype(F32) + near.astype(F32)
+        if after:
+            waiting = [summed[0]] + [one.astype(BF16) for one in summed[1:]]
+        else:
+            pending += [(mask, halve_gy(summed[:, turn], turn)) for turn, mask in enumerate(masks)]
     for mask, total in pending:
         if mask:
             total = swap(total.astype(BF16), "gx", mask).astype(F32)
         result = result + total
     return (result.astype(BF16), compacted)
-
-
-def send_far(held):
-    return [swap(one, "gy", 2 * place) for place, one in enumerate(held) if place]
 
 
 def gather_far(value):

time: 226 us -> 213 us (0.942)
  starting transfers between devices: 69.6 us -> 54.8 us
  Pallas kernels: 63.3 us -> 58.3 us
  local copies, waits for them, and re-layouts: 20.1 us -> 24.6 us
    ppermute x68 -> x56, starting transfers between devices: 68 us -> 53.2 us  [swap(): lax.ppermute(value, axis, [(one, one ^ mask) for one in range(count)])]
    reshape x1 -> x0, local copies, waits for them, and re-layouts: 14.1 us -> none  [per_device(): gate_up = gate_up_weight.reshape(experts, depth, 2 * units)]
    optimization_barrier x0 -> x2, local copies, waits for them, and re-layouts: none -> 9.88 us  [the longest x1 7.91 us: per_device(): source, moved = lax.optimization_barrier((gate_up_weight, moved))]
    unnamed x109 -> x84, local copies, waits for them, and re-layouts: 3.08 us -> 9.28 us
    pallas_call x2, Pallas kernels: 32 us -> 27.1 us  [per_device(): pl.pallas_call(lambda *refs: expert_kernel(gy_count, masks, number > 0, *...]
    squeeze x1 -> x2, local copies, waits for them, and re-layouts: 0.04 us -> 4.45 us  [the longest x1 4.41 us: per_device(): source[:, :, 1]]
    ppermute x68 -> x56, waiting for transfers between devices: 43.3 us -> 45.3 us  [swap(): lax.ppermute(value, axis, [(one, one ^ mask) for one in range(count)])]
  transfers between devices with their start and end apart: 70 -> 58, of which waited for: 23 -> 18; matrix products, arithmetic and copies ran while one was open for 13% -> 16% of each run, Pallas kernels for 27% -> 26%
where the time goes in v4:
time: 213 us
  Pallas kernels  58.3 us (27%)
  starting transfers between devices  54.8 us (26%)
  waiting for transfers between devices  45.3 us (21%)
  local copies, waits for them, and re-layouts  24.6 us (12%)
  between operations  14.9 us (7%)
  other arithmetic  12.3 us (6%)
  matrix products  2.54 us (1%)
    ppermute x56, starting transfers between devices, swap(): lax.ppermute(value, axis, [(one, one ^ mask) for one in range(count)])  53.2 us
    ppermute x56, waiting for transfers between devices, swap(): lax.ppermute(value, axis, [(one, one ^ mask) for one in range(count)])  45.3 us
    pallas_call x2, Pallas kernels, per_device(): pl.pallas_call(lambda *refs: expert_kernel(gy_count, masks, number > 0, *...  27.1 us
    pallas_call x1, Pallas kernels, per_device(): pl.pallas_call(lambda *refs: cache_kernel(requests, draft, heads, gx_coun...  21 us
    unnamed x84, local copies, waits for them, and re-layouts  9.28 us
    optimization_barrier x1, local copies, waits for them, and re-layouts, per_device(): source, moved = lax.optimization_barrier((gate_up_weight, moved))  7.91 us
    squeeze x1, local copies, waits for them, and re-layouts, per_device(): source[:, :, 1]  4.41 us
  transfers between devices with their start and end apart: 58, of which 18 were waited for; matrix products, arithmetic and copies ran while one was open for 16% of the time, Pallas kernels for 26%

profile of v4, /device:TPU:0, one launch (start us, length us, event | category | flops | bytes accessed | tf_op | source)
XLA Modules:
  0.0 212.6 jit_solution(2662272934068059494)
XLA Ops:
  7.2 1.6 collective-permute-start.3
  11.9 1.3 convolution_minimum_fusion.4
  16.8 6.2 %copy.42 = bf16[4,2048,1,256]{3,1,0,2:T(8,128)(2,1)} copy(bf16[4,2048,1,256]{3,2,1,0:T(2,128)(2,1)} %bitcast.99) | data formatting | bytes 8388608
  23.0 4.7 %collective-permute-start.1 = (f32[256,1]{1,0:T(8,128)S(1)}, f32[256,1]{1,0:T(8,128)S(1)}, u32[]{:S(2)}, u32[]{:S(2)}) collective-permute-start(f32[256,1]{1,0:T(8,128)S(1)} %add.110), channel_id=1, source_target_pairs={{0,2},{1,3},{2,0},{3,1},{4,6},{5,7},{6,4},{7,5},{8,10},{9,11},{10,... | collective-permute-start | bytes 3080 | tf_op jit(solution)/shard_map/ppermute | solution.py:32
  27.9 3.3 %collective-permute-start.5 = (bf16[256,256]{1,0:T(8,128)(2,1)S(1)}, bf16[256,256]{1,0:T(8,128)(2,1)S(1)}, u32[]{:S(2)}, u32[]{:S(2)}) collective-permute-start(bf16[256,256]{1,0:T(8,128)(2,1)S(1)} %collective-permute-done.3.refs_3_), channel_id=1, source_target_pairs={{0,4},{1,5},{2,6},{3,7},{4,0},{5,1},{6,2},{7,3},{8,12},{9,13},{10,... | collective-permute-start | bytes 393224 | tf_op jit(solution)/shard_map/ppermute | solution.py:32
  31.2 1.4 collective-permute-start.6
  32.5 7.9 %copy.35 = bf16[4,2048,2,256]{3,1,0,2:T(8,128)(2,1)} copy(bf16[4,2048,2,256]{3,2,1,0:T(2,128)(2,1)} %param.24) | data formatting | bytes 16777216 | tf_op jit(solution)/shard_map/optimization_barrier | solution.py:278
  40.5 4.4 %slice_bitcast_fusion.refs_4_ = bf16[4,2048,256]{2,1,0:T(8,128)(2,1)} fusion(bf16[4,2048,2,256]{3,1,0,2:T(8,128)(2,1)} %copy.35), kind=kLoop, calls=%fused_computation | loop fusion | bytes 8388608 | tf_op jit(solution)/shard_map/squeeze | solution.py:279
  46.7 2.1 collective-permute-start.2
  50.9 3.6 %project.1 = (f32[256,256]{1,0:T(8,128)}, bf16[256,256]{1,0:T(8,128)(2,1)}, bf16[256,256]{1,0:T(8,128)(2,1)}, bf16[256,256]{1,0:T(8,128)(2,1)}, f32[2,256,256]{2...) custom-call(s32[2]{0:T(128)} %pad_add_fusion.refs_0_, ...), custom_call_target="tpu_custom_call" | custom-call | tf_op jit(solution)/shard_map/project/pallas_call | solution.py:282
  55.4 3.5 %collective-permute-start.16 = (bf16[256,256]{1,0:T(8,128)(2,1)}, bf16[256,256]{1,0:T(8,128)(2,1)S(1)}, u32[]{:S(2)}, u32[]{:S(2)}) collective-permute-start(bf16[256,256]{1,0:T(8,128)(2,1)} %get-tuple-element.84), channel_id=1, source_target_pairs={{0,24},{8,16},{16,8},{24,0},{1,25},{9,17},{17,9},{25,1},{2,26},{10... | collective-permute-start | bytes 393224 | tf_op jit(solution)/shard_map/ppermute | solution.py:32
  60.4 1.4 collective-permute-done.14.refs_6_
  61.8 2.1 collective-permute-start.13
  64.0 4.0 %collective-permute-done.15.refs_7_ = bf16[256,256]{1,0:T(8,128)(2,1)S(1)} collective-permute-done((bf16[256,256]{1,0:T(8,128)(2,1)}, bf16[256,256]{1,0:T(8,128)(2,1)S(1)}, u32[]{:S(2)}, u32[]{:S(2)}) %collective-permute-start.15) | collective-permute-done | bytes 131104 | tf_op jit(solution)/shard_map/ppermute | solution.py:32
  68.7 21.0 %cache.1 = (f32[512,128]{1,0:T(8,128)}, f32[512,128]{1,0:T(8,128)}, f32[512,256]{1,0:T(8,128)}, bf16[256,256]{1,0:T(8,128)(2,1)}) custom-call(s32[2]{0:T(128)} %refs_0_.1, s32[2]{0:T(128)} %get-tuple-element.147.refs_1_, s32[2]{0:T(128)} %get-tuple-element.146.refs_2_, s32[4]{0:T(128)} %convert_reduce_fusion.refs_3_.refs_0_, ...), custom_call_target="tpu_custom_call" | custom-call | flops 10737418240 | bytes 16777216 | tf_op jit(solution)/shard_map/cache/pallas_call | solution.py:316
  90.6 3.8 %draft.1 = (bf16[256,256]{1,0:T(8,128)(2,1)}, bf16[2,32,256]{2,1,0:T(8,128)(2,1)}) custom-call(s32[4]{0:T(128)} %convert_reduce_fusion.refs_3_.refs_0_, f32[256,1]{1,0:T(8,128)} %add_rsqrt_fusion.refs_4_.refs_1_, f32[2,256,256]{2,1,0:T(8,128)} %get-tuple-element.77.refs_2_, bf16[2,256,256]{2,1,0:T(8,128)(2,1)} %copy-done.3, bf16[2,256,256]{2,1,0:T(8,128)(2,1)} %copy-done.4, ...), custom_call_target="tpu_custom_call" | custom-call | tf_op jit(solution)/shard_map/draft/pallas_call | solution.py:357
  94.4 2.8 %output.1 = (bf16[4,256,256]{2,1,0:T(8,128)(2,1)}, bf16[4,256,256]{2,1,0:T(8,128)(2,1)}) custom-call(s32[2]{0:T(128)} %pad_add_fusion.refs_0_, bf16[256,256]{1,0:T(8,128)(2,1)} %get-tuple-element.89.refs_1_, bf16[2048,256]{1,0:T(8,128)(2,1)} %all-gather.2.cloned.1.call-done.refs_2_), custom_call_target="tpu_custom_call" | custom-call | tf_op jit(solution)/shard_map/output/pallas_call | solution.py:375
  97.2 2.1 collective-permute-done.17
  101.5 2.6 %collective-permute-start.20 = (bf16[256,256]{1,0:T(8,128)(2,1)S(1)}, bf16[256,256]{1,0:T(8,128)(2,1)S(1)}, u32[]{:S(2)}, u32[]{:S(2)}) collective-permute-start(bf16[256,256]{1,0:T(8,128)(2,1)S(1)} %get-tuple-element.166), channel_id=1, source_target_pairs={{0,6},{1,7},{2,4},{3,5},{4,2},{5,3},{6,0},{7,1},{8,14},{9,15},{10,... | collective-permute-start | bytes 393224 | tf_op jit(solution)/shard_map/ppermute | solution.py:32
  104.0 2.9 %collective-permute-done.18 = bf16[256,256]{1,0:T(8,128)(2,1)S(1)} collective-permute-done((bf16[256,256]{1,0:T(8,128)(2,1)S(1)}, bf16[256,256]{1,0:T(8,128)(2,1)S(1)}, u32[]{:S(2)}, u32[]{:S(2)}) %collective-permute-start.18) | collective-permute-done | bytes 131104 | tf_op jit(solution)/shard_map/ppermute | solution.py:32
  106.9 2.1 collective-permute-done.19
  109.1 4.1 %collective-permute-start.36 = (bf16[256,256]{1,0:T(8,128)(2,1)S(1)}, bf16[256,256]{1,0:T(8,128)(2,1)S(1)}, u32[]{:S(2)}, u32[]{:S(2)}) collective-permute-start(bf16[256,256]{1,0:T(8,128)(2,1)S(1)} %fusion.4.refs_6_), channel_id=1, source_target_pairs={{0,8},{8,0},{16,24},{24,16},{1,9},{9,1},{17,25},{25,17},{2,10},{10... | collective-permute-start | bytes 393224 | tf_op jit(solution)/shard_map/ppermute | solution.py:32
  113.3 1.7 collective-permute-start.22
  114.9 2.2 %collective-permute-start.37 = (bf16[256,256]{1,0:T(8,128)(2,1)S(1)}, bf16[256,256]{1,0:T(8,128)(2,1)S(1)}, u32[]{:S(2)}, u32[]{:S(2)}) collective-permute-start(bf16[256,256]{1,0:T(8,128)(2,1)S(1)} %fusion.4.refs_6_), channel_id=1, source_target_pairs={{0,24},{8,16},{16,8},{24,0},{1,25},{9,17},{17,9},{25,1},{2,26},{10... | collective-permute-start | bytes 393224 | tf_op jit(solution)/shard_map/ppermute | solution.py:32
  117.6 7.2 %collective-permute-done.28.refs_14_ = bf16[256,256]{1,0:T(8,128)(2,1)S(1)} collective-permute-done((bf16[256,256]{1,0:T(8,128)(2,1)S(1)}, bf16[256,256]{1,0:T(8,128)(2,1)S(1)}, u32[]{:S(2)}, u32[]{:S(2)}) %collective-permute-start.28) | collective-permute-done | bytes 131104 | tf_op jit(solution)/shard_map/ppermute | solution.py:32
  124.8 1.7 collective-permute-start.32
  126.8 1.2 collective-permute-start.30
  128.5 1.2 collective-permute-done.32.refs_18_
  129.7 1.7 collective-permute-start.34
  133.0 1.7 collective-permute-done.34.refs_20_
  134.7 2.0 copy.37.refs_2_
  136.8 1.8 collective-permute-start.38
  138.9 1.4 collective-permute-start.40
  140.5 13.7 %experts.2 = (bf16[4,2,256,256]{3,2,1,0:T(8,128)(2,1)}, bf16[4,2,256,256]{3,2,1,0:T(8,128)(2,1)}) custom-call(s32[2]{0:T(128)} %pad_add_fusion.refs_0_, f32[1,2048]{1,0:T(1,128)} %bitcast.111, f32[4,1024,1]{2,1,0:T(8,128)} %copy.37.refs_2_, bf16[4,2048,256]{2,1,0:T(8,128)(2,1)} %bitcast.100, bf16[4,2048,256]{2,1,0:T(8,128)(2,1)} %slice_bitcast_fusion.refs_4_, ...), custom_call_target="tpu_custom_call" | custom-call | flops 6442450944 | bytes 12582912 | tf_op jit(solution)/shard_map/experts/pallas_call | solution.py:403
  155.5 2.4 %collective-permute-done.45 = bf16[4,2,256,256]{3,2,1,0:T(8,128)(2,1)S(1)} collective-permute-done((bf16[4,2,256,256]{3,2,1,0:T(8,128)(2,1)}, bf16[4,2,256,256]{3,2,1,0:T(8,128)(2,1)S(1)}, u32[]{:S(2)}, u32[]{:S(2)}) %collective-permute-start.45) | collective-permute-done | bytes 1048608 | tf_op jit(solution)/shard_map/ppermute | solution.py:32
  157.8 1.5 fusion.40
  159.6 1.8 collective-permute-start.46
  161.7 1.4 collective-permute-start.48
  163.2 13.4 %experts.3 = (bf16[4,2,256,256]{3,2,1,0:T(8,128)(2,1)}, bf16[4,2,256,256]{3,2,1,0:T(8,128)(2,1)}) custom-call(s32[2]{0:T(128)} %pad_add_fusion.refs_0_, f32[1,2048]{1,0:T(1,128)} %bitcast.112, f32[4,1024,1]{2,1,0:T(8,128)} %copy.37.refs_2_, bf16[4,2048,256]{2,1,0:T(8,128)(2,1)} %bitcast.101, bf16[4,2048,256]{2,1,0:T(8,128)(2,1)} %slice_bitcast_fusion.refs_4_, ...), custom_call_target="tpu_custom_call" | custom-call | flops 6442450944 | bytes 12582912 | tf_op jit(solution)/shard_map/experts/pallas_call | solution.py:403
  176.7 2.9 %collective-permute-done.50 = bf16[4,2,256,256]{3,2,1,0:T(8,128)(2,1)S(1)} collective-permute-done((bf16[4,2,256,256]{3,2,1,0:T(8,128)(2,1)}, bf16[4,2,256,256]{3,2,1,0:T(8,128)(2,1)S(1)}, u32[]{:S(2)}, u32[]{:S(2)}) %collective-permute-start.50) | collective-permute-done | bytes 1048608 | tf_op jit(solution)/shard_map/ppermute | solution.py:32
  179.5 1.5 convert_add_fusion
  181.2 1.7 collective-permute-start.54
  183.5 6.1 %collective-permute-done.54 = bf16[2,256,256]{2,1,0:T(8,128)(2,1)S(1)} collective-permute-done((bf16[2,256,256]{2,1,0:T(8,128)(2,1)S(1)}, bf16[2,256,256]{2,1,0:T(8,128)(2,1)S(1)}, u32[]{:S(2)}, u32[]{:S(2)}) %collective-permute-start.54) | collective-permute-done | bytes 262176 | tf_op jit(solution)/shard_map/ppermute | solution.py:32
  189.6 1.4 collective-permute-done.51
  191.6 1.7 collective-permute-start.55
  193.4 2.8 %collective-permute-done.52 = bf16[1,256,256]{2,1,0:T(8,128)(2,1)S(1)} collective-permute-done((bf16[1,256,256]{2,1,0:T(8,128)(2,1)S(1)}, bf16[1,256,256]{2,1,0:T(8,128)(2,1)S(1)}, u32[]{:S(2)}, u32[]{:S(2)}) %collective-permute-start.52) | collective-permute-done | bytes 131104 | tf_op jit(solution)/shard_map/ppermute | solution.py:32
  196.8 1.9 collective-permute-start.56
  199.4 5.0 %collective-permute-done.49 = bf16[256,256]{1,0:T(8,128)(2,1)S(1)} collective-permute-done((bf16[256,256]{1,0:T(8,128)(2,1)S(1)}, bf16[256,256]{1,0:T(8,128)(2,1)S(1)}, u32[]{:S(2)}, u32[]{:S(2)}) %collective-permute-start.49) | collective-permute-done | bytes 131104 | tf_op jit(solution)/shard_map/ppermute | solution.py:32
  (199 shorter events, 25.9 us)
Async XLA Ops:
  7.2 87.2 %all-gather.2.cloned.1.call-start = ((), (), s32[]{:S(2)}) async-start(), calls=%async_computation | async-start | bytes 1310720 | tf_op jit(solution)/shard_map/all_gather | solution.py:256
  7.2 20.6 %collective-permute-start.3 = (bf16[256,256]{1,0:T(8,128)(2,1)}, bf16[256,256]{1,0:T(8,128)(2,1)S(1)}, u32[]{:S(2)}, u32[]{:S(2)}) collective-permute-start(bf16[256,256]{1,0:T(8,128)(2,1)} %param.14), channel_id=1, source_target_pairs={{0,0},{1,1},{2,8},{3,9},{4,16},{5,17},{6,24},{7,25},{8,2},{9,3},{1... | collective-permute-start | bytes 393224 | tf_op jit(solution)/shard_map/ppermute | solution.py:270
  9.9 13.1 %collective-permute-start = (f32[256,1]{1,0:T(8,128)S(1)}, f32[256,1]{1,0:T(8,128)S(1)}, u32[]{:S(2)}, u32[]{:S(2)}) collective-permute-start(f32[256,1]{1,0:T(8,128)S(1)} %copy.33), channel_id=1, source_target_pairs={{0,1},{1,0},{2,3},{3,2},{4,5},{5,4},{6,7},{7,6},{8,9},{9,8},{10,11... | collective-permute-start | bytes 3080 | tf_op jit(solution)/shard_map/ppermute | solution.py:32
  23.0 23.7 %collective-permute-start.1 = (f32[256,1]{1,0:T(8,128)S(1)}, f32[256,1]{1,0:T(8,128)S(1)}, u32[]{:S(2)}, u32[]{:S(2)}) collective-permute-start(f32[256,1]{1,0:T(8,128)S(1)} %add.110), channel_id=1, source_target_pairs={{0,2},{1,3},{2,0},{3,1},{4,6},{5,7},{6,4},{7,5},{8,10},{9,11},{10,... | collective-permute-start | bytes 3080 | tf_op jit(solution)/shard_map/ppermute | solution.py:32
  27.8 17.1 %collective-permute-start.4 = (bf16[256,256]{1,0:T(8,128)(2,1)S(1)}, bf16[256,256]{1,0:T(8,128)(2,1)S(1)}, u32[]{:S(2)}, u32[]{:S(2)}) collective-permute-start(bf16[256,256]{1,0:T(8,128)(2,1)S(1)} %collective-permute-done.3.refs_3_), channel_id=1, source_target_pairs={{0,2},{1,3},{2,0},{3,1},{4,6},{5,7},{6,4},{7,5},{8,10},{9,11},{10,... | collective-permute-start | bytes 393224 | tf_op jit(solution)/shard_map/ppermute | solution.py:32
  27.9 17.0 %collective-permute-start.5 = (bf16[256,256]{1,0:T(8,128)(2,1)S(1)}, bf16[256,256]{1,0:T(8,128)(2,1)S(1)}, u32[]{:S(2)}, u32[]{:S(2)}) collective-permute-start(bf16[256,256]{1,0:T(8,128)(2,1)S(1)} %collective-permute-done.3.refs_3_), channel_id=1, source_target_pairs={{0,4},{1,5},{2,6},{3,7},{4,0},{5,1},{6,2},{7,3},{8,12},{9,13},{10,... | collective-permute-start | bytes 393224 | tf_op jit(solution)/shard_map/ppermute | solution.py:32
  31.2 13.7 %collective-permute-start.6 = (bf16[256,256]{1,0:T(8,128)(2,1)S(1)}, bf16[256,256]{1,0:T(8,128)(2,1)S(1)}, u32[]{:S(2)}, u32[]{:S(2)}) collective-permute-start(bf16[256,256]{1,0:T(8,128)(2,1)S(1)} %collective-permute-done.3.refs_3_), channel_id=1, source_target_pairs={{0,6},{1,7},{2,4},{3,5},{4,2},{5,3},{6,0},{7,1},{8,14},{9,15},{10,... | collective-permute-start | bytes 393224 | tf_op jit(solution)/shard_map/ppermute | solution.py:32
  44.9 5.2 %collective-permute-start.10 = (bf16[256,256]{1,0:T(8,128)(2,1)S(1)}, bf16[256,256]{1,0:T(8,128)(2,1)S(1)}, u32[]{:S(2)}, u32[]{:S(2)}) collective-permute-start(bf16[256,256]{1,0:T(8,128)(2,1)S(1)} %collective-permute-done.6.refs_9_), channel_id=1, source_target_pairs={{0,1},{1,0},{2,3},{3,2},{4,5},{5,4},{6,7},{7,6},{8,9},{9,8},{10,11... | collective-permute-start | bytes 393224 | tf_op jit(solution)/shard_map/ppermute | solution.py:32
  45.0 5.1 %collective-permute-start.7 = (bf16[256,256]{1,0:T(8,128)(2,1)S(1)}, bf16[256,256]{1,0:T(8,128)(2,1)S(1)}, u32[]{:S(2)}, u32[]{:S(2)}) collective-permute-start(bf16[256,256]{1,0:T(8,128)(2,1)S(1)} %collective-permute-done.3.refs_3_), channel_id=1, source_target_pairs={{0,1},{1,0},{2,3},{3,2},{4,5},{5,4},{6,7},{7,6},{8,9},{9,8},{10,11... | collective-permute-start | bytes 393224 | tf_op jit(solution)/shard_map/ppermute | solution.py:32
  45.5 4.6 %collective-permute-start.8 = (bf16[256,256]{1,0:T(8,128)(2,1)S(1)}, bf16[256,256]{1,0:T(8,128)(2,1)S(1)}, u32[]{:S(2)}, u32[]{:S(2)}) collective-permute-start(bf16[256,256]{1,0:T(8,128)(2,1)S(1)} %collective-permute-done.4.refs_5_), channel_id=1, source_target_pairs={{0,1},{1,0},{2,3},{3,2},{4,5},{5,4},{6,7},{7,6},{8,9},{9,8},{10,11... | collective-permute-start | bytes 393224 | tf_op jit(solution)/shard_map/ppermute | solution.py:32
  46.7 12.1 %collective-permute-start.2 = (f32[256,1]{1,0:T(8,128)S(1)}, f32[256,1]{1,0:T(8,128)S(1)}, u32[]{:S(2)}, u32[]{:S(2)}) collective-permute-start(f32[256,1]{1,0:T(8,128)S(1)} %add.111), channel_id=1, source_target_pairs={{0,4},{1,5},{2,6},{3,7},{4,0},{5,1},{6,2},{7,3},{8,12},{9,13},{10,... | collective-permute-start | bytes 3080 | tf_op jit(solution)/shard_map/ppermute | solution.py:32
  54.5 7.3 %collective-permute-start.14 = (bf16[256,256]{1,0:T(8,128)(2,1)}, bf16[256,256]{1,0:T(8,128)(2,1)S(1)}, u32[]{:S(2)}, u32[]{:S(2)}) collective-permute-start(bf16[256,256]{1,0:T(8,128)(2,1)} %get-tuple-element.82), channel_id=1, source_target_pairs={{0,8},{8,0},{16,24},{24,16},{1,9},{9,1},{17,25},{25,17},{2,10},{10... | collective-permute-start | bytes 393224 | tf_op jit(solution)/shard_map/ppermute | solution.py:32
  55.2 12.8 %collective-permute-start.15 = (bf16[256,256]{1,0:T(8,128)(2,1)}, bf16[256,256]{1,0:T(8,128)(2,1)S(1)}, u32[]{:S(2)}, u32[]{:S(2)}) collective-permute-start(bf16[256,256]{1,0:T(8,128)(2,1)} %get-tuple-element.83), channel_id=1, source_target_pairs={{0,16},{8,24},{16,0},{24,8},{1,17},{9,25},{17,1},{25,9},{2,18},{10... | collective-permute-start | bytes 393224 | tf_op jit(solution)/shard_map/ppermute | solution.py:32
  55.4 12.6 %collective-permute-start.16 = (bf16[256,256]{1,0:T(8,128)(2,1)}, bf16[256,256]{1,0:T(8,128)(2,1)S(1)}, u32[]{:S(2)}, u32[]{:S(2)}) collective-permute-start(bf16[256,256]{1,0:T(8,128)(2,1)} %get-tuple-element.84), channel_id=1, source_target_pairs={{0,24},{8,16},{16,8},{24,0},{1,25},{9,17},{17,9},{25,1},{2,26},{10... | collective-permute-start | bytes 393224 | tf_op jit(solution)/shard_map/ppermute | solution.py:32
  59.6 30.1 %collective-permute-start.11 = (bf16[2,256,256]{2,1,0:T(8,128)(2,1)}, bf16[2,256,256]{2,1,0:T(8,128)(2,1)S(1)}, u32[]{:S(2)}, u32[]{:S(2)}) collective-permute-start(bf16[2,256,256]{2,1,0:T(8,128)(2,1)} %get-tuple-element.78), channel_id=1, source_target_pairs={{0,8},{8,0},{16,24},{24,16},{1,9},{9,1},{17,25},{25,17},{2,10},{10... | collective-permute-start | bytes 786440 | tf_op jit(solution)/shard_map/ppermute | solution.py:32
  59.6 30.1 %collective-permute-start.12 = (bf16[2,256,256]{2,1,0:T(8,128)(2,1)}, bf16[2,256,256]{2,1,0:T(8,128)(2,1)S(1)}, u32[]{:S(2)}, u32[]{:S(2)}) collective-permute-start(bf16[2,256,256]{2,1,0:T(8,128)(2,1)} %get-tuple-element.79), channel_id=1, source_target_pairs={{0,16},{8,24},{16,0},{24,8},{1,17},{9,25},{17,1},{25,9},{2,18},{10... | collective-permute-start | bytes 786440 | tf_op jit(solution)/shard_map/ppermute | solution.py:32
  61.8 27.8 %collective-permute-start.13 = (bf16[2,256,256]{2,1,0:T(8,128)(2,1)}, bf16[2,256,256]{2,1,0:T(8,128)(2,1)S(1)}, u32[]{:S(2)}, u32[]{:S(2)}) collective-permute-start(bf16[2,256,256]{2,1,0:T(8,128)(2,1)} %get-tuple-element.80), channel_id=1, source_target_pairs={{0,24},{8,16},{16,8},{24,0},{1,25},{9,17},{17,9},{25,1},{2,26},{10... | collective-permute-start | bytes 786440 | tf_op jit(solution)/shard_map/ppermute | solution.py:32
  100.5 6.4 %collective-permute-start.18 = (bf16[256,256]{1,0:T(8,128)(2,1)S(1)}, bf16[256,256]{1,0:T(8,128)(2,1)S(1)}, u32[]{:S(2)}, u32[]{:S(2)}) collective-permute-start(bf16[256,256]{1,0:T(8,128)(2,1)S(1)} %get-tuple-element.165), channel_id=1, source_target_pairs={{0,2},{1,3},{2,0},{3,1},{4,6},{5,7},{6,4},{7,5},{8,10},{9,11},{10,... | collective-permute-start | bytes 393224 | tf_op jit(solution)/shard_map/ppermute | solution.py:32
  100.9 8.1 %collective-permute-start.19 = (bf16[256,256]{1,0:T(8,128)(2,1)S(1)}, bf16[256,256]{1,0:T(8,128)(2,1)S(1)}, u32[]{:S(2)}, u32[]{:S(2)}) collective-permute-start(bf16[256,256]{1,0:T(8,128)(2,1)S(1)} %get-tuple-element.167), channel_id=1, source_target_pairs={{0,4},{1,5},{2,6},{3,7},{4,0},{5,1},{6,2},{7,3},{8,12},{9,13},{10,... | collective-permute-start | bytes 393224 | tf_op jit(solution)/shard_map/ppermute | solution.py:32
  101.5 7.5 %collective-permute-start.20 = (bf16[256,256]{1,0:T(8,128)(2,1)S(1)}, bf16[256,256]{1,0:T(8,128)(2,1)S(1)}, u32[]{:S(2)}, u32[]{:S(2)}) collective-permute-start(bf16[256,256]{1,0:T(8,128)(2,1)S(1)} %get-tuple-element.166), channel_id=1, source_target_pairs={{0,6},{1,7},{2,4},{3,5},{4,2},{5,3},{6,0},{7,1},{8,14},{9,15},{10,... | collective-permute-start | bytes 393224 | tf_op jit(solution)/shard_map/ppermute | solution.py:32
  109.1 8.5 %collective-permute-start.36 = (bf16[256,256]{1,0:T(8,128)(2,1)S(1)}, bf16[256,256]{1,0:T(8,128)(2,1)S(1)}, u32[]{:S(2)}, u32[]{:S(2)}) collective-permute-start(bf16[256,256]{1,0:T(8,128)(2,1)S(1)} %fusion.4.refs_6_), channel_id=1, source_target_pairs={{0,8},{8,0},{16,24},{24,16},{1,9},{9,1},{17,25},{25,17},{2,10},{10... | collective-permute-start | bytes 393224 | tf_op jit(solution)/shard_map/ppermute | solution.py:32
  113.2 11.5 %collective-permute-start.28 = (bf16[256,256]{1,0:T(8,128)(2,1)S(1)}, bf16[256,256]{1,0:T(8,128)(2,1)S(1)}, u32[]{:S(2)}, u32[]{:S(2)}) collective-permute-start(bf16[256,256]{1,0:T(8,128)(2,1)S(1)} %fusion.4.refs_6_), channel_id=1, source_target_pairs={{0,16},{8,24},{16,0},{24,8},{1,17},{9,25},{17,1},{25,9},{2,18},{10... | collective-permute-start | bytes 393224 | tf_op jit(solution)/shard_map/ppermute | solution.py:32
  113.3 13.2 %collective-permute-start.22 = (bf16[256,256]{1,0:T(8,128)(2,1)S(1)}, bf16[256,256]{1,0:T(8,128)(2,1)S(1)}, u32[]{:S(2)}, u32[]{:S(2)}) collective-permute-start(bf16[256,256]{1,0:T(8,128)(2,1)S(1)} %fusion.4.refs_6_), channel_id=1, source_target_pairs={{0,2},{1,3},{2,0},{3,1},{4,6},{5,7},{6,4},{7,5},{8,10},{9,11},{10,... | collective-permute-start | bytes 393224 | tf_op jit(solution)/shard_map/ppermute | solution.py:32
  114.9 11.9 %collective-permute-start.37 = (bf16[256,256]{1,0:T(8,128)(2,1)S(1)}, bf16[256,256]{1,0:T(8,128)(2,1)S(1)}, u32[]{:S(2)}, u32[]{:S(2)}) collective-permute-start(bf16[256,256]{1,0:T(8,128)(2,1)S(1)} %fusion.4.refs_6_), channel_id=1, source_target_pairs={{0,24},{8,16},{16,8},{24,0},{1,25},{9,17},{17,9},{25,1},{2,26},{10... | collective-permute-start | bytes 393224 | tf_op jit(solution)/shard_map/ppermute | solution.py:32
  117.2 10.8 %collective-permute-start.24 = (bf16[256,256]{1,0:T(8,128)(2,1)S(1)}, bf16[256,256]{1,0:T(8,128)(2,1)S(1)}, u32[]{:S(2)}, u32[]{:S(2)}) collective-permute-start(bf16[256,256]{1,0:T(8,128)(2,1)S(1)} %fusion.4.refs_6_), channel_id=1, source_target_pairs={{0,4},{1,5},{2,6},{3,7},{4,0},{5,1},{6,2},{7,3},{8,12},{9,13},{10,... | collective-permute-start | bytes 393224 | tf_op jit(solution)/shard_map/ppermute | solution.py:32
  117.6 10.4 %collective-permute-start.21 = (bf16[256,256]{1,0:T(8,128)(2,1)S(1)}, bf16[256,256]{1,0:T(8,128)(2,1)S(1)}, u32[]{:S(2)}, u32[]{:S(2)}) collective-permute-start(bf16[256,256]{1,0:T(8,128)(2,1)S(1)} %fusion.4.refs_6_), channel_id=1, source_target_pairs={{0,1},{1,0},{2,3},{3,2},{4,5},{5,4},{6,7},{7,6},{8,9},{9,8},{10,11... | collective-permute-start | bytes 393224 | tf_op jit(solution)/shard_map/ppermute | solution.py:32
  124.8 5.0 %collective-permute-start.32 = (bf16[256,256]{1,0:T(8,128)(2,1)S(1)}, bf16[256,256]{1,0:T(8,128)(2,1)S(1)}, u32[]{:S(2)}, u32[]{:S(2)}) collective-permute-start(bf16[256,256]{1,0:T(8,128)(2,1)S(1)} %collective-permute-done.28.refs_14_), channel_id=1, source_target_pairs={{0,4},{1,5},{2,6},{3,7},{4,0},{5,1},{6,2},{7,3},{8,12},{9,13},{10,... | collective-permute-start | bytes 393224 | tf_op jit(solution)/shard_map/ppermute | solution.py:32
  126.4 5.0 %collective-permute-start.26 = (bf16[256,256]{1,0:T(8,128)(2,1)S(1)}, bf16[256,256]{1,0:T(8,128)(2,1)S(1)}, u32[]{:S(2)}, u32[]{:S(2)}) collective-permute-start(bf16[256,256]{1,0:T(8,128)(2,1)S(1)} %collective-permute-done.22.refs_8_), channel_id=1, source_target_pairs={{0,4},{1,5},{2,6},{3,7},{4,0},{5,1},{6,2},{7,3},{8,12},{9,13},{10,... | collective-permute-start | bytes 393224 | tf_op jit(solution)/shard_map/ppermute | solution.py:32
  126.8 5.6 %collective-permute-start.30 = (bf16[256,256]{1,0:T(8,128)(2,1)S(1)}, bf16[256,256]{1,0:T(8,128)(2,1)S(1)}, u32[]{:S(2)}, u32[]{:S(2)}) collective-permute-start(bf16[256,256]{1,0:T(8,128)(2,1)S(1)} %collective-permute-done.28.refs_14_), channel_id=1, source_target_pairs={{0,2},{1,3},{2,0},{3,1},{4,6},{5,7},{6,4},{7,5},{8,10},{9,11},{10,... | collective-permute-start | bytes 393224 | tf_op jit(solution)/shard_map/ppermute | solution.py:32
  128.0 4.9 %collective-permute-start.25 = (bf16[256,256]{1,0:T(8,128)(2,1)S(1)}, bf16[256,256]{1,0:T(8,128)(2,1)S(1)}, u32[]{:S(2)}, u32[]{:S(2)}) collective-permute-start(bf16[256,256]{1,0:T(8,128)(2,1)S(1)} %collective-permute-done.24.refs_10_), channel_id=1, source_target_pairs={{0,1},{1,0},{2,3},{3,2},{4,5},{5,4},{6,7},{7,6},{8,9},{9,8},{10,11... | collective-permute-start | bytes 393224 | tf_op jit(solution)/shard_map/ppermute | solution.py:32
  129.7 5.0 %collective-permute-start.34 = (bf16[256,256]{1,0:T(8,128)(2,1)S(1)}, bf16[256,256]{1,0:T(8,128)(2,1)S(1)}, u32[]{:S(2)}, u32[]{:S(2)}) collective-permute-start(bf16[256,256]{1,0:T(8,128)(2,1)S(1)} %collective-permute-done.32.refs_18_), channel_id=1, source_target_pairs={{0,2},{1,3},{2,0},{3,1},{4,6},{5,7},{6,4},{7,5},{8,10},{9,11},{10,... | collective-permute-start | bytes 393224 | tf_op jit(solution)/shard_map/ppermute | solution.py:32
  131.4 5.3 %collective-permute-start.29 = (bf16[256,256]{1,0:T(8,128)(2,1)S(1)}, bf16[256,256]{1,0:T(8,128)(2,1)S(1)}, u32[]{:S(2)}, u32[]{:S(2)}) collective-permute-start(bf16[256,256]{1,0:T(8,128)(2,1)S(1)} %collective-permute-done.28.refs_14_), channel_id=1, source_target_pairs={{0,1},{1,0},{2,3},{3,2},{4,5},{5,4},{6,7},{7,6},{8,9},{9,8},{10,11... | collective-permute-start | bytes 393224 | tf_op jit(solution)/shard_map/ppermute | solution.py:32
  136.8 17.4 %collective-permute-start.38 = (bf16[2,256,256]{2,1,0:T(8,128)(2,1)S(1)}, bf16[2,256,256]{2,1,0:T(8,128)(2,1)S(1)}, u32[]{:S(2)}, u32[]{:S(2)}) collective-permute-start(bf16[2,256,256]{2,1,0:T(8,128)(2,1)S(1)} %pad_maximum_fusion.refs_6_), channel_id=1, source_target_pairs={{0,2},{1,3},{2,0},{3,1},{4,6},{5,7},{6,4},{7,5},{8,10},{9,11},{10,... | collective-permute-start | bytes 786440 | tf_op jit(solution)/shard_map/ppermute | solution.py:32
  138.6 15.7 %collective-permute-start.39 = (bf16[2,256,256]{2,1,0:T(8,128)(2,1)S(1)}, bf16[2,256,256]{2,1,0:T(8,128)(2,1)S(1)}, u32[]{:S(2)}, u32[]{:S(2)}) collective-permute-start(bf16[2,256,256]{2,1,0:T(8,128)(2,1)S(1)} %pad_maximum_fusion.refs_6_), channel_id=1, source_target_pairs={{0,4},{1,5},{2,6},{3,7},{4,0},{5,1},{6,2},{7,3},{8,12},{9,13},{10,... | collective-permute-start | bytes 786440 | tf_op jit(solution)/shard_map/ppermute | solution.py:32
  138.9 15.4 %collective-permute-start.40 = (bf16[2,256,256]{2,1,0:T(8,128)(2,1)S(1)}, bf16[2,256,256]{2,1,0:T(8,128)(2,1)S(1)}, u32[]{:S(2)}, u32[]{:S(2)}) collective-permute-start(bf16[2,256,256]{2,1,0:T(8,128)(2,1)S(1)} %pad_maximum_fusion.refs_6_), channel_id=1, source_target_pairs={{0,6},{1,7},{2,4},{3,5},{4,2},{5,3},{6,0},{7,1},{8,14},{9,15},{10,... | collective-permute-start | bytes 786440 | tf_op jit(solution)/shard_map/ppermute | solution.py:32
  154.4 5.1 %collective-permute-start.41 = (bf16[2,256,256]{2,1,0:T(8,128)(2,1)S(1)}, bf16[2,256,256]{2,1,0:T(8,128)(2,1)S(1)}, u32[]{:S(2)}, u32[]{:S(2)}) collective-permute-start(bf16[2,256,256]{2,1,0:T(8,128)(2,1)S(1)} %pad_maximum_fusion.refs_6_), channel_id=1, source_target_pairs={{0,1},{1,0},{2,3},{3,2},{4,5},{5,4},{6,7},{7,6},{8,9},{9,8},{10,11... | collective-permute-start | bytes 786440 | tf_op jit(solution)/shard_map/ppermute | solution.py:32
  154.9 4.7 %collective-permute-start.42 = (bf16[2,256,256]{2,1,0:T(8,128)(2,1)S(1)}, bf16[2,256,256]{2,1,0:T(8,128)(2,1)S(1)}, u32[]{:S(2)}, u32[]{:S(2)}) collective-permute-start(bf16[2,256,256]{2,1,0:T(8,128)(2,1)S(1)} %collective-permute-done.38.refs_8_), channel_id=1, source_target_pairs={{0,1},{1,0},{2,3},{3,2},{4,5},{5,4},{6,7},{7,6},{8,9},{9,8},{10,11... | collective-permute-start | bytes 786440 | tf_op jit(solution)/shard_map/ppermute | solution.py:32
  154.9 4.6 %collective-permute-start.43 = (bf16[2,256,256]{2,1,0:T(8,128)(2,1)S(1)}, bf16[2,256,256]{2,1,0:T(8,128)(2,1)S(1)}, u32[]{:S(2)}, u32[]{:S(2)}) collective-permute-start(bf16[2,256,256]{2,1,0:T(8,128)(2,1)S(1)} %collective-permute-done.39.refs_10_), channel_id=1, source_target_pairs={{0,1},{1,0},{2,3},{3,2},{4,5},{5,4},{6,7},{7,6},{8,9},{9,8},{10,11... | collective-permute-start | bytes 786440 | tf_op jit(solution)/shard_map/ppermute | solution.py:32
  159.6 17.0 %collective-permute-start.46 = (bf16[2,256,256]{2,1,0:T(8,128)(2,1)S(1)}, bf16[2,256,256]{2,1,0:T(8,128)(2,1)S(1)}, u32[]{:S(2)}, u32[]{:S(2)}) collective-permute-start(bf16[2,256,256]{2,1,0:T(8,128)(2,1)S(1)} %get-tuple-element.131), channel_id=1, source_target_pairs={{0,2},{1,3},{2,0},{3,1},{4,6},{5,7},{6,4},{7,5},{8,10},{9,11},{10,... | collective-permute-start | bytes 786440 | tf_op jit(solution)/shard_map/ppermute | solution.py:32
  161.4 15.2 %collective-permute-start.47 = (bf16[2,256,256]{2,1,0:T(8,128)(2,1)S(1)}, bf16[2,256,256]{2,1,0:T(8,128)(2,1)S(1)}, u32[]{:S(2)}, u32[]{:S(2)}) collective-permute-start(bf16[2,256,256]{2,1,0:T(8,128)(2,1)S(1)} %get-tuple-element.132), channel_id=1, source_target_pairs={{0,4},{1,5},{2,6},{3,7},{4,0},{5,1},{6,2},{7,3},{8,12},{9,13},{10,... | collective-permute-start | bytes 786440 | tf_op jit(solution)/shard_map/ppermute | solution.py:32
  161.7 14.9 %collective-permute-start.48 = (bf16[2,256,256]{2,1,0:T(8,128)(2,1)S(1)}, bf16[2,256,256]{2,1,0:T(8,128)(2,1)S(1)}, u32[]{:S(2)}, u32[]{:S(2)}) collective-permute-start(bf16[2,256,256]{2,1,0:T(8,128)(2,1)S(1)} %get-tuple-element.133), channel_id=1, source_target_pairs={{0,6},{1,7},{2,4},{3,5},{4,2},{5,3},{6,0},{7,1},{8,14},{9,15},{10,... | collective-permute-start | bytes 786440 | tf_op jit(solution)/shard_map/ppermute | solution.py:32
  181.2 8.4 %collective-permute-start.54 = (bf16[2,256,256]{2,1,0:T(8,128)(2,1)S(1)}, bf16[2,256,256]{2,1,0:T(8,128)(2,1)S(1)}, u32[]{:S(2)}, u32[]{:S(2)}) collective-permute-start(bf16[2,256,256]{2,1,0:T(8,128)(2,1)S(1)} %pad_maximum_fusion.2), channel_id=1, source_target_pairs={{0,4},{1,5},{2,6},{3,7},{4,0},{5,1},{6,2},{7,3},{8,12},{9,13},{10,... | collective-permute-start | bytes 786440 | tf_op jit(solution)/shard_map/ppermute | solution.py:32
  182.9 8.1 %collective-permute-start.51 = (bf16[2,256,256]{2,1,0:T(8,128)(2,1)S(1)}, bf16[2,256,256]{2,1,0:T(8,128)(2,1)S(1)}, u32[]{:S(2)}, u32[]{:S(2)}) collective-permute-start(bf16[2,256,256]{2,1,0:T(8,128)(2,1)S(1)} %pad_maximum_fusion.1), channel_id=1, source_target_pairs={{0,2},{1,3},{2,0},{3,1},{4,6},{5,7},{6,4},{7,5},{8,10},{9,11},{10,... | collective-permute-start | bytes 786440 | tf_op jit(solution)/shard_map/ppermute | solution.py:32
  191.2 5.0 %collective-permute-start.52 = (bf16[1,256,256]{2,1,0:T(8,128)(2,1)S(1)}, bf16[1,256,256]{2,1,0:T(8,128)(2,1)S(1)}, u32[]{:S(2)}, u32[]{:S(2)}) collective-permute-start(bf16[1,256,256]{2,1,0:T(8,128)(2,1)S(1)} %get-tuple-element.150), channel_id=1, source_target_pairs={{0,4},{1,5},{2,6},{3,7},{4,0},{5,1},{6,2},{7,3},{8,12},{9,13},{10,... | collective-permute-start | bytes 393224 | tf_op jit(solution)/shard_map/ppermute | solution.py:32
  191.6 5.0 %collective-permute-start.55 = (bf16[1,256,256]{2,1,0:T(8,128)(2,1)S(1)}, bf16[1,256,256]{2,1,0:T(8,128)(2,1)S(1)}, u32[]{:S(2)}, u32[]{:S(2)}) collective-permute-start(bf16[1,256,256]{2,1,0:T(8,128)(2,1)S(1)} %get-tuple-element.151), channel_id=1, source_target_pairs={{0,2},{1,3},{2,0},{3,1},{4,6},{5,7},{6,4},{7,5},{8,10},{9,11},{10,... | collective-permute-start | bytes 393224 | tf_op jit(solution)/shard_map/ppermute | solution.py:32
  193.4 11.0 %collective-permute-start.49 = (bf16[256,256]{1,0:T(8,128)(2,1)S(1)}, bf16[256,256]{1,0:T(8,128)(2,1)S(1)}, u32[]{:S(2)}, u32[]{:S(2)}) collective-permute-start(bf16[256,256]{1,0:T(8,128)(2,1)S(1)} %fusion.18), channel_id=1, source_target_pairs={{0,16},{8,24},{16,0},{24,8},{1,17},{9,25},{17,1},{25,9},{2,18},{10... | collective-permute-start | bytes 393224 | tf_op jit(solution)/shard_map/ppermute | solution.py:32
  196.7 8.3 %collective-permute-start.53 = (bf16[256,256]{1,0:T(8,128)(2,1)S(1)}, bf16[256,256]{1,0:T(8,128)(2,1)S(1)}, u32[]{:S(2)}, u32[]{:S(2)}) collective-permute-start(bf16[256,256]{1,0:T(8,128)(2,1)S(1)} %get-tuple-element.148), channel_id=1, source_target_pairs={{0,8},{8,0},{16,24},{24,16},{1,9},{9,1},{17,25},{25,17},{2,10},{10... | collective-permute-start | bytes 393224 | tf_op jit(solution)/shard_map/ppermute | solution.py:32
  196.8 8.2 %collective-permute-start.56 = (bf16[256,256]{1,0:T(8,128)(2,1)S(1)}, bf16[256,256]{1,0:T(8,128)(2,1)S(1)}, u32[]{:S(2)}, u32[]{:S(2)}) collective-permute-start(bf16[256,256]{1,0:T(8,128)(2,1)S(1)} %get-tuple-element.149), channel_id=1, source_target_pairs={{0,24},{8,16},{16,8},{24,0},{1,25},{9,17},{17,9},{25,1},{2,26},{10... | collective-permute-start | bytes 393224 | tf_op jit(solution)/shard_map/ppermute | solution.py:32
  (51 other events, 321.9 us)
Sparse Core Ops, SparseCore 0:
  10.6 31.2 all-gather.1

commit v5 on v4

--- a/solution.py
+++ b/solution.py
@@ -119,11 +119,12 @@
             scores = scores + jnp.where(column < left, 0.0, -jnp.inf)
             before = top[rows, :]
             now = jnp.maximum(before, jnp.max(scores, axis=1, keepdims=True))
-            powered = jnp.exp2((scores - now[:, :1]) * EXPONENT)
+            spread = jnp.concatenate([now] * (slots // now.shape[1]), axis=1)
+            powered = jnp.exp2((scores - spread) * EXPONENT)
             fade = jnp.exp2((before - now) * EXPONENT)
             top[rows, :] = now
             mass[rows, :] = mass[rows, :] * fade + jnp.sum(powered, axis=1, keepdims=True)
-            mixed[rows, :] = mixed[rows, :] * fade[:, :1] + jnp.dot(
+            mixed[rows, :] = mixed[rows, :] * jnp.concatenate([fade] * heads, axis=1) + jnp.dot(
                 powered.astype(BF16), cache[0, 1], preferred_element_type=F32
             )
 
@@ -181,7 +182,7 @@
         outs[mask % 2][mask // 2] = value
 
 
-def expert_kernel(count, masks, stacked, ids, gain, gates, gate_weight, up_weight, down, *refs):
+def expert_kernel(count, masks, stacked, ids, gain, route, route_gate, weight, down, *refs):
     blocks = len(masks)
     pieces, (odd, even, normed, hidden, held, arrival) = refs[:-6], refs[-6:]
     me_x, me_y = ids[0], ids[1]
@@ -208,13 +209,21 @@
                 value = piece[...].astype(F32) * scale * gain[:, columns]
                 normed[place, columns] = value.astype(BF16)
 
-    gate = jnp.dot(normed[...], gate_weight[0], preferred_element_type=F32)
-    up = jnp.dot(normed[...], up_weight[0], preferred_element_type=F32)
+    gate = jnp.dot(normed[...], weight[0, 0], preferred_element_type=F32)
+    up = jnp.dot(normed[...], weight[1, 0], preferred_element_type=F32)
+    expert = me_y * pl.num_programs(0) + step
     value = gate / (1.0 + jnp.exp(-gate)) * up
     for block, mask in enumerate(masks):
         place = slice(block * rows, (block + 1) * rows)
         source = pl.ds(pl.multiple_of((me_x ^ mask) * rows, rows), rows)
-        hidden[step, place, :] = (value[place, :] * gates[0, source, :]).astype(BF16)
+        chosen = jnp.where(route[:, source] == expert, route_gate[:, source], 0.0)
+        factor = lax.dot_general(
+            chosen.astype(BF16),
+            jnp.ones((chosen.shape[0], value.shape[1]), BF16),
+            (((0,), (0,)), ((), ())),
+            preferred_element_type=F32,
+        )
+        hidden[step, place, :] = (value[place, :] * factor).astype(BF16)
 
     @pl.when(step == pl.num_programs(0) - 1)
     def _():
@@ -253,8 +262,6 @@
     groups = prompt_cache.shape[0]
     heads = width // HD
 
-    output_full = lax.all_gather(output_weight, "gx", axis=0, tiled=True)
-
     wide_tokens = tokens.astype(F32)
     squares = jnp.sum(wide_tokens * wide_tokens, axis=1, keepdims=True)
     for bit in range(gy_count.bit_length() - 1):
@@ -270,13 +277,9 @@
     moved = lax.ppermute(tokens, ("gx", "gy"), route)
     experts = gate_up_weight.shape[0]
     units = gate_up_weight.shape[3]
-    expert_ids = lax.axis_index("gy") * experts + jnp.arange(experts, dtype=jnp.int32)
-    hit = route_experts[None] == expert_ids[:, None, None]
-    gates = jnp.sum(jnp.where(hit, route_gates.astype(F32)[None], 0.0), axis=2)[:, :, None]
-    gate_weight, moved = lax.optimization_barrier((gate_up_weight[:, :, 0], moved))
+    output_full = lax.all_gather(output_weight, "gx", axis=0, tiled=True)
     far = gather_far(moved)
-    source, moved = lax.optimization_barrier((gate_up_weight, moved))
-    up_weight, gates, far = lax.optimization_barrier((source[:, :, 1], gates, far))
+    gate_up, far = lax.optimization_barrier((jnp.transpose(gate_up_weight, (2, 0, 1, 3)), far))
     pieces = gather_near(far)
     types = [F32] + [BF16] * (gx_count - 1)
     projected = pl.pallas_call(
@@ -292,6 +295,7 @@
         ids, attention_gain.reshape(1, depth), jnp.transpose(projection_weight, (1, 0, 2)), *pieces
     )
     query_terms, pair_terms = projected[:gx_count], projected[gx_count:]
+    parents, query_terms = lax.optimization_barrier((parents, query_terms))
     query_terms = [query_terms[0]] + [
         swap(query_terms[mask], "gx", mask) for mask in range(1, gx_count)
     ]
@@ -391,7 +395,7 @@
     blocks = [stream] + [swap(stream, "gx", mask) for mask in range(1, gx_count)]
     inputs = [one for turn, mask in enumerate(units_of[0]) for one in double_gy(blocks[mask], turn)]
     result = stream.astype(F32)
-    pending, waiting, last = [], [], None
+    waiting, last = [], None
     half = jax.ShapeDtypeStruct((gy_count // 2, 2, rows, width), BF16)
     for number, masks in enumerate(units_of):
         after = []
@@ -406,9 +410,9 @@
             in_specs=[
                 smem(),
                 pl.BlockSpec((1, depth), lambda expert: (0, 0)),
-                pl.BlockSpec((1, gx_count * rows, 1), lambda expert: (expert, 0, 0)),
-                pl.BlockSpec((1, depth, units), lambda expert: (expert, 0, 0)),
-                pl.BlockSpec((1, depth, units), lambda expert: (expert, 0, 0)),
+                vmem(),
+                vmem(),
+                pl.BlockSpec((2, 1, depth, units), lambda expert: (0, expert, 0, 0)),
                 pl.BlockSpec(memory_space=pl.ANY),
             ]
             + [vmem()] * len(inputs),
@@ -426,16 +430,19 @@
         )(
             ids,
             expert_gain.reshape(1, depth),
-            gates,
-            gate_weight,
-            up_weight,
+            route_experts.T,
+            route_gates.astype(F32).T,
+            gate_up,
             down_weight.reshape(experts * units, depth),
             *inputs,
         )
         odd, even, far, arrived = lax.optimization_barrier((odd, even, far, arrived))
         if waiting:
             total = sum([one.astype(F32) for one in arrived], waiting[0])
-            pending += list(zip(last, total))
+            for mask, one in zip(last, total):
+                if mask:
+                    one = swap(one.astype(BF16), "gx", mask).astype(F32)
+                result = result + one
         last = masks
         near = swap(odd, "gy", 1)
         inputs = [one for pieces in far for one in gather_near(pieces)]
@@ -443,11 +450,11 @@
         if after:
             waiting = [summed[0]] + [one.astype(BF16) for one in summed[1:]]
         else:
-            pending += [(mask, halve_gy(summed[:, turn], turn)) for turn, mask in enumerate(masks)]
-    for mask, total in pending:
+            totals, result = halve_gy([summed[:, turn] for turn in range(len(masks))], result)
+    for mask, one in zip(masks, totals):
         if mask:
-            total = swap(total.astype(BF16), "gx", mask).astype(F32)
-        result = result + total
+            one = swap(one.astype(BF16), "gx", mask).astype(F32)
+        result = result + one
     return (result.astype(BF16), compacted)
 
 
@@ -476,14 +483,21 @@
     return [held[mask] for mask in range(len(held))]
 
 
-def halve_gy(value, turn):
-    held = [(2 * place, value[place]) for place in range(value.shape[0])]
-    for bit in far_bits(turn):
-        mine = [(mask, one) for mask, one in held if not mask >> bit & 1]
-        sent = jnp.stack([one for mask, one in held if mask >> bit & 1]).astype(BF16)
-        got = swap(sent, "gy", 1 << bit).astype(F32)
-        held = [(mask, one + got[place]) for place, (mask, one) in enumerate(mine)]
-    return held[0][1]
+def halve_gy(values, early):
+    many = [[(2 * place, value[place]) for place in range(value.shape[0])] for value in values]
+    orders = [far_bits(turn % 2) for turn in range(len(values))]
+    for step in range(len(orders[0])):
+        sent = [
+            jnp.stack([one for mask, one in held if mask >> order[step] & 1]).astype(BF16)
+            for held, order in zip(many, orders)
+        ]
+        if step + 1 == len(orders[0]):
+            sent, early = lax.optimization_barrier((sent, early))
+        for turn, order in enumerate(orders):
+            got = swap(sent[turn], "gy", 1 << order[step]).astype(F32)
+            mine = [(mask, one) for mask, one in many[turn] if not mask >> order[step] & 1]
+            many[turn] = [(mask, one + got[place]) for place, (mask, one) in enumerate(mine)]
+    return [held[0][1] for held in many], early
 
 
 def solution(mesh):

time: 213 us -> 199 us (0.934)
  local copies, waits for them, and re-layouts: 24.6 us -> 11.8 us
  starting transfers between devices: 54.8 us -> 64.3 us
  Pallas kernels: 58.3 us -> 50.5 us
    optimization_barrier x2 -> x0, local copies, waits for them, and re-layouts: 9.88 us -> none  [the longest x1 7.91 us: per_device(): source, moved = lax.optimization_barrier((gate_up_weight, moved))]
    ppermute x56, starting transfers between devices: 53.2 us -> 62.7 us  [swap(): lax.ppermute(value, axis, [(one, one ^ mask) for one in range(count)])]
    pallas_call x1, Pallas kernels: 21 us -> 14.3 us  [per_device(): pl.pallas_call(lambda *refs: cache_kernel(requests, draft, heads, gx_coun...]
    squeeze x1 -> x0, local copies, waits for them, and re-layouts: 4.41 us -> none  [per_device(): source[:, :, 1]]
    unnamed x84 -> x90, local copies, waits for them, and re-layouts: 9.28 us -> 10.8 us
  transfers between devices with their start and end apart: 58 -> 58, of which waited for: 18 -> 21; matrix products, arithmetic and copies ran while one was open for 16% -> 10% of each run, Pallas kernels for 26% -> 24%
where the time goes in v5:
time: 199 us
  starting transfers between devices  64.3 us (32%)
  Pallas kernels  50.5 us (25%)
  waiting for transfers between devices  45.5 us (23%)
  between operations  14.8 us (7%)
  local copies, waits for them, and re-layouts  11.8 us (6%)
  other arithmetic  10.2 us (5%)
    ppermute x56, starting transfers between devices, swap(): lax.ppermute(value, axis, [(one, one ^ mask) for one in range(count)])  62.7 us
    ppermute x56, waiting for transfers between devices, swap(): lax.ppermute(value, axis, [(one, one ^ mask) for one in range(count)])  45.5 us
    pallas_call x2, Pallas kernels, per_device(): pl.pallas_call(lambda *refs: expert_kernel(gy_count, masks, number > 0, *...  26 us
    pallas_call x1, Pallas kernels, per_device(): pl.pallas_call(lambda *refs: cache_kernel(requests, draft, heads, gx_coun...  14.3 us
    unnamed x90, local copies, waits for them, and re-layouts  10.8 us
  transfers between devices with their start and end apart: 58, of which 21 were waited for; matrix products, arithmetic and copies ran while one was open for 10% of the time, Pallas kernels for 24%

profile of v5, /device:TPU:0, one launch (start us, length us, event | category | flops | bytes accessed | tf_op | source)
XLA Modules:
  0.0 198.7 jit_solution(3476430381332176911)
XLA Ops:
  7.2 1.6 collective-permute-start
  8.8 1.0 fusion
  12.7 4.5 %collective-permute-start.5 = (f32[256,1]{1,0:T(8,128)S(1)}, f32[256,1]{1,0:T(8,128)S(1)}, u32[]{:S(2)}, u32[]{:S(2)}) collective-permute-start(f32[256,1]{1,0:T(8,128)S(1)} %add.100), channel_id=1, source_target_pairs={{0,2},{1,3},{2,0},{3,1},{4,6},{5,7},{6,4},{7,5},{8,10},{9,11},{10,... | collective-permute-start | bytes 3080 | tf_op jit(solution)/shard_map/ppermute | solution.py:32
  17.2 6.9 %collective-permute-start.1 = (bf16[256,256]{1,0:T(8,128)(2,1)S(1)}, bf16[256,256]{1,0:T(8,128)(2,1)S(1)}, u32[]{:S(2)}, u32[]{:S(2)}) collective-permute-start(bf16[256,256]{1,0:T(8,128)(2,1)S(1)} %collective-permute-done.refs_3_), channel_id=1, source_target_pairs={{0,2},{1,3},{2,0},{3,1},{4,6},{5,7},{6,4},{7,5},{8,10},{9,11},{10,... | collective-permute-start | bytes 393224 | tf_op jit(solution)/shard_map/ppermute | solution.py:32
  24.1 1.5 collective-permute-start.3
  27.6 7.9 %copy.30 = bf16[4,2048,2,256]{3,1,0,2:T(8,128)(2,1)} copy(bf16[4,2048,2,256]{3,2,1,0:T(2,128)(2,1)} %param.24) | data formatting | bytes 16777216 | tf_op args[10]
  39.0 3.6 %project.1 = (f32[256,256]{1,0:T(8,128)}, bf16[256,256]{1,0:T(8,128)(2,1)}, bf16[256,256]{1,0:T(8,128)(2,1)}, bf16[256,256]{1,0:T(8,128)(2,1)}, f32[2,256,256]{2...) custom-call(s32[2]{0:T(128)} %pad_add_fusion.refs_0_, ...), custom_call_target="tpu_custom_call" | custom-call | tf_op jit(solution)/shard_map/project/pallas_call | solution.py:285
  42.6 1.2 collective-permute-start.14
  43.8 4.5 %collective-permute-start.15 = (bf16[256,256]{1,0:T(8,128)(2,1)}, bf16[256,256]{1,0:T(8,128)(2,1)S(1)}, u32[]{:S(2)}, u32[]{:S(2)}) collective-permute-start(bf16[256,256]{1,0:T(8,128)(2,1)} %get-tuple-element.90), channel_id=1, source_target_pairs={{0,16},{8,24},{16,0},{24,8},{1,17},{9,25},{17,1},{25,9},{2,18},{10... | collective-permute-start | bytes 393224 | tf_op jit(solution)/shard_map/ppermute | solution.py:32
  48.8 3.8 %collective-permute-start.12 = (bf16[2,256,256]{2,1,0:T(8,128)(2,1)}, bf16[2,256,256]{2,1,0:T(8,128)(2,1)S(1)}, u32[]{:S(2)}, u32[]{:S(2)}) collective-permute-start(bf16[2,256,256]{2,1,0:T(8,128)(2,1)} %get-tuple-element.82), channel_id=1, source_target_pairs={{0,16},{8,24},{16,0},{24,8},{1,17},{9,25},{17,1},{25,9},{2,18},{10... | collective-permute-start | bytes 786440 | tf_op jit(solution)/shard_map/ppermute | solution.py:32
  53.4 1.0 convolution_minimum_fusion.refs_7_
  54.4 1.0 collective-permute-start.13
  55.4 3.0 %collective-permute-done.15.refs_7_ = bf16[256,256]{1,0:T(8,128)(2,1)S(1)} collective-permute-done((bf16[256,256]{1,0:T(8,128)(2,1)}, bf16[256,256]{1,0:T(8,128)(2,1)S(1)}, u32[]{:S(2)}, u32[]{:S(2)}) %collective-permute-start.15) | collective-permute-done | bytes 131104 | tf_op jit(solution)/shard_map/ppermute | solution.py:32
  59.1 14.3 %cache.1 = (f32[512,128]{1,0:T(8,128)}, f32[512,128]{1,0:T(8,128)}, f32[512,256]{1,0:T(8,128)}, bf16[256,256]{1,0:T(8,128)(2,1)}) custom-call(s32[2]{0:T(128)} %refs_0_.1, s32[2]{0:T(128)} %get-tuple-element.155.refs_1_, s32[2]{0:T(128)} %get-tuple-element.154.refs_2_, s32[4]{0:T(128)} %convert_reduce_fusion.refs_3_.refs_0_, ...), custom_call_target="tpu_custom_call" | custom-call | flops 10737418240 | bytes 16777216 | tf_op jit(solution)/shard_map/cache/pallas_call | solution.py:320
  73.4 4.6 %collective-permute-done.12.refs_4_ = bf16[2,256,256]{2,1,0:T(8,128)(2,1)S(1)} collective-permute-done((bf16[2,256,256]{2,1,0:T(8,128)(2,1)}, bf16[2,256,256]{2,1,0:T(8,128)(2,1)S(1)}, u32[]{:S(2)}, u32[]{:S(2)}) %collective-permute-start.12) | collective-permute-done | bytes 262176 | tf_op jit(solution)/shard_map/ppermute | solution.py:32
  78.9 3.8 %draft.1 = (bf16[256,256]{1,0:T(8,128)(2,1)}, bf16[2,32,256]{2,1,0:T(8,128)(2,1)}) custom-call(s32[4]{0:T(128)} %convert_reduce_fusion.refs_3_.refs_0_, f32[256,1]{1,0:T(8,128)} %add_rsqrt_fusion.refs_4_.refs_1_, f32[2,256,256]{2,1,0:T(8,128)} %get-tuple-element.80.refs_2_, bf16[2,256,256]{2,1,0:T(8,128)(2,1)} %copy-done.4, bf16[2,256,256]{2,1,0:T(8,128)(2,1)} %copy-done.5, ...), custom_call_target="tpu_custom_call" | custom-call | tf_op jit(solution)/shard_map/draft/pallas_call | solution.py:361
  82.7 2.8 %output.1 = (bf16[4,256,256]{2,1,0:T(8,128)(2,1)}, bf16[4,256,256]{2,1,0:T(8,128)(2,1)}) custom-call(s32[2]{0:T(128)} %pad_add_fusion.refs_0_, bf16[256,256]{1,0:T(8,128)(2,1)} %get-tuple-element.97.refs_1_, bf16[2048,256]{1,0:T(8,128)(2,1)} %all-gather.2.cloned.1.call-done.refs_2_), custom_call_target="tpu_custom_call" | custom-call | tf_op jit(solution)/shard_map/output/pallas_call | solution.py:379
  85.5 2.1 %collective-permute-done.17 = bf16[4,256,256]{2,1,0:T(8,128)(2,1)S(1)} collective-permute-done((bf16[4,256,256]{2,1,0:T(8,128)(2,1)}, bf16[4,256,256]{2,1,0:T(8,128)(2,1)S(1)}, u32[]{:S(2)}, u32[]{:S(2)}) %collective-permute-start.17) | collective-permute-done | bytes 524320 | tf_op jit(solution)/shard_map/ppermute | solution.py:32
  87.6 1.2 fusion.36
  89.8 2.6 %collective-permute-start.20 = (bf16[256,256]{1,0:T(8,128)(2,1)S(1)}, bf16[256,256]{1,0:T(8,128)(2,1)S(1)}, u32[]{:S(2)}, u32[]{:S(2)}) collective-permute-start(bf16[256,256]{1,0:T(8,128)(2,1)S(1)} %get-tuple-element.174), channel_id=1, source_target_pairs={{0,6},{1,7},{2,4},{3,5},{4,2},{5,3},{6,0},{7,1},{8,14},{9,15},{10,... | collective-permute-start | bytes 393224 | tf_op jit(solution)/shard_map/ppermute | solution.py:32
  92.4 2.9 %collective-permute-done.18 = bf16[256,256]{1,0:T(8,128)(2,1)S(1)} collective-permute-done((bf16[256,256]{1,0:T(8,128)(2,1)S(1)}, bf16[256,256]{1,0:T(8,128)(2,1)S(1)}, u32[]{:S(2)}, u32[]{:S(2)}) %collective-permute-start.18) | collective-permute-done | bytes 131104 | tf_op jit(solution)/shard_map/ppermute | solution.py:32
  95.2 2.1 %collective-permute-done.19 = bf16[256,256]{1,0:T(8,128)(2,1)S(1)} collective-permute-done((bf16[256,256]{1,0:T(8,128)(2,1)S(1)}, bf16[256,256]{1,0:T(8,128)(2,1)S(1)}, u32[]{:S(2)}, u32[]{:S(2)}) %collective-permute-start.19) | collective-permute-done | bytes 131104 | tf_op jit(solution)/shard_map/ppermute | solution.py:32
  97.4 6.1 %collective-permute-start.36 = (bf16[256,256]{1,0:T(8,128)(2,1)S(1)}, bf16[256,256]{1,0:T(8,128)(2,1)S(1)}, u32[]{:S(2)}, u32[]{:S(2)}) collective-permute-start(bf16[256,256]{1,0:T(8,128)(2,1)S(1)} %fusion.4.refs_6_), channel_id=1, source_target_pairs={{0,8},{8,0},{16,24},{24,16},{1,9},{9,1},{17,25},{25,17},{2,10},{10... | collective-permute-start | bytes 393224 | tf_op jit(solution)/shard_map/ppermute | solution.py:32
  104.2 1.7 collective-permute-start.22
  105.9 1.8 collective-permute-start.37
  108.0 7.2 %collective-permute-done.28.refs_14_ = bf16[256,256]{1,0:T(8,128)(2,1)S(1)} collective-permute-done((bf16[256,256]{1,0:T(8,128)(2,1)S(1)}, bf16[256,256]{1,0:T(8,128)(2,1)S(1)}, u32[]{:S(2)}, u32[]{:S(2)}) %collective-permute-start.28) | collective-permute-done | bytes 131104 | tf_op jit(solution)/shard_map/ppermute | solution.py:32
  115.1 2.0 collective-permute-start.32
  117.2 2.0 %collective-permute-start.30 = (bf16[256,256]{1,0:T(8,128)(2,1)S(1)}, bf16[256,256]{1,0:T(8,128)(2,1)S(1)}, u32[]{:S(2)}, u32[]{:S(2)}) collective-permute-start(bf16[256,256]{1,0:T(8,128)(2,1)S(1)} %collective-permute-done.28.refs_14_), channel_id=1, source_target_pairs={{0,2},{1,3},{2,0},{3,1},{4,6},{5,7},{6,4},{7,5},{8,10},{9,11},{10,... | collective-permute-start | bytes 393224 | tf_op jit(solution)/shard_map/ppermute | solution.py:32
  120.1 2.0 %collective-permute-start.34 = (bf16[256,256]{1,0:T(8,128)(2,1)S(1)}, bf16[256,256]{1,0:T(8,128)(2,1)S(1)}, u32[]{:S(2)}, u32[]{:S(2)}) collective-permute-start(bf16[256,256]{1,0:T(8,128)(2,1)S(1)} %collective-permute-done.32.refs_18_), channel_id=1, source_target_pairs={{0,2},{1,3},{2,0},{3,1},{4,6},{5,7},{6,4},{7,5},{8,10},{9,11},{10,... | collective-permute-start | bytes 393224 | tf_op jit(solution)/shard_map/ppermute | solution.py:32
  123.6 1.6 collective-permute-done.34.refs_20_
  126.5 1.9 collective-permute-start.38
  128.5 1.5 collective-permute-start.40
  130.2 13.0 %experts.2 = (bf16[4,2,256,256]{3,2,1,0:T(8,128)(2,1)}, bf16[4,2,256,256]{3,2,1,0:T(8,128)(2,1)}) custom-call(s32[2]{0:T(128)} %pad_add_fusion.refs_0_, f32[1,2048]{1,0:T(1,128)} %bitcast.104, s32[8,1024]{1,0:T(8,128)} %bitcast.102, f32[8,1024]{1,0:T(8,128)} %convert_bitcast_fusion.refs_3_, bf16[2,4,2048,256]{3,2,1,0:T(8,128)(2,1)} %bitcast.92, ...), custom_call_target="tpu_custom_call" | custom-call | flops 6442450944 | bytes 12582912 | tf_op jit(solution)/shard_map/experts/pallas_call | solution.py:407
  144.4 2.4 %collective-permute-done.45 = bf16[4,2,256,256]{3,2,1,0:T(8,128)(2,1)S(1)} collective-permute-done((bf16[4,2,256,256]{3,2,1,0:T(8,128)(2,1)}, bf16[4,2,256,256]{3,2,1,0:T(8,128)(2,1)S(1)}, u32[]{:S(2)}, u32[]{:S(2)}) %collective-permute-start.45) | collective-permute-done | bytes 1048608 | tf_op jit(solution)/shard_map/ppermute | solution.py:32
  146.8 1.5 fusion.37
  148.5 2.0 collective-permute-start.46
  150.6 1.5 collective-permute-start.48
  152.1 13.0 %experts.3 = (bf16[4,2,256,256]{3,2,1,0:T(8,128)(2,1)}, bf16[4,2,256,256]{3,2,1,0:T(8,128)(2,1)}) custom-call(s32[2]{0:T(128)} %pad_add_fusion.refs_0_, f32[1,2048]{1,0:T(1,128)} %bitcast.105, s32[8,1024]{1,0:T(8,128)} %bitcast.103, f32[8,1024]{1,0:T(8,128)} %convert_bitcast_fusion.refs_3_, bf16[2,4,2048,256]{3,2,1,0:T(8,128)(2,1)} %bitcast.93, ...), custom_call_target="tpu_custom_call" | custom-call | flops 6442450944 | bytes 12582912 | tf_op jit(solution)/shard_map/experts/pallas_call | solution.py:407
  166.0 2.1 %collective-permute-done.49 = bf16[4,2,256,256]{3,2,1,0:T(8,128)(2,1)S(1)} collective-permute-done((bf16[4,2,256,256]{3,2,1,0:T(8,128)(2,1)}, bf16[4,2,256,256]{3,2,1,0:T(8,128)(2,1)S(1)}, u32[]{:S(2)}, u32[]{:S(2)}) %collective-permute-start.49) | collective-permute-done | bytes 1048608 | tf_op jit(solution)/shard_map/ppermute | solution.py:32
  168.4 1.9 collective-permute-start.51
  170.6 4.0 %collective-permute-done.52 = bf16[256,256]{1,0:T(8,128)(2,1)S(1)} collective-permute-done((bf16[256,256]{1,0:T(8,128)(2,1)S(1)}, bf16[256,256]{1,0:T(8,128)(2,1)S(1)}, u32[]{:S(2)}, u32[]{:S(2)}) %collective-permute-start.52) | collective-permute-done | bytes 131104 | tf_op jit(solution)/shard_map/ppermute | solution.py:32
  174.6 2.3 %collective-permute-done.51 = bf16[2,256,256]{2,1,0:T(8,128)(2,1)S(1)} collective-permute-done((bf16[2,256,256]{2,1,0:T(8,128)(2,1)S(1)}, bf16[2,256,256]{2,1,0:T(8,128)(2,1)S(1)}, u32[]{:S(2)}, u32[]{:S(2)}) %collective-permute-start.51) | collective-permute-done | bytes 262176 | tf_op jit(solution)/shard_map/ppermute | solution.py:32
  177.0 1.5 collective-permute-done.50
  179.1 1.7 collective-permute-start.55
  180.8 2.9 %collective-permute-done.53 = bf16[1,256,256]{2,1,0:T(8,128)(2,1)S(1)} collective-permute-done((bf16[1,256,256]{2,1,0:T(8,128)(2,1)S(1)}, bf16[1,256,256]{2,1,0:T(8,128)(2,1)S(1)}, u32[]{:S(2)}, u32[]{:S(2)}) %collective-permute-start.53) | collective-permute-done | bytes 131104 | tf_op jit(solution)/shard_map/ppermute | solution.py:32
  184.2 2.0 collective-permute-start.56
  186.8 2.5 %collective-permute-done.54 = bf16[256,256]{1,0:T(8,128)(2,1)S(1)} collective-permute-done((bf16[256,256]{1,0:T(8,128)(2,1)S(1)}, bf16[256,256]{1,0:T(8,128)(2,1)S(1)}, u32[]{:S(2)}, u32[]{:S(2)}) %collective-permute-start.54) | collective-permute-done | bytes 131104 | tf_op jit(solution)/shard_map/ppermute | solution.py:32
  189.3 1.8 collective-permute-done.56
  (201 shorter events, 22.5 us)
Async XLA Ops:
  7.2 75.5 %all-gather.2.cloned.1.call-start = ((), (), s32[]{:S(2)}) async-start(), calls=%async_computation | async-start | bytes 1310720 | tf_op jit(solution)/shard_map/all_gather | solution.py:280
  7.2 10.0 %collective-permute-start = (bf16[256,256]{1,0:T(8,128)(2,1)}, bf16[256,256]{1,0:T(8,128)(2,1)S(1)}, u32[]{:S(2)}, u32[]{:S(2)}) collective-permute-start(bf16[256,256]{1,0:T(8,128)(2,1)} %param.14), channel_id=1, source_target_pairs={{0,0},{1,1},{2,8},{3,9},{4,16},{5,17},{6,24},{7,25},{8,2},{9,3},{1... | collective-permute-start | bytes 393224 | tf_op jit(solution)/shard_map/ppermute | solution.py:277
  12.7 13.6 %collective-permute-start.5 = (f32[256,1]{1,0:T(8,128)S(1)}, f32[256,1]{1,0:T(8,128)S(1)}, u32[]{:S(2)}, u32[]{:S(2)}) collective-permute-start(f32[256,1]{1,0:T(8,128)S(1)} %add.100), channel_id=1, source_target_pairs={{0,2},{1,3},{2,0},{3,1},{4,6},{5,7},{6,4},{7,5},{8,10},{9,11},{10,... | collective-permute-start | bytes 3080 | tf_op jit(solution)/shard_map/ppermute | solution.py:32
  17.2 19.0 %collective-permute-start.1 = (bf16[256,256]{1,0:T(8,128)(2,1)S(1)}, bf16[256,256]{1,0:T(8,128)(2,1)S(1)}, u32[]{:S(2)}, u32[]{:S(2)}) collective-permute-start(bf16[256,256]{1,0:T(8,128)(2,1)S(1)} %collective-permute-done.refs_3_), channel_id=1, source_target_pairs={{0,2},{1,3},{2,0},{3,1},{4,6},{5,7},{6,4},{7,5},{8,10},{9,11},{10,... | collective-permute-start | bytes 393224 | tf_op jit(solution)/shard_map/ppermute | solution.py:32
  24.1 12.1 %collective-permute-start.2 = (bf16[256,256]{1,0:T(8,128)(2,1)S(1)}, bf16[256,256]{1,0:T(8,128)(2,1)S(1)}, u32[]{:S(2)}, u32[]{:S(2)}) collective-permute-start(bf16[256,256]{1,0:T(8,128)(2,1)S(1)} %collective-permute-done.refs_3_), channel_id=1, source_target_pairs={{0,4},{1,5},{2,6},{3,7},{4,0},{5,1},{6,2},{7,3},{8,12},{9,13},{10,... | collective-permute-start | bytes 393224 | tf_op jit(solution)/shard_map/ppermute | solution.py:32
  24.1 12.1 %collective-permute-start.3 = (bf16[256,256]{1,0:T(8,128)(2,1)S(1)}, bf16[256,256]{1,0:T(8,128)(2,1)S(1)}, u32[]{:S(2)}, u32[]{:S(2)}) collective-permute-start(bf16[256,256]{1,0:T(8,128)(2,1)S(1)} %collective-permute-done.refs_3_), channel_id=1, source_target_pairs={{0,6},{1,7},{2,4},{3,5},{4,2},{5,3},{6,0},{7,1},{8,14},{9,15},{10,... | collective-permute-start | bytes 393224 | tf_op jit(solution)/shard_map/ppermute | solution.py:32
  26.3 11.0 %collective-permute-start.6 = (f32[256,1]{1,0:T(8,128)S(1)}, f32[256,1]{1,0:T(8,128)S(1)}, u32[]{:S(2)}, u32[]{:S(2)}) collective-permute-start(f32[256,1]{1,0:T(8,128)S(1)} %add.101), channel_id=1, source_target_pairs={{0,4},{1,5},{2,6},{3,7},{4,0},{5,1},{6,2},{7,3},{8,12},{9,13},{10,... | collective-permute-start | bytes 3080 | tf_op jit(solution)/shard_map/ppermute | solution.py:32
  42.6 11.8 %collective-permute-start.14 = (bf16[256,256]{1,0:T(8,128)(2,1)}, bf16[256,256]{1,0:T(8,128)(2,1)S(1)}, u32[]{:S(2)}, u32[]{:S(2)}) collective-permute-start(bf16[256,256]{1,0:T(8,128)(2,1)} %get-tuple-element.89), channel_id=1, source_target_pairs={{0,8},{8,0},{16,24},{24,16},{1,9},{9,1},{17,25},{25,17},{2,10},{10... | collective-permute-start | bytes 393224 | tf_op jit(solution)/shard_map/ppermute | solution.py:32
  43.8 14.7 %collective-permute-start.15 = (bf16[256,256]{1,0:T(8,128)(2,1)}, bf16[256,256]{1,0:T(8,128)(2,1)S(1)}, u32[]{:S(2)}, u32[]{:S(2)}) collective-permute-start(bf16[256,256]{1,0:T(8,128)(2,1)} %get-tuple-element.90), channel_id=1, source_target_pairs={{0,16},{8,24},{16,0},{24,8},{1,17},{9,25},{17,1},{25,9},{2,18},{10... | collective-permute-start | bytes 393224 | tf_op jit(solution)/shard_map/ppermute | solution.py:32
  48.3 10.2 %collective-permute-start.16 = (bf16[256,256]{1,0:T(8,128)(2,1)}, bf16[256,256]{1,0:T(8,128)(2,1)S(1)}, u32[]{:S(2)}, u32[]{:S(2)}) collective-permute-start(bf16[256,256]{1,0:T(8,128)(2,1)} %get-tuple-element.91), channel_id=1, source_target_pairs={{0,24},{8,16},{16,8},{24,0},{1,25},{9,17},{17,9},{25,1},{2,26},{10... | collective-permute-start | bytes 393224 | tf_op jit(solution)/shard_map/ppermute | solution.py:32
  48.3 25.2 %collective-permute-start.11 = (bf16[2,256,256]{2,1,0:T(8,128)(2,1)}, bf16[2,256,256]{2,1,0:T(8,128)(2,1)S(1)}, u32[]{:S(2)}, u32[]{:S(2)}) collective-permute-start(bf16[2,256,256]{2,1,0:T(8,128)(2,1)} %get-tuple-element.81), channel_id=1, source_target_pairs={{0,8},{8,0},{16,24},{24,16},{1,9},{9,1},{17,25},{25,17},{2,10},{10... | collective-permute-start | bytes 786440 | tf_op jit(solution)/shard_map/ppermute | solution.py:32
  48.8 29.3 %collective-permute-start.12 = (bf16[2,256,256]{2,1,0:T(8,128)(2,1)}, bf16[2,256,256]{2,1,0:T(8,128)(2,1)S(1)}, u32[]{:S(2)}, u32[]{:S(2)}) collective-permute-start(bf16[2,256,256]{2,1,0:T(8,128)(2,1)} %get-tuple-element.82), channel_id=1, source_target_pairs={{0,16},{8,24},{16,0},{24,8},{1,17},{9,25},{17,1},{25,9},{2,18},{10... | collective-permute-start | bytes 786440 | tf_op jit(solution)/shard_map/ppermute | solution.py:32
  54.4 23.7 %collective-permute-start.13 = (bf16[2,256,256]{2,1,0:T(8,128)(2,1)}, bf16[2,256,256]{2,1,0:T(8,128)(2,1)S(1)}, u32[]{:S(2)}, u32[]{:S(2)}) collective-permute-start(bf16[2,256,256]{2,1,0:T(8,128)(2,1)} %get-tuple-element.83), channel_id=1, source_target_pairs={{0,24},{8,16},{16,8},{24,0},{1,25},{9,17},{17,9},{25,1},{2,26},{10... | collective-permute-start | bytes 786440 | tf_op jit(solution)/shard_map/ppermute | solution.py:32
  88.8 6.4 %collective-permute-start.18 = (bf16[256,256]{1,0:T(8,128)(2,1)S(1)}, bf16[256,256]{1,0:T(8,128)(2,1)S(1)}, u32[]{:S(2)}, u32[]{:S(2)}) collective-permute-start(bf16[256,256]{1,0:T(8,128)(2,1)S(1)} %get-tuple-element.173), channel_id=1, source_target_pairs={{0,2},{1,3},{2,0},{3,1},{4,6},{5,7},{6,4},{7,5},{8,10},{9,11},{10,... | collective-permute-start | bytes 393224 | tf_op jit(solution)/shard_map/ppermute | solution.py:32
  89.0 8.3 %collective-permute-start.19 = (bf16[256,256]{1,0:T(8,128)(2,1)S(1)}, bf16[256,256]{1,0:T(8,128)(2,1)S(1)}, u32[]{:S(2)}, u32[]{:S(2)}) collective-permute-start(bf16[256,256]{1,0:T(8,128)(2,1)S(1)} %get-tuple-element.175), channel_id=1, source_target_pairs={{0,4},{1,5},{2,6},{3,7},{4,0},{5,1},{6,2},{7,3},{8,12},{9,13},{10,... | collective-permute-start | bytes 393224 | tf_op jit(solution)/shard_map/ppermute | solution.py:32
  89.8 7.5 %collective-permute-start.20 = (bf16[256,256]{1,0:T(8,128)(2,1)S(1)}, bf16[256,256]{1,0:T(8,128)(2,1)S(1)}, u32[]{:S(2)}, u32[]{:S(2)}) collective-permute-start(bf16[256,256]{1,0:T(8,128)(2,1)S(1)} %get-tuple-element.174), channel_id=1, source_target_pairs={{0,6},{1,7},{2,4},{3,5},{4,2},{5,3},{6,0},{7,1},{8,14},{9,15},{10,... | collective-permute-start | bytes 393224 | tf_op jit(solution)/shard_map/ppermute | solution.py:32
  97.4 10.5 %collective-permute-start.36 = (bf16[256,256]{1,0:T(8,128)(2,1)S(1)}, bf16[256,256]{1,0:T(8,128)(2,1)S(1)}, u32[]{:S(2)}, u32[]{:S(2)}) collective-permute-start(bf16[256,256]{1,0:T(8,128)(2,1)S(1)} %fusion.4.refs_6_), channel_id=1, source_target_pairs={{0,8},{8,0},{16,24},{24,16},{1,9},{9,1},{17,25},{25,17},{2,10},{10... | collective-permute-start | bytes 393224 | tf_op jit(solution)/shard_map/ppermute | solution.py:32
  103.6 11.6 %collective-permute-start.28 = (bf16[256,256]{1,0:T(8,128)(2,1)S(1)}, bf16[256,256]{1,0:T(8,128)(2,1)S(1)}, u32[]{:S(2)}, u32[]{:S(2)}) collective-permute-start(bf16[256,256]{1,0:T(8,128)(2,1)S(1)} %fusion.4.refs_6_), channel_id=1, source_target_pairs={{0,16},{8,24},{16,0},{24,8},{1,17},{9,25},{17,1},{25,9},{2,18},{10... | collective-permute-start | bytes 393224 | tf_op jit(solution)/shard_map/ppermute | solution.py:32
  104.2 12.8 %collective-permute-start.22 = (bf16[256,256]{1,0:T(8,128)(2,1)S(1)}, bf16[256,256]{1,0:T(8,128)(2,1)S(1)}, u32[]{:S(2)}, u32[]{:S(2)}) collective-permute-start(bf16[256,256]{1,0:T(8,128)(2,1)S(1)} %fusion.4.refs_6_), channel_id=1, source_target_pairs={{0,2},{1,3},{2,0},{3,1},{4,6},{5,7},{6,4},{7,5},{8,10},{9,11},{10,... | collective-permute-start | bytes 393224 | tf_op jit(solution)/shard_map/ppermute | solution.py:32
  105.9 11.3 %collective-permute-start.37 = (bf16[256,256]{1,0:T(8,128)(2,1)S(1)}, bf16[256,256]{1,0:T(8,128)(2,1)S(1)}, u32[]{:S(2)}, u32[]{:S(2)}) collective-permute-start(bf16[256,256]{1,0:T(8,128)(2,1)S(1)} %fusion.4.refs_6_), channel_id=1, source_target_pairs={{0,24},{8,16},{16,8},{24,0},{1,25},{9,17},{17,9},{25,1},{2,26},{10... | collective-permute-start | bytes 393224 | tf_op jit(solution)/shard_map/ppermute | solution.py:32
  107.7 11.5 %collective-permute-start.24 = (bf16[256,256]{1,0:T(8,128)(2,1)S(1)}, bf16[256,256]{1,0:T(8,128)(2,1)S(1)}, u32[]{:S(2)}, u32[]{:S(2)}) collective-permute-start(bf16[256,256]{1,0:T(8,128)(2,1)S(1)} %fusion.4.refs_6_), channel_id=1, source_target_pairs={{0,4},{1,5},{2,6},{3,7},{4,0},{5,1},{6,2},{7,3},{8,12},{9,13},{10,... | collective-permute-start | bytes 393224 | tf_op jit(solution)/shard_map/ppermute | solution.py:32
  108.0 11.2 %collective-permute-start.21 = (bf16[256,256]{1,0:T(8,128)(2,1)S(1)}, bf16[256,256]{1,0:T(8,128)(2,1)S(1)}, u32[]{:S(2)}, u32[]{:S(2)}) collective-permute-start(bf16[256,256]{1,0:T(8,128)(2,1)S(1)} %fusion.4.refs_6_), channel_id=1, source_target_pairs={{0,1},{1,0},{2,3},{3,2},{4,5},{5,4},{6,7},{7,6},{8,9},{9,8},{10,11... | collective-permute-start | bytes 393224 | tf_op jit(solution)/shard_map/ppermute | solution.py:32
  115.1 5.0 %collective-permute-start.32 = (bf16[256,256]{1,0:T(8,128)(2,1)S(1)}, bf16[256,256]{1,0:T(8,128)(2,1)S(1)}, u32[]{:S(2)}, u32[]{:S(2)}) collective-permute-start(bf16[256,256]{1,0:T(8,128)(2,1)S(1)} %collective-permute-done.28.refs_14_), channel_id=1, source_target_pairs={{0,4},{1,5},{2,6},{3,7},{4,0},{5,1},{6,2},{7,3},{8,12},{9,13},{10,... | collective-permute-start | bytes 393224 | tf_op jit(solution)/shard_map/ppermute | solution.py:32
  117.1 5.0 %collective-permute-start.26 = (bf16[256,256]{1,0:T(8,128)(2,1)S(1)}, bf16[256,256]{1,0:T(8,128)(2,1)S(1)}, u32[]{:S(2)}, u32[]{:S(2)}) collective-permute-start(bf16[256,256]{1,0:T(8,128)(2,1)S(1)} %collective-permute-done.22.refs_8_), channel_id=1, source_target_pairs={{0,4},{1,5},{2,6},{3,7},{4,0},{5,1},{6,2},{7,3},{8,12},{9,13},{10,... | collective-permute-start | bytes 393224 | tf_op jit(solution)/shard_map/ppermute | solution.py:32
  117.2 5.8 %collective-permute-start.30 = (bf16[256,256]{1,0:T(8,128)(2,1)S(1)}, bf16[256,256]{1,0:T(8,128)(2,1)S(1)}, u32[]{:S(2)}, u32[]{:S(2)}) collective-permute-start(bf16[256,256]{1,0:T(8,128)(2,1)S(1)} %collective-permute-done.28.refs_14_), channel_id=1, source_target_pairs={{0,2},{1,3},{2,0},{3,1},{4,6},{5,7},{6,4},{7,5},{8,10},{9,11},{10,... | collective-permute-start | bytes 393224 | tf_op jit(solution)/shard_map/ppermute | solution.py:32
  119.2 3.8 %collective-permute-start.23 = (bf16[256,256]{1,0:T(8,128)(2,1)S(1)}, bf16[256,256]{1,0:T(8,128)(2,1)S(1)}, u32[]{:S(2)}, u32[]{:S(2)}) collective-permute-start(bf16[256,256]{1,0:T(8,128)(2,1)S(1)} %collective-permute-done.22.refs_8_), channel_id=1, source_target_pairs={{0,1},{1,0},{2,3},{3,2},{4,5},{5,4},{6,7},{7,6},{8,9},{9,8},{10,11... | collective-permute-start | bytes 393224 | tf_op jit(solution)/shard_map/ppermute | solution.py:32
  119.2 4.3 %collective-permute-start.25 = (bf16[256,256]{1,0:T(8,128)(2,1)S(1)}, bf16[256,256]{1,0:T(8,128)(2,1)S(1)}, u32[]{:S(2)}, u32[]{:S(2)}) collective-permute-start(bf16[256,256]{1,0:T(8,128)(2,1)S(1)} %collective-permute-done.24.refs_10_), channel_id=1, source_target_pairs={{0,1},{1,0},{2,3},{3,2},{4,5},{5,4},{6,7},{7,6},{8,9},{9,8},{10,11... | collective-permute-start | bytes 393224 | tf_op jit(solution)/shard_map/ppermute | solution.py:32
  120.1 5.1 %collective-permute-start.34 = (bf16[256,256]{1,0:T(8,128)(2,1)S(1)}, bf16[256,256]{1,0:T(8,128)(2,1)S(1)}, u32[]{:S(2)}, u32[]{:S(2)}) collective-permute-start(bf16[256,256]{1,0:T(8,128)(2,1)S(1)} %collective-permute-done.32.refs_18_), channel_id=1, source_target_pairs={{0,2},{1,3},{2,0},{3,1},{4,6},{5,7},{6,4},{7,5},{8,10},{9,11},{10,... | collective-permute-start | bytes 393224 | tf_op jit(solution)/shard_map/ppermute | solution.py:32
  122.1 3.8 %collective-permute-start.29 = (bf16[256,256]{1,0:T(8,128)(2,1)S(1)}, bf16[256,256]{1,0:T(8,128)(2,1)S(1)}, u32[]{:S(2)}, u32[]{:S(2)}) collective-permute-start(bf16[256,256]{1,0:T(8,128)(2,1)S(1)} %collective-permute-done.28.refs_14_), channel_id=1, source_target_pairs={{0,1},{1,0},{2,3},{3,2},{4,5},{5,4},{6,7},{7,6},{8,9},{9,8},{10,11... | collective-permute-start | bytes 393224 | tf_op jit(solution)/shard_map/ppermute | solution.py:32
  123.0 3.0 %collective-permute-start.33 = (bf16[256,256]{1,0:T(8,128)(2,1)S(1)}, bf16[256,256]{1,0:T(8,128)(2,1)S(1)}, u32[]{:S(2)}, u32[]{:S(2)}) collective-permute-start(bf16[256,256]{1,0:T(8,128)(2,1)S(1)} %collective-permute-done.32.refs_18_), channel_id=1, source_target_pairs={{0,1},{1,0},{2,3},{3,2},{4,5},{5,4},{6,7},{7,6},{8,9},{9,8},{10,11... | collective-permute-start | bytes 393224 | tf_op jit(solution)/shard_map/ppermute | solution.py:32
  126.5 16.6 %collective-permute-start.38 = (bf16[2,256,256]{2,1,0:T(8,128)(2,1)S(1)}, bf16[2,256,256]{2,1,0:T(8,128)(2,1)S(1)}, u32[]{:S(2)}, u32[]{:S(2)}) collective-permute-start(bf16[2,256,256]{2,1,0:T(8,128)(2,1)S(1)} %pad_maximum_fusion.refs_6_), channel_id=1, source_target_pairs={{0,2},{1,3},{2,0},{3,1},{4,6},{5,7},{6,4},{7,5},{8,10},{9,11},{10,... | collective-permute-start | bytes 786440 | tf_op jit(solution)/shard_map/ppermute | solution.py:32
  128.4 14.8 %collective-permute-start.39 = (bf16[2,256,256]{2,1,0:T(8,128)(2,1)S(1)}, bf16[2,256,256]{2,1,0:T(8,128)(2,1)S(1)}, u32[]{:S(2)}, u32[]{:S(2)}) collective-permute-start(bf16[2,256,256]{2,1,0:T(8,128)(2,1)S(1)} %pad_maximum_fusion.refs_6_), channel_id=1, source_target_pairs={{0,4},{1,5},{2,6},{3,7},{4,0},{5,1},{6,2},{7,3},{8,12},{9,13},{10,... | collective-permute-start | bytes 786440 | tf_op jit(solution)/shard_map/ppermute | solution.py:32
  128.5 14.7 %collective-permute-start.40 = (bf16[2,256,256]{2,1,0:T(8,128)(2,1)S(1)}, bf16[2,256,256]{2,1,0:T(8,128)(2,1)S(1)}, u32[]{:S(2)}, u32[]{:S(2)}) collective-permute-start(bf16[2,256,256]{2,1,0:T(8,128)(2,1)S(1)} %pad_maximum_fusion.refs_6_), channel_id=1, source_target_pairs={{0,6},{1,7},{2,4},{3,5},{4,2},{5,3},{6,0},{7,1},{8,14},{9,15},{10,... | collective-permute-start | bytes 786440 | tf_op jit(solution)/shard_map/ppermute | solution.py:32
  143.2 3.6 %collective-permute-start.45 = (bf16[4,2,256,256]{3,2,1,0:T(8,128)(2,1)}, bf16[4,2,256,256]{3,2,1,0:T(8,128)(2,1)S(1)}, u32[]{:S(2)}, u32[]{:S(2)}) collective-permute-start(bf16[4,2,256,256]{3,2,1,0:T(8,128)(2,1)} %get-tuple-element.124), channel_id=1, source_target_pairs={{0,1},{1,0},{2,3},{3,2},{4,5},{5,4},{6,7},{7,6},{8,9},{9,8},{10,11... | collective-permute-start | bytes 3145736 | tf_op jit(solution)/shard_map/ppermute | solution.py:32
  143.3 5.1 %collective-permute-start.41 = (bf16[2,256,256]{2,1,0:T(8,128)(2,1)S(1)}, bf16[2,256,256]{2,1,0:T(8,128)(2,1)S(1)}, u32[]{:S(2)}, u32[]{:S(2)}) collective-permute-start(bf16[2,256,256]{2,1,0:T(8,128)(2,1)S(1)} %pad_maximum_fusion.refs_6_), channel_id=1, source_target_pairs={{0,1},{1,0},{2,3},{3,2},{4,5},{5,4},{6,7},{7,6},{8,9},{9,8},{10,11... | collective-permute-start | bytes 786440 | tf_op jit(solution)/shard_map/ppermute | solution.py:32
  143.8 4.7 %collective-permute-start.42 = (bf16[2,256,256]{2,1,0:T(8,128)(2,1)S(1)}, bf16[2,256,256]{2,1,0:T(8,128)(2,1)S(1)}, u32[]{:S(2)}, u32[]{:S(2)}) collective-permute-start(bf16[2,256,256]{2,1,0:T(8,128)(2,1)S(1)} %collective-permute-done.38.refs_8_), channel_id=1, source_target_pairs={{0,1},{1,0},{2,3},{3,2},{4,5},{5,4},{6,7},{7,6},{8,9},{9,8},{10,11... | collective-permute-start | bytes 786440 | tf_op jit(solution)/shard_map/ppermute | solution.py:32
  143.9 4.6 %collective-permute-start.43 = (bf16[2,256,256]{2,1,0:T(8,128)(2,1)S(1)}, bf16[2,256,256]{2,1,0:T(8,128)(2,1)S(1)}, u32[]{:S(2)}, u32[]{:S(2)}) collective-permute-start(bf16[2,256,256]{2,1,0:T(8,128)(2,1)S(1)} %collective-permute-done.39.refs_10_), channel_id=1, source_target_pairs={{0,1},{1,0},{2,3},{3,2},{4,5},{5,4},{6,7},{7,6},{8,9},{9,8},{10,11... | collective-permute-start | bytes 786440 | tf_op jit(solution)/shard_map/ppermute | solution.py:32
  144.3 4.2 %collective-permute-start.44 = (bf16[2,256,256]{2,1,0:T(8,128)(2,1)S(1)}, bf16[2,256,256]{2,1,0:T(8,128)(2,1)S(1)}, u32[]{:S(2)}, u32[]{:S(2)}) collective-permute-start(bf16[2,256,256]{2,1,0:T(8,128)(2,1)S(1)} %collective-permute-done.40.refs_12_), channel_id=1, source_target_pairs={{0,1},{1,0},{2,3},{3,2},{4,5},{5,4},{6,7},{7,6},{8,9},{9,8},{10,11... | collective-permute-start | bytes 786440 | tf_op jit(solution)/shard_map/ppermute | solution.py:32
  148.5 16.6 %collective-permute-start.46 = (bf16[2,256,256]{2,1,0:T(8,128)(2,1)S(1)}, bf16[2,256,256]{2,1,0:T(8,128)(2,1)S(1)}, u32[]{:S(2)}, u32[]{:S(2)}) collective-permute-start(bf16[2,256,256]{2,1,0:T(8,128)(2,1)S(1)} %get-tuple-element.135), channel_id=1, source_target_pairs={{0,2},{1,3},{2,0},{3,1},{4,6},{5,7},{6,4},{7,5},{8,10},{9,11},{10,... | collective-permute-start | bytes 786440 | tf_op jit(solution)/shard_map/ppermute | solution.py:32
  150.5 14.6 %collective-permute-start.47 = (bf16[2,256,256]{2,1,0:T(8,128)(2,1)S(1)}, bf16[2,256,256]{2,1,0:T(8,128)(2,1)S(1)}, u32[]{:S(2)}, u32[]{:S(2)}) collective-permute-start(bf16[2,256,256]{2,1,0:T(8,128)(2,1)S(1)} %get-tuple-element.136), channel_id=1, source_target_pairs={{0,4},{1,5},{2,6},{3,7},{4,0},{5,1},{6,2},{7,3},{8,12},{9,13},{10,... | collective-permute-start | bytes 786440 | tf_op jit(solution)/shard_map/ppermute | solution.py:32
  150.6 14.5 %collective-permute-start.48 = (bf16[2,256,256]{2,1,0:T(8,128)(2,1)S(1)}, bf16[2,256,256]{2,1,0:T(8,128)(2,1)S(1)}, u32[]{:S(2)}, u32[]{:S(2)}) collective-permute-start(bf16[2,256,256]{2,1,0:T(8,128)(2,1)S(1)} %get-tuple-element.137), channel_id=1, source_target_pairs={{0,6},{1,7},{2,4},{3,5},{4,2},{5,3},{6,0},{7,1},{8,14},{9,15},{10,... | collective-permute-start | bytes 786440 | tf_op jit(solution)/shard_map/ppermute | solution.py:32
  165.3 9.2 %collective-permute-start.52 = (bf16[256,256]{1,0:T(8,128)(2,1)S(1)}, bf16[256,256]{1,0:T(8,128)(2,1)S(1)}, u32[]{:S(2)}, u32[]{:S(2)}) collective-permute-start(bf16[256,256]{1,0:T(8,128)(2,1)S(1)} %fusion.15), channel_id=1, source_target_pairs={{0,16},{8,24},{16,0},{24,8},{1,17},{9,25},{17,1},{25,9},{2,18},{10... | collective-permute-start | bytes 393224 | tf_op jit(solution)/shard_map/ppermute | solution.py:32
  168.4 8.5 %collective-permute-start.51 = (bf16[2,256,256]{2,1,0:T(8,128)(2,1)S(1)}, bf16[2,256,256]{2,1,0:T(8,128)(2,1)S(1)}, u32[]{:S(2)}, u32[]{:S(2)}) collective-permute-start(bf16[2,256,256]{2,1,0:T(8,128)(2,1)S(1)} %pad_maximum_fusion.2), channel_id=1, source_target_pairs={{0,4},{1,5},{2,6},{3,7},{4,0},{5,1},{6,2},{7,3},{8,12},{9,13},{10,... | collective-permute-start | bytes 786440 | tf_op jit(solution)/shard_map/ppermute | solution.py:32
  170.4 8.1 %collective-permute-start.50 = (bf16[2,256,256]{2,1,0:T(8,128)(2,1)S(1)}, bf16[2,256,256]{2,1,0:T(8,128)(2,1)S(1)}, u32[]{:S(2)}, u32[]{:S(2)}) collective-permute-start(bf16[2,256,256]{2,1,0:T(8,128)(2,1)S(1)} %pad_maximum_fusion.1), channel_id=1, source_target_pairs={{0,2},{1,3},{2,0},{3,1},{4,6},{5,7},{6,4},{7,5},{8,10},{9,11},{10,... | collective-permute-start | bytes 786440 | tf_op jit(solution)/shard_map/ppermute | solution.py:32
  178.6 5.0 %collective-permute-start.53 = (bf16[1,256,256]{2,1,0:T(8,128)(2,1)S(1)}, bf16[1,256,256]{2,1,0:T(8,128)(2,1)S(1)}, u32[]{:S(2)}, u32[]{:S(2)}) collective-permute-start(bf16[1,256,256]{2,1,0:T(8,128)(2,1)S(1)} %get-tuple-element.145), channel_id=1, source_target_pairs={{0,4},{1,5},{2,6},{3,7},{4,0},{5,1},{6,2},{7,3},{8,12},{9,13},{10,... | collective-permute-start | bytes 393224 | tf_op jit(solution)/shard_map/ppermute | solution.py:32
  179.1 5.0 %collective-permute-start.55 = (bf16[1,256,256]{2,1,0:T(8,128)(2,1)S(1)}, bf16[1,256,256]{2,1,0:T(8,128)(2,1)S(1)}, u32[]{:S(2)}, u32[]{:S(2)}) collective-permute-start(bf16[1,256,256]{2,1,0:T(8,128)(2,1)S(1)} %get-tuple-element.146), channel_id=1, source_target_pairs={{0,2},{1,3},{2,0},{3,1},{4,6},{5,7},{6,4},{7,5},{8,10},{9,11},{10,... | collective-permute-start | bytes 393224 | tf_op jit(solution)/shard_map/ppermute | solution.py:32
  184.1 5.2 %collective-permute-start.54 = (bf16[256,256]{1,0:T(8,128)(2,1)S(1)}, bf16[256,256]{1,0:T(8,128)(2,1)S(1)}, u32[]{:S(2)}, u32[]{:S(2)}) collective-permute-start(bf16[256,256]{1,0:T(8,128)(2,1)S(1)} %get-tuple-element.156), channel_id=1, source_target_pairs={{0,8},{8,0},{16,24},{24,16},{1,9},{9,1},{17,25},{25,17},{2,10},{10... | collective-permute-start | bytes 393224 | tf_op jit(solution)/shard_map/ppermute | solution.py:32
  184.2 6.9 %collective-permute-start.56 = (bf16[256,256]{1,0:T(8,128)(2,1)S(1)}, bf16[256,256]{1,0:T(8,128)(2,1)S(1)}, u32[]{:S(2)}, u32[]{:S(2)}) collective-permute-start(bf16[256,256]{1,0:T(8,128)(2,1)S(1)} %get-tuple-element.157), channel_id=1, source_target_pairs={{0,24},{8,16},{16,8},{24,0},{1,25},{9,17},{17,9},{25,1},{2,26},{10... | collective-permute-start | bytes 393224 | tf_op jit(solution)/shard_map/ppermute | solution.py:32
  (54 other events, 344.1 us)
Sparse Core Ops, SparseCore 0:
  10.6 31.2 all-gather.1

commit v6 on v5

--- a/solution.py
+++ b/solution.py
@@ -129,9 +129,11 @@
             )
 
 
-def draft_kernel(requests, draft, heads, parts, place, scale_of, *refs):
+def draft_kernel(requests, draft, heads, parts, count, ids, place, scale_of, *refs):
     pairs = refs[:parts]
-    query, reach, rows, top, mass, mixed, attended, picked, key, value = refs[parts:]
+    query, reach, rows, top, mass, mixed, output = refs[parts : parts + 7]
+    even, odd, picked, key, value, attended = refs[parts + 7 :]
+    me = ids[1]
     for which, kept in ((0, key), (1, value)):
         total = pairs[0][which]
         for pair in pairs[1:]:
@@ -166,20 +168,16 @@
             attended[own, head * HD : (head + 1) * HD] = total[
                 head * draft : (head + 1) * draft, head * HD : (head + 1) * HD
             ]
-
-
-def output_kernel(count, ids, attended, output, *outs):
-    me = ids[1]
-    rows, width = outs[0].shape[-2:]
+    width = even.shape[-1]
     for mask in range(count):
-        place = pl.ds(pl.multiple_of((me ^ mask) * width, width), width)
+        columns = pl.ds(pl.multiple_of((me ^ mask) * width, width), width)
         value = lax.dot_general(
             attended[...],
-            output[place, :],
+            output[columns, :],
             (((1,), (1,)), ((), ())),
             preferred_element_type=F32,
         ).astype(BF16)
-        outs[mask % 2][mask // 2] = value
+        (odd if mask % 2 else even)[mask // 2] = value
 
 
 def expert_kernel(count, masks, stacked, ids, gain, route, route_gate, weight, down, *refs):
@@ -358,32 +356,33 @@
 
     accepted = accepted_path.shape[1]
     chosen = (jnp.arange(requests, dtype=jnp.int32)[:, None] * draft + accepted_path).reshape(-1, 1)
-    attended, picked = pl.pallas_call(
-        lambda *refs: draft_kernel(requests, draft, heads, gx_count, *refs),
+    half = jax.ShapeDtypeStruct((gy_count // 2, rows, width), BF16)
+    even, odd, picked = pl.pallas_call(
+        lambda *refs: draft_kernel(requests, draft, heads, gx_count, gy_count, *refs),
         out_shape=(
-            jax.ShapeDtypeStruct((rows, width), BF16),
+            half,
+            half,
             jax.ShapeDtypeStruct((2, requests * accepted, width), BF16),
         ),
-        in_specs=[smem()] + [vmem()] * (gx_count + 7),
-        out_specs=(vmem(), vmem()),
-        scratch_shapes=[
-            pltpu.VMEM((rows, width), BF16),
-            pltpu.VMEM((rows, width), BF16),
-        ],
+        in_specs=[smem(), smem()] + [vmem()] * (gx_count + 8),
+        out_specs=(vmem(), vmem(), vmem()),
+        scratch_shapes=[pltpu.VMEM((rows, width), BF16)] * 3,
         compiler_params=params(),
         name="draft",
-    )(place, row_scale, *pair_terms, query, ancestor_table(parents), chosen, top, mass, mixed)
+    )(
+        ids,
+        place,
+        row_scale,
+        *pair_terms,
+        query,
+        ancestor_table(parents),
+        chosen,
+        top,
+        mass,
+        mixed,
+        output_full,
+    )
     compacted = jnp.transpose(picked, (1, 0, 2))
-
-    half = jax.ShapeDtypeStruct((gy_count // 2, rows, width), BF16)
-    even, odd = pl.pallas_call(
-        lambda *refs: output_kernel(gy_count, *refs),
-        out_shape=(half, half),
-        in_specs=[smem(), vmem(), vmem()],
-        out_specs=(vmem(), vmem()),
-        compiler_params=params(),
-        name="output",
-    )(ids, attended, output_full)
 
     summed = even.astype(F32) + swap(odd, "gy", 1).astype(F32)
     stream = tokens.astype(F32) + summed[0]
@@ -392,8 +391,12 @@
     stream = stream.astype(BF16)
 
     units_of = [(one, one + 2) for one in range(gx_count) if not one & 2]
-    blocks = [stream] + [swap(stream, "gx", mask) for mask in range(1, gx_count)]
-    inputs = [one for turn, mask in enumerate(units_of[0]) for one in double_gy(blocks[mask], turn)]
+    blocks = {0: stream, units_of[0][1]: swap(stream, "gx", units_of[0][1])}
+    later, blocks[units_of[0][1]] = lax.optimization_barrier((stream, blocks[units_of[0][1]]))
+    for mask in range(gx_count):
+        if mask not in blocks:
+            blocks[mask] = swap(later, "gx", mask)
+    inputs = [one for mask in units_of[0] for one in gather_gy(blocks[mask])]
     result = stream.astype(F32)
     waiting, last = [], None
     half = jax.ShapeDtypeStruct((gy_count // 2, 2, rows, width), BF16)
@@ -475,14 +478,6 @@
     return bits[::-1] if turn else bits
 
 
-def double_gy(value, turn):
-    held = {0: value}
-    for bit in far_bits(turn):
-        held.update({mask | 1 << bit: swap(one, "gy", 1 << bit) for mask, one in held.items()})
-    held.update({mask | 1: swap(one, "gy", 1) for mask, one in held.items()})
-    return [held[mask] for mask in range(len(held))]
-
-
 def halve_gy(values, early):
     many = [[(2 * place, value[place]) for place in range(value.shape[0])] for value in values]
     orders = [far_bits(turn % 2) for turn in range(len(values))]

time: 199 us -> 193 us (0.970)
  waiting for transfers between devices: 45.5 us -> 39.2 us
    ppermute x56, waiting for transfers between devices: 45.5 us -> 39.1 us  [swap(): lax.ppermute(value, axis, [(one, one ^ mask) for one in range(count)])]
    pallas_call x1, Pallas kernels: 14.3 us -> 17.6 us  [per_device(): pl.pallas_call(lambda *refs: cache_kernel(requests, draft, heads, gx_coun...]
    pallas_call x1 -> x0, Pallas kernels: 2.78 us -> none  [per_device(): pl.pallas_call(lambda *refs: output_kernel(gy_count, *refs), out_shape=(h...]
  transfers between devices with their start and end apart: 58 -> 58, of which waited for: 21 -> 25; matrix products, arithmetic and copies ran while one was open for 10% -> 10% of each run, Pallas kernels for 24% -> 24%
where the time goes in v6:
time: 193 us; the launch traced here: 192 us
  starting transfers between devices  63 us (33%)
  Pallas kernels  51.7 us (27%)
  waiting for transfers between devices  39.2 us (20%)
  between operations  14.7 us (8%)
  local copies, waits for them, and re-layouts  11.8 us (6%)
  other arithmetic  10.2 us (5%)
    ppermute x56, starting transfers between devices, swap(): lax.ppermute(value, axis, [(one, one ^ mask) for one in range(count)])  61.4 us
    ppermute x56, waiting for transfers between devices, swap(): lax.ppermute(value, axis, [(one, one ^ mask) for one in range(count)])  39.1 us
    pallas_call x2, Pallas kernels, per_device(): pl.pallas_call(lambda *refs: expert_kernel(gy_count, masks, number > 0, *...  25.9 us
    pallas_call x1, Pallas kernels, per_device(): pl.pallas_call(lambda *refs: cache_kernel(requests, draft, heads, gx_coun...  17.6 us
    unnamed x90, local copies, waits for them, and re-layouts  10.8 us
    pallas_call x1, Pallas kernels, per_device(): pl.pallas_call(lambda *refs: draft_kernel(requests, draft, heads, gx_coun...  4.61 us
  transfers between devices with their start and end apart: 58, of which 25 were waited for; matrix products, arithmetic and copies ran while one was open for 10% of the time, Pallas kernels for 24%

profile of v6, /device:TPU:0, one launch (start us, length us, event | category | flops | bytes accessed | tf_op | source)
XLA Modules:
  0.0 192.3 jit_solution(1516233946016061694)
XLA Ops:
  7.2 1.6 collective-permute-start
  12.7 4.5 %collective-permute-start.5 = (f32[256,1]{1,0:T(8,128)S(1)}, f32[256,1]{1,0:T(8,128)S(1)}, u32[]{:S(2)}, u32[]{:S(2)}) collective-permute-start(f32[256,1]{1,0:T(8,128)S(1)} %add.100), channel_id=1, source_target_pairs={{0,2},{1,3},{2,0},{3,1},{4,6},{5,7},{6,4},{7,5},{8,10},{9,11},{10,... | collective-permute-start | bytes 3080 | tf_op jit(solution)/shard_map/ppermute | solution.py:32
  17.2 6.9 %collective-permute-start.1 = (bf16[256,256]{1,0:T(8,128)(2,1)S(1)}, bf16[256,256]{1,0:T(8,128)(2,1)S(1)}, u32[]{:S(2)}, u32[]{:S(2)}) collective-permute-start(bf16[256,256]{1,0:T(8,128)(2,1)S(1)} %collective-permute-done.refs_3_), channel_id=1, source_target_pairs={{0,2},{1,3},{2,0},{3,1},{4,6},{5,7},{6,4},{7,5},{8,10},{9,11},{10,... | collective-permute-start | bytes 393224 | tf_op jit(solution)/shard_map/ppermute | solution.py:32
  24.1 1.5 collective-permute-start.3
  27.6 7.9 %copy.30 = bf16[4,2048,2,256]{3,1,0,2:T(8,128)(2,1)} copy(bf16[4,2048,2,256]{3,2,1,0:T(2,128)(2,1)} %param.24) | data formatting | bytes 16777216 | tf_op args[10]
  39.0 3.6 %project.1 = (f32[256,256]{1,0:T(8,128)}, bf16[256,256]{1,0:T(8,128)(2,1)}, bf16[256,256]{1,0:T(8,128)(2,1)}, bf16[256,256]{1,0:T(8,128)(2,1)}, f32[2,256,256]{2...) custom-call(s32[2]{0:T(128)} %pad_add_fusion.refs_0_, ...), custom_call_target="tpu_custom_call" | custom-call | tf_op jit(solution)/shard_map/project/pallas_call | solution.py:283
  42.6 1.2 collective-permute-start.14
  43.8 4.5 %collective-permute-start.15 = (bf16[256,256]{1,0:T(8,128)(2,1)}, bf16[256,256]{1,0:T(8,128)(2,1)S(1)}, u32[]{:S(2)}, u32[]{:S(2)}) collective-permute-start(bf16[256,256]{1,0:T(8,128)(2,1)} %get-tuple-element.91), channel_id=1, source_target_pairs={{0,16},{8,24},{16,0},{24,8},{1,17},{9,25},{17,1},{25,9},{2,18},{10... | collective-permute-start | bytes 393224 | tf_op jit(solution)/shard_map/ppermute | solution.py:32
  48.8 3.8 %collective-permute-start.12 = (bf16[2,256,256]{2,1,0:T(8,128)(2,1)}, bf16[2,256,256]{2,1,0:T(8,128)(2,1)S(1)}, u32[]{:S(2)}, u32[]{:S(2)}) collective-permute-start(bf16[2,256,256]{2,1,0:T(8,128)(2,1)} %get-tuple-element.83), channel_id=1, source_target_pairs={{0,16},{8,24},{16,0},{24,8},{1,17},{9,25},{17,1},{25,9},{2,18},{10... | collective-permute-start | bytes 786440 | tf_op jit(solution)/shard_map/ppermute | solution.py:32
  55.4 3.0 %collective-permute-done.15.refs_7_ = bf16[256,256]{1,0:T(8,128)(2,1)S(1)} collective-permute-done((bf16[256,256]{1,0:T(8,128)(2,1)}, bf16[256,256]{1,0:T(8,128)(2,1)S(1)}, u32[]{:S(2)}, u32[]{:S(2)}) %collective-permute-start.15) | collective-permute-done | bytes 131104 | tf_op jit(solution)/shard_map/ppermute | solution.py:32
  59.1 17.6 %cache.1 = (f32[512,128]{1,0:T(8,128)}, f32[512,128]{1,0:T(8,128)}, f32[512,256]{1,0:T(8,128)}, bf16[256,256]{1,0:T(8,128)(2,1)}) custom-call(s32[2]{0:T(128)} %refs_0_.1, s32[2]{0:T(128)} %get-tuple-element.157.refs_1_, s32[2]{0:T(128)} %get-tuple-element.156.refs_2_, s32[4]{0:T(128)} %convert_reduce_fusion.refs_3_.refs_1_, ...), custom_call_target="tpu_custom_call" | custom-call | flops 10737418240 | bytes 16777216 | tf_op jit(solution)/shard_map/cache/pallas_call | solution.py:318
  76.7 1.4 collective-permute-done.12.refs_5_
  78.9 4.6 %draft.1 = (bf16[4,256,256]{2,1,0:T(8,128)(2,1)}, bf16[4,256,256]{2,1,0:T(8,128)(2,1)}, bf16[2,32,256]{2,1,0:T(8,128)(2,1)}) custom-call(s32[2]{0:T(128)} %pad_add_fusion.refs_0_, s32[4]{0:T(128)} %convert_reduce_fusion.refs_3_.refs_1_, f32[256,1]{1,0:T(8,128)} %add_rsqrt_fusion.refs_4_.refs_2_, f32[2,256,256]{2,1,0:T(8,128)} %get-tuple-element.81.refs_3_, ...), custom_call_target="tpu_custom_call" | custom-call | tf_op jit(solution)/shard_map/draft/pallas_call | solution.py:360
  83.5 2.1 %collective-permute-done.17 = bf16[4,256,256]{2,1,0:T(8,128)(2,1)S(1)} collective-permute-done((bf16[4,256,256]{2,1,0:T(8,128)(2,1)}, bf16[4,256,256]{2,1,0:T(8,128)(2,1)S(1)}, u32[]{:S(2)}, u32[]{:S(2)}) %collective-permute-start.17) | collective-permute-done | bytes 524320 | tf_op jit(solution)/shard_map/ppermute | solution.py:32
  85.6 1.2 fusion.36
  87.8 2.6 %collective-permute-start.20 = (bf16[256,256]{1,0:T(8,128)(2,1)S(1)}, bf16[256,256]{1,0:T(8,128)(2,1)S(1)}, u32[]{:S(2)}, u32[]{:S(2)}) collective-permute-start(bf16[256,256]{1,0:T(8,128)(2,1)S(1)} %get-tuple-element.176), channel_id=1, source_target_pairs={{0,6},{1,7},{2,4},{3,5},{4,2},{5,3},{6,0},{7,1},{8,14},{9,15},{10,... | collective-permute-start | bytes 393224 | tf_op jit(solution)/shard_map/ppermute | solution.py:32
  90.4 2.9 %collective-permute-done.18 = bf16[256,256]{1,0:T(8,128)(2,1)S(1)} collective-permute-done((bf16[256,256]{1,0:T(8,128)(2,1)S(1)}, bf16[256,256]{1,0:T(8,128)(2,1)S(1)}, u32[]{:S(2)}, u32[]{:S(2)}) %collective-permute-start.18) | collective-permute-done | bytes 131104 | tf_op jit(solution)/shard_map/ppermute | solution.py:32
  93.3 2.1 %collective-permute-done.19 = bf16[256,256]{1,0:T(8,128)(2,1)S(1)} collective-permute-done((bf16[256,256]{1,0:T(8,128)(2,1)S(1)}, bf16[256,256]{1,0:T(8,128)(2,1)S(1)}, u32[]{:S(2)}, u32[]{:S(2)}) %collective-permute-start.19) | collective-permute-done | bytes 131104 | tf_op jit(solution)/shard_map/ppermute | solution.py:32
  95.5 6.6 %collective-permute-start.28 = (bf16[256,256]{1,0:T(8,128)(2,1)S(1)}, bf16[256,256]{1,0:T(8,128)(2,1)S(1)}, u32[]{:S(2)}, u32[]{:S(2)}) collective-permute-start(bf16[256,256]{1,0:T(8,128)(2,1)S(1)} %fusion.4.refs_6_), channel_id=1, source_target_pairs={{0,16},{8,24},{16,0},{24,8},{1,17},{9,25},{17,1},{25,9},{2,18},{10... | collective-permute-start | bytes 393224 | tf_op jit(solution)/shard_map/ppermute | solution.py:32
  102.0 1.7 collective-permute-start.22
  104.0 1.5 collective-permute-start.26
  105.5 1.7 collective-permute-done.28.refs_14_
  108.1 1.4 collective-permute-start.37
  110.5 1.2 collective-permute-start.30
  112.4 1.6 collective-permute-start.34
  115.5 1.2 collective-permute-done.32.refs_18_
  116.7 1.6 collective-permute-done.34.refs_20_
  120.1 1.1 collective-permute-start.38
  121.2 1.1 collective-permute-start.39
  122.3 1.4 collective-permute-start.40
  123.8 13.0 %experts.2 = (bf16[4,2,256,256]{3,2,1,0:T(8,128)(2,1)}, bf16[4,2,256,256]{3,2,1,0:T(8,128)(2,1)}) custom-call(s32[2]{0:T(128)} %pad_add_fusion.refs_0_, f32[1,2048]{1,0:T(1,128)} %bitcast.104, s32[8,1024]{1,0:T(8,128)} %bitcast.102, f32[8,1024]{1,0:T(8,128)} %convert_bitcast_fusion.refs_3_, bf16[2,4,2048,256]{3,2,1,0:T(8,128)(2,1)} %bitcast.92, ...), custom_call_target="tpu_custom_call" | custom-call | flops 6442450944 | bytes 12582912 | tf_op jit(solution)/shard_map/experts/pallas_call | solution.py:410
  138.0 2.4 %collective-permute-done.45 = bf16[4,2,256,256]{3,2,1,0:T(8,128)(2,1)S(1)} collective-permute-done((bf16[4,2,256,256]{3,2,1,0:T(8,128)(2,1)}, bf16[4,2,256,256]{3,2,1,0:T(8,128)(2,1)S(1)}, u32[]{:S(2)}, u32[]{:S(2)}) %collective-permute-start.45) | collective-permute-done | bytes 1048608 | tf_op jit(solution)/shard_map/ppermute | solution.py:32
  140.4 1.5 fusion.37
  142.1 1.1 collective-permute-start.46
  143.3 1.1 collective-permute-start.47
  144.3 1.3 collective-permute-start.48
  145.7 13.0 %experts.3 = (bf16[4,2,256,256]{3,2,1,0:T(8,128)(2,1)}, bf16[4,2,256,256]{3,2,1,0:T(8,128)(2,1)}) custom-call(s32[2]{0:T(128)} %pad_add_fusion.refs_0_, f32[1,2048]{1,0:T(1,128)} %bitcast.105, s32[8,1024]{1,0:T(8,128)} %bitcast.103, f32[8,1024]{1,0:T(8,128)} %convert_bitcast_fusion.refs_3_, bf16[2,4,2048,256]{3,2,1,0:T(8,128)(2,1)} %bitcast.93, ...), custom_call_target="tpu_custom_call" | custom-call | flops 6442450944 | bytes 12582912 | tf_op jit(solution)/shard_map/experts/pallas_call | solution.py:410
  158.9 1.1 collective-permute-start.52
  160.0 1.6 collective-permute-done.49
  162.0 1.4 collective-permute-start.51
  164.3 3.9 %collective-permute-done.52 = bf16[256,256]{1,0:T(8,128)(2,1)S(1)} collective-permute-done((bf16[256,256]{1,0:T(8,128)(2,1)S(1)}, bf16[256,256]{1,0:T(8,128)(2,1)S(1)}, u32[]{:S(2)}, u32[]{:S(2)}) %collective-permute-start.52) | collective-permute-done | bytes 131104 | tf_op jit(solution)/shard_map/ppermute | solution.py:32
  168.3 2.1 %collective-permute-done.51 = bf16[2,256,256]{2,1,0:T(8,128)(2,1)S(1)} collective-permute-done((bf16[2,256,256]{2,1,0:T(8,128)(2,1)S(1)}, bf16[2,256,256]{2,1,0:T(8,128)(2,1)S(1)}, u32[]{:S(2)}, u32[]{:S(2)}) %collective-permute-start.51) | collective-permute-done | bytes 262176 | tf_op jit(solution)/shard_map/ppermute | solution.py:32
  170.5 1.1 collective-permute-done.50
  172.5 1.1 collective-permute-start.55
  173.6 3.2 %collective-permute-done.53 = bf16[1,256,256]{2,1,0:T(8,128)(2,1)S(1)} collective-permute-done((bf16[1,256,256]{2,1,0:T(8,128)(2,1)S(1)}, bf16[1,256,256]{2,1,0:T(8,128)(2,1)S(1)}, u32[]{:S(2)}, u32[]{:S(2)}) %collective-permute-start.53) | collective-permute-done | bytes 131104 | tf_op jit(solution)/shard_map/ppermute | solution.py:32
  177.8 2.2 %collective-permute-start.56 = (bf16[256,256]{1,0:T(8,128)(2,1)S(1)}, bf16[256,256]{1,0:T(8,128)(2,1)S(1)}, u32[]{:S(2)}, u32[]{:S(2)}) collective-permute-start(bf16[256,256]{1,0:T(8,128)(2,1)S(1)} %get-tuple-element.159), channel_id=1, source_target_pairs={{0,24},{8,16},{16,8},{24,0},{1,25},{9,17},{17,9},{25,1},{2,26},{10... | collective-permute-start | bytes 393224 | tf_op jit(solution)/shard_map/ppermute | solution.py:32
  180.7 1.8 collective-permute-done.54
  182.6 2.1 %collective-permute-done.56 = bf16[256,256]{1,0:T(8,128)(2,1)S(1)} collective-permute-done((bf16[256,256]{1,0:T(8,128)(2,1)S(1)}, bf16[256,256]{1,0:T(8,128)(2,1)S(1)}, u32[]{:S(2)}, u32[]{:S(2)}) %collective-permute-start.56) | collective-permute-done | bytes 131104 | tf_op jit(solution)/shard_map/ppermute | solution.py:32
  (200 shorter events, 27.9 us)
Async XLA Ops:
  7.2 71.0 %all-gather.2.cloned.1.call-start = ((), (), s32[]{:S(2)}) async-start(), calls=%async_computation | async-start | bytes 1310720 | tf_op jit(solution)/shard_map/all_gather | solution.py:278
  7.2 10.0 %collective-permute-start = (bf16[256,256]{1,0:T(8,128)(2,1)}, bf16[256,256]{1,0:T(8,128)(2,1)S(1)}, u32[]{:S(2)}, u32[]{:S(2)}) collective-permute-start(bf16[256,256]{1,0:T(8,128)(2,1)} %param.14), channel_id=1, source_target_pairs={{0,0},{1,1},{2,8},{3,9},{4,16},{5,17},{6,24},{7,25},{8,2},{9,3},{1... | collective-permute-start | bytes 393224 | tf_op jit(solution)/shard_map/ppermute | solution.py:275
  12.7 13.6 %collective-permute-start.5 = (f32[256,1]{1,0:T(8,128)S(1)}, f32[256,1]{1,0:T(8,128)S(1)}, u32[]{:S(2)}, u32[]{:S(2)}) collective-permute-start(f32[256,1]{1,0:T(8,128)S(1)} %add.100), channel_id=1, source_target_pairs={{0,2},{1,3},{2,0},{3,1},{4,6},{5,7},{6,4},{7,5},{8,10},{9,11},{10,... | collective-permute-start | bytes 3080 | tf_op jit(solution)/shard_map/ppermute | solution.py:32
  17.2 19.0 %collective-permute-start.1 = (bf16[256,256]{1,0:T(8,128)(2,1)S(1)}, bf16[256,256]{1,0:T(8,128)(2,1)S(1)}, u32[]{:S(2)}, u32[]{:S(2)}) collective-permute-start(bf16[256,256]{1,0:T(8,128)(2,1)S(1)} %collective-permute-done.refs_3_), channel_id=1, source_target_pairs={{0,2},{1,3},{2,0},{3,1},{4,6},{5,7},{6,4},{7,5},{8,10},{9,11},{10,... | collective-permute-start | bytes 393224 | tf_op jit(solution)/shard_map/ppermute | solution.py:32
  24.1 12.1 %collective-permute-start.2 = (bf16[256,256]{1,0:T(8,128)(2,1)S(1)}, bf16[256,256]{1,0:T(8,128)(2,1)S(1)}, u32[]{:S(2)}, u32[]{:S(2)}) collective-permute-start(bf16[256,256]{1,0:T(8,128)(2,1)S(1)} %collective-permute-done.refs_3_), channel_id=1, source_target_pairs={{0,4},{1,5},{2,6},{3,7},{4,0},{5,1},{6,2},{7,3},{8,12},{9,13},{10,... | collective-permute-start | bytes 393224 | tf_op jit(solution)/shard_map/ppermute | solution.py:32
  24.1 12.1 %collective-permute-start.3 = (bf16[256,256]{1,0:T(8,128)(2,1)S(1)}, bf16[256,256]{1,0:T(8,128)(2,1)S(1)}, u32[]{:S(2)}, u32[]{:S(2)}) collective-permute-start(bf16[256,256]{1,0:T(8,128)(2,1)S(1)} %collective-permute-done.refs_3_), channel_id=1, source_target_pairs={{0,6},{1,7},{2,4},{3,5},{4,2},{5,3},{6,0},{7,1},{8,14},{9,15},{10,... | collective-permute-start | bytes 393224 | tf_op jit(solution)/shard_map/ppermute | solution.py:32
  26.3 11.0 %collective-permute-start.6 = (f32[256,1]{1,0:T(8,128)S(1)}, f32[256,1]{1,0:T(8,128)S(1)}, u32[]{:S(2)}, u32[]{:S(2)}) collective-permute-start(f32[256,1]{1,0:T(8,128)S(1)} %add.101), channel_id=1, source_target_pairs={{0,4},{1,5},{2,6},{3,7},{4,0},{5,1},{6,2},{7,3},{8,12},{9,13},{10,... | collective-permute-start | bytes 3080 | tf_op jit(solution)/shard_map/ppermute | solution.py:32
  42.6 11.8 %collective-permute-start.14 = (bf16[256,256]{1,0:T(8,128)(2,1)}, bf16[256,256]{1,0:T(8,128)(2,1)S(1)}, u32[]{:S(2)}, u32[]{:S(2)}) collective-permute-start(bf16[256,256]{1,0:T(8,128)(2,1)} %get-tuple-element.90), channel_id=1, source_target_pairs={{0,8},{8,0},{16,24},{24,16},{1,9},{9,1},{17,25},{25,17},{2,10},{10... | collective-permute-start | bytes 393224 | tf_op jit(solution)/shard_map/ppermute | solution.py:32
  43.8 14.7 %collective-permute-start.15 = (bf16[256,256]{1,0:T(8,128)(2,1)}, bf16[256,256]{1,0:T(8,128)(2,1)S(1)}, u32[]{:S(2)}, u32[]{:S(2)}) collective-permute-start(bf16[256,256]{1,0:T(8,128)(2,1)} %get-tuple-element.91), channel_id=1, source_target_pairs={{0,16},{8,24},{16,0},{24,8},{1,17},{9,25},{17,1},{25,9},{2,18},{10... | collective-permute-start | bytes 393224 | tf_op jit(solution)/shard_map/ppermute | solution.py:32
  48.3 10.2 %collective-permute-start.16 = (bf16[256,256]{1,0:T(8,128)(2,1)}, bf16[256,256]{1,0:T(8,128)(2,1)S(1)}, u32[]{:S(2)}, u32[]{:S(2)}) collective-permute-start(bf16[256,256]{1,0:T(8,128)(2,1)} %get-tuple-element.92), channel_id=1, source_target_pairs={{0,24},{8,16},{16,8},{24,0},{1,25},{9,17},{17,9},{25,1},{2,26},{10... | collective-permute-start | bytes 393224 | tf_op jit(solution)/shard_map/ppermute | solution.py:32
  48.3 28.4 %collective-permute-start.11 = (bf16[2,256,256]{2,1,0:T(8,128)(2,1)}, bf16[2,256,256]{2,1,0:T(8,128)(2,1)S(1)}, u32[]{:S(2)}, u32[]{:S(2)}) collective-permute-start(bf16[2,256,256]{2,1,0:T(8,128)(2,1)} %get-tuple-element.82), channel_id=1, source_target_pairs={{0,8},{8,0},{16,24},{24,16},{1,9},{9,1},{17,25},{25,17},{2,10},{10... | collective-permute-start | bytes 786440 | tf_op jit(solution)/shard_map/ppermute | solution.py:32
  48.8 29.3 %collective-permute-start.12 = (bf16[2,256,256]{2,1,0:T(8,128)(2,1)}, bf16[2,256,256]{2,1,0:T(8,128)(2,1)S(1)}, u32[]{:S(2)}, u32[]{:S(2)}) collective-permute-start(bf16[2,256,256]{2,1,0:T(8,128)(2,1)} %get-tuple-element.83), channel_id=1, source_target_pairs={{0,16},{8,24},{16,0},{24,8},{1,17},{9,25},{17,1},{25,9},{2,18},{10... | collective-permute-start | bytes 786440 | tf_op jit(solution)/shard_map/ppermute | solution.py:32
  54.4 23.7 %collective-permute-start.13 = (bf16[2,256,256]{2,1,0:T(8,128)(2,1)}, bf16[2,256,256]{2,1,0:T(8,128)(2,1)S(1)}, u32[]{:S(2)}, u32[]{:S(2)}) collective-permute-start(bf16[2,256,256]{2,1,0:T(8,128)(2,1)} %get-tuple-element.84), channel_id=1, source_target_pairs={{0,24},{8,16},{16,8},{24,0},{1,25},{9,17},{17,9},{25,1},{2,26},{10... | collective-permute-start | bytes 786440 | tf_op jit(solution)/shard_map/ppermute | solution.py:32
  86.9 6.4 %collective-permute-start.18 = (bf16[256,256]{1,0:T(8,128)(2,1)S(1)}, bf16[256,256]{1,0:T(8,128)(2,1)S(1)}, u32[]{:S(2)}, u32[]{:S(2)}) collective-permute-start(bf16[256,256]{1,0:T(8,128)(2,1)S(1)} %get-tuple-element.175), channel_id=1, source_target_pairs={{0,2},{1,3},{2,0},{3,1},{4,6},{5,7},{6,4},{7,5},{8,10},{9,11},{10,... | collective-permute-start | bytes 393224 | tf_op jit(solution)/shard_map/ppermute | solution.py:32
  87.0 8.3 %collective-permute-start.19 = (bf16[256,256]{1,0:T(8,128)(2,1)S(1)}, bf16[256,256]{1,0:T(8,128)(2,1)S(1)}, u32[]{:S(2)}, u32[]{:S(2)}) collective-permute-start(bf16[256,256]{1,0:T(8,128)(2,1)S(1)} %get-tuple-element.177), channel_id=1, source_target_pairs={{0,4},{1,5},{2,6},{3,7},{4,0},{5,1},{6,2},{7,3},{8,12},{9,13},{10,... | collective-permute-start | bytes 393224 | tf_op jit(solution)/shard_map/ppermute | solution.py:32
  87.8 7.5 %collective-permute-start.20 = (bf16[256,256]{1,0:T(8,128)(2,1)S(1)}, bf16[256,256]{1,0:T(8,128)(2,1)S(1)}, u32[]{:S(2)}, u32[]{:S(2)}) collective-permute-start(bf16[256,256]{1,0:T(8,128)(2,1)S(1)} %get-tuple-element.176), channel_id=1, source_target_pairs={{0,6},{1,7},{2,4},{3,5},{4,2},{5,3},{6,0},{7,1},{8,14},{9,15},{10,... | collective-permute-start | bytes 393224 | tf_op jit(solution)/shard_map/ppermute | solution.py:32
  95.5 11.8 %collective-permute-start.28 = (bf16[256,256]{1,0:T(8,128)(2,1)S(1)}, bf16[256,256]{1,0:T(8,128)(2,1)S(1)}, u32[]{:S(2)}, u32[]{:S(2)}) collective-permute-start(bf16[256,256]{1,0:T(8,128)(2,1)S(1)} %fusion.4.refs_6_), channel_id=1, source_target_pairs={{0,16},{8,24},{16,0},{24,8},{1,17},{9,25},{17,1},{25,9},{2,18},{10... | collective-permute-start | bytes 393224 | tf_op jit(solution)/shard_map/ppermute | solution.py:32
  102.0 6.1 %collective-permute-start.22 = (bf16[256,256]{1,0:T(8,128)(2,1)S(1)}, bf16[256,256]{1,0:T(8,128)(2,1)S(1)}, u32[]{:S(2)}, u32[]{:S(2)}) collective-permute-start(bf16[256,256]{1,0:T(8,128)(2,1)S(1)} %fusion.4.refs_6_), channel_id=1, source_target_pairs={{0,2},{1,3},{2,0},{3,1},{4,6},{5,7},{6,4},{7,5},{8,10},{9,11},{10,... | collective-permute-start | bytes 393224 | tf_op jit(solution)/shard_map/ppermute | solution.py:32
  103.7 6.8 %collective-permute-start.24 = (bf16[256,256]{1,0:T(8,128)(2,1)S(1)}, bf16[256,256]{1,0:T(8,128)(2,1)S(1)}, u32[]{:S(2)}, u32[]{:S(2)}) collective-permute-start(bf16[256,256]{1,0:T(8,128)(2,1)S(1)} %fusion.4.refs_6_), channel_id=1, source_target_pairs={{0,4},{1,5},{2,6},{3,7},{4,0},{5,1},{6,2},{7,3},{8,12},{9,13},{10,... | collective-permute-start | bytes 393224 | tf_op jit(solution)/shard_map/ppermute | solution.py:32
  104.0 7.7 %collective-permute-start.26 = (bf16[256,256]{1,0:T(8,128)(2,1)S(1)}, bf16[256,256]{1,0:T(8,128)(2,1)S(1)}, u32[]{:S(2)}, u32[]{:S(2)}) collective-permute-start(bf16[256,256]{1,0:T(8,128)(2,1)S(1)} %fusion.4.refs_6_), channel_id=1, source_target_pairs={{0,6},{1,7},{2,4},{3,5},{4,2},{5,3},{6,0},{7,1},{8,14},{9,15},{10,... | collective-permute-start | bytes 393224 | tf_op jit(solution)/shard_map/ppermute | solution.py:32
  105.5 6.9 %collective-permute-start.21 = (bf16[256,256]{1,0:T(8,128)(2,1)S(1)}, bf16[256,256]{1,0:T(8,128)(2,1)S(1)}, u32[]{:S(2)}, u32[]{:S(2)}) collective-permute-start(bf16[256,256]{1,0:T(8,128)(2,1)S(1)} %fusion.4.refs_6_), channel_id=1, source_target_pairs={{0,1},{1,0},{2,3},{3,2},{4,5},{5,4},{6,7},{7,6},{8,9},{9,8},{10,11... | collective-permute-start | bytes 393224 | tf_op jit(solution)/shard_map/ppermute | solution.py:32
  107.2 6.8 %collective-permute-start.36 = (bf16[256,256]{1,0:T(8,128)(2,1)S(1)}, bf16[256,256]{1,0:T(8,128)(2,1)S(1)}, u32[]{:S(2)}, u32[]{:S(2)}) collective-permute-start(bf16[256,256]{1,0:T(8,128)(2,1)S(1)} %fusion.4.refs_6_), channel_id=1, source_target_pairs={{0,8},{8,0},{16,24},{24,16},{1,9},{9,1},{17,25},{25,17},{2,10},{10... | collective-permute-start | bytes 393224 | tf_op jit(solution)/shard_map/ppermute | solution.py:32
  108.1 6.9 %collective-permute-start.37 = (bf16[256,256]{1,0:T(8,128)(2,1)S(1)}, bf16[256,256]{1,0:T(8,128)(2,1)S(1)}, u32[]{:S(2)}, u32[]{:S(2)}) collective-permute-start(bf16[256,256]{1,0:T(8,128)(2,1)S(1)} %fusion.4.refs_6_), channel_id=1, source_target_pairs={{0,24},{8,16},{16,8},{24,0},{1,25},{9,17},{17,9},{25,1},{2,26},{10... | collective-permute-start | bytes 393224 | tf_op jit(solution)/shard_map/ppermute | solution.py:32
  110.5 5.0 %collective-permute-start.30 = (bf16[256,256]{1,0:T(8,128)(2,1)S(1)}, bf16[256,256]{1,0:T(8,128)(2,1)S(1)}, u32[]{:S(2)}, u32[]{:S(2)}) collective-permute-start(bf16[256,256]{1,0:T(8,128)(2,1)S(1)} %collective-permute-done.28.refs_14_), channel_id=1, source_target_pairs={{0,2},{1,3},{2,0},{3,1},{4,6},{5,7},{6,4},{7,5},{8,10},{9,11},{10,... | collective-permute-start | bytes 393224 | tf_op jit(solution)/shard_map/ppermute | solution.py:32
  111.7 5.0 %collective-permute-start.32 = (bf16[256,256]{1,0:T(8,128)(2,1)S(1)}, bf16[256,256]{1,0:T(8,128)(2,1)S(1)}, u32[]{:S(2)}, u32[]{:S(2)}) collective-permute-start(bf16[256,256]{1,0:T(8,128)(2,1)S(1)} %collective-permute-done.28.refs_14_), channel_id=1, source_target_pairs={{0,4},{1,5},{2,6},{3,7},{4,0},{5,1},{6,2},{7,3},{8,12},{9,13},{10,... | collective-permute-start | bytes 393224 | tf_op jit(solution)/shard_map/ppermute | solution.py:32
  112.4 5.9 %collective-permute-start.34 = (bf16[256,256]{1,0:T(8,128)(2,1)S(1)}, bf16[256,256]{1,0:T(8,128)(2,1)S(1)}, u32[]{:S(2)}, u32[]{:S(2)}) collective-permute-start(bf16[256,256]{1,0:T(8,128)(2,1)S(1)} %collective-permute-done.28.refs_14_), channel_id=1, source_target_pairs={{0,6},{1,7},{2,4},{3,5},{4,2},{5,3},{6,0},{7,1},{8,14},{9,15},{10,... | collective-permute-start | bytes 393224 | tf_op jit(solution)/shard_map/ppermute | solution.py:32
  114.0 4.3 %collective-permute-start.29 = (bf16[256,256]{1,0:T(8,128)(2,1)S(1)}, bf16[256,256]{1,0:T(8,128)(2,1)S(1)}, u32[]{:S(2)}, u32[]{:S(2)}) collective-permute-start(bf16[256,256]{1,0:T(8,128)(2,1)S(1)} %collective-permute-done.28.refs_14_), channel_id=1, source_target_pairs={{0,1},{1,0},{2,3},{3,2},{4,5},{5,4},{6,7},{7,6},{8,9},{9,8},{10,11... | collective-permute-start | bytes 393224 | tf_op jit(solution)/shard_map/ppermute | solution.py:32
  115.0 3.8 %collective-permute-start.23 = (bf16[256,256]{1,0:T(8,128)(2,1)S(1)}, bf16[256,256]{1,0:T(8,128)(2,1)S(1)}, u32[]{:S(2)}, u32[]{:S(2)}) collective-permute-start(bf16[256,256]{1,0:T(8,128)(2,1)S(1)} %collective-permute-done.22.refs_8_), channel_id=1, source_target_pairs={{0,1},{1,0},{2,3},{3,2},{4,5},{5,4},{6,7},{7,6},{8,9},{9,8},{10,11... | collective-permute-start | bytes 393224 | tf_op jit(solution)/shard_map/ppermute | solution.py:32
  115.4 4.1 %collective-permute-start.25 = (bf16[256,256]{1,0:T(8,128)(2,1)S(1)}, bf16[256,256]{1,0:T(8,128)(2,1)S(1)}, u32[]{:S(2)}, u32[]{:S(2)}) collective-permute-start(bf16[256,256]{1,0:T(8,128)(2,1)S(1)} %collective-permute-done.24.refs_10_), channel_id=1, source_target_pairs={{0,1},{1,0},{2,3},{3,2},{4,5},{5,4},{6,7},{7,6},{8,9},{9,8},{10,11... | collective-permute-start | bytes 393224 | tf_op jit(solution)/shard_map/ppermute | solution.py:32
  120.1 16.6 %collective-permute-start.38 = (bf16[2,256,256]{2,1,0:T(8,128)(2,1)S(1)}, bf16[2,256,256]{2,1,0:T(8,128)(2,1)S(1)}, u32[]{:S(2)}, u32[]{:S(2)}) collective-permute-start(bf16[2,256,256]{2,1,0:T(8,128)(2,1)S(1)} %pad_maximum_fusion.refs_6_), channel_id=1, source_target_pairs={{0,2},{1,3},{2,0},{3,1},{4,6},{5,7},{6,4},{7,5},{8,10},{9,11},{10,... | collective-permute-start | bytes 786440 | tf_op jit(solution)/shard_map/ppermute | solution.py:32
  121.2 15.6 %collective-permute-start.39 = (bf16[2,256,256]{2,1,0:T(8,128)(2,1)S(1)}, bf16[2,256,256]{2,1,0:T(8,128)(2,1)S(1)}, u32[]{:S(2)}, u32[]{:S(2)}) collective-permute-start(bf16[2,256,256]{2,1,0:T(8,128)(2,1)S(1)} %pad_maximum_fusion.refs_6_), channel_id=1, source_target_pairs={{0,4},{1,5},{2,6},{3,7},{4,0},{5,1},{6,2},{7,3},{8,12},{9,13},{10,... | collective-permute-start | bytes 786440 | tf_op jit(solution)/shard_map/ppermute | solution.py:32
  122.3 14.5 %collective-permute-start.40 = (bf16[2,256,256]{2,1,0:T(8,128)(2,1)S(1)}, bf16[2,256,256]{2,1,0:T(8,128)(2,1)S(1)}, u32[]{:S(2)}, u32[]{:S(2)}) collective-permute-start(bf16[2,256,256]{2,1,0:T(8,128)(2,1)S(1)} %pad_maximum_fusion.refs_6_), channel_id=1, source_target_pairs={{0,6},{1,7},{2,4},{3,5},{4,2},{5,3},{6,0},{7,1},{8,14},{9,15},{10,... | collective-permute-start | bytes 786440 | tf_op jit(solution)/shard_map/ppermute | solution.py:32
  136.8 3.6 %collective-permute-start.45 = (bf16[4,2,256,256]{3,2,1,0:T(8,128)(2,1)}, bf16[4,2,256,256]{3,2,1,0:T(8,128)(2,1)S(1)}, u32[]{:S(2)}, u32[]{:S(2)}) collective-permute-start(bf16[4,2,256,256]{3,2,1,0:T(8,128)(2,1)} %get-tuple-element.126), channel_id=1, source_target_pairs={{0,1},{1,0},{2,3},{3,2},{4,5},{5,4},{6,7},{7,6},{8,9},{9,8},{10,11... | collective-permute-start | bytes 3145736 | tf_op jit(solution)/shard_map/ppermute | solution.py:32
  136.9 5.1 %collective-permute-start.41 = (bf16[2,256,256]{2,1,0:T(8,128)(2,1)S(1)}, bf16[2,256,256]{2,1,0:T(8,128)(2,1)S(1)}, u32[]{:S(2)}, u32[]{:S(2)}) collective-permute-start(bf16[2,256,256]{2,1,0:T(8,128)(2,1)S(1)} %pad_maximum_fusion.refs_6_), channel_id=1, source_target_pairs={{0,1},{1,0},{2,3},{3,2},{4,5},{5,4},{6,7},{7,6},{8,9},{9,8},{10,11... | collective-permute-start | bytes 786440 | tf_op jit(solution)/shard_map/ppermute | solution.py:32
  137.4 4.7 %collective-permute-start.42 = (bf16[2,256,256]{2,1,0:T(8,128)(2,1)S(1)}, bf16[2,256,256]{2,1,0:T(8,128)(2,1)S(1)}, u32[]{:S(2)}, u32[]{:S(2)}) collective-permute-start(bf16[2,256,256]{2,1,0:T(8,128)(2,1)S(1)} %collective-permute-done.38.refs_8_), channel_id=1, source_target_pairs={{0,1},{1,0},{2,3},{3,2},{4,5},{5,4},{6,7},{7,6},{8,9},{9,8},{10,11... | collective-permute-start | bytes 786440 | tf_op jit(solution)/shard_map/ppermute | solution.py:32
  137.5 4.6 %collective-permute-start.43 = (bf16[2,256,256]{2,1,0:T(8,128)(2,1)S(1)}, bf16[2,256,256]{2,1,0:T(8,128)(2,1)S(1)}, u32[]{:S(2)}, u32[]{:S(2)}) collective-permute-start(bf16[2,256,256]{2,1,0:T(8,128)(2,1)S(1)} %collective-permute-done.39.refs_10_), channel_id=1, source_target_pairs={{0,1},{1,0},{2,3},{3,2},{4,5},{5,4},{6,7},{7,6},{8,9},{9,8},{10,11... | collective-permute-start | bytes 786440 | tf_op jit(solution)/shard_map/ppermute | solution.py:32
  137.9 4.2 %collective-permute-start.44 = (bf16[2,256,256]{2,1,0:T(8,128)(2,1)S(1)}, bf16[2,256,256]{2,1,0:T(8,128)(2,1)S(1)}, u32[]{:S(2)}, u32[]{:S(2)}) collective-permute-start(bf16[2,256,256]{2,1,0:T(8,128)(2,1)S(1)} %collective-permute-done.40.refs_12_), channel_id=1, source_target_pairs={{0,1},{1,0},{2,3},{3,2},{4,5},{5,4},{6,7},{7,6},{8,9},{9,8},{10,11... | collective-permute-start | bytes 786440 | tf_op jit(solution)/shard_map/ppermute | solution.py:32
  142.1 16.5 %collective-permute-start.46 = (bf16[2,256,256]{2,1,0:T(8,128)(2,1)S(1)}, bf16[2,256,256]{2,1,0:T(8,128)(2,1)S(1)}, u32[]{:S(2)}, u32[]{:S(2)}) collective-permute-start(bf16[2,256,256]{2,1,0:T(8,128)(2,1)S(1)} %get-tuple-element.137), channel_id=1, source_target_pairs={{0,2},{1,3},{2,0},{3,1},{4,6},{5,7},{6,4},{7,5},{8,10},{9,11},{10,... | collective-permute-start | bytes 786440 | tf_op jit(solution)/shard_map/ppermute | solution.py:32
  143.3 15.4 %collective-permute-start.47 = (bf16[2,256,256]{2,1,0:T(8,128)(2,1)S(1)}, bf16[2,256,256]{2,1,0:T(8,128)(2,1)S(1)}, u32[]{:S(2)}, u32[]{:S(2)}) collective-permute-start(bf16[2,256,256]{2,1,0:T(8,128)(2,1)S(1)} %get-tuple-element.138), channel_id=1, source_target_pairs={{0,4},{1,5},{2,6},{3,7},{4,0},{5,1},{6,2},{7,3},{8,12},{9,13},{10,... | collective-permute-start | bytes 786440 | tf_op jit(solution)/shard_map/ppermute | solution.py:32
  144.3 14.3 %collective-permute-start.48 = (bf16[2,256,256]{2,1,0:T(8,128)(2,1)S(1)}, bf16[2,256,256]{2,1,0:T(8,128)(2,1)S(1)}, u32[]{:S(2)}, u32[]{:S(2)}) collective-permute-start(bf16[2,256,256]{2,1,0:T(8,128)(2,1)S(1)} %get-tuple-element.139), channel_id=1, source_target_pairs={{0,6},{1,7},{2,4},{3,5},{4,2},{5,3},{6,0},{7,1},{8,14},{9,15},{10,... | collective-permute-start | bytes 786440 | tf_op jit(solution)/shard_map/ppermute | solution.py:32
  158.7 2.9 %collective-permute-start.49 = (bf16[4,2,256,256]{3,2,1,0:T(8,128)(2,1)}, bf16[4,2,256,256]{3,2,1,0:T(8,128)(2,1)S(1)}, u32[]{:S(2)}, u32[]{:S(2)}) collective-permute-start(bf16[4,2,256,256]{3,2,1,0:T(8,128)(2,1)} %get-tuple-element.141), channel_id=1, source_target_pairs={{0,1},{1,0},{2,3},{3,2},{4,5},{5,4},{6,7},{7,6},{8,9},{9,8},{10,11... | collective-permute-start | bytes 3145736 | tf_op jit(solution)/shard_map/ppermute | solution.py:32
  158.9 9.3 %collective-permute-start.52 = (bf16[256,256]{1,0:T(8,128)(2,1)S(1)}, bf16[256,256]{1,0:T(8,128)(2,1)S(1)}, u32[]{:S(2)}, u32[]{:S(2)}) collective-permute-start(bf16[256,256]{1,0:T(8,128)(2,1)S(1)} %fusion.15), channel_id=1, source_target_pairs={{0,16},{8,24},{16,0},{24,8},{1,17},{9,25},{17,1},{25,9},{2,18},{10... | collective-permute-start | bytes 393224 | tf_op jit(solution)/shard_map/ppermute | solution.py:32
  162.0 8.4 %collective-permute-start.51 = (bf16[2,256,256]{2,1,0:T(8,128)(2,1)S(1)}, bf16[2,256,256]{2,1,0:T(8,128)(2,1)S(1)}, u32[]{:S(2)}, u32[]{:S(2)}) collective-permute-start(bf16[2,256,256]{2,1,0:T(8,128)(2,1)S(1)} %pad_maximum_fusion.2), channel_id=1, source_target_pairs={{0,4},{1,5},{2,6},{3,7},{4,0},{5,1},{6,2},{7,3},{8,12},{9,13},{10,... | collective-permute-start | bytes 786440 | tf_op jit(solution)/shard_map/ppermute | solution.py:32
  163.4 8.1 %collective-permute-start.50 = (bf16[2,256,256]{2,1,0:T(8,128)(2,1)S(1)}, bf16[2,256,256]{2,1,0:T(8,128)(2,1)S(1)}, u32[]{:S(2)}, u32[]{:S(2)}) collective-permute-start(bf16[2,256,256]{2,1,0:T(8,128)(2,1)S(1)} %pad_maximum_fusion.1), channel_id=1, source_target_pairs={{0,2},{1,3},{2,0},{3,1},{4,6},{5,7},{6,4},{7,5},{8,10},{9,11},{10,... | collective-permute-start | bytes 786440 | tf_op jit(solution)/shard_map/ppermute | solution.py:32
  171.7 5.0 %collective-permute-start.53 = (bf16[1,256,256]{2,1,0:T(8,128)(2,1)S(1)}, bf16[1,256,256]{2,1,0:T(8,128)(2,1)S(1)}, u32[]{:S(2)}, u32[]{:S(2)}) collective-permute-start(bf16[1,256,256]{2,1,0:T(8,128)(2,1)S(1)} %get-tuple-element.147), channel_id=1, source_target_pairs={{0,4},{1,5},{2,6},{3,7},{4,0},{5,1},{6,2},{7,3},{8,12},{9,13},{10,... | collective-permute-start | bytes 393224 | tf_op jit(solution)/shard_map/ppermute | solution.py:32
  172.5 5.0 %collective-permute-start.55 = (bf16[1,256,256]{2,1,0:T(8,128)(2,1)S(1)}, bf16[1,256,256]{2,1,0:T(8,128)(2,1)S(1)}, u32[]{:S(2)}, u32[]{:S(2)}) collective-permute-start(bf16[1,256,256]{2,1,0:T(8,128)(2,1)S(1)} %get-tuple-element.148), channel_id=1, source_target_pairs={{0,2},{1,3},{2,0},{3,1},{4,6},{5,7},{6,4},{7,5},{8,10},{9,11},{10,... | collective-permute-start | bytes 393224 | tf_op jit(solution)/shard_map/ppermute | solution.py:32
  177.5 5.0 %collective-permute-start.54 = (bf16[256,256]{1,0:T(8,128)(2,1)S(1)}, bf16[256,256]{1,0:T(8,128)(2,1)S(1)}, u32[]{:S(2)}, u32[]{:S(2)}) collective-permute-start(bf16[256,256]{1,0:T(8,128)(2,1)S(1)} %get-tuple-element.158), channel_id=1, source_target_pairs={{0,8},{8,0},{16,24},{24,16},{1,9},{9,1},{17,25},{25,17},{2,10},{10... | collective-permute-start | bytes 393224 | tf_op jit(solution)/shard_map/ppermute | solution.py:32
  177.8 6.9 %collective-permute-start.56 = (bf16[256,256]{1,0:T(8,128)(2,1)S(1)}, bf16[256,256]{1,0:T(8,128)(2,1)S(1)}, u32[]{:S(2)}, u32[]{:S(2)}) collective-permute-start(bf16[256,256]{1,0:T(8,128)(2,1)S(1)} %get-tuple-element.159), channel_id=1, source_target_pairs={{0,24},{8,16},{16,8},{24,0},{1,25},{9,17},{17,9},{25,1},{2,26},{10... | collective-permute-start | bytes 393224 | tf_op jit(solution)/shard_map/ppermute | solution.py:32
  (54 other events, 333.0 us)
Sparse Core Ops, SparseCore 0:
  10.6 31.2 all-gather.1

commit v7 on v6

--- a/solution.py
+++ b/solution.py
@@ -46,29 +46,35 @@
     return reach
 
 
-def project_kernel(count, ids, gain, weight, *refs):
+def project_kernel(count, share, ids, gain, weight, other_weight, *refs):
     pieces, outs, scaled = refs[:count], refs[count:-1], refs[-1]
     me_x, me_y = ids[0], ids[1]
     rows, width = pieces[0].shape
-    share = scaled.shape[1] // width
     for mask, piece in enumerate(pieces):
         source = me_y ^ mask
-        block, part = source // share, source % share
-        columns = pl.ds(pl.multiple_of((me_x * share + part) * width, width), width)
+        place, part = source // share, source % share
+        block, side = place // 2, place % 2
+        feature = ((me_x // 2 * 2 + side) * share + part) * width
+        columns = pl.ds(pl.multiple_of(feature, width), width)
         value = (piece[...].astype(F32) * gain[:, columns]).astype(BF16)
         scaled[
+            side,
             pl.ds(pl.multiple_of(block * rows, rows), rows),
             pl.ds(pl.multiple_of(part * width, width), width),
         ] = value
     blocks = len(outs) // 2
-    for mask in range(blocks):
-        place = pl.ds(pl.multiple_of((me_x ^ mask) * rows, rows), rows)
+    for far in range(blocks):
+        place = pl.ds(pl.multiple_of((me_x ^ (2 * far)) // 2 * rows, rows), rows)
         for which in range(3):
-            value = jnp.dot(scaled[place, :], weight[which], preferred_element_type=F32)
+            value = jnp.dot(
+                scaled[me_x % 2, place, :], weight[which], preferred_element_type=F32
+            ) + jnp.dot(
+                scaled[1 - me_x % 2, place, :], other_weight[which], preferred_element_type=F32
+            )
             if which == 0:
-                outs[mask][...] = value.astype(outs[mask].dtype)
+                outs[far][...] = value.astype(outs[far].dtype)
             else:
-                out = outs[blocks + mask]
+                out = outs[blocks + far]
                 out[which - 1] = value.astype(out.dtype)
 
 
@@ -266,39 +272,46 @@
         squares = squares + swap(squares, "gy", 1 << bit)
     row_scale = lax.rsqrt(squares / depth + 1e-05)
 
+    weight = jnp.transpose(projection_weight, (1, 0, 2))
     share = gy_count // gx_count
+    terms_of = gx_count // 2
     route = [
-        (a * gy_count + b, (b // share) * gy_count + a * share + b % share)
+        (
+            a * gy_count + b,
+            (b // share // 2 * 2 + a % 2) * gy_count
+            + (a // 2 * 2 + b // share % 2) * share
+            + b % share,
+        )
         for a in range(gx_count)
         for b in range(gy_count)
     ]
     moved = lax.ppermute(tokens, ("gx", "gy"), route)
+    other_weight = swap(weight, "gx", 1)
+    output_weight, moved = lax.optimization_barrier((output_weight, moved))
     experts = gate_up_weight.shape[0]
     units = gate_up_weight.shape[3]
     output_full = lax.all_gather(output_weight, "gx", axis=0, tiled=True)
     far = gather_far(moved)
     gate_up, far = lax.optimization_barrier((jnp.transpose(gate_up_weight, (2, 0, 1, 3)), far))
     pieces = gather_near(far)
-    types = [F32] + [BF16] * (gx_count - 1)
+    types = [F32] + [BF16] * (terms_of - 1)
     projected = pl.pallas_call(
-        lambda *refs: project_kernel(gy_count, *refs),
+        lambda *refs: project_kernel(gy_count, share, *refs),
         out_shape=[jax.ShapeDtypeStruct((rows, width), kind) for kind in types]
         + [jax.ShapeDtypeStruct((2, rows, width), kind) for kind in types],
-        in_specs=[smem()] + [vmem()] * (2 + gy_count),
-        out_specs=[vmem()] * (2 * gx_count),
-        scratch_shapes=[pltpu.VMEM((gx_count * rows, share * width), BF16)],
+        in_specs=[smem()] + [vmem()] * (3 + gy_count),
+        out_specs=[vmem()] * (2 * terms_of),
+        scratch_shapes=[pltpu.VMEM((2, terms_of * rows, share * width), BF16)],
         compiler_params=params(),
         name="project",
-    )(
-        ids, attention_gain.reshape(1, depth), jnp.transpose(projection_weight, (1, 0, 2)), *pieces
-    )
-    query_terms, pair_terms = projected[:gx_count], projected[gx_count:]
+    )(ids, attention_gain.reshape(1, depth), weight, other_weight, *pieces)
+    query_terms, pair_terms = projected[:terms_of], projected[terms_of:]
     parents, query_terms = lax.optimization_barrier((parents, query_terms))
     query_terms = [query_terms[0]] + [
-        swap(query_terms[mask], "gx", mask) for mask in range(1, gx_count)
+        swap(query_terms[far], "gx", 2 * far) for far in range(1, terms_of)
     ]
     pair_terms = [pair_terms[0]] + [
-        swap(pair_terms[mask], "gx", mask) for mask in range(1, gx_count)
+        swap(pair_terms[far], "gx", 2 * far) for far in range(1, terms_of)
     ]
 
     owner = prompt_group % groups
@@ -316,12 +329,12 @@
     wide_rows = heads * draft
     flat = lambda *_: (0, 0)
     top, mass, mixed, query = pl.pallas_call(
-        lambda *refs: cache_kernel(requests, draft, heads, gx_count, *refs),
+        lambda *refs: cache_kernel(requests, draft, heads, terms_of, *refs),
         grid_spec=pltpu.PrefetchScalarGridSpec(
             num_scalar_prefetch=4,
             grid=(groups, slots // step),
             in_specs=[pl.BlockSpec((rows, 1), flat)]
-            + [pl.BlockSpec((rows, width), flat)] * gx_count
+            + [pl.BlockSpec((rows, width), flat)] * terms_of
             + [
                 pl.BlockSpec(
                     (1, 2, step, width),
@@ -358,13 +371,13 @@
     chosen = (jnp.arange(requests, dtype=jnp.int32)[:, None] * draft + accepted_path).reshape(-1, 1)
     half = jax.ShapeDtypeStruct((gy_count // 2, rows, width), BF16)
     even, odd, picked = pl.pallas_call(
-        lambda *refs: draft_kernel(requests, draft, heads, gx_count, gy_count, *refs),
+        lambda *refs: draft_kernel(requests, draft, heads, terms_of, gy_count, *refs),
         out_shape=(
             half,
             half,
             jax.ShapeDtypeStruct((2, requests * accepted, width), BF16),
         ),
-        in_specs=[smem(), smem()] + [vmem()] * (gx_count + 8),
+        in_specs=[smem(), smem()] + [vmem()] * (terms_of + 8),
         out_specs=(vmem(), vmem(), vmem()),
         scratch_shapes=[pltpu.VMEM((rows, width), BF16)] * 3,
         compiler_params=params(),

time: 193 us -> 195 us (1.010)
  waiting for transfers between devices: 39.2 us -> 54.9 us
  Pallas kernels: 51.7 us -> 45.3 us
  starting transfers between devices: 63 us -> 57.7 us
    ppermute x56 -> x53, waiting for transfers between devices: 39.1 us -> 54.5 us  [swap(): lax.ppermute(value, axis, [(one, one ^ mask) for one in range(count)])]
    pallas_call x3, Pallas kernels: 25.8 us -> 19.4 us  [the longest x1 11.3 us: per_device(): pl.pallas_call(lambda *refs: cache_kernel(requests, draft, heads, terms_o...]
    ppermute x56 -> x53, starting transfers between devices: 61.4 us -> 56.1 us  [swap(): lax.ppermute(value, axis, [(one, one ^ mask) for one in range(count)])]
    unnamed x90 -> x84, local copies, waits for them, and re-layouts: 10.8 us -> 10.5 us
  transfers between devices with their start and end apart: 58 -> 55, of which waited for: 25 -> 24; matrix products, arithmetic and copies ran while one was open for 10% -> 10% of each run, Pallas kernels for 24% -> 21%
where the time goes in v7:
time: 195 us; the launch traced here: 196 us
  starting transfers between devices  57.7 us (30%)
  waiting for transfers between devices  54.9 us (28%)
  Pallas kernels  45.3 us (23%)
  between operations  14.7 us (8%)
  local copies, waits for them, and re-layouts  11.5 us (6%)
  other arithmetic  10.1 us (5%)
    ppermute x53, starting transfers between devices, swap(): lax.ppermute(value, axis, [(one, one ^ mask) for one in range(count)])  56.1 us
    ppermute x53, waiting for transfers between devices, swap(): lax.ppermute(value, axis, [(one, one ^ mask) for one in range(count)])  54.5 us
    pallas_call x2, Pallas kernels, per_device(): pl.pallas_call(lambda *refs: expert_kernel(gy_count, masks, number > 0, *...  25.9 us
    pallas_call x1, Pallas kernels, per_device(): pl.pallas_call(lambda *refs: cache_kernel(requests, draft, heads, terms_o...  11.3 us
    unnamed x84, local copies, waits for them, and re-layouts  10.5 us
    pallas_call x1, Pallas kernels, per_device(): pl.pallas_call(lambda *refs: draft_kernel(requests, draft, heads, terms_o...  4.48 us
  transfers between devices with their start and end apart: 55, of which 24 were waited for; matrix products, arithmetic and copies ran while one was open for 10% of the time, Pallas kernels for 21%

profile of v7, /device:TPU:0, one launch (start us, length us, event | category | flops | bytes accessed | tf_op | source)
XLA Modules:
  0.0 195.9 jit_solution(12017917912415406480)
XLA Ops:
  7.2 1.6 collective-permute-start
  8.8 3.0 %collective-permute-start.7 = (bf16[3,512,256]{2,1,0:T(8,128)(2,1)}, bf16[3,512,256]{2,1,0:T(8,128)(2,1)S(1)}, u32[]{:S(2)}, u32[]{:S(2)}) collective-permute-start(bf16[3,512,256]{2,1,0:T(8,128)(2,1)} %bitcast.94), channel_id=1, source_target_pairs={{0,8},{8,0},{16,24},{24,16},{1,9},{9,1},{17,25},{25,17},{2,10},{10... | collective-permute-start | bytes 2359304 | tf_op jit(solution)/shard_map/ppermute | solution.py:32
  11.8 1.0 fusion
  15.2 1.6 collective-permute-start.5
  17.3 6.5 %collective-permute-start.2 = (bf16[256,256]{1,0:T(8,128)(2,1)S(1)}, bf16[256,256]{1,0:T(8,128)(2,1)S(1)}, u32[]{:S(2)}, u32[]{:S(2)}) collective-permute-start(bf16[256,256]{1,0:T(8,128)(2,1)S(1)} %collective-permute-done.refs_4_), channel_id=1, source_target_pairs={{0,4},{1,5},{2,6},{3,7},{4,0},{5,1},{6,2},{7,3},{8,12},{9,13},{10,... | collective-permute-start | bytes 393224 | tf_op jit(solution)/shard_map/ppermute | solution.py:32
  24.5 2.1 %collective-permute-start.6 = (f32[256,1]{1,0:T(8,128)S(1)}, f32[256,1]{1,0:T(8,128)S(1)}, u32[]{:S(2)}, u32[]{:S(2)}) collective-permute-start(f32[256,1]{1,0:T(8,128)S(1)} %add.101), channel_id=1, source_target_pairs={{0,4},{1,5},{2,6},{3,7},{4,0},{5,1},{6,2},{7,3},{8,12},{9,13},{10,... | collective-permute-start | bytes 3080 | tf_op jit(solution)/shard_map/ppermute | solution.py:32
  27.2 7.9 %copy.30 = bf16[4,2048,2,256]{3,1,0,2:T(8,128)(2,1)} copy(bf16[4,2048,2,256]{3,2,1,0:T(2,128)(2,1)} %param.24) | data formatting | bytes 16777216 | tf_op args[10]
  38.8 3.6 %project.1 = (f32[256,256]{1,0:T(8,128)}, bf16[256,256]{1,0:T(8,128)(2,1)}, f32[2,256,256]{2,1,0:T(8,128)}, bf16[2,256,256]{2,1,0:T(8,128)(2,1)}) custom-call(s32[2]{0:T(128)} %pad_add_fusion.refs_0_, f32[1,2048]{1,0:T(1,128)} %bitcast.99, bf16[3,512,256]{2,1,0:T(8,128)(2,1)} %bitcast.95, bf16[3,512,256]{2,1,0:T(8,128)(2,1)} %copy-done.1, ...), custom_call_target="tpu_custom_call" | custom-call | tf_op jit(solution)/shard_map/project/pallas_call | solution.py:298
  42.4 3.0 %collective-permute-start.12 = (bf16[2,256,256]{2,1,0:T(8,128)(2,1)}, bf16[2,256,256]{2,1,0:T(8,128)(2,1)S(1)}, u32[]{:S(2)}, u32[]{:S(2)}) collective-permute-start(bf16[2,256,256]{2,1,0:T(8,128)(2,1)} %get-tuple-element.79), channel_id=1, source_target_pairs={{0,16},{8,24},{16,0},{24,8},{1,17},{9,25},{17,1},{25,9},{2,18},{10... | collective-permute-start | bytes 786440 | tf_op jit(solution)/shard_map/ppermute | solution.py:32
  46.1 1.0 convolution_minimum_fusion.refs_6_
  47.1 17.2 %collective-permute-done.13.refs_6_ = bf16[256,256]{1,0:T(8,128)(2,1)S(1)} collective-permute-done((bf16[256,256]{1,0:T(8,128)(2,1)}, bf16[256,256]{1,0:T(8,128)(2,1)S(1)}, u32[]{:S(2)}, u32[]{:S(2)}) %collective-permute-start.13) | collective-permute-done | bytes 131104 | tf_op jit(solution)/shard_map/ppermute | solution.py:32
  64.9 11.3 %cache.1 = (f32[512,128]{1,0:T(8,128)}, f32[512,128]{1,0:T(8,128)}, f32[512,256]{1,0:T(8,128)}, bf16[256,256]{1,0:T(8,128)(2,1)}) custom-call(s32[2]{0:T(128)} %refs_0_.1, s32[2]{0:T(128)} %get-tuple-element.149.refs_1_, s32[2]{0:T(128)} %get-tuple-element.148.refs_2_, s32[4]{0:T(128)} %convert_reduce_fusion.refs_3_.refs_1_, ...), custom_call_target="tpu_custom_call" | custom-call | flops 10737418240 | bytes 16777216 | tf_op jit(solution)/shard_map/cache/pallas_call | solution.py:331
  76.2 3.3 %collective-permute-done.12.refs_4_ = bf16[2,256,256]{2,1,0:T(8,128)(2,1)S(1)} collective-permute-done((bf16[2,256,256]{2,1,0:T(8,128)(2,1)}, bf16[2,256,256]{2,1,0:T(8,128)(2,1)S(1)}, u32[]{:S(2)}, u32[]{:S(2)}) %collective-permute-start.12) | collective-permute-done | bytes 262176 | tf_op jit(solution)/shard_map/ppermute | solution.py:32
  80.2 4.5 %draft.1 = (bf16[4,256,256]{2,1,0:T(8,128)(2,1)}, bf16[4,256,256]{2,1,0:T(8,128)(2,1)}, bf16[2,32,256]{2,1,0:T(8,128)(2,1)}) custom-call(s32[2]{0:T(128)} %pad_add_fusion.refs_0_, s32[4]{0:T(128)} %convert_reduce_fusion.refs_3_.refs_1_, f32[256,1]{1,0:T(8,128)} %add_rsqrt_fusion.refs_4_.refs_2_, f32[2,256,256]{2,1,0:T(8,128)} %get-tuple-element.78.refs_3_, ...), custom_call_target="tpu_custom_call" | custom-call | tf_op jit(solution)/shard_map/draft/pallas_call | solution.py:373
  84.7 2.1 %collective-permute-done.14 = bf16[4,256,256]{2,1,0:T(8,128)(2,1)S(1)} collective-permute-done((bf16[4,256,256]{2,1,0:T(8,128)(2,1)}, bf16[4,256,256]{2,1,0:T(8,128)(2,1)S(1)}, u32[]{:S(2)}, u32[]{:S(2)}) %collective-permute-start.14) | collective-permute-done | bytes 524320 | tf_op jit(solution)/shard_map/ppermute | solution.py:32
  86.8 1.2 fusion.36
  88.1 1.6 collective-permute-start.15
  89.9 1.7 collective-permute-start.17
  91.6 2.4 %collective-permute-done.15 = bf16[256,256]{1,0:T(8,128)(2,1)S(1)} collective-permute-done((bf16[256,256]{1,0:T(8,128)(2,1)S(1)}, bf16[256,256]{1,0:T(8,128)(2,1)S(1)}, u32[]{:S(2)}, u32[]{:S(2)}) %collective-permute-start.15) | collective-permute-done | bytes 131104 | tf_op jit(solution)/shard_map/ppermute | solution.py:32
  94.0 3.7 %collective-permute-done.16 = bf16[256,256]{1,0:T(8,128)(2,1)S(1)} collective-permute-done((bf16[256,256]{1,0:T(8,128)(2,1)S(1)}, bf16[256,256]{1,0:T(8,128)(2,1)S(1)}, u32[]{:S(2)}, u32[]{:S(2)}) %collective-permute-start.16) | collective-permute-done | bytes 131104 | tf_op jit(solution)/shard_map/ppermute | solution.py:32
  97.8 7.6 %collective-permute-start.25 = (bf16[256,256]{1,0:T(8,128)(2,1)S(1)}, bf16[256,256]{1,0:T(8,128)(2,1)S(1)}, u32[]{:S(2)}, u32[]{:S(2)}) collective-permute-start(bf16[256,256]{1,0:T(8,128)(2,1)S(1)} %fusion.4.refs_6_), channel_id=1, source_target_pairs={{0,16},{8,24},{16,0},{24,8},{1,17},{9,25},{17,1},{25,9},{2,18},{10... | collective-permute-start | bytes 393224 | tf_op jit(solution)/shard_map/ppermute | solution.py:32
  105.9 1.2 collective-permute-start.21
  107.1 1.8 collective-permute-start.23
  108.8 1.4 collective-permute-done.25.refs_14_
  111.0 2.3 %collective-permute-start.34 = (bf16[256,256]{1,0:T(8,128)(2,1)S(1)}, bf16[256,256]{1,0:T(8,128)(2,1)S(1)}, u32[]{:S(2)}, u32[]{:S(2)}) collective-permute-start(bf16[256,256]{1,0:T(8,128)(2,1)S(1)} %fusion.4.refs_6_), channel_id=1, source_target_pairs={{0,24},{8,16},{16,8},{24,0},{1,25},{9,17},{17,9},{25,1},{2,26},{10... | collective-permute-start | bytes 393224 | tf_op jit(solution)/shard_map/ppermute | solution.py:32
  114.2 1.2 collective-permute-start.29
  115.4 1.5 collective-permute-start.31
  116.9 1.9 collective-permute-done.34
  119.4 1.8 collective-permute-done.31.refs_20_
  123.8 1.4 collective-permute-start.36
  125.2 1.4 collective-permute-start.37
  126.8 13.0 %experts.2 = (bf16[4,2,256,256]{3,2,1,0:T(8,128)(2,1)}, bf16[4,2,256,256]{3,2,1,0:T(8,128)(2,1)}) custom-call(s32[2]{0:T(128)} %pad_add_fusion.refs_0_, f32[1,2048]{1,0:T(1,128)} %bitcast.105, s32[8,1024]{1,0:T(8,128)} %bitcast.103, f32[8,1024]{1,0:T(8,128)} %convert_bitcast_fusion.refs_3_, bf16[2,4,2048,256]{3,2,1,0:T(8,128)(2,1)} %bitcast.92, ...), custom_call_target="tpu_custom_call" | custom-call | flops 6442450944 | bytes 12582912 | tf_op jit(solution)/shard_map/experts/pallas_call | solution.py:423
  141.0 2.4 %collective-permute-done.42 = bf16[4,2,256,256]{3,2,1,0:T(8,128)(2,1)S(1)} collective-permute-done((bf16[4,2,256,256]{3,2,1,0:T(8,128)(2,1)}, bf16[4,2,256,256]{3,2,1,0:T(8,128)(2,1)S(1)}, u32[]{:S(2)}, u32[]{:S(2)}) %collective-permute-start.42) | collective-permute-done | bytes 1048608 | tf_op jit(solution)/shard_map/ppermute | solution.py:32
  143.4 1.5 fusion.37
  145.9 1.4 collective-permute-start.44
  147.3 1.4 collective-permute-start.45
  148.7 13.0 %experts.3 = (bf16[4,2,256,256]{3,2,1,0:T(8,128)(2,1)}, bf16[4,2,256,256]{3,2,1,0:T(8,128)(2,1)}) custom-call(s32[2]{0:T(128)} %pad_add_fusion.refs_0_, f32[1,2048]{1,0:T(1,128)} %bitcast.106, s32[8,1024]{1,0:T(8,128)} %bitcast.104, f32[8,1024]{1,0:T(8,128)} %convert_bitcast_fusion.refs_3_, bf16[2,4,2048,256]{3,2,1,0:T(8,128)(2,1)} %bitcast.93, ...), custom_call_target="tpu_custom_call" | custom-call | flops 6442450944 | bytes 12582912 | tf_op jit(solution)/shard_map/experts/pallas_call | solution.py:423
  161.9 1.4 collective-permute-start.49
  163.4 1.3 collective-permute-done.46
  165.9 1.4 collective-permute-start.47
  167.3 4.3 %collective-permute-done.49 = bf16[256,256]{1,0:T(8,128)(2,1)S(1)} collective-permute-done((bf16[256,256]{1,0:T(8,128)(2,1)S(1)}, bf16[256,256]{1,0:T(8,128)(2,1)S(1)}, u32[]{:S(2)}, u32[]{:S(2)}) %collective-permute-start.49) | collective-permute-done | bytes 131104 | tf_op jit(solution)/shard_map/ppermute | solution.py:32
  171.7 1.8 collective-permute-done.48
  174.2 1.3 collective-permute-start.50
  176.2 3.0 %collective-permute-done.50 = bf16[1,256,256]{2,1,0:T(8,128)(2,1)S(1)} collective-permute-done((bf16[1,256,256]{2,1,0:T(8,128)(2,1)S(1)}, bf16[1,256,256]{2,1,0:T(8,128)(2,1)S(1)}, u32[]{:S(2)}, u32[]{:S(2)}) %collective-permute-start.50) | collective-permute-done | bytes 131104 | tf_op jit(solution)/shard_map/ppermute | solution.py:32
  179.2 1.2 collective-permute-done.52
  181.5 2.0 %collective-permute-start.53 = (bf16[256,256]{1,0:T(8,128)(2,1)S(1)}, bf16[256,256]{1,0:T(8,128)(2,1)S(1)}, u32[]{:S(2)}, u32[]{:S(2)}) collective-permute-start(bf16[256,256]{1,0:T(8,128)(2,1)S(1)} %get-tuple-element.151), channel_id=1, source_target_pairs={{0,24},{8,16},{16,8},{24,0},{1,25},{9,17},{17,9},{25,1},{2,26},{10... | collective-permute-start | bytes 393224 | tf_op jit(solution)/shard_map/ppermute | solution.py:32
  184.1 2.2 %collective-permute-done.51 = bf16[256,256]{1,0:T(8,128)(2,1)S(1)} collective-permute-done((bf16[256,256]{1,0:T(8,128)(2,1)S(1)}, bf16[256,256]{1,0:T(8,128)(2,1)S(1)}, u32[]{:S(2)}, u32[]{:S(2)}) %collective-permute-start.51) | collective-permute-done | bytes 131104 | tf_op jit(solution)/shard_map/ppermute | solution.py:32
  186.3 2.0 %collective-permute-done.53 = bf16[256,256]{1,0:T(8,128)(2,1)S(1)} collective-permute-done((bf16[256,256]{1,0:T(8,128)(2,1)S(1)}, bf16[256,256]{1,0:T(8,128)(2,1)S(1)}, u32[]{:S(2)}, u32[]{:S(2)}) %collective-permute-start.53) | collective-permute-done | bytes 131104 | tf_op jit(solution)/shard_map/ppermute | solution.py:32
  (188 shorter events, 23.1 us)
Async XLA Ops:
  7.2 72.8 %all-gather.2.cloned.1.call-start = ((), (), s32[]{:S(2)}) async-start(), calls=%async_computation | async-start | bytes 1310720 | tf_op jit(solution)/shard_map/all_gather | solution.py:293
  7.2 9.6 %collective-permute-start = (bf16[256,256]{1,0:T(8,128)(2,1)}, bf16[256,256]{1,0:T(8,128)(2,1)S(1)}, u32[]{:S(2)}, u32[]{:S(2)}) collective-permute-start(bf16[256,256]{1,0:T(8,128)(2,1)} %param.14), channel_id=1, source_target_pairs={{0,0},{1,1},{2,2},{3,3},{4,16},{5,17},{6,18},{7,19},{8,8},{9,9},{1... | collective-permute-start | bytes 393224 | tf_op jit(solution)/shard_map/ppermute | solution.py:288
  8.8 29.1 %collective-permute-start.7 = (bf16[3,512,256]{2,1,0:T(8,128)(2,1)}, bf16[3,512,256]{2,1,0:T(8,128)(2,1)S(1)}, u32[]{:S(2)}, u32[]{:S(2)}) collective-permute-start(bf16[3,512,256]{2,1,0:T(8,128)(2,1)} %bitcast.94), channel_id=1, source_target_pairs={{0,8},{8,0},{16,24},{24,16},{1,9},{9,1},{17,25},{25,17},{2,10},{10... | collective-permute-start | bytes 2359304 | tf_op jit(solution)/shard_map/ppermute | solution.py:32
  13.0 2.2 %collective-permute-start.4 = (f32[256,1]{1,0:T(8,128)S(1)}, f32[256,1]{1,0:T(8,128)S(1)}, u32[]{:S(2)}, u32[]{:S(2)}) collective-permute-start(f32[256,1]{1,0:T(8,128)S(1)} %copy.26), channel_id=1, source_target_pairs={{0,1},{1,0},{2,3},{3,2},{4,5},{5,4},{6,7},{7,6},{8,9},{9,8},{10,11... | collective-permute-start | bytes 3080 | tf_op jit(solution)/shard_map/ppermute | solution.py:32
  15.2 9.3 %collective-permute-start.5 = (f32[256,1]{1,0:T(8,128)S(1)}, f32[256,1]{1,0:T(8,128)S(1)}, u32[]{:S(2)}, u32[]{:S(2)}) collective-permute-start(f32[256,1]{1,0:T(8,128)S(1)} %add.100), channel_id=1, source_target_pairs={{0,2},{1,3},{2,0},{3,1},{4,6},{5,7},{6,4},{7,5},{8,10},{9,11},{10,... | collective-permute-start | bytes 3080 | tf_op jit(solution)/shard_map/ppermute | solution.py:32
  16.8 19.0 %collective-permute-start.1 = (bf16[256,256]{1,0:T(8,128)(2,1)S(1)}, bf16[256,256]{1,0:T(8,128)(2,1)S(1)}, u32[]{:S(2)}, u32[]{:S(2)}) collective-permute-start(bf16[256,256]{1,0:T(8,128)(2,1)S(1)} %collective-permute-done.refs_4_), channel_id=1, source_target_pairs={{0,2},{1,3},{2,0},{3,1},{4,6},{5,7},{6,4},{7,5},{8,10},{9,11},{10,... | collective-permute-start | bytes 393224 | tf_op jit(solution)/shard_map/ppermute | solution.py:32
  17.3 18.4 %collective-permute-start.2 = (bf16[256,256]{1,0:T(8,128)(2,1)S(1)}, bf16[256,256]{1,0:T(8,128)(2,1)S(1)}, u32[]{:S(2)}, u32[]{:S(2)}) collective-permute-start(bf16[256,256]{1,0:T(8,128)(2,1)S(1)} %collective-permute-done.refs_4_), channel_id=1, source_target_pairs={{0,4},{1,5},{2,6},{3,7},{4,0},{5,1},{6,2},{7,3},{8,12},{9,13},{10,... | collective-permute-start | bytes 393224 | tf_op jit(solution)/shard_map/ppermute | solution.py:32
  23.8 12.0 %collective-permute-start.3 = (bf16[256,256]{1,0:T(8,128)(2,1)S(1)}, bf16[256,256]{1,0:T(8,128)(2,1)S(1)}, u32[]{:S(2)}, u32[]{:S(2)}) collective-permute-start(bf16[256,256]{1,0:T(8,128)(2,1)S(1)} %collective-permute-done.refs_4_), channel_id=1, source_target_pairs={{0,6},{1,7},{2,4},{3,5},{4,2},{5,3},{6,0},{7,1},{8,14},{9,15},{10,... | collective-permute-start | bytes 393224 | tf_op jit(solution)/shard_map/ppermute | solution.py:32
  24.5 11.9 %collective-permute-start.6 = (f32[256,1]{1,0:T(8,128)S(1)}, f32[256,1]{1,0:T(8,128)S(1)}, u32[]{:S(2)}, u32[]{:S(2)}) collective-permute-start(f32[256,1]{1,0:T(8,128)S(1)} %add.101), channel_id=1, source_target_pairs={{0,4},{1,5},{2,6},{3,7},{4,0},{5,1},{6,2},{7,3},{8,12},{9,13},{10,... | collective-permute-start | bytes 3080 | tf_op jit(solution)/shard_map/ppermute | solution.py:32
  42.4 21.8 %collective-permute-start.13 = (bf16[256,256]{1,0:T(8,128)(2,1)}, bf16[256,256]{1,0:T(8,128)(2,1)S(1)}, u32[]{:S(2)}, u32[]{:S(2)}) collective-permute-start(bf16[256,256]{1,0:T(8,128)(2,1)} %get-tuple-element.83), channel_id=1, source_target_pairs={{0,16},{8,24},{16,0},{24,8},{1,17},{9,25},{17,1},{25,9},{2,18},{10... | collective-permute-start | bytes 393224 | tf_op jit(solution)/shard_map/ppermute | solution.py:32
  42.4 37.1 %collective-permute-start.12 = (bf16[2,256,256]{2,1,0:T(8,128)(2,1)}, bf16[2,256,256]{2,1,0:T(8,128)(2,1)S(1)}, u32[]{:S(2)}, u32[]{:S(2)}) collective-permute-start(bf16[2,256,256]{2,1,0:T(8,128)(2,1)} %get-tuple-element.79), channel_id=1, source_target_pairs={{0,16},{8,24},{16,0},{24,8},{1,17},{9,25},{17,1},{25,9},{2,18},{10... | collective-permute-start | bytes 786440 | tf_op jit(solution)/shard_map/ppermute | solution.py:32
  84.7 2.1 %collective-permute-start.14 = (bf16[4,256,256]{2,1,0:T(8,128)(2,1)}, bf16[4,256,256]{2,1,0:T(8,128)(2,1)S(1)}, u32[]{:S(2)}, u32[]{:S(2)}) collective-permute-start(bf16[4,256,256]{2,1,0:T(8,128)(2,1)} %get-tuple-element.91), channel_id=1, source_target_pairs={{0,1},{1,0},{2,3},{3,2},{4,5},{5,4},{6,7},{7,6},{8,9},{9,8},{10,11... | collective-permute-start | bytes 1572872 | tf_op jit(solution)/shard_map/ppermute | solution.py:32
  88.1 5.9 %collective-permute-start.15 = (bf16[256,256]{1,0:T(8,128)(2,1)S(1)}, bf16[256,256]{1,0:T(8,128)(2,1)S(1)}, u32[]{:S(2)}, u32[]{:S(2)}) collective-permute-start(bf16[256,256]{1,0:T(8,128)(2,1)S(1)} %get-tuple-element.167), channel_id=1, source_target_pairs={{0,2},{1,3},{2,0},{3,1},{4,6},{5,7},{6,4},{7,5},{8,10},{9,11},{10,... | collective-permute-start | bytes 393224 | tf_op jit(solution)/shard_map/ppermute | solution.py:32
  89.6 8.1 %collective-permute-start.16 = (bf16[256,256]{1,0:T(8,128)(2,1)S(1)}, bf16[256,256]{1,0:T(8,128)(2,1)S(1)}, u32[]{:S(2)}, u32[]{:S(2)}) collective-permute-start(bf16[256,256]{1,0:T(8,128)(2,1)S(1)} %get-tuple-element.169), channel_id=1, source_target_pairs={{0,4},{1,5},{2,6},{3,7},{4,0},{5,1},{6,2},{7,3},{8,12},{9,13},{10,... | collective-permute-start | bytes 393224 | tf_op jit(solution)/shard_map/ppermute | solution.py:32
  89.9 7.8 %collective-permute-start.17 = (bf16[256,256]{1,0:T(8,128)(2,1)S(1)}, bf16[256,256]{1,0:T(8,128)(2,1)S(1)}, u32[]{:S(2)}, u32[]{:S(2)}) collective-permute-start(bf16[256,256]{1,0:T(8,128)(2,1)S(1)} %get-tuple-element.168), channel_id=1, source_target_pairs={{0,6},{1,7},{2,4},{3,5},{4,2},{5,3},{6,0},{7,1},{8,14},{9,15},{10,... | collective-permute-start | bytes 393224 | tf_op jit(solution)/shard_map/ppermute | solution.py:32
  97.8 12.5 %collective-permute-start.25 = (bf16[256,256]{1,0:T(8,128)(2,1)S(1)}, bf16[256,256]{1,0:T(8,128)(2,1)S(1)}, u32[]{:S(2)}, u32[]{:S(2)}) collective-permute-start(bf16[256,256]{1,0:T(8,128)(2,1)S(1)} %fusion.4.refs_6_), channel_id=1, source_target_pairs={{0,16},{8,24},{16,0},{24,8},{1,17},{9,25},{17,1},{25,9},{2,18},{10... | collective-permute-start | bytes 393224 | tf_op jit(solution)/shard_map/ppermute | solution.py:32
  105.4 5.6 %collective-permute-start.19 = (bf16[256,256]{1,0:T(8,128)(2,1)S(1)}, bf16[256,256]{1,0:T(8,128)(2,1)S(1)}, u32[]{:S(2)}, u32[]{:S(2)}) collective-permute-start(bf16[256,256]{1,0:T(8,128)(2,1)S(1)} %fusion.4.refs_6_), channel_id=1, source_target_pairs={{0,2},{1,3},{2,0},{3,1},{4,6},{5,7},{6,4},{7,5},{8,10},{9,11},{10,... | collective-permute-start | bytes 393224 | tf_op jit(solution)/shard_map/ppermute | solution.py:32
  105.9 7.5 %collective-permute-start.21 = (bf16[256,256]{1,0:T(8,128)(2,1)S(1)}, bf16[256,256]{1,0:T(8,128)(2,1)S(1)}, u32[]{:S(2)}, u32[]{:S(2)}) collective-permute-start(bf16[256,256]{1,0:T(8,128)(2,1)S(1)} %fusion.4.refs_6_), channel_id=1, source_target_pairs={{0,4},{1,5},{2,6},{3,7},{4,0},{5,1},{6,2},{7,3},{8,12},{9,13},{10,... | collective-permute-start | bytes 393224 | tf_op jit(solution)/shard_map/ppermute | solution.py:32
  107.1 7.1 %collective-permute-start.23 = (bf16[256,256]{1,0:T(8,128)(2,1)S(1)}, bf16[256,256]{1,0:T(8,128)(2,1)S(1)}, u32[]{:S(2)}, u32[]{:S(2)}) collective-permute-start(bf16[256,256]{1,0:T(8,128)(2,1)S(1)} %fusion.4.refs_6_), channel_id=1, source_target_pairs={{0,6},{1,7},{2,4},{3,5},{4,2},{5,3},{6,0},{7,1},{8,14},{9,15},{10,... | collective-permute-start | bytes 393224 | tf_op jit(solution)/shard_map/ppermute | solution.py:32
  108.8 6.6 %collective-permute-start.18 = (bf16[256,256]{1,0:T(8,128)(2,1)S(1)}, bf16[256,256]{1,0:T(8,128)(2,1)S(1)}, u32[]{:S(2)}, u32[]{:S(2)}) collective-permute-start(bf16[256,256]{1,0:T(8,128)(2,1)S(1)} %fusion.4.refs_6_), channel_id=1, source_target_pairs={{0,1},{1,0},{2,3},{3,2},{4,5},{5,4},{6,7},{7,6},{8,9},{9,8},{10,11... | collective-permute-start | bytes 393224 | tf_op jit(solution)/shard_map/ppermute | solution.py:32
  110.3 6.7 %collective-permute-start.33 = (bf16[256,256]{1,0:T(8,128)(2,1)S(1)}, bf16[256,256]{1,0:T(8,128)(2,1)S(1)}, u32[]{:S(2)}, u32[]{:S(2)}) collective-permute-start(bf16[256,256]{1,0:T(8,128)(2,1)S(1)} %fusion.4.refs_6_), channel_id=1, source_target_pairs={{0,8},{8,0},{16,24},{24,16},{1,9},{9,1},{17,25},{25,17},{2,10},{10... | collective-permute-start | bytes 393224 | tf_op jit(solution)/shard_map/ppermute | solution.py:32
  111.0 7.8 %collective-permute-start.34 = (bf16[256,256]{1,0:T(8,128)(2,1)S(1)}, bf16[256,256]{1,0:T(8,128)(2,1)S(1)}, u32[]{:S(2)}, u32[]{:S(2)}) collective-permute-start(bf16[256,256]{1,0:T(8,128)(2,1)S(1)} %fusion.4.refs_6_), channel_id=1, source_target_pairs={{0,24},{8,16},{16,8},{24,0},{1,25},{9,17},{17,9},{25,1},{2,26},{10... | collective-permute-start | bytes 393224 | tf_op jit(solution)/shard_map/ppermute | solution.py:32
  113.4 5.4 %collective-permute-start.27 = (bf16[256,256]{1,0:T(8,128)(2,1)S(1)}, bf16[256,256]{1,0:T(8,128)(2,1)S(1)}, u32[]{:S(2)}, u32[]{:S(2)}) collective-permute-start(bf16[256,256]{1,0:T(8,128)(2,1)S(1)} %collective-permute-done.25.refs_14_), channel_id=1, source_target_pairs={{0,2},{1,3},{2,0},{3,1},{4,6},{5,7},{6,4},{7,5},{8,10},{9,11},{10,... | collective-permute-start | bytes 393224 | tf_op jit(solution)/shard_map/ppermute | solution.py:32
  114.2 5.2 %collective-permute-start.29 = (bf16[256,256]{1,0:T(8,128)(2,1)S(1)}, bf16[256,256]{1,0:T(8,128)(2,1)S(1)}, u32[]{:S(2)}, u32[]{:S(2)}) collective-permute-start(bf16[256,256]{1,0:T(8,128)(2,1)S(1)} %collective-permute-done.25.refs_14_), channel_id=1, source_target_pairs={{0,4},{1,5},{2,6},{3,7},{4,0},{5,1},{6,2},{7,3},{8,12},{9,13},{10,... | collective-permute-start | bytes 393224 | tf_op jit(solution)/shard_map/ppermute | solution.py:32
  115.4 5.9 %collective-permute-start.31 = (bf16[256,256]{1,0:T(8,128)(2,1)S(1)}, bf16[256,256]{1,0:T(8,128)(2,1)S(1)}, u32[]{:S(2)}, u32[]{:S(2)}) collective-permute-start(bf16[256,256]{1,0:T(8,128)(2,1)S(1)} %collective-permute-done.25.refs_14_), channel_id=1, source_target_pairs={{0,6},{1,7},{2,4},{3,5},{4,2},{5,3},{6,0},{7,1},{8,14},{9,15},{10,... | collective-permute-start | bytes 393224 | tf_op jit(solution)/shard_map/ppermute | solution.py:32
  116.9 4.4 %collective-permute-start.26 = (bf16[256,256]{1,0:T(8,128)(2,1)S(1)}, bf16[256,256]{1,0:T(8,128)(2,1)S(1)}, u32[]{:S(2)}, u32[]{:S(2)}) collective-permute-start(bf16[256,256]{1,0:T(8,128)(2,1)S(1)} %collective-permute-done.25.refs_14_), channel_id=1, source_target_pairs={{0,1},{1,0},{2,3},{3,2},{4,5},{5,4},{6,7},{7,6},{8,9},{9,8},{10,11... | collective-permute-start | bytes 393224 | tf_op jit(solution)/shard_map/ppermute | solution.py:32
  118.8 3.0 %collective-permute-start.20 = (bf16[256,256]{1,0:T(8,128)(2,1)S(1)}, bf16[256,256]{1,0:T(8,128)(2,1)S(1)}, u32[]{:S(2)}, u32[]{:S(2)}) collective-permute-start(bf16[256,256]{1,0:T(8,128)(2,1)S(1)} %collective-permute-done.19.refs_8_), channel_id=1, source_target_pairs={{0,1},{1,0},{2,3},{3,2},{4,5},{5,4},{6,7},{7,6},{8,9},{9,8},{10,11... | collective-permute-start | bytes 393224 | tf_op jit(solution)/shard_map/ppermute | solution.py:32
  118.8 3.7 %collective-permute-start.22 = (bf16[256,256]{1,0:T(8,128)(2,1)S(1)}, bf16[256,256]{1,0:T(8,128)(2,1)S(1)}, u32[]{:S(2)}, u32[]{:S(2)}) collective-permute-start(bf16[256,256]{1,0:T(8,128)(2,1)S(1)} %collective-permute-done.21.refs_10_), channel_id=1, source_target_pairs={{0,1},{1,0},{2,3},{3,2},{4,5},{5,4},{6,7},{7,6},{8,9},{9,8},{10,11... | collective-permute-start | bytes 393224 | tf_op jit(solution)/shard_map/ppermute | solution.py:32
  119.3 3.2 %collective-permute-start.24 = (bf16[256,256]{1,0:T(8,128)(2,1)S(1)}, bf16[256,256]{1,0:T(8,128)(2,1)S(1)}, u32[]{:S(2)}, u32[]{:S(2)}) collective-permute-start(bf16[256,256]{1,0:T(8,128)(2,1)S(1)} %collective-permute-done.23.refs_12_), channel_id=1, source_target_pairs={{0,1},{1,0},{2,3},{3,2},{4,5},{5,4},{6,7},{7,6},{8,9},{9,8},{10,11... | collective-permute-start | bytes 393224 | tf_op jit(solution)/shard_map/ppermute | solution.py:32
  123.2 16.6 %collective-permute-start.35 = (bf16[2,256,256]{2,1,0:T(8,128)(2,1)S(1)}, bf16[2,256,256]{2,1,0:T(8,128)(2,1)S(1)}, u32[]{:S(2)}, u32[]{:S(2)}) collective-permute-start(bf16[2,256,256]{2,1,0:T(8,128)(2,1)S(1)} %pad_maximum_fusion.refs_6_), channel_id=1, source_target_pairs={{0,2},{1,3},{2,0},{3,1},{4,6},{5,7},{6,4},{7,5},{8,10},{9,11},{10,... | collective-permute-start | bytes 786440 | tf_op jit(solution)/shard_map/ppermute | solution.py:32
  123.8 16.0 %collective-permute-start.36 = (bf16[2,256,256]{2,1,0:T(8,128)(2,1)S(1)}, bf16[2,256,256]{2,1,0:T(8,128)(2,1)S(1)}, u32[]{:S(2)}, u32[]{:S(2)}) collective-permute-start(bf16[2,256,256]{2,1,0:T(8,128)(2,1)S(1)} %pad_maximum_fusion.refs_6_), channel_id=1, source_target_pairs={{0,4},{1,5},{2,6},{3,7},{4,0},{5,1},{6,2},{7,3},{8,12},{9,13},{10,... | collective-permute-start | bytes 786440 | tf_op jit(solution)/shard_map/ppermute | solution.py:32
  125.2 14.6 %collective-permute-start.37 = (bf16[2,256,256]{2,1,0:T(8,128)(2,1)S(1)}, bf16[2,256,256]{2,1,0:T(8,128)(2,1)S(1)}, u32[]{:S(2)}, u32[]{:S(2)}) collective-permute-start(bf16[2,256,256]{2,1,0:T(8,128)(2,1)S(1)} %pad_maximum_fusion.refs_6_), channel_id=1, source_target_pairs={{0,6},{1,7},{2,4},{3,5},{4,2},{5,3},{6,0},{7,1},{8,14},{9,15},{10,... | collective-permute-start | bytes 786440 | tf_op jit(solution)/shard_map/ppermute | solution.py:32
  139.8 3.6 %collective-permute-start.42 = (bf16[4,2,256,256]{3,2,1,0:T(8,128)(2,1)}, bf16[4,2,256,256]{3,2,1,0:T(8,128)(2,1)S(1)}, u32[]{:S(2)}, u32[]{:S(2)}) collective-permute-start(bf16[4,2,256,256]{3,2,1,0:T(8,128)(2,1)} %get-tuple-element.118), channel_id=1, source_target_pairs={{0,1},{1,0},{2,3},{3,2},{4,5},{5,4},{6,7},{7,6},{8,9},{9,8},{10,11... | collective-permute-start | bytes 3145736 | tf_op jit(solution)/shard_map/ppermute | solution.py:32
  139.9 5.1 %collective-permute-start.38 = (bf16[2,256,256]{2,1,0:T(8,128)(2,1)S(1)}, bf16[2,256,256]{2,1,0:T(8,128)(2,1)S(1)}, u32[]{:S(2)}, u32[]{:S(2)}) collective-permute-start(bf16[2,256,256]{2,1,0:T(8,128)(2,1)S(1)} %pad_maximum_fusion.refs_6_), channel_id=1, source_target_pairs={{0,1},{1,0},{2,3},{3,2},{4,5},{5,4},{6,7},{7,6},{8,9},{9,8},{10,11... | collective-permute-start | bytes 786440 | tf_op jit(solution)/shard_map/ppermute | solution.py:32
  140.4 4.7 %collective-permute-start.39 = (bf16[2,256,256]{2,1,0:T(8,128)(2,1)S(1)}, bf16[2,256,256]{2,1,0:T(8,128)(2,1)S(1)}, u32[]{:S(2)}, u32[]{:S(2)}) collective-permute-start(bf16[2,256,256]{2,1,0:T(8,128)(2,1)S(1)} %collective-permute-done.35.refs_8_), channel_id=1, source_target_pairs={{0,1},{1,0},{2,3},{3,2},{4,5},{5,4},{6,7},{7,6},{8,9},{9,8},{10,11... | collective-permute-start | bytes 786440 | tf_op jit(solution)/shard_map/ppermute | solution.py:32
  140.5 4.6 %collective-permute-start.40 = (bf16[2,256,256]{2,1,0:T(8,128)(2,1)S(1)}, bf16[2,256,256]{2,1,0:T(8,128)(2,1)S(1)}, u32[]{:S(2)}, u32[]{:S(2)}) collective-permute-start(bf16[2,256,256]{2,1,0:T(8,128)(2,1)S(1)} %collective-permute-done.36.refs_10_), channel_id=1, source_target_pairs={{0,1},{1,0},{2,3},{3,2},{4,5},{5,4},{6,7},{7,6},{8,9},{9,8},{10,11... | collective-permute-start | bytes 786440 | tf_op jit(solution)/shard_map/ppermute | solution.py:32
  140.9 4.2 %collective-permute-start.41 = (bf16[2,256,256]{2,1,0:T(8,128)(2,1)S(1)}, bf16[2,256,256]{2,1,0:T(8,128)(2,1)S(1)}, u32[]{:S(2)}, u32[]{:S(2)}) collective-permute-start(bf16[2,256,256]{2,1,0:T(8,128)(2,1)S(1)} %collective-permute-done.37.refs_12_), channel_id=1, source_target_pairs={{0,1},{1,0},{2,3},{3,2},{4,5},{5,4},{6,7},{7,6},{8,9},{9,8},{10,11... | collective-permute-start | bytes 786440 | tf_op jit(solution)/shard_map/ppermute | solution.py:32
  145.2 16.6 %collective-permute-start.43 = (bf16[2,256,256]{2,1,0:T(8,128)(2,1)S(1)}, bf16[2,256,256]{2,1,0:T(8,128)(2,1)S(1)}, u32[]{:S(2)}, u32[]{:S(2)}) collective-permute-start(bf16[2,256,256]{2,1,0:T(8,128)(2,1)S(1)} %get-tuple-element.129), channel_id=1, source_target_pairs={{0,2},{1,3},{2,0},{3,1},{4,6},{5,7},{6,4},{7,5},{8,10},{9,11},{10,... | collective-permute-start | bytes 786440 | tf_op jit(solution)/shard_map/ppermute | solution.py:32
  145.9 15.8 %collective-permute-start.44 = (bf16[2,256,256]{2,1,0:T(8,128)(2,1)S(1)}, bf16[2,256,256]{2,1,0:T(8,128)(2,1)S(1)}, u32[]{:S(2)}, u32[]{:S(2)}) collective-permute-start(bf16[2,256,256]{2,1,0:T(8,128)(2,1)S(1)} %get-tuple-element.130), channel_id=1, source_target_pairs={{0,4},{1,5},{2,6},{3,7},{4,0},{5,1},{6,2},{7,3},{8,12},{9,13},{10,... | collective-permute-start | bytes 786440 | tf_op jit(solution)/shard_map/ppermute | solution.py:32
  147.3 14.4 %collective-permute-start.45 = (bf16[2,256,256]{2,1,0:T(8,128)(2,1)S(1)}, bf16[2,256,256]{2,1,0:T(8,128)(2,1)S(1)}, u32[]{:S(2)}, u32[]{:S(2)}) collective-permute-start(bf16[2,256,256]{2,1,0:T(8,128)(2,1)S(1)} %get-tuple-element.131), channel_id=1, source_target_pairs={{0,6},{1,7},{2,4},{3,5},{4,2},{5,3},{6,0},{7,1},{8,14},{9,15},{10,... | collective-permute-start | bytes 786440 | tf_op jit(solution)/shard_map/ppermute | solution.py:32
  161.7 2.9 %collective-permute-start.46 = (bf16[4,2,256,256]{3,2,1,0:T(8,128)(2,1)}, bf16[4,2,256,256]{3,2,1,0:T(8,128)(2,1)S(1)}, u32[]{:S(2)}, u32[]{:S(2)}) collective-permute-start(bf16[4,2,256,256]{3,2,1,0:T(8,128)(2,1)} %get-tuple-element.133), channel_id=1, source_target_pairs={{0,1},{1,0},{2,3},{3,2},{4,5},{5,4},{6,7},{7,6},{8,9},{9,8},{10,11... | collective-permute-start | bytes 3145736 | tf_op jit(solution)/shard_map/ppermute | solution.py:32
  161.9 9.7 %collective-permute-start.49 = (bf16[256,256]{1,0:T(8,128)(2,1)S(1)}, bf16[256,256]{1,0:T(8,128)(2,1)S(1)}, u32[]{:S(2)}, u32[]{:S(2)}) collective-permute-start(bf16[256,256]{1,0:T(8,128)(2,1)S(1)} %fusion.15), channel_id=1, source_target_pairs={{0,16},{8,24},{16,0},{24,8},{1,17},{9,25},{17,1},{25,9},{2,18},{10... | collective-permute-start | bytes 393224 | tf_op jit(solution)/shard_map/ppermute | solution.py:32
  165.1 8.4 %collective-permute-start.48 = (bf16[2,256,256]{2,1,0:T(8,128)(2,1)S(1)}, bf16[2,256,256]{2,1,0:T(8,128)(2,1)S(1)}, u32[]{:S(2)}, u32[]{:S(2)}) collective-permute-start(bf16[2,256,256]{2,1,0:T(8,128)(2,1)S(1)} %pad_maximum_fusion.2), channel_id=1, source_target_pairs={{0,4},{1,5},{2,6},{3,7},{4,0},{5,1},{6,2},{7,3},{8,12},{9,13},{10,... | collective-permute-start | bytes 786440 | tf_op jit(solution)/shard_map/ppermute | solution.py:32
  165.9 8.1 %collective-permute-start.47 = (bf16[2,256,256]{2,1,0:T(8,128)(2,1)S(1)}, bf16[2,256,256]{2,1,0:T(8,128)(2,1)S(1)}, u32[]{:S(2)}, u32[]{:S(2)}) collective-permute-start(bf16[2,256,256]{2,1,0:T(8,128)(2,1)S(1)} %pad_maximum_fusion.1), channel_id=1, source_target_pairs={{0,2},{1,3},{2,0},{3,1},{4,6},{5,7},{6,4},{7,5},{8,10},{9,11},{10,... | collective-permute-start | bytes 786440 | tf_op jit(solution)/shard_map/ppermute | solution.py:32
  174.2 5.0 %collective-permute-start.50 = (bf16[1,256,256]{2,1,0:T(8,128)(2,1)S(1)}, bf16[1,256,256]{2,1,0:T(8,128)(2,1)S(1)}, u32[]{:S(2)}, u32[]{:S(2)}) collective-permute-start(bf16[1,256,256]{2,1,0:T(8,128)(2,1)S(1)} %get-tuple-element.139), channel_id=1, source_target_pairs={{0,4},{1,5},{2,6},{3,7},{4,0},{5,1},{6,2},{7,3},{8,12},{9,13},{10,... | collective-permute-start | bytes 393224 | tf_op jit(solution)/shard_map/ppermute | solution.py:32
  175.5 5.0 %collective-permute-start.52 = (bf16[1,256,256]{2,1,0:T(8,128)(2,1)S(1)}, bf16[1,256,256]{2,1,0:T(8,128)(2,1)S(1)}, u32[]{:S(2)}, u32[]{:S(2)}) collective-permute-start(bf16[1,256,256]{2,1,0:T(8,128)(2,1)S(1)} %get-tuple-element.140), channel_id=1, source_target_pairs={{0,2},{1,3},{2,0},{3,1},{4,6},{5,7},{6,4},{7,5},{8,10},{9,11},{10,... | collective-permute-start | bytes 393224 | tf_op jit(solution)/shard_map/ppermute | solution.py:32
  180.6 5.8 %collective-permute-start.51 = (bf16[256,256]{1,0:T(8,128)(2,1)S(1)}, bf16[256,256]{1,0:T(8,128)(2,1)S(1)}, u32[]{:S(2)}, u32[]{:S(2)}) collective-permute-start(bf16[256,256]{1,0:T(8,128)(2,1)S(1)} %get-tuple-element.150), channel_id=1, source_target_pairs={{0,8},{8,0},{16,24},{24,16},{1,9},{9,1},{17,25},{25,17},{2,10},{10... | collective-permute-start | bytes 393224 | tf_op jit(solution)/shard_map/ppermute | solution.py:32
  181.5 6.9 %collective-permute-start.53 = (bf16[256,256]{1,0:T(8,128)(2,1)S(1)}, bf16[256,256]{1,0:T(8,128)(2,1)S(1)}, u32[]{:S(2)}, u32[]{:S(2)}) collective-permute-start(bf16[256,256]{1,0:T(8,128)(2,1)S(1)} %get-tuple-element.151), channel_id=1, source_target_pairs={{0,24},{8,16},{16,8},{24,0},{1,25},{9,17},{17,9},{25,1},{2,26},{10... | collective-permute-start | bytes 393224 | tf_op jit(solution)/shard_map/ppermute | solution.py:32
  (48 other events, 317.4 us)
Sparse Core Ops, SparseCore 0:
  37.7 42.2 all-gather.1

commit v8 on v7

--- a/solution.py
+++ b/solution.py
@@ -287,7 +287,6 @@
     ]
     moved = lax.ppermute(tokens, ("gx", "gy"), route)
     other_weight = swap(weight, "gx", 1)
-    output_weight, moved = lax.optimization_barrier((output_weight, moved))
     experts = gate_up_weight.shape[0]
     units = gate_up_weight.shape[3]
     output_full = lax.all_gather(output_weight, "gx", axis=0, tiled=True)

time: 195 us -> 199 us (1.021)
  Pallas kernels: 45.3 us -> 52.9 us
  waiting for transfers between devices: 54.9 us -> 51.9 us
  starting transfers between devices: 57.7 us -> 54.9 us
    pallas_call x1, Pallas kernels: 11.3 us -> 18.9 us  [per_device(): pl.pallas_call(lambda *refs: cache_kernel(requests, draft, heads, terms_o...]
    ppermute x53, starting transfers between devices: 56.1 us -> 53.3 us  [swap(): lax.ppermute(value, axis, [(one, one ^ mask) for one in range(count)])]
    ppermute x53, waiting for transfers between devices: 54.5 us -> 51.8 us  [swap(): lax.ppermute(value, axis, [(one, one ^ mask) for one in range(count)])]
  transfers between devices with their start and end apart: 55 -> 55, of which waited for: 24 -> 23; matrix products, arithmetic and copies ran while one was open for 10% -> 10% of each run, Pallas kernels for 21% -> 24%
where the time goes in v8:
time: 199 us; the launch traced here: 198 us
  starting transfers between devices  54.9 us (28%)
  Pallas kernels  52.9 us (27%)
  waiting for transfers between devices  51.9 us (26%)
  between operations  14.8 us (7%)
  local copies, waits for them, and re-layouts  11.8 us (6%)
  other arithmetic  10.1 us (5%)
    ppermute x53, starting transfers between devices, swap(): lax.ppermute(value, axis, [(one, one ^ mask) for one in range(count)])  53.3 us
    ppermute x53, waiting for transfers between devices, swap(): lax.ppermute(value, axis, [(one, one ^ mask) for one in range(count)])  51.8 us
    pallas_call x2, Pallas kernels, per_device(): pl.pallas_call(lambda *refs: expert_kernel(gy_count, masks, number > 0, *...  25.9 us
    pallas_call x1, Pallas kernels, per_device(): pl.pallas_call(lambda *refs: cache_kernel(requests, draft, heads, terms_o...  18.9 us
    unnamed x84, local copies, waits for them, and re-layouts  10.9 us
    pallas_call x1, Pallas kernels, per_device(): pl.pallas_call(lambda *refs: draft_kernel(requests, draft, heads, terms_o...  4.48 us
  transfers between devices with their start and end apart: 55, of which 23 were waited for; matrix products, arithmetic and copies ran while one was open for 10% of the time, Pallas kernels for 24%

profile of v8, /device:TPU:0, one launch (start us, length us, event | category | flops | bytes accessed | tf_op | source)
XLA Modules:
  0.0 198.0 jit_solution(7550850136435132849)
XLA Ops:
  7.2 1.6 collective-permute-start
  8.8 3.0 %collective-permute-start.7 = (bf16[3,512,256]{2,1,0:T(8,128)(2,1)}, bf16[3,512,256]{2,1,0:T(8,128)(2,1)S(1)}, u32[]{:S(2)}, u32[]{:S(2)}) collective-permute-start(bf16[3,512,256]{2,1,0:T(8,128)(2,1)} %bitcast.94), channel_id=1, source_target_pairs={{0,8},{8,0},{16,24},{24,16},{1,9},{9,1},{17,25},{25,17},{2,10},{10... | collective-permute-start | bytes 2359304 | tf_op jit(solution)/shard_map/ppermute | solution.py:32
  11.8 1.0 fusion
  15.2 1.6 collective-permute-start.5
  17.3 6.4 %collective-permute-start.2 = (bf16[256,256]{1,0:T(8,128)(2,1)S(1)}, bf16[256,256]{1,0:T(8,128)(2,1)S(1)}, u32[]{:S(2)}, u32[]{:S(2)}) collective-permute-start(bf16[256,256]{1,0:T(8,128)(2,1)S(1)} %collective-permute-done.refs_4_), channel_id=1, source_target_pairs={{0,4},{1,5},{2,6},{3,7},{4,0},{5,1},{6,2},{7,3},{8,12},{9,13},{10,... | collective-permute-start | bytes 393224 | tf_op jit(solution)/shard_map/ppermute | solution.py:32
  24.5 2.1 %collective-permute-start.6 = (f32[256,1]{1,0:T(8,128)S(1)}, f32[256,1]{1,0:T(8,128)S(1)}, u32[]{:S(2)}, u32[]{:S(2)}) collective-permute-start(f32[256,1]{1,0:T(8,128)S(1)} %add.101), channel_id=1, source_target_pairs={{0,4},{1,5},{2,6},{3,7},{4,0},{5,1},{6,2},{7,3},{8,12},{9,13},{10,... | collective-permute-start | bytes 3080 | tf_op jit(solution)/shard_map/ppermute | solution.py:32
  27.2 7.9 %copy.30 = bf16[4,2048,2,256]{3,1,0,2:T(8,128)(2,1)} copy(bf16[4,2048,2,256]{3,2,1,0:T(2,128)(2,1)} %param.24) | data formatting | bytes 16777216 | tf_op args[10]
  37.9 8.2 %collective-permute-done.7.refs_3_ = bf16[3,512,256]{2,1,0:T(8,128)(2,1)S(1)} collective-permute-done((bf16[3,512,256]{2,1,0:T(8,128)(2,1)}, bf16[3,512,256]{2,1,0:T(8,128)(2,1)S(1)}, u32[]{:S(2)}, u32[]{:S(2)}) %collective-permute-start.7) | collective-permute-done | bytes 786464 | tf_op jit(solution)/shard_map/ppermute | solution.py:32
  47.0 3.6 %project.1 = (f32[256,256]{1,0:T(8,128)}, bf16[256,256]{1,0:T(8,128)(2,1)}, f32[2,256,256]{2,1,0:T(8,128)}, bf16[2,256,256]{2,1,0:T(8,128)(2,1)}) custom-call(s32[2]{0:T(128)} %pad_add_fusion.refs_0_, f32[1,2048]{1,0:T(1,128)} %bitcast.99, bf16[3,512,256]{2,1,0:T(8,128)(2,1)} %bitcast.95, bf16[3,512,256]{2,1,0:T(8,128)(2,1)} %copy-done.1, ...), custom_call_target="tpu_custom_call" | custom-call | tf_op jit(solution)/shard_map/project/pallas_call | solution.py:297
  50.5 2.9 %collective-permute-start.13 = (bf16[256,256]{1,0:T(8,128)(2,1)}, bf16[256,256]{1,0:T(8,128)(2,1)S(1)}, u32[]{:S(2)}, u32[]{:S(2)}) collective-permute-start(bf16[256,256]{1,0:T(8,128)(2,1)} %get-tuple-element.80), channel_id=1, source_target_pairs={{0,16},{8,24},{16,0},{24,8},{1,17},{9,25},{17,1},{25,9},{2,18},{10... | collective-permute-start | bytes 393224 | tf_op jit(solution)/shard_map/ppermute | solution.py:32
  55.3 8.8 %collective-permute-done.13.refs_6_ = bf16[256,256]{1,0:T(8,128)(2,1)S(1)} collective-permute-done((bf16[256,256]{1,0:T(8,128)(2,1)}, bf16[256,256]{1,0:T(8,128)(2,1)S(1)}, u32[]{:S(2)}, u32[]{:S(2)}) %collective-permute-start.13) | collective-permute-done | bytes 131104 | tf_op jit(solution)/shard_map/ppermute | solution.py:32
  64.7 18.9 %cache.1 = (f32[512,128]{1,0:T(8,128)}, f32[512,128]{1,0:T(8,128)}, f32[512,256]{1,0:T(8,128)}, bf16[256,256]{1,0:T(8,128)(2,1)}) custom-call(s32[2]{0:T(128)} %refs_0_.1, s32[2]{0:T(128)} %get-tuple-element.145.refs_1_, s32[2]{0:T(128)} %get-tuple-element.144.refs_2_, s32[4]{0:T(128)} %convert_reduce_fusion.refs_3_.refs_1_, ...), custom_call_target="tpu_custom_call" | custom-call | flops 10737418240 | bytes 16777216 | tf_op jit(solution)/shard_map/cache/pallas_call | solution.py:330
  84.2 4.5 %draft.1 = (bf16[4,256,256]{2,1,0:T(8,128)(2,1)}, bf16[4,256,256]{2,1,0:T(8,128)(2,1)}, bf16[2,32,256]{2,1,0:T(8,128)(2,1)}) custom-call(s32[2]{0:T(128)} %pad_add_fusion.refs_0_, s32[4]{0:T(128)} %convert_reduce_fusion.refs_3_.refs_1_, f32[256,1]{1,0:T(8,128)} %add_rsqrt_fusion.refs_4_.refs_2_, f32[2,256,256]{2,1,0:T(8,128)} %get-tuple-element.75.refs_3_, ...), custom_call_target="tpu_custom_call" | custom-call | tf_op jit(solution)/shard_map/draft/pallas_call | solution.py:372
  88.7 2.1 %collective-permute-done.14 = bf16[4,256,256]{2,1,0:T(8,128)(2,1)S(1)} collective-permute-done((bf16[4,256,256]{2,1,0:T(8,128)(2,1)}, bf16[4,256,256]{2,1,0:T(8,128)(2,1)S(1)}, u32[]{:S(2)}, u32[]{:S(2)}) %collective-permute-start.14) | collective-permute-done | bytes 524320 | tf_op jit(solution)/shard_map/ppermute | solution.py:32
  90.8 1.2 fusion.36
  92.1 1.6 collective-permute-start.15
  93.6 5.8 %collective-permute-start.16 = (bf16[256,256]{1,0:T(8,128)(2,1)S(1)}, bf16[256,256]{1,0:T(8,128)(2,1)S(1)}, u32[]{:S(2)}, u32[]{:S(2)}) collective-permute-start(bf16[256,256]{1,0:T(8,128)(2,1)S(1)} %get-tuple-element.165), channel_id=1, source_target_pairs={{0,4},{1,5},{2,6},{3,7},{4,0},{5,1},{6,2},{7,3},{8,12},{9,13},{10,... | collective-permute-start | bytes 393224 | tf_op jit(solution)/shard_map/ppermute | solution.py:32
  99.4 5.6 %collective-permute-done.16 = bf16[256,256]{1,0:T(8,128)(2,1)S(1)} collective-permute-done((bf16[256,256]{1,0:T(8,128)(2,1)S(1)}, bf16[256,256]{1,0:T(8,128)(2,1)S(1)}, u32[]{:S(2)}, u32[]{:S(2)}) %collective-permute-start.16) | collective-permute-done | bytes 131104 | tf_op jit(solution)/shard_map/ppermute | solution.py:32
  105.9 1.5 collective-permute-start.19
  108.2 1.2 collective-permute-start.23
  109.4 2.3 %collective-permute-done.25.refs_14_ = bf16[256,256]{1,0:T(8,128)(2,1)S(1)} collective-permute-done((bf16[256,256]{1,0:T(8,128)(2,1)S(1)}, bf16[256,256]{1,0:T(8,128)(2,1)S(1)}, u32[]{:S(2)}, u32[]{:S(2)}) %collective-permute-start.25) | collective-permute-done | bytes 131104 | tf_op jit(solution)/shard_map/ppermute | solution.py:32
  111.7 2.1 %collective-permute-start.34 = (bf16[256,256]{1,0:T(8,128)(2,1)S(1)}, bf16[256,256]{1,0:T(8,128)(2,1)S(1)}, u32[]{:S(2)}, u32[]{:S(2)}) collective-permute-start(bf16[256,256]{1,0:T(8,128)(2,1)S(1)} %fusion.4.refs_6_), channel_id=1, source_target_pairs={{0,24},{8,16},{16,8},{24,0},{1,25},{9,17},{17,9},{25,1},{2,26},{10... | collective-permute-start | bytes 393224 | tf_op jit(solution)/shard_map/ppermute | solution.py:32
  114.6 1.1 collective-permute-start.27
  115.7 1.0 collective-permute-start.29
  116.8 1.4 collective-permute-start.31
  118.1 2.4 %collective-permute-done.34 = bf16[256,256]{1,0:T(8,128)(2,1)S(1)} collective-permute-done((bf16[256,256]{1,0:T(8,128)(2,1)S(1)}, bf16[256,256]{1,0:T(8,128)(2,1)S(1)}, u32[]{:S(2)}, u32[]{:S(2)}) %collective-permute-start.34) | collective-permute-done | bytes 131104 | tf_op jit(solution)/shard_map/ppermute | solution.py:32
  121.1 2.3 %collective-permute-done.29.refs_18_ = bf16[256,256]{1,0:T(8,128)(2,1)S(1)} collective-permute-done((bf16[256,256]{1,0:T(8,128)(2,1)S(1)}, bf16[256,256]{1,0:T(8,128)(2,1)S(1)}, u32[]{:S(2)}, u32[]{:S(2)}) %collective-permute-start.29) | collective-permute-done | bytes 131104 | tf_op jit(solution)/shard_map/ppermute | solution.py:32
  125.4 1.1 collective-permute-start.35
  126.5 1.0 collective-permute-start.36
  127.5 1.4 collective-permute-start.37
  129.0 13.0 %experts.2 = (bf16[4,2,256,256]{3,2,1,0:T(8,128)(2,1)}, bf16[4,2,256,256]{3,2,1,0:T(8,128)(2,1)}) custom-call(s32[2]{0:T(128)} %pad_add_fusion.refs_0_, f32[1,2048]{1,0:T(1,128)} %bitcast.105, s32[8,1024]{1,0:T(8,128)} %bitcast.103, f32[8,1024]{1,0:T(8,128)} %convert_bitcast_fusion.refs_3_, bf16[2,4,2048,256]{3,2,1,0:T(8,128)(2,1)} %bitcast.92, ...), custom_call_target="tpu_custom_call" | custom-call | flops 6442450944 | bytes 12582912 | tf_op jit(solution)/shard_map/experts/pallas_call | solution.py:422
  143.3 2.4 %collective-permute-done.42 = bf16[4,2,256,256]{3,2,1,0:T(8,128)(2,1)S(1)} collective-permute-done((bf16[4,2,256,256]{3,2,1,0:T(8,128)(2,1)}, bf16[4,2,256,256]{3,2,1,0:T(8,128)(2,1)S(1)}, u32[]{:S(2)}, u32[]{:S(2)}) %collective-permute-start.42) | collective-permute-done | bytes 1048608 | tf_op jit(solution)/shard_map/ppermute | solution.py:32
  145.6 1.5 fusion.37
  147.4 1.2 collective-permute-start.43
  149.6 1.4 collective-permute-start.45
  151.0 13.0 %experts.3 = (bf16[4,2,256,256]{3,2,1,0:T(8,128)(2,1)}, bf16[4,2,256,256]{3,2,1,0:T(8,128)(2,1)}) custom-call(s32[2]{0:T(128)} %pad_add_fusion.refs_0_, f32[1,2048]{1,0:T(1,128)} %bitcast.106, s32[8,1024]{1,0:T(8,128)} %bitcast.104, f32[8,1024]{1,0:T(8,128)} %convert_bitcast_fusion.refs_3_, bf16[2,4,2048,256]{3,2,1,0:T(8,128)(2,1)} %bitcast.93, ...), custom_call_target="tpu_custom_call" | custom-call | flops 6442450944 | bytes 12582912 | tf_op jit(solution)/shard_map/experts/pallas_call | solution.py:422
  164.2 1.7 collective-permute-start.49
  165.9 1.0 collective-permute-done.46
  167.3 1.1 collective-permute-start.48
  168.5 1.1 collective-permute-start.47
  169.6 3.9 %collective-permute-done.49 = bf16[256,256]{1,0:T(8,128)(2,1)S(1)} collective-permute-done((bf16[256,256]{1,0:T(8,128)(2,1)S(1)}, bf16[256,256]{1,0:T(8,128)(2,1)S(1)}, u32[]{:S(2)}, u32[]{:S(2)}) %collective-permute-start.49) | collective-permute-done | bytes 131104 | tf_op jit(solution)/shard_map/ppermute | solution.py:32
  173.5 2.2 %collective-permute-done.48 = bf16[2,256,256]{2,1,0:T(8,128)(2,1)S(1)} collective-permute-done((bf16[2,256,256]{2,1,0:T(8,128)(2,1)S(1)}, bf16[2,256,256]{2,1,0:T(8,128)(2,1)S(1)}, u32[]{:S(2)}, u32[]{:S(2)}) %collective-permute-start.48) | collective-permute-done | bytes 262176 | tf_op jit(solution)/shard_map/ppermute | solution.py:32
  176.7 1.0 collective-permute-start.50
  177.7 1.1 collective-permute-start.52
  178.9 2.9 %collective-permute-done.50 = bf16[1,256,256]{2,1,0:T(8,128)(2,1)S(1)} collective-permute-done((bf16[1,256,256]{2,1,0:T(8,128)(2,1)S(1)}, bf16[1,256,256]{2,1,0:T(8,128)(2,1)S(1)}, u32[]{:S(2)}, u32[]{:S(2)}) %collective-permute-start.50) | collective-permute-done | bytes 131104 | tf_op jit(solution)/shard_map/ppermute | solution.py:32
  183.0 3.0 %collective-permute-start.53 = (bf16[256,256]{1,0:T(8,128)(2,1)S(1)}, bf16[256,256]{1,0:T(8,128)(2,1)S(1)}, u32[]{:S(2)}, u32[]{:S(2)}) collective-permute-start(bf16[256,256]{1,0:T(8,128)(2,1)S(1)} %get-tuple-element.147), channel_id=1, source_target_pairs={{0,24},{8,16},{16,8},{24,0},{1,25},{9,17},{17,9},{25,1},{2,26},{10... | collective-permute-start | bytes 393224 | tf_op jit(solution)/shard_map/ppermute | solution.py:32
  186.7 1.8 collective-permute-done.51
  188.4 2.0 %collective-permute-done.53 = bf16[256,256]{1,0:T(8,128)(2,1)S(1)} collective-permute-done((bf16[256,256]{1,0:T(8,128)(2,1)S(1)}, bf16[256,256]{1,0:T(8,128)(2,1)S(1)}, u32[]{:S(2)}, u32[]{:S(2)}) %collective-permute-start.53) | collective-permute-done | bytes 131104 | tf_op jit(solution)/shard_map/ppermute | solution.py:32
  (188 shorter events, 22.7 us)
Async XLA Ops:
  7.2 76.4 %all-gather.2.cloned.1.call-start = ((), (), s32[]{:S(2)}) async-start(), calls=%async_computation | async-start | bytes 1310720 | tf_op jit(solution)/shard_map/all_gather | solution.py:292
  7.2 9.6 %collective-permute-start = (bf16[256,256]{1,0:T(8,128)(2,1)}, bf16[256,256]{1,0:T(8,128)(2,1)S(1)}, u32[]{:S(2)}, u32[]{:S(2)}) collective-permute-start(bf16[256,256]{1,0:T(8,128)(2,1)} %param.14), channel_id=1, source_target_pairs={{0,0},{1,1},{2,2},{3,3},{4,16},{5,17},{6,18},{7,19},{8,8},{9,9},{1... | collective-permute-start | bytes 393224 | tf_op jit(solution)/shard_map/ppermute | solution.py:288
  8.8 37.3 %collective-permute-start.7 = (bf16[3,512,256]{2,1,0:T(8,128)(2,1)}, bf16[3,512,256]{2,1,0:T(8,128)(2,1)S(1)}, u32[]{:S(2)}, u32[]{:S(2)}) collective-permute-start(bf16[3,512,256]{2,1,0:T(8,128)(2,1)} %bitcast.94), channel_id=1, source_target_pairs={{0,8},{8,0},{16,24},{24,16},{1,9},{9,1},{17,25},{25,17},{2,10},{10... | collective-permute-start | bytes 2359304 | tf_op jit(solution)/shard_map/ppermute | solution.py:32
  13.0 2.2 %collective-permute-start.4 = (f32[256,1]{1,0:T(8,128)S(1)}, f32[256,1]{1,0:T(8,128)S(1)}, u32[]{:S(2)}, u32[]{:S(2)}) collective-permute-start(f32[256,1]{1,0:T(8,128)S(1)} %copy.26), channel_id=1, source_target_pairs={{0,1},{1,0},{2,3},{3,2},{4,5},{5,4},{6,7},{7,6},{8,9},{9,8},{10,11... | collective-permute-start | bytes 3080 | tf_op jit(solution)/shard_map/ppermute | solution.py:32
  15.2 9.3 %collective-permute-start.5 = (f32[256,1]{1,0:T(8,128)S(1)}, f32[256,1]{1,0:T(8,128)S(1)}, u32[]{:S(2)}, u32[]{:S(2)}) collective-permute-start(f32[256,1]{1,0:T(8,128)S(1)} %add.100), channel_id=1, source_target_pairs={{0,2},{1,3},{2,0},{3,1},{4,6},{5,7},{6,4},{7,5},{8,10},{9,11},{10,... | collective-permute-start | bytes 3080 | tf_op jit(solution)/shard_map/ppermute | solution.py:32
  16.8 19.0 %collective-permute-start.1 = (bf16[256,256]{1,0:T(8,128)(2,1)S(1)}, bf16[256,256]{1,0:T(8,128)(2,1)S(1)}, u32[]{:S(2)}, u32[]{:S(2)}) collective-permute-start(bf16[256,256]{1,0:T(8,128)(2,1)S(1)} %collective-permute-done.refs_4_), channel_id=1, source_target_pairs={{0,2},{1,3},{2,0},{3,1},{4,6},{5,7},{6,4},{7,5},{8,10},{9,11},{10,... | collective-permute-start | bytes 393224 | tf_op jit(solution)/shard_map/ppermute | solution.py:32
  17.3 18.4 %collective-permute-start.2 = (bf16[256,256]{1,0:T(8,128)(2,1)S(1)}, bf16[256,256]{1,0:T(8,128)(2,1)S(1)}, u32[]{:S(2)}, u32[]{:S(2)}) collective-permute-start(bf16[256,256]{1,0:T(8,128)(2,1)S(1)} %collective-permute-done.refs_4_), channel_id=1, source_target_pairs={{0,4},{1,5},{2,6},{3,7},{4,0},{5,1},{6,2},{7,3},{8,12},{9,13},{10,... | collective-permute-start | bytes 393224 | tf_op jit(solution)/shard_map/ppermute | solution.py:32
  23.8 12.0 %collective-permute-start.3 = (bf16[256,256]{1,0:T(8,128)(2,1)S(1)}, bf16[256,256]{1,0:T(8,128)(2,1)S(1)}, u32[]{:S(2)}, u32[]{:S(2)}) collective-permute-start(bf16[256,256]{1,0:T(8,128)(2,1)S(1)} %collective-permute-done.refs_4_), channel_id=1, source_target_pairs={{0,6},{1,7},{2,4},{3,5},{4,2},{5,3},{6,0},{7,1},{8,14},{9,15},{10,... | collective-permute-start | bytes 393224 | tf_op jit(solution)/shard_map/ppermute | solution.py:32
  24.5 11.9 %collective-permute-start.6 = (f32[256,1]{1,0:T(8,128)S(1)}, f32[256,1]{1,0:T(8,128)S(1)}, u32[]{:S(2)}, u32[]{:S(2)}) collective-permute-start(f32[256,1]{1,0:T(8,128)S(1)} %add.101), channel_id=1, source_target_pairs={{0,4},{1,5},{2,6},{3,7},{4,0},{5,1},{6,2},{7,3},{8,12},{9,13},{10,... | collective-permute-start | bytes 3080 | tf_op jit(solution)/shard_map/ppermute | solution.py:32
  35.8 1.8 collective-permute-start.10
  50.5 13.5 %collective-permute-start.13 = (bf16[256,256]{1,0:T(8,128)(2,1)}, bf16[256,256]{1,0:T(8,128)(2,1)S(1)}, u32[]{:S(2)}, u32[]{:S(2)}) collective-permute-start(bf16[256,256]{1,0:T(8,128)(2,1)} %get-tuple-element.80), channel_id=1, source_target_pairs={{0,16},{8,24},{16,0},{24,8},{1,17},{9,25},{17,1},{25,9},{2,18},{10... | collective-permute-start | bytes 393224 | tf_op jit(solution)/shard_map/ppermute | solution.py:32
  53.5 30.0 %collective-permute-start.12 = (bf16[2,256,256]{2,1,0:T(8,128)(2,1)}, bf16[2,256,256]{2,1,0:T(8,128)(2,1)S(1)}, u32[]{:S(2)}, u32[]{:S(2)}) collective-permute-start(bf16[2,256,256]{2,1,0:T(8,128)(2,1)} %get-tuple-element.76), channel_id=1, source_target_pairs={{0,16},{8,24},{16,0},{24,8},{1,17},{9,25},{17,1},{25,9},{2,18},{10... | collective-permute-start | bytes 786440 | tf_op jit(solution)/shard_map/ppermute | solution.py:32
  88.7 2.1 %collective-permute-start.14 = (bf16[4,256,256]{2,1,0:T(8,128)(2,1)}, bf16[4,256,256]{2,1,0:T(8,128)(2,1)S(1)}, u32[]{:S(2)}, u32[]{:S(2)}) collective-permute-start(bf16[4,256,256]{2,1,0:T(8,128)(2,1)} %get-tuple-element.87), channel_id=1, source_target_pairs={{0,1},{1,0},{2,3},{3,2},{4,5},{5,4},{6,7},{7,6},{8,9},{9,8},{10,11... | collective-permute-start | bytes 1572872 | tf_op jit(solution)/shard_map/ppermute | solution.py:32
  92.1 7.3 %collective-permute-start.15 = (bf16[256,256]{1,0:T(8,128)(2,1)S(1)}, bf16[256,256]{1,0:T(8,128)(2,1)S(1)}, u32[]{:S(2)}, u32[]{:S(2)}) collective-permute-start(bf16[256,256]{1,0:T(8,128)(2,1)S(1)} %get-tuple-element.163), channel_id=1, source_target_pairs={{0,2},{1,3},{2,0},{3,1},{4,6},{5,7},{6,4},{7,5},{8,10},{9,11},{10,... | collective-permute-start | bytes 393224 | tf_op jit(solution)/shard_map/ppermute | solution.py:32
  93.6 11.3 %collective-permute-start.16 = (bf16[256,256]{1,0:T(8,128)(2,1)S(1)}, bf16[256,256]{1,0:T(8,128)(2,1)S(1)}, u32[]{:S(2)}, u32[]{:S(2)}) collective-permute-start(bf16[256,256]{1,0:T(8,128)(2,1)S(1)} %get-tuple-element.165), channel_id=1, source_target_pairs={{0,4},{1,5},{2,6},{3,7},{4,0},{5,1},{6,2},{7,3},{8,12},{9,13},{10,... | collective-permute-start | bytes 393224 | tf_op jit(solution)/shard_map/ppermute | solution.py:32
  99.4 6.3 %collective-permute-start.17 = (bf16[256,256]{1,0:T(8,128)(2,1)S(1)}, bf16[256,256]{1,0:T(8,128)(2,1)S(1)}, u32[]{:S(2)}, u32[]{:S(2)}) collective-permute-start(bf16[256,256]{1,0:T(8,128)(2,1)S(1)} %get-tuple-element.164), channel_id=1, source_target_pairs={{0,6},{1,7},{2,4},{3,5},{4,2},{5,3},{6,0},{7,1},{8,14},{9,15},{10,... | collective-permute-start | bytes 393224 | tf_op jit(solution)/shard_map/ppermute | solution.py:32
  105.8 5.9 %collective-permute-start.25 = (bf16[256,256]{1,0:T(8,128)(2,1)S(1)}, bf16[256,256]{1,0:T(8,128)(2,1)S(1)}, u32[]{:S(2)}, u32[]{:S(2)}) collective-permute-start(bf16[256,256]{1,0:T(8,128)(2,1)S(1)} %fusion.4.refs_6_), channel_id=1, source_target_pairs={{0,16},{8,24},{16,0},{24,8},{1,17},{9,25},{17,1},{25,9},{2,18},{10... | collective-permute-start | bytes 393224 | tf_op jit(solution)/shard_map/ppermute | solution.py:32
  105.9 5.9 %collective-permute-start.19 = (bf16[256,256]{1,0:T(8,128)(2,1)S(1)}, bf16[256,256]{1,0:T(8,128)(2,1)S(1)}, u32[]{:S(2)}, u32[]{:S(2)}) collective-permute-start(bf16[256,256]{1,0:T(8,128)(2,1)S(1)} %fusion.4.refs_6_), channel_id=1, source_target_pairs={{0,2},{1,3},{2,0},{3,1},{4,6},{5,7},{6,4},{7,5},{8,10},{9,11},{10,... | collective-permute-start | bytes 393224 | tf_op jit(solution)/shard_map/ppermute | solution.py:32
  107.4 7.2 %collective-permute-start.21 = (bf16[256,256]{1,0:T(8,128)(2,1)S(1)}, bf16[256,256]{1,0:T(8,128)(2,1)S(1)}, u32[]{:S(2)}, u32[]{:S(2)}) collective-permute-start(bf16[256,256]{1,0:T(8,128)(2,1)S(1)} %fusion.4.refs_6_), channel_id=1, source_target_pairs={{0,4},{1,5},{2,6},{3,7},{4,0},{5,1},{6,2},{7,3},{8,12},{9,13},{10,... | collective-permute-start | bytes 393224 | tf_op jit(solution)/shard_map/ppermute | solution.py:32
  108.2 7.5 %collective-permute-start.23 = (bf16[256,256]{1,0:T(8,128)(2,1)S(1)}, bf16[256,256]{1,0:T(8,128)(2,1)S(1)}, u32[]{:S(2)}, u32[]{:S(2)}) collective-permute-start(bf16[256,256]{1,0:T(8,128)(2,1)S(1)} %fusion.4.refs_6_), channel_id=1, source_target_pairs={{0,6},{1,7},{2,4},{3,5},{4,2},{5,3},{6,0},{7,1},{8,14},{9,15},{10,... | collective-permute-start | bytes 393224 | tf_op jit(solution)/shard_map/ppermute | solution.py:32
  109.4 7.4 %collective-permute-start.18 = (bf16[256,256]{1,0:T(8,128)(2,1)S(1)}, bf16[256,256]{1,0:T(8,128)(2,1)S(1)}, u32[]{:S(2)}, u32[]{:S(2)}) collective-permute-start(bf16[256,256]{1,0:T(8,128)(2,1)S(1)} %fusion.4.refs_6_), channel_id=1, source_target_pairs={{0,1},{1,0},{2,3},{3,2},{4,5},{5,4},{6,7},{7,6},{8,9},{9,8},{10,11... | collective-permute-start | bytes 393224 | tf_op jit(solution)/shard_map/ppermute | solution.py:32
  111.7 6.4 %collective-permute-start.33 = (bf16[256,256]{1,0:T(8,128)(2,1)S(1)}, bf16[256,256]{1,0:T(8,128)(2,1)S(1)}, u32[]{:S(2)}, u32[]{:S(2)}) collective-permute-start(bf16[256,256]{1,0:T(8,128)(2,1)S(1)} %fusion.4.refs_6_), channel_id=1, source_target_pairs={{0,8},{8,0},{16,24},{24,16},{1,9},{9,1},{17,25},{25,17},{2,10},{10... | collective-permute-start | bytes 393224 | tf_op jit(solution)/shard_map/ppermute | solution.py:32
  111.7 8.8 %collective-permute-start.34 = (bf16[256,256]{1,0:T(8,128)(2,1)S(1)}, bf16[256,256]{1,0:T(8,128)(2,1)S(1)}, u32[]{:S(2)}, u32[]{:S(2)}) collective-permute-start(bf16[256,256]{1,0:T(8,128)(2,1)S(1)} %fusion.4.refs_6_), channel_id=1, source_target_pairs={{0,24},{8,16},{16,8},{24,0},{1,25},{9,17},{17,9},{25,1},{2,26},{10... | collective-permute-start | bytes 393224 | tf_op jit(solution)/shard_map/ppermute | solution.py:32
  114.6 6.0 %collective-permute-start.27 = (bf16[256,256]{1,0:T(8,128)(2,1)S(1)}, bf16[256,256]{1,0:T(8,128)(2,1)S(1)}, u32[]{:S(2)}, u32[]{:S(2)}) collective-permute-start(bf16[256,256]{1,0:T(8,128)(2,1)S(1)} %collective-permute-done.25.refs_14_), channel_id=1, source_target_pairs={{0,2},{1,3},{2,0},{3,1},{4,6},{5,7},{6,4},{7,5},{8,10},{9,11},{10,... | collective-permute-start | bytes 393224 | tf_op jit(solution)/shard_map/ppermute | solution.py:32
  115.7 7.6 %collective-permute-start.29 = (bf16[256,256]{1,0:T(8,128)(2,1)S(1)}, bf16[256,256]{1,0:T(8,128)(2,1)S(1)}, u32[]{:S(2)}, u32[]{:S(2)}) collective-permute-start(bf16[256,256]{1,0:T(8,128)(2,1)S(1)} %collective-permute-done.25.refs_14_), channel_id=1, source_target_pairs={{0,4},{1,5},{2,6},{3,7},{4,0},{5,1},{6,2},{7,3},{8,12},{9,13},{10,... | collective-permute-start | bytes 393224 | tf_op jit(solution)/shard_map/ppermute | solution.py:32
  116.8 6.6 %collective-permute-start.31 = (bf16[256,256]{1,0:T(8,128)(2,1)S(1)}, bf16[256,256]{1,0:T(8,128)(2,1)S(1)}, u32[]{:S(2)}, u32[]{:S(2)}) collective-permute-start(bf16[256,256]{1,0:T(8,128)(2,1)S(1)} %collective-permute-done.25.refs_14_), channel_id=1, source_target_pairs={{0,6},{1,7},{2,4},{3,5},{4,2},{5,3},{6,0},{7,1},{8,14},{9,15},{10,... | collective-permute-start | bytes 393224 | tf_op jit(solution)/shard_map/ppermute | solution.py:32
  118.1 5.7 %collective-permute-start.26 = (bf16[256,256]{1,0:T(8,128)(2,1)S(1)}, bf16[256,256]{1,0:T(8,128)(2,1)S(1)}, u32[]{:S(2)}, u32[]{:S(2)}) collective-permute-start(bf16[256,256]{1,0:T(8,128)(2,1)S(1)} %collective-permute-done.25.refs_14_), channel_id=1, source_target_pairs={{0,1},{1,0},{2,3},{3,2},{4,5},{5,4},{6,7},{7,6},{8,9},{9,8},{10,11... | collective-permute-start | bytes 393224 | tf_op jit(solution)/shard_map/ppermute | solution.py:32
  120.5 3.4 %collective-permute-start.20 = (bf16[256,256]{1,0:T(8,128)(2,1)S(1)}, bf16[256,256]{1,0:T(8,128)(2,1)S(1)}, u32[]{:S(2)}, u32[]{:S(2)}) collective-permute-start(bf16[256,256]{1,0:T(8,128)(2,1)S(1)} %collective-permute-done.19.refs_8_), channel_id=1, source_target_pairs={{0,1},{1,0},{2,3},{3,2},{4,5},{5,4},{6,7},{7,6},{8,9},{9,8},{10,11... | collective-permute-start | bytes 393224 | tf_op jit(solution)/shard_map/ppermute | solution.py:32
  120.6 4.4 %collective-permute-start.22 = (bf16[256,256]{1,0:T(8,128)(2,1)S(1)}, bf16[256,256]{1,0:T(8,128)(2,1)S(1)}, u32[]{:S(2)}, u32[]{:S(2)}) collective-permute-start(bf16[256,256]{1,0:T(8,128)(2,1)S(1)} %collective-permute-done.21.refs_10_), channel_id=1, source_target_pairs={{0,1},{1,0},{2,3},{3,2},{4,5},{5,4},{6,7},{7,6},{8,9},{9,8},{10,11... | collective-permute-start | bytes 393224 | tf_op jit(solution)/shard_map/ppermute | solution.py:32
  125.4 16.6 %collective-permute-start.35 = (bf16[2,256,256]{2,1,0:T(8,128)(2,1)S(1)}, bf16[2,256,256]{2,1,0:T(8,128)(2,1)S(1)}, u32[]{:S(2)}, u32[]{:S(2)}) collective-permute-start(bf16[2,256,256]{2,1,0:T(8,128)(2,1)S(1)} %pad_maximum_fusion.refs_6_), channel_id=1, source_target_pairs={{0,2},{1,3},{2,0},{3,1},{4,6},{5,7},{6,4},{7,5},{8,10},{9,11},{10,... | collective-permute-start | bytes 786440 | tf_op jit(solution)/shard_map/ppermute | solution.py:32
  126.5 15.5 %collective-permute-start.36 = (bf16[2,256,256]{2,1,0:T(8,128)(2,1)S(1)}, bf16[2,256,256]{2,1,0:T(8,128)(2,1)S(1)}, u32[]{:S(2)}, u32[]{:S(2)}) collective-permute-start(bf16[2,256,256]{2,1,0:T(8,128)(2,1)S(1)} %pad_maximum_fusion.refs_6_), channel_id=1, source_target_pairs={{0,4},{1,5},{2,6},{3,7},{4,0},{5,1},{6,2},{7,3},{8,12},{9,13},{10,... | collective-permute-start | bytes 786440 | tf_op jit(solution)/shard_map/ppermute | solution.py:32
  127.5 14.6 %collective-permute-start.37 = (bf16[2,256,256]{2,1,0:T(8,128)(2,1)S(1)}, bf16[2,256,256]{2,1,0:T(8,128)(2,1)S(1)}, u32[]{:S(2)}, u32[]{:S(2)}) collective-permute-start(bf16[2,256,256]{2,1,0:T(8,128)(2,1)S(1)} %pad_maximum_fusion.refs_6_), channel_id=1, source_target_pairs={{0,6},{1,7},{2,4},{3,5},{4,2},{5,3},{6,0},{7,1},{8,14},{9,15},{10,... | collective-permute-start | bytes 786440 | tf_op jit(solution)/shard_map/ppermute | solution.py:32
  142.1 3.6 %collective-permute-start.42 = (bf16[4,2,256,256]{3,2,1,0:T(8,128)(2,1)}, bf16[4,2,256,256]{3,2,1,0:T(8,128)(2,1)S(1)}, u32[]{:S(2)}, u32[]{:S(2)}) collective-permute-start(bf16[4,2,256,256]{3,2,1,0:T(8,128)(2,1)} %get-tuple-element.114), channel_id=1, source_target_pairs={{0,1},{1,0},{2,3},{3,2},{4,5},{5,4},{6,7},{7,6},{8,9},{9,8},{10,11... | collective-permute-start | bytes 3145736 | tf_op jit(solution)/shard_map/ppermute | solution.py:32
  142.2 5.1 %collective-permute-start.38 = (bf16[2,256,256]{2,1,0:T(8,128)(2,1)S(1)}, bf16[2,256,256]{2,1,0:T(8,128)(2,1)S(1)}, u32[]{:S(2)}, u32[]{:S(2)}) collective-permute-start(bf16[2,256,256]{2,1,0:T(8,128)(2,1)S(1)} %pad_maximum_fusion.refs_6_), channel_id=1, source_target_pairs={{0,1},{1,0},{2,3},{3,2},{4,5},{5,4},{6,7},{7,6},{8,9},{9,8},{10,11... | collective-permute-start | bytes 786440 | tf_op jit(solution)/shard_map/ppermute | solution.py:32
  142.7 4.7 %collective-permute-start.39 = (bf16[2,256,256]{2,1,0:T(8,128)(2,1)S(1)}, bf16[2,256,256]{2,1,0:T(8,128)(2,1)S(1)}, u32[]{:S(2)}, u32[]{:S(2)}) collective-permute-start(bf16[2,256,256]{2,1,0:T(8,128)(2,1)S(1)} %collective-permute-done.35.refs_8_), channel_id=1, source_target_pairs={{0,1},{1,0},{2,3},{3,2},{4,5},{5,4},{6,7},{7,6},{8,9},{9,8},{10,11... | collective-permute-start | bytes 786440 | tf_op jit(solution)/shard_map/ppermute | solution.py:32
  142.7 4.6 %collective-permute-start.40 = (bf16[2,256,256]{2,1,0:T(8,128)(2,1)S(1)}, bf16[2,256,256]{2,1,0:T(8,128)(2,1)S(1)}, u32[]{:S(2)}, u32[]{:S(2)}) collective-permute-start(bf16[2,256,256]{2,1,0:T(8,128)(2,1)S(1)} %collective-permute-done.36.refs_10_), channel_id=1, source_target_pairs={{0,1},{1,0},{2,3},{3,2},{4,5},{5,4},{6,7},{7,6},{8,9},{9,8},{10,11... | collective-permute-start | bytes 786440 | tf_op jit(solution)/shard_map/ppermute | solution.py:32
  143.2 4.2 %collective-permute-start.41 = (bf16[2,256,256]{2,1,0:T(8,128)(2,1)S(1)}, bf16[2,256,256]{2,1,0:T(8,128)(2,1)S(1)}, u32[]{:S(2)}, u32[]{:S(2)}) collective-permute-start(bf16[2,256,256]{2,1,0:T(8,128)(2,1)S(1)} %collective-permute-done.37.refs_12_), channel_id=1, source_target_pairs={{0,1},{1,0},{2,3},{3,2},{4,5},{5,4},{6,7},{7,6},{8,9},{9,8},{10,11... | collective-permute-start | bytes 786440 | tf_op jit(solution)/shard_map/ppermute | solution.py:32
  147.4 16.6 %collective-permute-start.43 = (bf16[2,256,256]{2,1,0:T(8,128)(2,1)S(1)}, bf16[2,256,256]{2,1,0:T(8,128)(2,1)S(1)}, u32[]{:S(2)}, u32[]{:S(2)}) collective-permute-start(bf16[2,256,256]{2,1,0:T(8,128)(2,1)S(1)} %get-tuple-element.125), channel_id=1, source_target_pairs={{0,2},{1,3},{2,0},{3,1},{4,6},{5,7},{6,4},{7,5},{8,10},{9,11},{10,... | collective-permute-start | bytes 786440 | tf_op jit(solution)/shard_map/ppermute | solution.py:32
  148.6 15.4 %collective-permute-start.44 = (bf16[2,256,256]{2,1,0:T(8,128)(2,1)S(1)}, bf16[2,256,256]{2,1,0:T(8,128)(2,1)S(1)}, u32[]{:S(2)}, u32[]{:S(2)}) collective-permute-start(bf16[2,256,256]{2,1,0:T(8,128)(2,1)S(1)} %get-tuple-element.126), channel_id=1, source_target_pairs={{0,4},{1,5},{2,6},{3,7},{4,0},{5,1},{6,2},{7,3},{8,12},{9,13},{10,... | collective-permute-start | bytes 786440 | tf_op jit(solution)/shard_map/ppermute | solution.py:32
  149.6 14.4 %collective-permute-start.45 = (bf16[2,256,256]{2,1,0:T(8,128)(2,1)S(1)}, bf16[2,256,256]{2,1,0:T(8,128)(2,1)S(1)}, u32[]{:S(2)}, u32[]{:S(2)}) collective-permute-start(bf16[2,256,256]{2,1,0:T(8,128)(2,1)S(1)} %get-tuple-element.127), channel_id=1, source_target_pairs={{0,6},{1,7},{2,4},{3,5},{4,2},{5,3},{6,0},{7,1},{8,14},{9,15},{10,... | collective-permute-start | bytes 786440 | tf_op jit(solution)/shard_map/ppermute | solution.py:32
  164.0 2.9 %collective-permute-start.46 = (bf16[4,2,256,256]{3,2,1,0:T(8,128)(2,1)}, bf16[4,2,256,256]{3,2,1,0:T(8,128)(2,1)S(1)}, u32[]{:S(2)}, u32[]{:S(2)}) collective-permute-start(bf16[4,2,256,256]{3,2,1,0:T(8,128)(2,1)} %get-tuple-element.129), channel_id=1, source_target_pairs={{0,1},{1,0},{2,3},{3,2},{4,5},{5,4},{6,7},{7,6},{8,9},{9,8},{10,11... | collective-permute-start | bytes 3145736 | tf_op jit(solution)/shard_map/ppermute | solution.py:32
  164.2 9.2 %collective-permute-start.49 = (bf16[256,256]{1,0:T(8,128)(2,1)S(1)}, bf16[256,256]{1,0:T(8,128)(2,1)S(1)}, u32[]{:S(2)}, u32[]{:S(2)}) collective-permute-start(bf16[256,256]{1,0:T(8,128)(2,1)S(1)} %fusion.15), channel_id=1, source_target_pairs={{0,16},{8,24},{16,0},{24,8},{1,17},{9,25},{17,1},{25,9},{2,18},{10... | collective-permute-start | bytes 393224 | tf_op jit(solution)/shard_map/ppermute | solution.py:32
  167.3 8.4 %collective-permute-start.48 = (bf16[2,256,256]{2,1,0:T(8,128)(2,1)S(1)}, bf16[2,256,256]{2,1,0:T(8,128)(2,1)S(1)}, u32[]{:S(2)}, u32[]{:S(2)}) collective-permute-start(bf16[2,256,256]{2,1,0:T(8,128)(2,1)S(1)} %pad_maximum_fusion.2), channel_id=1, source_target_pairs={{0,4},{1,5},{2,6},{3,7},{4,0},{5,1},{6,2},{7,3},{8,12},{9,13},{10,... | collective-permute-start | bytes 786440 | tf_op jit(solution)/shard_map/ppermute | solution.py:32
  168.5 8.1 %collective-permute-start.47 = (bf16[2,256,256]{2,1,0:T(8,128)(2,1)S(1)}, bf16[2,256,256]{2,1,0:T(8,128)(2,1)S(1)}, u32[]{:S(2)}, u32[]{:S(2)}) collective-permute-start(bf16[2,256,256]{2,1,0:T(8,128)(2,1)S(1)} %pad_maximum_fusion.1), channel_id=1, source_target_pairs={{0,2},{1,3},{2,0},{3,1},{4,6},{5,7},{6,4},{7,5},{8,10},{9,11},{10,... | collective-permute-start | bytes 786440 | tf_op jit(solution)/shard_map/ppermute | solution.py:32
  176.7 5.0 %collective-permute-start.50 = (bf16[1,256,256]{2,1,0:T(8,128)(2,1)S(1)}, bf16[1,256,256]{2,1,0:T(8,128)(2,1)S(1)}, u32[]{:S(2)}, u32[]{:S(2)}) collective-permute-start(bf16[1,256,256]{2,1,0:T(8,128)(2,1)S(1)} %get-tuple-element.135), channel_id=1, source_target_pairs={{0,4},{1,5},{2,6},{3,7},{4,0},{5,1},{6,2},{7,3},{8,12},{9,13},{10,... | collective-permute-start | bytes 393224 | tf_op jit(solution)/shard_map/ppermute | solution.py:32
  177.7 5.0 %collective-permute-start.52 = (bf16[1,256,256]{2,1,0:T(8,128)(2,1)S(1)}, bf16[1,256,256]{2,1,0:T(8,128)(2,1)S(1)}, u32[]{:S(2)}, u32[]{:S(2)}) collective-permute-start(bf16[1,256,256]{2,1,0:T(8,128)(2,1)S(1)} %get-tuple-element.136), channel_id=1, source_target_pairs={{0,2},{1,3},{2,0},{3,1},{4,6},{5,7},{6,4},{7,5},{8,10},{9,11},{10,... | collective-permute-start | bytes 393224 | tf_op jit(solution)/shard_map/ppermute | solution.py:32
  182.8 5.6 %collective-permute-start.51 = (bf16[256,256]{1,0:T(8,128)(2,1)S(1)}, bf16[256,256]{1,0:T(8,128)(2,1)S(1)}, u32[]{:S(2)}, u32[]{:S(2)}) collective-permute-start(bf16[256,256]{1,0:T(8,128)(2,1)S(1)} %get-tuple-element.146), channel_id=1, source_target_pairs={{0,8},{8,0},{16,24},{24,16},{1,9},{9,1},{17,25},{25,17},{2,10},{10... | collective-permute-start | bytes 393224 | tf_op jit(solution)/shard_map/ppermute | solution.py:32
  183.0 7.5 %collective-permute-start.53 = (bf16[256,256]{1,0:T(8,128)(2,1)S(1)}, bf16[256,256]{1,0:T(8,128)(2,1)S(1)}, u32[]{:S(2)}, u32[]{:S(2)}) collective-permute-start(bf16[256,256]{1,0:T(8,128)(2,1)S(1)} %get-tuple-element.147), channel_id=1, source_target_pairs={{0,24},{8,16},{16,8},{24,0},{1,25},{9,17},{17,9},{25,1},{2,26},{10... | collective-permute-start | bytes 393224 | tf_op jit(solution)/shard_map/ppermute | solution.py:32
  (48 other events, 380.7 us)
Sparse Core Ops, SparseCore 0:
  13.2 36.9 all-gather.1

commit v9 on v8

--- a/solution.py
+++ b/solution.py
@@ -137,9 +137,13 @@
 
 def draft_kernel(requests, draft, heads, parts, count, ids, place, scale_of, *refs):
     pairs = refs[:parts]
-    query, reach, rows, top, mass, mixed, output = refs[parts : parts + 7]
-    even, odd, picked, key, value, attended = refs[parts + 7 :]
+    query, reach, rows, top, mass, mixed = refs[parts : parts + 6]
+    blocks = refs[parts + 6 : -7]
+    even, odd, picked, key, value, attended, output = refs[-7:]
     me = ids[1]
+    depth = blocks[0].shape[0]
+    for mask, one in enumerate(blocks):
+        output[pl.ds(pl.multiple_of((ids[0] ^ mask) * depth, depth), depth), :] = one[...]
     for which, kept in ((0, key), (1, value)):
         total = pairs[0][which]
         for pair in pairs[1:]:
@@ -289,9 +293,14 @@
     other_weight = swap(weight, "gx", 1)
     experts = gate_up_weight.shape[0]
     units = gate_up_weight.shape[3]
-    output_full = lax.all_gather(output_weight, "gx", axis=0, tiled=True)
+    output_weight, moved = lax.optimization_barrier((output_weight, moved))
+    near_output = [output_weight] + [
+        swap(output_weight, "gx", 2 * far) for far in range(1, terms_of)
+    ]
     far = gather_far(moved)
-    gate_up, far = lax.optimization_barrier((jnp.transpose(gate_up_weight, (2, 0, 1, 3)), far))
+    gate_up, far, near_output = lax.optimization_barrier(
+        (jnp.transpose(gate_up_weight, (2, 0, 1, 3)), far, near_output)
+    )
     pieces = gather_near(far)
     types = [F32] + [BF16] * (terms_of - 1)
     projected = pl.pallas_call(
@@ -309,9 +318,13 @@
     query_terms = [query_terms[0]] + [
         swap(query_terms[far], "gx", 2 * far) for far in range(1, terms_of)
     ]
+    pair_terms, near_output, query_terms = lax.optimization_barrier(
+        (list(pair_terms), near_output, query_terms)
+    )
     pair_terms = [pair_terms[0]] + [
         swap(pair_terms[far], "gx", 2 * far) for far in range(1, terms_of)
     ]
+    output_blocks = [one for held in near_output for one in (held, swap(held, "gx", 1))]
 
     owner = prompt_group % groups
     order = jnp.arange(requests, dtype=jnp.int32)
@@ -376,9 +389,9 @@
             half,
             jax.ShapeDtypeStruct((2, requests * accepted, width), BF16),
         ),
-        in_specs=[smem(), smem()] + [vmem()] * (terms_of + 8),
+        in_specs=[smem(), smem()] + [vmem()] * (terms_of + 7 + gx_count),
         out_specs=(vmem(), vmem(), vmem()),
-        scratch_shapes=[pltpu.VMEM((rows, width), BF16)] * 3,
+        scratch_shapes=[pltpu.VMEM((rows, width), BF16)] * 3 + [pltpu.VMEM((depth, width), BF16)],
         compiler_params=params(),
         name="draft",
     )(
@@ -392,7 +405,7 @@
         top,
         mass,
         mixed,
-        output_full,
+        *output_blocks,
     )
     compacted = jnp.transpose(picked, (1, 0, 2))
 

time: 199 us -> 175 us (0.88); the launches traced: 198 us -> 177 us
  between operations: 14.8 us -> 1.38 us
  waiting for transfers between devices: 51.9 us -> 41.9 us
    ppermute x53 -> x56, waiting for transfers between devices: 51.8 us -> 41.9 us  [swap(): lax.ppermute(value, axis, [(one, one ^ mask) for one in range(count)])]
    ppermute x53 -> x56, starting transfers between devices: 53.3 us -> 54.6 us  [swap(): lax.ppermute(value, axis, [(one, one ^ mask) for one in range(count)])]
    unnamed x84 -> x92, local copies, waits for them, and re-layouts: 10.9 us -> 10.5 us
  transfers between devices with their start and end apart: 55 -> 57, of which waited for: 23 -> 22; matrix products, arithmetic and copies ran while one was open for 10% -> 11% of each run, Pallas kernels for 24% -> 26%
where the time goes in v9:
time: 175 us; the launch traced here: 177 us
  starting transfers between devices  56.1 us (32%)
  Pallas kernels  54.1 us (31%)
  waiting for transfers between devices  41.9 us (24%)
  local copies, waits for them, and re-layouts  11.5 us (7%)
  other arithmetic  10.2 us (6%)
    ppermute x56, starting transfers between devices, swap(): lax.ppermute(value, axis, [(one, one ^ mask) for one in range(count)])  54.6 us
    ppermute x56, waiting for transfers between devices, swap(): lax.ppermute(value, axis, [(one, one ^ mask) for one in range(count)])  41.9 us
    pallas_call x2, Pallas kernels, per_device(): pl.pallas_call(lambda *refs: expert_kernel(gy_count, masks, number > 0, *...  25.9 us
    pallas_call x1, Pallas kernels, per_device(): pl.pallas_call(lambda *refs: cache_kernel(requests, draft, heads, terms_o...  20.2 us
    unnamed x92, local copies, waits for them, and re-layouts  10.5 us
    pallas_call x1, Pallas kernels, per_device(): pl.pallas_call(lambda *refs: draft_kernel(requests, draft, heads, terms_o...  4.39 us
    pallas_call x1, Pallas kernels, per_device(): pl.pallas_call(lambda *refs: project_kernel(gy_count, share, *refs), out_...  3.57 us
  transfers between devices with their start and end apart: 57, of which 22 were waited for; matrix products, arithmetic and copies ran while one was open for 11% of the time, Pallas kernels for 26%

profile of v9, /device:TPU:0, one launch (start us, length us, event | category | flops | bytes accessed | tf_op | source)
XLA Modules:
  0.0 176.9 jit_solution(2747935385909204797)
XLA Ops:
  0.6 1.6 collective-permute-start
  2.2 3.0 %collective-permute-start.8 = (bf16[3,512,256]{2,1,0:T(8,128)(2,1)}, bf16[3,512,256]{2,1,0:T(8,128)(2,1)S(1)}, u32[]{:S(2)}, u32[]{:S(2)}) collective-permute-start(bf16[3,512,256]{2,1,0:T(8,128)(2,1)} %bitcast.94), channel_id=1, source_target_pairs={{0,8},{8,0},{16,24},{24,16},{1,9},{9,1},{17,25},{25,17},{2,10},{10... | collective-permute-start | bytes 2359304 | tf_op jit(solution)/shard_map/ppermute | solution.py:32
  5.2 1.0 fusion
  8.7 1.6 collective-permute-start.6
  10.8 5.7 %collective-permute-start.4 = (bf16[512,256]{1,0:T(8,128)(2,1)}, bf16[512,256]{1,0:T(8,128)(2,1)S(1)}, u32[]{:S(2)}, u32[]{:S(2)}) collective-permute-start(bf16[512,256]{1,0:T(8,128)(2,1)} %refs_11_), channel_id=1, source_target_pairs={{0,16},{8,24},{16,0},{24,8},{1,17},{9,25},{17,1},{25,9},{2,18},{10... | collective-permute-start | bytes 786440 | tf_op jit(solution)/shard_map/ppermute | solution.py:32
  17.3 3.2 %collective-permute-start.3 = (bf16[256,256]{1,0:T(8,128)(2,1)S(1)}, bf16[256,256]{1,0:T(8,128)(2,1)S(1)}, u32[]{:S(2)}, u32[]{:S(2)}) collective-permute-start(bf16[256,256]{1,0:T(8,128)(2,1)S(1)} %collective-permute-done.refs_4_), channel_id=1, source_target_pairs={{0,6},{1,7},{2,4},{3,5},{4,2},{5,3},{6,0},{7,1},{8,14},{9,15},{10,... | collective-permute-start | bytes 393224 | tf_op jit(solution)/shard_map/ppermute | solution.py:32
  21.2 1.1 collective-permute-start.7
  23.0 7.9 %copy.30 = bf16[4,2048,2,256]{3,1,0,2:T(8,128)(2,1)} copy(bf16[4,2048,2,256]{3,2,1,0:T(2,128)(2,1)} %param.24) | data formatting | bytes 16777216 | tf_op args[10]
  34.6 3.6 %project.1 = (f32[256,256]{1,0:T(8,128)}, bf16[256,256]{1,0:T(8,128)(2,1)}, f32[2,256,256]{2,1,0:T(8,128)}, bf16[2,256,256]{2,1,0:T(8,128)(2,1)}) custom-call(s32[2]{0:T(128)} %pad_add_fusion.refs_0_, f32[1,2048]{1,0:T(1,128)} %bitcast.99, bf16[3,512,256]{2,1,0:T(8,128)(2,1)} %bitcast.95, bf16[3,512,256]{2,1,0:T(8,128)(2,1)} %copy-done.1, ...), custom_call_target="tpu_custom_call" | custom-call | tf_op jit(solution)/shard_map/project/pallas_call | solution.py:306
  39.8 1.0 convolution_minimum_fusion.refs_6_
  40.7 4.3 %collective-permute-done.13.refs_6_ = bf16[256,256]{1,0:T(8,128)(2,1)S(1)} collective-permute-done((bf16[256,256]{1,0:T(8,128)(2,1)}, bf16[256,256]{1,0:T(8,128)(2,1)S(1)}, u32[]{:S(2)}, u32[]{:S(2)}) %collective-permute-start.13) | collective-permute-done | bytes 131104 | tf_op jit(solution)/shard_map/ppermute | solution.py:32
  46.0 4.2 %collective-permute-start.15 = (bf16[512,256]{1,0:T(8,128)(2,1)S(1)}, bf16[512,256]{1,0:T(8,128)(2,1)S(1)}, u32[]{:S(2)}, u32[]{:S(2)}) collective-permute-start(bf16[512,256]{1,0:T(8,128)(2,1)S(1)} %copy-done.5), channel_id=1, source_target_pairs={{0,8},{8,0},{16,24},{24,16},{1,9},{9,1},{17,25},{25,17},{2,10},{10... | collective-permute-start | bytes 786440 | tf_op jit(solution)/shard_map/ppermute | solution.py:32
  50.2 20.2 %cache.1 = (f32[512,128]{1,0:T(8,128)}, f32[512,128]{1,0:T(8,128)}, f32[512,256]{1,0:T(8,128)}, bf16[256,256]{1,0:T(8,128)(2,1)}) custom-call(s32[2]{0:T(128)} %refs_0_.1, s32[2]{0:T(128)} %get-tuple-element.165.refs_1_, s32[2]{0:T(128)} %get-tuple-element.164.refs_2_, s32[4]{0:T(128)} %convert_reduce_fusion.refs_3_.refs_1_, ...), custom_call_target="tpu_custom_call" | custom-call | flops 10737418240 | bytes 16777216 | tf_op jit(solution)/shard_map/cache/pallas_call | solution.py:343
  71.3 4.4 %draft.1 = (bf16[4,256,256]{2,1,0:T(8,128)(2,1)}, bf16[4,256,256]{2,1,0:T(8,128)(2,1)}, bf16[2,32,256]{2,1,0:T(8,128)(2,1)}) custom-call(s32[2]{0:T(128)} %pad_add_fusion.refs_0_, s32[4]{0:T(128)} %convert_reduce_fusion.refs_3_.refs_1_, f32[256,1]{1,0:T(8,128)} %add_rsqrt_fusion.refs_4_.refs_2_, f32[2,256,256]{2,1,0:T(8,128)} %get-tuple-element.95.refs_3_, ...), custom_call_target="tpu_custom_call" | custom-call | tf_op jit(solution)/shard_map/draft/pallas_call | solution.py:385
  75.7 2.1 %collective-permute-done.17 = bf16[4,256,256]{2,1,0:T(8,128)(2,1)S(1)} collective-permute-done((bf16[4,256,256]{2,1,0:T(8,128)(2,1)}, bf16[4,256,256]{2,1,0:T(8,128)(2,1)S(1)}, u32[]{:S(2)}, u32[]{:S(2)}) %collective-permute-start.17) | collective-permute-done | bytes 524320 | tf_op jit(solution)/shard_map/ppermute | solution.py:32
  77.9 1.2 fusion.36
  79.1 1.4 collective-permute-start.18
  80.5 2.4 %collective-permute-start.19 = (bf16[256,256]{1,0:T(8,128)(2,1)S(1)}, bf16[256,256]{1,0:T(8,128)(2,1)S(1)}, u32[]{:S(2)}, u32[]{:S(2)}) collective-permute-start(bf16[256,256]{1,0:T(8,128)(2,1)S(1)} %get-tuple-element.185), channel_id=1, source_target_pairs={{0,4},{1,5},{2,6},{3,7},{4,0},{5,1},{6,2},{7,3},{8,12},{9,13},{10,... | collective-permute-start | bytes 393224 | tf_op jit(solution)/shard_map/ppermute | solution.py:32
  82.9 1.8 %collective-permute-done.18 = bf16[256,256]{1,0:T(8,128)(2,1)S(1)} collective-permute-done((bf16[256,256]{1,0:T(8,128)(2,1)S(1)}, bf16[256,256]{1,0:T(8,128)(2,1)S(1)}, u32[]{:S(2)}, u32[]{:S(2)}) %collective-permute-start.18) | collective-permute-done | bytes 131104 | tf_op jit(solution)/shard_map/ppermute | solution.py:32
  84.7 4.5 %collective-permute-done.19 = bf16[256,256]{1,0:T(8,128)(2,1)S(1)} collective-permute-done((bf16[256,256]{1,0:T(8,128)(2,1)S(1)}, bf16[256,256]{1,0:T(8,128)(2,1)S(1)}, u32[]{:S(2)}, u32[]{:S(2)}) %collective-permute-start.19) | collective-permute-done | bytes 131104 | tf_op jit(solution)/shard_map/ppermute | solution.py:32
  89.4 1.5 collective-permute-start.22
  91.6 1.3 collective-permute-start.26
  92.9 3.7 %collective-permute-done.28.refs_14_ = bf16[256,256]{1,0:T(8,128)(2,1)S(1)} collective-permute-done((bf16[256,256]{1,0:T(8,128)(2,1)S(1)}, bf16[256,256]{1,0:T(8,128)(2,1)S(1)}, u32[]{:S(2)}, u32[]{:S(2)}) %collective-permute-start.28) | collective-permute-done | bytes 131104 | tf_op jit(solution)/shard_map/ppermute | solution.py:32
  96.6 2.4 %collective-permute-start.36 = (bf16[256,256]{1,0:T(8,128)(2,1)S(1)}, bf16[256,256]{1,0:T(8,128)(2,1)S(1)}, u32[]{:S(2)}, u32[]{:S(2)}) collective-permute-start(bf16[256,256]{1,0:T(8,128)(2,1)S(1)} %fusion.4.refs_6_), channel_id=1, source_target_pairs={{0,8},{8,0},{16,24},{24,16},{1,9},{9,1},{17,25},{25,17},{2,10},{10... | collective-permute-start | bytes 393224 | tf_op jit(solution)/shard_map/ppermute | solution.py:32
  99.0 2.5 %collective-permute-start.37 = (bf16[256,256]{1,0:T(8,128)(2,1)S(1)}, bf16[256,256]{1,0:T(8,128)(2,1)S(1)}, u32[]{:S(2)}, u32[]{:S(2)}) collective-permute-start(bf16[256,256]{1,0:T(8,128)(2,1)S(1)} %fusion.4.refs_6_), channel_id=1, source_target_pairs={{0,24},{8,16},{16,8},{24,0},{1,25},{9,17},{17,9},{25,1},{2,26},{10... | collective-permute-start | bytes 393224 | tf_op jit(solution)/shard_map/ppermute | solution.py:32
  101.6 1.3 collective-permute-start.30
  103.7 1.3 collective-permute-start.34
  105.1 1.0 collective-permute-done.37
  106.1 1.0 collective-permute-done.30.refs_16_
  107.8 1.8 %collective-permute-done.34.refs_20_ = bf16[256,256]{1,0:T(8,128)(2,1)S(1)} collective-permute-done((bf16[256,256]{1,0:T(8,128)(2,1)S(1)}, bf16[256,256]{1,0:T(8,128)(2,1)S(1)}, u32[]{:S(2)}, u32[]{:S(2)}) %collective-permute-start.34) | collective-permute-done | bytes 131104 | tf_op jit(solution)/shard_map/ppermute | solution.py:32
  111.5 1.2 collective-permute-start.38
  113.4 1.6 collective-permute-start.40
  115.1 13.0 %experts.2 = (bf16[4,2,256,256]{3,2,1,0:T(8,128)(2,1)}, bf16[4,2,256,256]{3,2,1,0:T(8,128)(2,1)}) custom-call(s32[2]{0:T(128)} %pad_add_fusion.refs_0_, f32[1,2048]{1,0:T(1,128)} %bitcast.105, s32[8,1024]{1,0:T(8,128)} %bitcast.103, f32[8,1024]{1,0:T(8,128)} %convert_bitcast_fusion.refs_3_, bf16[2,4,2048,256]{3,2,1,0:T(8,128)(2,1)} %bitcast.92, ...), custom_call_target="tpu_custom_call" | custom-call | flops 6442450944 | bytes 12582912 | tf_op jit(solution)/shard_map/experts/pallas_call | solution.py:435
  129.3 2.4 %collective-permute-done.45 = bf16[4,2,256,256]{3,2,1,0:T(8,128)(2,1)S(1)} collective-permute-done((bf16[4,2,256,256]{3,2,1,0:T(8,128)(2,1)}, bf16[4,2,256,256]{3,2,1,0:T(8,128)(2,1)S(1)}, u32[]{:S(2)}, u32[]{:S(2)}) %collective-permute-start.45) | collective-permute-done | bytes 1048608 | tf_op jit(solution)/shard_map/ppermute | solution.py:32
  131.7 1.5 fusion.37
  133.5 1.3 collective-permute-start.46
  135.4 1.6 collective-permute-start.48
  137.0 13.0 %experts.3 = (bf16[4,2,256,256]{3,2,1,0:T(8,128)(2,1)}, bf16[4,2,256,256]{3,2,1,0:T(8,128)(2,1)}) custom-call(s32[2]{0:T(128)} %pad_add_fusion.refs_0_, f32[1,2048]{1,0:T(1,128)} %bitcast.106, s32[8,1024]{1,0:T(8,128)} %bitcast.104, f32[8,1024]{1,0:T(8,128)} %convert_bitcast_fusion.refs_3_, bf16[2,4,2048,256]{3,2,1,0:T(8,128)(2,1)} %bitcast.93, ...), custom_call_target="tpu_custom_call" | custom-call | flops 6442450944 | bytes 12582912 | tf_op jit(solution)/shard_map/experts/pallas_call | solution.py:435
  150.4 2.5 %collective-permute-done.49 = bf16[4,2,256,256]{3,2,1,0:T(8,128)(2,1)S(1)} collective-permute-done((bf16[4,2,256,256]{3,2,1,0:T(8,128)(2,1)}, bf16[4,2,256,256]{3,2,1,0:T(8,128)(2,1)S(1)}, u32[]{:S(2)}, u32[]{:S(2)}) %collective-permute-start.49) | collective-permute-done | bytes 1048608 | tf_op jit(solution)/shard_map/ppermute | solution.py:32
  153.4 1.2 collective-permute-start.51
  155.4 4.3 %collective-permute-done.52 = bf16[256,256]{1,0:T(8,128)(2,1)S(1)} collective-permute-done((bf16[256,256]{1,0:T(8,128)(2,1)S(1)}, bf16[256,256]{1,0:T(8,128)(2,1)S(1)}, u32[]{:S(2)}, u32[]{:S(2)}) %collective-permute-start.52) | collective-permute-done | bytes 131104 | tf_op jit(solution)/shard_map/ppermute | solution.py:32
  159.8 2.0 %collective-permute-done.51 = bf16[2,256,256]{2,1,0:T(8,128)(2,1)S(1)} collective-permute-done((bf16[2,256,256]{2,1,0:T(8,128)(2,1)S(1)}, bf16[2,256,256]{2,1,0:T(8,128)(2,1)S(1)}, u32[]{:S(2)}, u32[]{:S(2)}) %collective-permute-start.51) | collective-permute-done | bytes 262176 | tf_op jit(solution)/shard_map/ppermute | solution.py:32
  162.8 1.0 collective-permute-start.53
  163.8 1.2 collective-permute-start.55
  165.0 2.9 %collective-permute-done.53 = bf16[1,256,256]{2,1,0:T(8,128)(2,1)S(1)} collective-permute-done((bf16[1,256,256]{2,1,0:T(8,128)(2,1)S(1)}, bf16[1,256,256]{2,1,0:T(8,128)(2,1)S(1)}, u32[]{:S(2)}, u32[]{:S(2)}) %collective-permute-start.53) | collective-permute-done | bytes 131104 | tf_op jit(solution)/shard_map/ppermute | solution.py:32
  169.3 2.1 %collective-permute-start.56 = (bf16[256,256]{1,0:T(8,128)(2,1)S(1)}, bf16[256,256]{1,0:T(8,128)(2,1)S(1)}, u32[]{:S(2)}, u32[]{:S(2)}) collective-permute-start(bf16[256,256]{1,0:T(8,128)(2,1)S(1)} %get-tuple-element.167), channel_id=1, source_target_pairs={{0,24},{8,16},{16,8},{24,0},{1,25},{9,17},{17,9},{25,1},{2,26},{10... | collective-permute-start | bytes 393224 | tf_op jit(solution)/shard_map/ppermute | solution.py:32
  172.0 2.3 %collective-permute-done.54 = bf16[256,256]{1,0:T(8,128)(2,1)S(1)} collective-permute-done((bf16[256,256]{1,0:T(8,128)(2,1)S(1)}, bf16[256,256]{1,0:T(8,128)(2,1)S(1)}, u32[]{:S(2)}, u32[]{:S(2)}) %collective-permute-start.54) | collective-permute-done | bytes 131104 | tf_op jit(solution)/shard_map/ppermute | solution.py:32
  174.3 1.9 %collective-permute-done.56 = bf16[256,256]{1,0:T(8,128)(2,1)S(1)} collective-permute-done((bf16[256,256]{1,0:T(8,128)(2,1)S(1)}, bf16[256,256]{1,0:T(8,128)(2,1)S(1)}, u32[]{:S(2)}, u32[]{:S(2)}) %collective-permute-start.56) | collective-permute-done | bytes 131104 | tf_op jit(solution)/shard_map/ppermute | solution.py:32
  (199 shorter events, 24.9 us)
Async XLA Ops:
  0.6 9.6 %collective-permute-start = (bf16[256,256]{1,0:T(8,128)(2,1)}, bf16[256,256]{1,0:T(8,128)(2,1)S(1)}, u32[]{:S(2)}, u32[]{:S(2)}) collective-permute-start(bf16[256,256]{1,0:T(8,128)(2,1)} %param.14), channel_id=1, source_target_pairs={{0,0},{1,1},{2,2},{3,3},{4,16},{5,17},{6,18},{7,19},{8,8},{9,9},{1... | collective-permute-start | bytes 393224 | tf_op jit(solution)/shard_map/ppermute | solution.py:292
  2.2 31.5 %collective-permute-start.8 = (bf16[3,512,256]{2,1,0:T(8,128)(2,1)}, bf16[3,512,256]{2,1,0:T(8,128)(2,1)S(1)}, u32[]{:S(2)}, u32[]{:S(2)}) collective-permute-start(bf16[3,512,256]{2,1,0:T(8,128)(2,1)} %bitcast.94), channel_id=1, source_target_pairs={{0,8},{8,0},{16,24},{24,16},{1,9},{9,1},{17,25},{25,17},{2,10},{10... | collective-permute-start | bytes 2359304 | tf_op jit(solution)/shard_map/ppermute | solution.py:32
  8.7 8.6 %collective-permute-start.6 = (f32[256,1]{1,0:T(8,128)S(1)}, f32[256,1]{1,0:T(8,128)S(1)}, u32[]{:S(2)}, u32[]{:S(2)}) collective-permute-start(f32[256,1]{1,0:T(8,128)S(1)} %add.100), channel_id=1, source_target_pairs={{0,2},{1,3},{2,0},{3,1},{4,6},{5,7},{6,4},{7,5},{8,10},{9,11},{10,... | collective-permute-start | bytes 3080 | tf_op jit(solution)/shard_map/ppermute | solution.py:32
  10.2 10.9 %collective-permute-start.1 = (bf16[256,256]{1,0:T(8,128)(2,1)S(1)}, bf16[256,256]{1,0:T(8,128)(2,1)S(1)}, u32[]{:S(2)}, u32[]{:S(2)}) collective-permute-start(bf16[256,256]{1,0:T(8,128)(2,1)S(1)} %collective-permute-done.refs_4_), channel_id=1, source_target_pairs={{0,2},{1,3},{2,0},{3,1},{4,6},{5,7},{6,4},{7,5},{8,10},{9,11},{10,... | collective-permute-start | bytes 393224 | tf_op jit(solution)/shard_map/ppermute | solution.py:32
  10.8 20.8 %collective-permute-start.4 = (bf16[512,256]{1,0:T(8,128)(2,1)}, bf16[512,256]{1,0:T(8,128)(2,1)S(1)}, u32[]{:S(2)}, u32[]{:S(2)}) collective-permute-start(bf16[512,256]{1,0:T(8,128)(2,1)} %refs_11_), channel_id=1, source_target_pairs={{0,16},{8,24},{16,0},{24,8},{1,17},{9,25},{17,1},{25,9},{2,18},{10... | collective-permute-start | bytes 786440 | tf_op jit(solution)/shard_map/ppermute | solution.py:32
  16.5 15.1 %collective-permute-start.2 = (bf16[256,256]{1,0:T(8,128)(2,1)S(1)}, bf16[256,256]{1,0:T(8,128)(2,1)S(1)}, u32[]{:S(2)}, u32[]{:S(2)}) collective-permute-start(bf16[256,256]{1,0:T(8,128)(2,1)S(1)} %collective-permute-done.refs_4_), channel_id=1, source_target_pairs={{0,4},{1,5},{2,6},{3,7},{4,0},{5,1},{6,2},{7,3},{8,12},{9,13},{10,... | collective-permute-start | bytes 393224 | tf_op jit(solution)/shard_map/ppermute | solution.py:32
  17.3 14.3 %collective-permute-start.3 = (bf16[256,256]{1,0:T(8,128)(2,1)S(1)}, bf16[256,256]{1,0:T(8,128)(2,1)S(1)}, u32[]{:S(2)}, u32[]{:S(2)}) collective-permute-start(bf16[256,256]{1,0:T(8,128)(2,1)S(1)} %collective-permute-done.refs_4_), channel_id=1, source_target_pairs={{0,6},{1,7},{2,4},{3,5},{4,2},{5,3},{6,0},{7,1},{8,14},{9,15},{10,... | collective-permute-start | bytes 393224 | tf_op jit(solution)/shard_map/ppermute | solution.py:32
  21.2 11.0 %collective-permute-start.7 = (f32[256,1]{1,0:T(8,128)S(1)}, f32[256,1]{1,0:T(8,128)S(1)}, u32[]{:S(2)}, u32[]{:S(2)}) collective-permute-start(f32[256,1]{1,0:T(8,128)S(1)} %add.101), channel_id=1, source_target_pairs={{0,4},{1,5},{2,6},{3,7},{4,0},{5,1},{6,2},{7,3},{8,12},{9,13},{10,... | collective-permute-start | bytes 3080 | tf_op jit(solution)/shard_map/ppermute | solution.py:32
  38.2 6.8 %collective-permute-start.13 = (bf16[256,256]{1,0:T(8,128)(2,1)}, bf16[256,256]{1,0:T(8,128)(2,1)S(1)}, u32[]{:S(2)}, u32[]{:S(2)}) collective-permute-start(bf16[256,256]{1,0:T(8,128)(2,1)} %get-tuple-element.94), channel_id=1, source_target_pairs={{0,16},{8,24},{16,0},{24,8},{1,17},{9,25},{17,1},{25,9},{2,18},{10... | collective-permute-start | bytes 393224 | tf_op jit(solution)/shard_map/ppermute | solution.py:32
  45.1 25.3 %collective-permute-start.14 = (bf16[2,256,256]{2,1,0:T(8,128)(2,1)}, bf16[2,256,256]{2,1,0:T(8,128)(2,1)S(1)}, u32[]{:S(2)}, u32[]{:S(2)}) collective-permute-start(bf16[2,256,256]{2,1,0:T(8,128)(2,1)} %get-tuple-element.96), channel_id=1, source_target_pairs={{0,16},{8,24},{16,0},{24,8},{1,17},{9,25},{17,1},{25,9},{2,18},{10... | collective-permute-start | bytes 786440 | tf_op jit(solution)/shard_map/ppermute | solution.py:32
  46.0 24.4 %collective-permute-start.15 = (bf16[512,256]{1,0:T(8,128)(2,1)S(1)}, bf16[512,256]{1,0:T(8,128)(2,1)S(1)}, u32[]{:S(2)}, u32[]{:S(2)}) collective-permute-start(bf16[512,256]{1,0:T(8,128)(2,1)S(1)} %copy-done.5), channel_id=1, source_target_pairs={{0,8},{8,0},{16,24},{24,16},{1,9},{9,1},{17,25},{25,17},{2,10},{10... | collective-permute-start | bytes 786440 | tf_op jit(solution)/shard_map/ppermute | solution.py:32
  50.1 20.3 %collective-permute-start.16 = (bf16[512,256]{1,0:T(8,128)(2,1)S(1)}, bf16[512,256]{1,0:T(8,128)(2,1)S(1)}, u32[]{:S(2)}, u32[]{:S(2)}) collective-permute-start(bf16[512,256]{1,0:T(8,128)(2,1)S(1)} %collective-permute-done.4.refs_13_), channel_id=1, source_target_pairs={{0,8},{8,0},{16,24},{24,16},{1,9},{9,1},{17,25},{25,17},{2,10},{10... | collective-permute-start | bytes 786440 | tf_op jit(solution)/shard_map/ppermute | solution.py:32
  79.1 5.6 %collective-permute-start.18 = (bf16[256,256]{1,0:T(8,128)(2,1)S(1)}, bf16[256,256]{1,0:T(8,128)(2,1)S(1)}, u32[]{:S(2)}, u32[]{:S(2)}) collective-permute-start(bf16[256,256]{1,0:T(8,128)(2,1)S(1)} %get-tuple-element.183), channel_id=1, source_target_pairs={{0,2},{1,3},{2,0},{3,1},{4,6},{5,7},{6,4},{7,5},{8,10},{9,11},{10,... | collective-permute-start | bytes 393224 | tf_op jit(solution)/shard_map/ppermute | solution.py:32
  80.5 8.7 %collective-permute-start.19 = (bf16[256,256]{1,0:T(8,128)(2,1)S(1)}, bf16[256,256]{1,0:T(8,128)(2,1)S(1)}, u32[]{:S(2)}, u32[]{:S(2)}) collective-permute-start(bf16[256,256]{1,0:T(8,128)(2,1)S(1)} %get-tuple-element.185), channel_id=1, source_target_pairs={{0,4},{1,5},{2,6},{3,7},{4,0},{5,1},{6,2},{7,3},{8,12},{9,13},{10,... | collective-permute-start | bytes 393224 | tf_op jit(solution)/shard_map/ppermute | solution.py:32
  82.9 6.3 %collective-permute-start.20 = (bf16[256,256]{1,0:T(8,128)(2,1)S(1)}, bf16[256,256]{1,0:T(8,128)(2,1)S(1)}, u32[]{:S(2)}, u32[]{:S(2)}) collective-permute-start(bf16[256,256]{1,0:T(8,128)(2,1)S(1)} %get-tuple-element.184), channel_id=1, source_target_pairs={{0,6},{1,7},{2,4},{3,5},{4,2},{5,3},{6,0},{7,1},{8,14},{9,15},{10,... | collective-permute-start | bytes 393224 | tf_op jit(solution)/shard_map/ppermute | solution.py:32
  89.3 7.3 %collective-permute-start.28 = (bf16[256,256]{1,0:T(8,128)(2,1)S(1)}, bf16[256,256]{1,0:T(8,128)(2,1)S(1)}, u32[]{:S(2)}, u32[]{:S(2)}) collective-permute-start(bf16[256,256]{1,0:T(8,128)(2,1)S(1)} %fusion.4.refs_6_), channel_id=1, source_target_pairs={{0,16},{8,24},{16,0},{24,8},{1,17},{9,25},{17,1},{25,9},{2,18},{10... | collective-permute-start | bytes 393224 | tf_op jit(solution)/shard_map/ppermute | solution.py:32
  89.4 9.7 %collective-permute-start.22 = (bf16[256,256]{1,0:T(8,128)(2,1)S(1)}, bf16[256,256]{1,0:T(8,128)(2,1)S(1)}, u32[]{:S(2)}, u32[]{:S(2)}) collective-permute-start(bf16[256,256]{1,0:T(8,128)(2,1)S(1)} %fusion.4.refs_6_), channel_id=1, source_target_pairs={{0,2},{1,3},{2,0},{3,1},{4,6},{5,7},{6,4},{7,5},{8,10},{9,11},{10,... | collective-permute-start | bytes 393224 | tf_op jit(solution)/shard_map/ppermute | solution.py:32
  90.9 10.7 %collective-permute-start.24 = (bf16[256,256]{1,0:T(8,128)(2,1)S(1)}, bf16[256,256]{1,0:T(8,128)(2,1)S(1)}, u32[]{:S(2)}, u32[]{:S(2)}) collective-permute-start(bf16[256,256]{1,0:T(8,128)(2,1)S(1)} %fusion.4.refs_6_), channel_id=1, source_target_pairs={{0,4},{1,5},{2,6},{3,7},{4,0},{5,1},{6,2},{7,3},{8,12},{9,13},{10,... | collective-permute-start | bytes 393224 | tf_op jit(solution)/shard_map/ppermute | solution.py:32
  91.6 11.2 %collective-permute-start.26 = (bf16[256,256]{1,0:T(8,128)(2,1)S(1)}, bf16[256,256]{1,0:T(8,128)(2,1)S(1)}, u32[]{:S(2)}, u32[]{:S(2)}) collective-permute-start(bf16[256,256]{1,0:T(8,128)(2,1)S(1)} %fusion.4.refs_6_), channel_id=1, source_target_pairs={{0,6},{1,7},{2,4},{3,5},{4,2},{5,3},{6,0},{7,1},{8,14},{9,15},{10,... | collective-permute-start | bytes 393224 | tf_op jit(solution)/shard_map/ppermute | solution.py:32
  92.9 10.8 %collective-permute-start.21 = (bf16[256,256]{1,0:T(8,128)(2,1)S(1)}, bf16[256,256]{1,0:T(8,128)(2,1)S(1)}, u32[]{:S(2)}, u32[]{:S(2)}) collective-permute-start(bf16[256,256]{1,0:T(8,128)(2,1)S(1)} %fusion.4.refs_6_), channel_id=1, source_target_pairs={{0,1},{1,0},{2,3},{3,2},{4,5},{5,4},{6,7},{7,6},{8,9},{9,8},{10,11... | collective-permute-start | bytes 393224 | tf_op jit(solution)/shard_map/ppermute | solution.py:32
  96.6 8.4 %collective-permute-start.36 = (bf16[256,256]{1,0:T(8,128)(2,1)S(1)}, bf16[256,256]{1,0:T(8,128)(2,1)S(1)}, u32[]{:S(2)}, u32[]{:S(2)}) collective-permute-start(bf16[256,256]{1,0:T(8,128)(2,1)S(1)} %fusion.4.refs_6_), channel_id=1, source_target_pairs={{0,8},{8,0},{16,24},{24,16},{1,9},{9,1},{17,25},{25,17},{2,10},{10... | collective-permute-start | bytes 393224 | tf_op jit(solution)/shard_map/ppermute | solution.py:32
  99.0 7.1 %collective-permute-start.37 = (bf16[256,256]{1,0:T(8,128)(2,1)S(1)}, bf16[256,256]{1,0:T(8,128)(2,1)S(1)}, u32[]{:S(2)}, u32[]{:S(2)}) collective-permute-start(bf16[256,256]{1,0:T(8,128)(2,1)S(1)} %fusion.4.refs_6_), channel_id=1, source_target_pairs={{0,24},{8,16},{16,8},{24,0},{1,25},{9,17},{17,9},{25,1},{2,26},{10... | collective-permute-start | bytes 393224 | tf_op jit(solution)/shard_map/ppermute | solution.py:32
  101.6 5.6 %collective-permute-start.30 = (bf16[256,256]{1,0:T(8,128)(2,1)S(1)}, bf16[256,256]{1,0:T(8,128)(2,1)S(1)}, u32[]{:S(2)}, u32[]{:S(2)}) collective-permute-start(bf16[256,256]{1,0:T(8,128)(2,1)S(1)} %collective-permute-done.28.refs_14_), channel_id=1, source_target_pairs={{0,2},{1,3},{2,0},{3,1},{4,6},{5,7},{6,4},{7,5},{8,10},{9,11},{10,... | collective-permute-start | bytes 393224 | tf_op jit(solution)/shard_map/ppermute | solution.py:32
  102.8 5.0 %collective-permute-start.32 = (bf16[256,256]{1,0:T(8,128)(2,1)S(1)}, bf16[256,256]{1,0:T(8,128)(2,1)S(1)}, u32[]{:S(2)}, u32[]{:S(2)}) collective-permute-start(bf16[256,256]{1,0:T(8,128)(2,1)S(1)} %collective-permute-done.28.refs_14_), channel_id=1, source_target_pairs={{0,4},{1,5},{2,6},{3,7},{4,0},{5,1},{6,2},{7,3},{8,12},{9,13},{10,... | collective-permute-start | bytes 393224 | tf_op jit(solution)/shard_map/ppermute | solution.py:32
  103.7 5.9 %collective-permute-start.34 = (bf16[256,256]{1,0:T(8,128)(2,1)S(1)}, bf16[256,256]{1,0:T(8,128)(2,1)S(1)}, u32[]{:S(2)}, u32[]{:S(2)}) collective-permute-start(bf16[256,256]{1,0:T(8,128)(2,1)S(1)} %collective-permute-done.28.refs_14_), channel_id=1, source_target_pairs={{0,6},{1,7},{2,4},{3,5},{4,2},{5,3},{6,0},{7,1},{8,14},{9,15},{10,... | collective-permute-start | bytes 393224 | tf_op jit(solution)/shard_map/ppermute | solution.py:32
  105.1 4.5 %collective-permute-start.29 = (bf16[256,256]{1,0:T(8,128)(2,1)S(1)}, bf16[256,256]{1,0:T(8,128)(2,1)S(1)}, u32[]{:S(2)}, u32[]{:S(2)}) collective-permute-start(bf16[256,256]{1,0:T(8,128)(2,1)S(1)} %collective-permute-done.28.refs_14_), channel_id=1, source_target_pairs={{0,1},{1,0},{2,3},{3,2},{4,5},{5,4},{6,7},{7,6},{8,9},{9,8},{10,11... | collective-permute-start | bytes 393224 | tf_op jit(solution)/shard_map/ppermute | solution.py:32
  106.1 4.0 %collective-permute-start.23 = (bf16[256,256]{1,0:T(8,128)(2,1)S(1)}, bf16[256,256]{1,0:T(8,128)(2,1)S(1)}, u32[]{:S(2)}, u32[]{:S(2)}) collective-permute-start(bf16[256,256]{1,0:T(8,128)(2,1)S(1)} %collective-permute-done.22.refs_8_), channel_id=1, source_target_pairs={{0,1},{1,0},{2,3},{3,2},{4,5},{5,4},{6,7},{7,6},{8,9},{9,8},{10,11... | collective-permute-start | bytes 393224 | tf_op jit(solution)/shard_map/ppermute | solution.py:32
  107.1 3.7 %collective-permute-start.25 = (bf16[256,256]{1,0:T(8,128)(2,1)S(1)}, bf16[256,256]{1,0:T(8,128)(2,1)S(1)}, u32[]{:S(2)}, u32[]{:S(2)}) collective-permute-start(bf16[256,256]{1,0:T(8,128)(2,1)S(1)} %collective-permute-done.24.refs_10_), channel_id=1, source_target_pairs={{0,1},{1,0},{2,3},{3,2},{4,5},{5,4},{6,7},{7,6},{8,9},{9,8},{10,11... | collective-permute-start | bytes 393224 | tf_op jit(solution)/shard_map/ppermute | solution.py:32
  107.8 3.1 %collective-permute-start.27 = (bf16[256,256]{1,0:T(8,128)(2,1)S(1)}, bf16[256,256]{1,0:T(8,128)(2,1)S(1)}, u32[]{:S(2)}, u32[]{:S(2)}) collective-permute-start(bf16[256,256]{1,0:T(8,128)(2,1)S(1)} %collective-permute-done.26.refs_12_), channel_id=1, source_target_pairs={{0,1},{1,0},{2,3},{3,2},{4,5},{5,4},{6,7},{7,6},{8,9},{9,8},{10,11... | collective-permute-start | bytes 393224 | tf_op jit(solution)/shard_map/ppermute | solution.py:32
  111.5 16.6 %collective-permute-start.38 = (bf16[2,256,256]{2,1,0:T(8,128)(2,1)S(1)}, bf16[2,256,256]{2,1,0:T(8,128)(2,1)S(1)}, u32[]{:S(2)}, u32[]{:S(2)}) collective-permute-start(bf16[2,256,256]{2,1,0:T(8,128)(2,1)S(1)} %pad_maximum_fusion.refs_6_), channel_id=1, source_target_pairs={{0,2},{1,3},{2,0},{3,1},{4,6},{5,7},{6,4},{7,5},{8,10},{9,11},{10,... | collective-permute-start | bytes 786440 | tf_op jit(solution)/shard_map/ppermute | solution.py:32
  112.6 15.5 %collective-permute-start.39 = (bf16[2,256,256]{2,1,0:T(8,128)(2,1)S(1)}, bf16[2,256,256]{2,1,0:T(8,128)(2,1)S(1)}, u32[]{:S(2)}, u32[]{:S(2)}) collective-permute-start(bf16[2,256,256]{2,1,0:T(8,128)(2,1)S(1)} %pad_maximum_fusion.refs_6_), channel_id=1, source_target_pairs={{0,4},{1,5},{2,6},{3,7},{4,0},{5,1},{6,2},{7,3},{8,12},{9,13},{10,... | collective-permute-start | bytes 786440 | tf_op jit(solution)/shard_map/ppermute | solution.py:32
  113.4 14.8 %collective-permute-start.40 = (bf16[2,256,256]{2,1,0:T(8,128)(2,1)S(1)}, bf16[2,256,256]{2,1,0:T(8,128)(2,1)S(1)}, u32[]{:S(2)}, u32[]{:S(2)}) collective-permute-start(bf16[2,256,256]{2,1,0:T(8,128)(2,1)S(1)} %pad_maximum_fusion.refs_6_), channel_id=1, source_target_pairs={{0,6},{1,7},{2,4},{3,5},{4,2},{5,3},{6,0},{7,1},{8,14},{9,15},{10,... | collective-permute-start | bytes 786440 | tf_op jit(solution)/shard_map/ppermute | solution.py:32
  128.1 3.6 %collective-permute-start.45 = (bf16[4,2,256,256]{3,2,1,0:T(8,128)(2,1)}, bf16[4,2,256,256]{3,2,1,0:T(8,128)(2,1)S(1)}, u32[]{:S(2)}, u32[]{:S(2)}) collective-permute-start(bf16[4,2,256,256]{3,2,1,0:T(8,128)(2,1)} %get-tuple-element.134), channel_id=1, source_target_pairs={{0,1},{1,0},{2,3},{3,2},{4,5},{5,4},{6,7},{7,6},{8,9},{9,8},{10,11... | collective-permute-start | bytes 3145736 | tf_op jit(solution)/shard_map/ppermute | solution.py:32
  128.2 5.1 %collective-permute-start.41 = (bf16[2,256,256]{2,1,0:T(8,128)(2,1)S(1)}, bf16[2,256,256]{2,1,0:T(8,128)(2,1)S(1)}, u32[]{:S(2)}, u32[]{:S(2)}) collective-permute-start(bf16[2,256,256]{2,1,0:T(8,128)(2,1)S(1)} %pad_maximum_fusion.refs_6_), channel_id=1, source_target_pairs={{0,1},{1,0},{2,3},{3,2},{4,5},{5,4},{6,7},{7,6},{8,9},{9,8},{10,11... | collective-permute-start | bytes 786440 | tf_op jit(solution)/shard_map/ppermute | solution.py:32
  128.7 4.7 %collective-permute-start.42 = (bf16[2,256,256]{2,1,0:T(8,128)(2,1)S(1)}, bf16[2,256,256]{2,1,0:T(8,128)(2,1)S(1)}, u32[]{:S(2)}, u32[]{:S(2)}) collective-permute-start(bf16[2,256,256]{2,1,0:T(8,128)(2,1)S(1)} %collective-permute-done.38.refs_8_), channel_id=1, source_target_pairs={{0,1},{1,0},{2,3},{3,2},{4,5},{5,4},{6,7},{7,6},{8,9},{9,8},{10,11... | collective-permute-start | bytes 786440 | tf_op jit(solution)/shard_map/ppermute | solution.py:32
  128.8 4.6 %collective-permute-start.43 = (bf16[2,256,256]{2,1,0:T(8,128)(2,1)S(1)}, bf16[2,256,256]{2,1,0:T(8,128)(2,1)S(1)}, u32[]{:S(2)}, u32[]{:S(2)}) collective-permute-start(bf16[2,256,256]{2,1,0:T(8,128)(2,1)S(1)} %collective-permute-done.39.refs_10_), channel_id=1, source_target_pairs={{0,1},{1,0},{2,3},{3,2},{4,5},{5,4},{6,7},{7,6},{8,9},{9,8},{10,11... | collective-permute-start | bytes 786440 | tf_op jit(solution)/shard_map/ppermute | solution.py:32
  129.2 4.2 %collective-permute-start.44 = (bf16[2,256,256]{2,1,0:T(8,128)(2,1)S(1)}, bf16[2,256,256]{2,1,0:T(8,128)(2,1)S(1)}, u32[]{:S(2)}, u32[]{:S(2)}) collective-permute-start(bf16[2,256,256]{2,1,0:T(8,128)(2,1)S(1)} %collective-permute-done.40.refs_12_), channel_id=1, source_target_pairs={{0,1},{1,0},{2,3},{3,2},{4,5},{5,4},{6,7},{7,6},{8,9},{9,8},{10,11... | collective-permute-start | bytes 786440 | tf_op jit(solution)/shard_map/ppermute | solution.py:32
  133.5 16.5 %collective-permute-start.46 = (bf16[2,256,256]{2,1,0:T(8,128)(2,1)S(1)}, bf16[2,256,256]{2,1,0:T(8,128)(2,1)S(1)}, u32[]{:S(2)}, u32[]{:S(2)}) collective-permute-start(bf16[2,256,256]{2,1,0:T(8,128)(2,1)S(1)} %get-tuple-element.145), channel_id=1, source_target_pairs={{0,2},{1,3},{2,0},{3,1},{4,6},{5,7},{6,4},{7,5},{8,10},{9,11},{10,... | collective-permute-start | bytes 786440 | tf_op jit(solution)/shard_map/ppermute | solution.py:32
  134.7 15.3 %collective-permute-start.47 = (bf16[2,256,256]{2,1,0:T(8,128)(2,1)S(1)}, bf16[2,256,256]{2,1,0:T(8,128)(2,1)S(1)}, u32[]{:S(2)}, u32[]{:S(2)}) collective-permute-start(bf16[2,256,256]{2,1,0:T(8,128)(2,1)S(1)} %get-tuple-element.146), channel_id=1, source_target_pairs={{0,4},{1,5},{2,6},{3,7},{4,0},{5,1},{6,2},{7,3},{8,12},{9,13},{10,... | collective-permute-start | bytes 786440 | tf_op jit(solution)/shard_map/ppermute | solution.py:32
  135.4 14.6 %collective-permute-start.48 = (bf16[2,256,256]{2,1,0:T(8,128)(2,1)S(1)}, bf16[2,256,256]{2,1,0:T(8,128)(2,1)S(1)}, u32[]{:S(2)}, u32[]{:S(2)}) collective-permute-start(bf16[2,256,256]{2,1,0:T(8,128)(2,1)S(1)} %get-tuple-element.147), channel_id=1, source_target_pairs={{0,6},{1,7},{2,4},{3,5},{4,2},{5,3},{6,0},{7,1},{8,14},{9,15},{10,... | collective-permute-start | bytes 786440 | tf_op jit(solution)/shard_map/ppermute | solution.py:32
  150.0 2.9 %collective-permute-start.49 = (bf16[4,2,256,256]{3,2,1,0:T(8,128)(2,1)}, bf16[4,2,256,256]{3,2,1,0:T(8,128)(2,1)S(1)}, u32[]{:S(2)}, u32[]{:S(2)}) collective-permute-start(bf16[4,2,256,256]{3,2,1,0:T(8,128)(2,1)} %get-tuple-element.149), channel_id=1, source_target_pairs={{0,1},{1,0},{2,3},{3,2},{4,5},{5,4},{6,7},{7,6},{8,9},{9,8},{10,11... | collective-permute-start | bytes 3145736 | tf_op jit(solution)/shard_map/ppermute | solution.py:32
  150.3 9.5 %collective-permute-start.52 = (bf16[256,256]{1,0:T(8,128)(2,1)S(1)}, bf16[256,256]{1,0:T(8,128)(2,1)S(1)}, u32[]{:S(2)}, u32[]{:S(2)}) collective-permute-start(bf16[256,256]{1,0:T(8,128)(2,1)S(1)} %fusion.15), channel_id=1, source_target_pairs={{0,16},{8,24},{16,0},{24,8},{1,17},{9,25},{17,1},{25,9},{2,18},{10... | collective-permute-start | bytes 393224 | tf_op jit(solution)/shard_map/ppermute | solution.py:32
  153.4 8.4 %collective-permute-start.51 = (bf16[2,256,256]{2,1,0:T(8,128)(2,1)S(1)}, bf16[2,256,256]{2,1,0:T(8,128)(2,1)S(1)}, u32[]{:S(2)}, u32[]{:S(2)}) collective-permute-start(bf16[2,256,256]{2,1,0:T(8,128)(2,1)S(1)} %pad_maximum_fusion.2), channel_id=1, source_target_pairs={{0,4},{1,5},{2,6},{3,7},{4,0},{5,1},{6,2},{7,3},{8,12},{9,13},{10,... | collective-permute-start | bytes 786440 | tf_op jit(solution)/shard_map/ppermute | solution.py:32
  154.6 8.1 %collective-permute-start.50 = (bf16[2,256,256]{2,1,0:T(8,128)(2,1)S(1)}, bf16[2,256,256]{2,1,0:T(8,128)(2,1)S(1)}, u32[]{:S(2)}, u32[]{:S(2)}) collective-permute-start(bf16[2,256,256]{2,1,0:T(8,128)(2,1)S(1)} %pad_maximum_fusion.1), channel_id=1, source_target_pairs={{0,2},{1,3},{2,0},{3,1},{4,6},{5,7},{6,4},{7,5},{8,10},{9,11},{10,... | collective-permute-start | bytes 786440 | tf_op jit(solution)/shard_map/ppermute | solution.py:32
  162.8 5.0 %collective-permute-start.53 = (bf16[1,256,256]{2,1,0:T(8,128)(2,1)S(1)}, bf16[1,256,256]{2,1,0:T(8,128)(2,1)S(1)}, u32[]{:S(2)}, u32[]{:S(2)}) collective-permute-start(bf16[1,256,256]{2,1,0:T(8,128)(2,1)S(1)} %get-tuple-element.155), channel_id=1, source_target_pairs={{0,4},{1,5},{2,6},{3,7},{4,0},{5,1},{6,2},{7,3},{8,12},{9,13},{10,... | collective-permute-start | bytes 393224 | tf_op jit(solution)/shard_map/ppermute | solution.py:32
  163.8 5.0 %collective-permute-start.55 = (bf16[1,256,256]{2,1,0:T(8,128)(2,1)S(1)}, bf16[1,256,256]{2,1,0:T(8,128)(2,1)S(1)}, u32[]{:S(2)}, u32[]{:S(2)}) collective-permute-start(bf16[1,256,256]{2,1,0:T(8,128)(2,1)S(1)} %get-tuple-element.156), channel_id=1, source_target_pairs={{0,2},{1,3},{2,0},{3,1},{4,6},{5,7},{6,4},{7,5},{8,10},{9,11},{10,... | collective-permute-start | bytes 393224 | tf_op jit(solution)/shard_map/ppermute | solution.py:32
  168.9 5.5 %collective-permute-start.54 = (bf16[256,256]{1,0:T(8,128)(2,1)S(1)}, bf16[256,256]{1,0:T(8,128)(2,1)S(1)}, u32[]{:S(2)}, u32[]{:S(2)}) collective-permute-start(bf16[256,256]{1,0:T(8,128)(2,1)S(1)} %get-tuple-element.166), channel_id=1, source_target_pairs={{0,8},{8,0},{16,24},{24,16},{1,9},{9,1},{17,25},{25,17},{2,10},{10... | collective-permute-start | bytes 393224 | tf_op jit(solution)/shard_map/ppermute | solution.py:32
  169.3 6.9 %collective-permute-start.56 = (bf16[256,256]{1,0:T(8,128)(2,1)S(1)}, bf16[256,256]{1,0:T(8,128)(2,1)S(1)}, u32[]{:S(2)}, u32[]{:S(2)}) collective-permute-start(bf16[256,256]{1,0:T(8,128)(2,1)S(1)} %get-tuple-element.167), channel_id=1, source_target_pairs={{0,24},{8,16},{16,8},{24,0},{1,25},{9,17},{17,9},{25,1},{2,26},{10... | collective-permute-start | bytes 393224 | tf_op jit(solution)/shard_map/ppermute | solution.py:32
  (54 other events, 386.6 us)
